TPU v7x, 32 devices: a whole 2x2x4 slice. The times are simulated.
32 devices in a mesh: groups: 2 (over y), image: 2 (over x), space: 4 (over z), yslab: 2 (over core).
Axes of the slice: x: 2, y: 2, z: 4, core: 2. Of those that a mesh axis runs over, the one named last changes fastest.
Arguments:
- images: float32 [8, 64, 128, 256], P(('groups', 'image'), 'space', 'yslab'), parts along dimension 0, may hold values from -4 to 4, as said below
Outputs:
- new_band: float32 [8, 64, 128, 256], P(('groups', 'image'), 'space', 'yslab'), parts along dimension 0
- parallel: float32 [8], P(('groups', 'image')), parts along dimension 0
There are 2 independent parts, one for each index of `groups`. A program takes and returns all parts, laid end to end along the dimension named above; each array names one. Nothing has to cross between parts.
Inputs may be any that keep to these rules, and one draw needn't show every extreme that they name: `images`: concentration fields of a path between two end states.
All inputs are finite; a program needn't handle non-finite values.
Results may differ from a plain program's by a relative error of at most 0.0001.
Values sent between devices are 32-bit elements; how exact they have to be, the bound alone decides.
No kernel may reach another device: no remote copies, remote signals or barrier semaphores. Data moves between devices by JAX's collectives and lax.ppermute only.
A program may use at most 64 MiB of HBM per device.

v0:
```python
import jax
import jax.numpy as jnp
from jax import lax
from jax.sharding import PartitionSpec as P

ITERS = 2


GRADIENT_COEF = 1.0
MOBILITY = 0.004
SPRING_K = 1.0
STEP_SIZE = 0.5
EPSILON = 1e-06


def passed_along(array, axis, by):
    peers = lax.axis_size(axis)
    pairs = [(i, i + by) for i in range(peers) if 0 <= i + by < peers]
    return lax.ppermute(array, axis, pairs)


def extended(cells, sides, width):
    for axis, dim in sides:
        count = lax.axis_size(axis)
        head = lax.slice_in_dim(cells, 0, width, axis=dim)
        tail = lax.slice_in_dim(cells, cells.shape[dim] - width, cells.shape[dim], axis=dim)
        cells = jnp.concatenate(
            [
                lax.ppermute(tail, axis, [(i, (i + 1) % count) for i in range(count)]),
                cells,
                lax.ppermute(head, axis, [((i + 1) % count, i) for i in range(count)]),
            ],
            axis=dim,
        )
    return cells


def stencil(padded):
    middle = padded[:, 1:-1, 1:-1]
    neighbours = padded[:, 2:, 1:-1] + padded[:, :-2, 1:-1]
    neighbours = neighbours + padded[:, 1:-1, 2:] + padded[:, 1:-1, :-2]
    neighbours = neighbours + jnp.roll(middle, -1, 3) + jnp.roll(middle, 1, 3)
    return neighbours - 6.0 * middle


def sum_cells(field):
    return jnp.sum(field, axis=(1, 2, 3))


def body(images):
    current = images
    per_device = current.shape[0]
    total_images = per_device * lax.axis_size("image")
    cell_total = float(
        current.shape[1]
        * lax.axis_size("space")
        * current.shape[2]
        * lax.axis_size("yslab")
        * current.shape[3]
    )
    image_ids = lax.axis_index("image") * per_device + jnp.arange(per_device, dtype=jnp.int32)
    interior = (image_ids > 0) & (image_ids < total_images - 1)
    parallel = jnp.zeros((per_device,), jnp.float32)
    for iteration in range(ITERS):
        next_first = passed_along(current[0], "image", -1)
        prev_last = passed_along(current[-1], "image", 1)
        ahead = jnp.concatenate([current[1:], next_first[None]], 0)
        behind = jnp.concatenate([prev_last[None], current[:-1]], 0)
        forward = ahead - current
        backward = current - behind
        tangent = forward + backward
        plus_sq, minus_sq, tangent_sq = lax.psum(
            (
                sum_cells(forward * forward),
                sum_cells(backward * backward),
                sum_cells(tangent * tangent),
            ),
            ("space", "yslab"),
        )
        wide_pad = extended(current, (("space", 1), ("yslab", 2)), 2)
        inner_field = wide_pad[:, 1:-1, 1:-1]
        potential = (
            inner_field * inner_field * inner_field
            - inner_field
            - GRADIENT_COEF * stencil(wide_pad)
        )
        driving = MOBILITY * stencil(potential)
        parallel_sum = lax.psum(sum_cells(driving * tangent), ("space", "yslab"))
        project_coef = parallel_sum / (tangent_sq + EPSILON)
        spring = (
            SPRING_K * (jnp.sqrt(plus_sq) - jnp.sqrt(minus_sq)) / jnp.sqrt(tangent_sq + EPSILON)
        )
        update = (
            driving
            - project_coef[:, None, None, None] * tangent
            + spring[:, None, None, None] * tangent
        )
        current = jnp.where(interior[:, None, None, None], current + STEP_SIZE * update, current)
        parallel = jnp.where(
            interior, parallel_sum / jnp.sqrt((tangent_sq + EPSILON) * cell_total), jnp.float32(0.0)
        )
    return (current, parallel)


def solution(mesh):
    in_specs = (P(("groups", "image"), "space", "yslab", None),)
    out_specs = (P(("groups", "image"), "space", "yslab", None), P(("groups", "image")))
    return jax.shard_map(body, mesh=mesh, in_specs=in_specs, out_specs=out_specs, check_vma=False)
```

profile of v0, /device:TPU:0, one launch (start us, length us, event | category | flops | bytes accessed | tf_op | source)
XLA Modules:
  0.0 129.9 jit_solution(13667418233148986394)
XLA Ops:
  0.6 1.9 %fusion.39 = (f32[2,2,64,256]{3,2,1,0:T(8,128)}, f32[2,2,64,256]{3,2,1,0:T(8,128)}) fusion(f32[2,16,64,256]{3,2,1,0:T(8,128)} %param.1), kind=kLoop, calls=%fused_computation.87 | loop fusion | bytes 1048576 | tf_op jit(solution)/shard_map/slice | solution.py:25
  2.5 3.0 %collective-permute-start = (f32[2,2,64,256]{3,2,1,0:T(8,128)}, f32[2,2,64,256]{3,2,1,0:T(8,128)}, u32[]{:S(2)}, u32[]{:S(2)}) collective-permute-start(f32[2,2,64,256]{3,2,1,0:T(8,128)} %get-tuple-element.61), channel_id=1, source_target_pairs={{0,2},{2,4},{4,6},{6,0},{1,3},{3,5},{5,7},{7,1},{8,10},{10,12},{12... | collective-permute-start | bytes 786440 | tf_op jit(solution)/shard_map/ppermute | solution.py:29
  5.5 2.0 %collective-permute-start.1 = (f32[2,2,64,256]{3,2,1,0:T(8,128)}, f32[2,2,64,256]{3,2,1,0:T(8,128)S(1)}, u32[]{:S(2)}, u32[]{:S(2)}) collective-permute-start(f32[2,2,64,256]{3,2,1,0:T(8,128)} %get-tuple-element.60), channel_id=1, source_target_pairs={{2,0},{4,2},{6,4},{0,6},{3,1},{5,3},{7,5},{1,7},{10,8},{12,10},{14... | collective-permute-start | bytes 786440 | tf_op jit(solution)/shard_map/ppermute | solution.py:31
  7.6 3.5 %fusion.38 = (f32[1,16,64,256]{3,2,1,0:T(8,128)S(1)}, f32[16,64,256]{2,1,0:T(8,128)}, f32[16,64,256]{2,1,0:T(8,128)}, f32[1,16,64,256]{3,2,1,0:T(8,128)}) fusion(f32[2,16,64,256]{3,2,1,0:T(8,128)} %param.1), kind=kLoop, calls=%fused_computation.86 | loop fusion | bytes 6291456 | tf_op jit(solution)/shard_map/slice | solution.py:67
  11.0 1.3 collective-permute-start.4
  12.3 6.5 %collective-permute-start.5 = (f32[16,64,256]{2,1,0:T(8,128)}, f32[16,64,256]{2,1,0:T(8,128)}, u32[]{:S(2)}, u32[]{:S(2)}) collective-permute-start(f32[16,64,256]{2,1,0:T(8,128)} %get-tuple-element.58), channel_id=1, source_target_pairs={{0,8},{1,9},{2,10},{3,11},{4,12},{5,13},{6,14},{7,15},{16,24},{17,... | collective-permute-start | bytes 3145736 | tf_op jit(solution)/shard_map/ppermute | solution.py:19
  18.8 0.0 collective-permute-done
  18.9 1.0 constant_dynamic-update-slice_fusion.2
  19.8 0.2 constant_dynamic-update-slice_fusion.1
  20.1 0.0 collective-permute-done.1
  20.1 0.1 fusion.35
  20.2 0.1 collective-permute-start.2
  20.3 0.5 collective-permute-start.3
  20.8 0.8 collective-permute-done.2
  21.5 0.2 collective-permute-done.3
  21.7 0.4 pad_maximum_fusion
  22.1 0.9 fusion.30
  23.0 0.4 fusion.29
  23.4 3.1 %fusion = f32[2,18,66,256]{3,2,1,0:T(8,128)S(1)} fusion(f32[2,20,64,256]{3,2,1,0:T(8,128)S(1)} %constant_dynamic-update-slice_fusion, f32[2,20,2,256]{3,2,1,0:T(2,128)S(1)} %collective-permute-done.2, f32[2,20,2,256]{3,2,1,0:T(2,128)S(1)} %collective-permute-done.3, f32[2,20,68,256]{3,2,1,0:T(8,128)S(1)} %pad_maximum_fusion, ...), kind=kLoop, calls=%fused_computation.6 | loop fusion | flops 9123840 | bytes 17383424 | tf_op jit(solution)/shard_map/sub | solution.py:83
  26.5 0.4 fusion.34
  26.9 0.8 fusion.33
  27.8 10.1 %collective-permute-done.4 = f32[16,64,256]{2,1,0:T(8,128)} collective-permute-done((f32[16,64,256]{2,1,0:T(8,128)}, f32[16,64,256]{2,1,0:T(8,128)}, u32[]{:S(2)}, u32[]{:S(2)}) %collective-permute-start.4) | collective-permute-done | bytes 1048608 | tf_op jit(solution)/shard_map/ppermute | solution.py:19
  37.9 2.2 %collective-permute-done.5 = f32[16,64,256]{2,1,0:T(8,128)} collective-permute-done((f32[16,64,256]{2,1,0:T(8,128)}, f32[16,64,256]{2,1,0:T(8,128)}, u32[]{:S(2)}, u32[]{:S(2)}) %collective-permute-start.5) | collective-permute-done | bytes 1048608 | tf_op jit(solution)/shard_map/ppermute | solution.py:19
  40.0 5.6 %multiply_reduce_fusion.5 = (f32[2]{0:T(128)S(1)}, f32[2]{0:T(128)S(1)}, f32[2]{0:T(128)S(1)}, f32[2]{0:T(128)S(1)}, f32[2,16,64,256]{3,2,1,0:T(8,128)}, /*index=5*/f32[2,16,64,256]{3,2,1,0:T(8,128)}) fusion(f32[2,16,64,256]{3,2,1,0:T(8,128)S(1)} %copy-done, f32[1,16,64,256]{3,2,1,0:T(8,128)} %bitcast.1, f32[1,16,64,256]{3,2,1,0:T(8,128)S(1)} %get-tuple-element.56, ...), kind=kLoop, calls=%fused_computation.53 | loop fusion | flops 12058616 | bytes 25165856 | tf_op jit(solution)/shard_map/reduce_sum | solution.py:47
  45.6 13.6 %all-reduce.1 = (f32[2]{0:T(128)S(1)}, f32[2]{0:T(128)S(1)}, f32[2]{0:T(128)S(1)}, f32[2]{0:T(128)S(1)}) all-reduce(f32[2]{0:T(128)S(1)} %get-tuple-element.9, f32[2]{0:T(128)S(1)} %get-tuple-element.8, f32[2]{0:T(128)S(1)} %get-tuple-element.26, ...), channel_id=1, replica_groups=mesh['groups'=2,'image'=2,'space'=4,'yslab'=2] {'space','yslab'}, use_global_device_ids=true, to_apply=%region_7.8 | all-reduce | flops 8 | bytes 64 | tf_op jit(solution)/shard_map/psum | solution.py:72
  59.2 3.6 %add_select_fusion.1 = f32[2,16,64,256]{3,2,1,0:T(8,128)S(1)} fusion(f32[2,16,64,256]{3,2,1,0:T(8,128)} %param.1, f32[2,16,64,256]{3,2,1,0:T(8,128)} %get-tuple-element.28, f32[2,16,64,256]{3,2,1,0:T(8,128)} %get-tuple-element.29, f32[2]{0:T(128)S(1)} %get-tuple-element.66, f32[2]{0:T(128)S(1)} %get-tuple-element.65, pred[2]{0:T(512)(128)(4,1)S(1)} %compare_and_fusion), kind=kLoop, calls=%fused_computation.3 | loop fusion | flops 3670016 | bytes 8388626 | tf_op jit(solution)/shard_map/jit(_where)/select_n | solution.py:98
  62.9 0.1 collective-permute-start.6
  62.9 3.8 %collective-permute-start.7 = (f32[2,2,64,256]{3,2,1,0:T(8,128)S(1)}, f32[2,2,64,256]{3,2,1,0:T(8,128)S(1)}, u32[]{:S(2)}, u32[]{:S(2)}) collective-permute-start(f32[2,2,64,256]{3,2,1,0:T(8,128)S(1)} %get-tuple-element.55), channel_id=1, source_target_pairs={{2,0},{4,2},{6,4},{0,6},{3,1},{5,3},{7,5},{1,7},{10,8},{12,10},{14... | collective-permute-start | bytes 786440 | tf_op jit(solution)/shard_map/ppermute | solution.py:31
  66.8 7.2 %collective-permute-done.6 = f32[2,2,64,256]{3,2,1,0:T(8,128)S(1)} collective-permute-done((f32[2,2,64,256]{3,2,1,0:T(8,128)S(1)}, f32[2,2,64,256]{3,2,1,0:T(8,128)S(1)}, u32[]{:S(2)}, u32[]{:S(2)}) %collective-permute-start.6) | collective-permute-done | bytes 262176 | tf_op jit(solution)/shard_map/ppermute | solution.py:29
  73.9 2.8 %collective-permute-done.7 = f32[2,2,64,256]{3,2,1,0:T(8,128)S(1)} collective-permute-done((f32[2,2,64,256]{3,2,1,0:T(8,128)S(1)}, f32[2,2,64,256]{3,2,1,0:T(8,128)S(1)}, u32[]{:S(2)}, u32[]{:S(2)}) %collective-permute-start.7) | collective-permute-done | bytes 262176 | tf_op jit(solution)/shard_map/ppermute | solution.py:31
  76.7 0.1 pad_maximum_fusion.10
  76.7 0.1 collective-permute-start.8
  76.8 0.5 collective-permute-start.9
  77.3 0.7 fusion.36
  78.0 1.3 collective-permute-start.10
  79.3 4.9 %collective-permute-start.11 = (f32[16,64,256]{2,1,0:T(8,128)S(1)}, f32[16,64,256]{2,1,0:T(8,128)S(1)}, u32[]{:S(2)}, u32[]{:S(2)}) collective-permute-start(f32[16,64,256]{2,1,0:T(8,128)S(1)} %get-tuple-element.52), channel_id=1, source_target_pairs={{0,8},{1,9},{2,10},{3,11},{4,12},{5,13},{6,14},{7,15},{16,24},{17,... | collective-permute-start | bytes 3145736 | tf_op jit(solution)/shard_map/ppermute | solution.py:19
  84.2 0.4 pad_maximum_fusion.1
  84.6 0.9 fusion.28
  85.5 0.4 fusion.27
  85.9 4.2 %fusion.1 = f32[2,18,66,256]{3,2,1,0:T(8,128)S(1)} fusion(f32[2,20,2,256]{3,2,1,0:T(2,128)S(1)} %collective-permute-done.8, f32[2,2,64,256]{3,2,1,0:T(8,128)S(1)} %collective-permute-done.7, f32[2,16,64,256]{3,2,1,0:T(8,128)S(1)} %add_select_fusion.1, f32[2,2,64,256]{3,2,1,0:T(8,128)S(1)} %collective-permute-done.6, ...), kind=kLoop, calls=%fused_computation.7 | loop fusion | flops 11556864 | bytes 17383424 | tf_op jit(solution)/shard_map/sub | solution.py:83
  90.2 0.4 fusion.32
  90.6 0.8 fusion.31
  91.5 13.7 %collective-permute-done.10 = f32[16,64,256]{2,1,0:T(8,128)S(1)} collective-permute-done((f32[16,64,256]{2,1,0:T(8,128)S(1)}, f32[16,64,256]{2,1,0:T(8,128)S(1)}, u32[]{:S(2)}, u32[]{:S(2)}) %collective-permute-start.10) | collective-permute-done | bytes 1048608 | tf_op jit(solution)/shard_map/ppermute | solution.py:19
  105.2 1.2 collective-permute-done.11
  106.4 4.4 %multiply_reduce_fusion.1 = (f32[2]{0:T(128)S(1)}, f32[2]{0:T(128)S(1)}, f32[2]{0:T(128)S(1)}, f32[2]{0:T(128)S(1)}, f32[2,16,64,256]{3,2,1,0:T(8,128)}, /*index=5*/f32[2,16,64,256]{3,2,1,0:T(8,128)}) fusion(f32[2,16,64,256]{3,2,1,0:T(8,128)S(1)} %add_select_fusion.1, f32[1,16,64,256]{3,2,1,0:T(8,128)S(1)} %bitcast.12, ...), kind=kLoop, calls=%fused_computation.49 | loop fusion | flops 12058616 | bytes 25165856 | tf_op jit(solution)/shard_map/reduce_sum | solution.py:47
  110.8 14.3 %all-reduce = (f32[2]{0:T(128)S(1)}, f32[2]{0:T(128)S(1)}, f32[2]{0:T(128)S(1)}, f32[2]{0:T(128)S(1)}) all-reduce(f32[2]{0:T(128)S(1)} %get-tuple-element.5, f32[2]{0:T(128)S(1)} %get-tuple-element.4, f32[2]{0:T(128)S(1)} %get-tuple-element.22, ...), channel_id=1, replica_groups=mesh['groups'=2,'image'=2,'space'=4,'yslab'=2] {'space','yslab'}, use_global_device_ids=true, to_apply=%region_15.16 | all-reduce | flops 8 | bytes 64 | tf_op jit(solution)/shard_map/psum | solution.py:72
  125.1 0.5 multiply_select_fusion
  125.6 4.3 %add_select_fusion = f32[2,16,64,256]{3,2,1,0:T(8,128)} fusion(f32[2,16,64,256]{3,2,1,0:T(8,128)S(1)} %add_select_fusion.1, f32[2,16,64,256]{3,2,1,0:T(8,128)} %get-tuple-element.24, f32[2,16,64,256]{3,2,1,0:T(8,128)} %get-tuple-element.25, f32[2]{0:T(128)S(1)} %get-tuple-element.64, f32[2]{0:T(128)S(1)} %get-tuple-element.63, pred[2]{0:T(512)(128)(4,1)S(1)} %compare_and_fusion), kind=kLoop, calls=%fused_computation.2 | loop fusion | flops 3670016 | bytes 8388626 | tf_op jit(solution)/shard_map/jit(_where)/select_n | solution.py:98
  (10 shorter events, 0.1 us)
Async XLA Ops:
  2.5 16.3 %collective-permute-start = (f32[2,2,64,256]{3,2,1,0:T(8,128)}, f32[2,2,64,256]{3,2,1,0:T(8,128)}, u32[]{:S(2)}, u32[]{:S(2)}) collective-permute-start(f32[2,2,64,256]{3,2,1,0:T(8,128)} %get-tuple-element.61), channel_id=1, source_target_pairs={{0,2},{2,4},{4,6},{6,0},{1,3},{3,5},{5,7},{7,1},{8,10},{10,12},{12... | collective-permute-start | bytes 786440 | tf_op jit(solution)/shard_map/ppermute | solution.py:29
  5.5 14.3 %copy-start = (f32[2,16,64,256]{3,2,1,0:T(8,128)S(1)}, f32[2,16,64,256]{3,2,1,0:T(8,128)}, u32[]{:S(2)}) copy-start(f32[2,16,64,256]{3,2,1,0:T(8,128)} %param.1) | copy-start | bytes 6291460
  5.5 14.5 %collective-permute-start.1 = (f32[2,2,64,256]{3,2,1,0:T(8,128)}, f32[2,2,64,256]{3,2,1,0:T(8,128)S(1)}, u32[]{:S(2)}, u32[]{:S(2)}) collective-permute-start(f32[2,2,64,256]{3,2,1,0:T(8,128)} %get-tuple-element.60), channel_id=1, source_target_pairs={{2,0},{4,2},{6,4},{0,6},{3,1},{5,3},{7,5},{1,7},{10,8},{12,10},{14... | collective-permute-start | bytes 786440 | tf_op jit(solution)/shard_map/ppermute | solution.py:31
  11.0 26.8 %collective-permute-start.4 = (f32[16,64,256]{2,1,0:T(8,128)}, f32[16,64,256]{2,1,0:T(8,128)}, u32[]{:S(2)}, u32[]{:S(2)}) collective-permute-start(f32[16,64,256]{2,1,0:T(8,128)} %get-tuple-element.57), channel_id=1, source_target_pairs={{8,0},{9,1},{10,2},{11,3},{12,4},{13,5},{14,6},{15,7},{24,16},{25,... | collective-permute-start | bytes 3145736 | tf_op jit(solution)/shard_map/ppermute | solution.py:19
  12.3 27.7 %collective-permute-start.5 = (f32[16,64,256]{2,1,0:T(8,128)}, f32[16,64,256]{2,1,0:T(8,128)}, u32[]{:S(2)}, u32[]{:S(2)}) collective-permute-start(f32[16,64,256]{2,1,0:T(8,128)} %get-tuple-element.58), channel_id=1, source_target_pairs={{0,8},{1,9},{2,10},{3,11},{4,12},{5,13},{6,14},{7,15},{16,24},{17,... | collective-permute-start | bytes 3145736 | tf_op jit(solution)/shard_map/ppermute | solution.py:19
  20.2 1.3 %collective-permute-start.2 = (f32[2,20,2,256]{3,2,1,0:T(2,128)S(1)}, f32[2,20,2,256]{3,2,1,0:T(2,128)S(1)}, u32[]{:S(2)}, u32[]{:S(2)}) collective-permute-start(f32[2,20,2,256]{3,2,1,0:T(2,128)S(1)} %get-tuple-element.49), channel_id=1, source_target_pairs={{0,1},{1,0},{2,3},{3,2},{4,5},{5,4},{6,7},{7,6},{8,9},{9,8},{10,11... | collective-permute-start | bytes 245768 | tf_op jit(solution)/shard_map/ppermute | solution.py:29
  20.3 1.4 %collective-permute-start.3 = (f32[2,20,2,256]{3,2,1,0:T(2,128)S(1)}, f32[2,20,2,256]{3,2,1,0:T(2,128)S(1)}, u32[]{:S(2)}, u32[]{:S(2)}) collective-permute-start(f32[2,20,2,256]{3,2,1,0:T(2,128)S(1)} %get-tuple-element.48), channel_id=1, source_target_pairs={{1,0},{0,1},{3,2},{2,3},{5,4},{4,5},{7,6},{6,7},{9,8},{8,9},{11,10... | collective-permute-start | bytes 245768 | tf_op jit(solution)/shard_map/ppermute | solution.py:31
  26.9 13.1 %copy-start.1 = (f32[1,16,64,256]{3,2,1,0:T(8,128)S(1)}, f32[1,16,64,256]{3,2,1,0:T(8,128)}, u32[]{:S(2)}) copy-start(f32[1,16,64,256]{3,2,1,0:T(8,128)} %get-tuple-element.59) | copy-start | bytes 3145732
  62.9 11.0 %collective-permute-start.6 = (f32[2,2,64,256]{3,2,1,0:T(8,128)S(1)}, f32[2,2,64,256]{3,2,1,0:T(8,128)S(1)}, u32[]{:S(2)}, u32[]{:S(2)}) collective-permute-start(f32[2,2,64,256]{3,2,1,0:T(8,128)S(1)} %get-tuple-element.54), channel_id=1, source_target_pairs={{0,2},{2,4},{4,6},{6,0},{1,3},{3,5},{5,7},{7,1},{8,10},{10,12},{12... | collective-permute-start | bytes 786440 | tf_op jit(solution)/shard_map/ppermute | solution.py:29
  62.9 13.7 %collective-permute-start.7 = (f32[2,2,64,256]{3,2,1,0:T(8,128)S(1)}, f32[2,2,64,256]{3,2,1,0:T(8,128)S(1)}, u32[]{:S(2)}, u32[]{:S(2)}) collective-permute-start(f32[2,2,64,256]{3,2,1,0:T(8,128)S(1)} %get-tuple-element.55), channel_id=1, source_target_pairs={{2,0},{4,2},{6,4},{0,6},{3,1},{5,3},{7,5},{1,7},{10,8},{12,10},{14... | collective-permute-start | bytes 786440 | tf_op jit(solution)/shard_map/ppermute | solution.py:31
  76.7 7.4 %collective-permute-start.8 = (f32[2,20,2,256]{3,2,1,0:T(2,128)S(1)}, f32[2,20,2,256]{3,2,1,0:T(2,128)S(1)}, u32[]{:S(2)}, u32[]{:S(2)}) collective-permute-start(f32[2,20,2,256]{3,2,1,0:T(2,128)S(1)} %get-tuple-element.47), channel_id=1, source_target_pairs={{0,1},{1,0},{2,3},{3,2},{4,5},{5,4},{6,7},{7,6},{8,9},{9,8},{10,11... | collective-permute-start | bytes 245768 | tf_op jit(solution)/shard_map/ppermute | solution.py:29
  76.8 7.3 %collective-permute-start.9 = (f32[2,20,2,256]{3,2,1,0:T(2,128)S(1)}, f32[2,20,2,256]{3,2,1,0:T(2,128)S(1)}, u32[]{:S(2)}, u32[]{:S(2)}) collective-permute-start(f32[2,20,2,256]{3,2,1,0:T(2,128)S(1)} %get-tuple-element.46), channel_id=1, source_target_pairs={{1,0},{0,1},{3,2},{2,3},{5,4},{4,5},{7,6},{6,7},{9,8},{8,9},{11,10... | collective-permute-start | bytes 245768 | tf_op jit(solution)/shard_map/ppermute | solution.py:31
  78.0 27.2 %collective-permute-start.10 = (f32[16,64,256]{2,1,0:T(8,128)S(1)}, f32[16,64,256]{2,1,0:T(8,128)S(1)}, u32[]{:S(2)}, u32[]{:S(2)}) collective-permute-start(f32[16,64,256]{2,1,0:T(8,128)S(1)} %get-tuple-element.51), channel_id=1, source_target_pairs={{8,0},{9,1},{10,2},{11,3},{12,4},{13,5},{14,6},{15,7},{24,16},{25,... | collective-permute-start | bytes 3145736 | tf_op jit(solution)/shard_map/ppermute | solution.py:19
  79.3 27.1 %collective-permute-start.11 = (f32[16,64,256]{2,1,0:T(8,128)S(1)}, f32[16,64,256]{2,1,0:T(8,128)S(1)}, u32[]{:S(2)}, u32[]{:S(2)}) collective-permute-start(f32[16,64,256]{2,1,0:T(8,128)S(1)} %get-tuple-element.52), channel_id=1, source_target_pairs={{0,8},{1,9},{2,10},{3,11},{4,12},{5,13},{6,14},{7,15},{16,24},{17,... | collective-permute-start | bytes 3145736 | tf_op jit(solution)/shard_map/ppermute | solution.py:19
where the time goes:
time: 130 us
  waiting for transfers between devices  38 us (29%)
  blocking collectives  27.9 us (21%)
  other arithmetic  26.5 us (20%)
  starting transfers between devices  24 us (18%)
  local copies, waits for them, and re-layouts  12.6 us (10%)
    psum x2, blocking collectives, body(): lax.psum((sum_cells(forward * forward), sum_cells(backward * backward), s...  27.9 us
    ppermute x4, waiting for transfers between devices, passed_along(): return lax.ppermute(array, axis, pairs)  27.2 us
    ppermute x4, starting transfers between devices, passed_along(): return lax.ppermute(array, axis, pairs)  13.9 us
    reduce_sum x2, other arithmetic, sum_cells(): return jnp.sum(field, axis=(1, 2, 3))  9.99 us
    ppermute x4, waiting for transfers between devices, extended(): lax.ppermute(tail, axis, [(i, (i + 1) % count) for i in range(count)])  7.93 us
    select_n x2, other arithmetic, body(): jnp.where(interior[:, None, None, None], current + STEP_SIZE * update, cu...  7.86 us
    sub x2, other arithmetic, body(): inner_field * inner_field * inner_field - inner_field  7.33 us
    ppermute x4, starting transfers between devices, extended(): lax.ppermute(head, axis, [((i + 1) % count, i) for i in range(count)])  6.83 us
  transfers between devices with their start and end apart: 12, of which 8 were waited for; matrix products, arithmetic and copies ran while one was open for 14% of the time, Pallas kernels for 0%

commit v1 on v0

--- a/solution.py
+++ b/solution.py
@@ -1,6 +1,10 @@
+import functools
+
 import jax
 import jax.numpy as jnp
 from jax import lax
+from jax.experimental import pallas as pl
+from jax.experimental.pallas import tpu as pltpu
 from jax.sharding import PartitionSpec as P
 
 ITERS = 2
@@ -11,6 +15,9 @@
 SPRING_K = 1.0
 STEP_SIZE = 0.5
 EPSILON = 1e-06
+
+PAD = 8
+VMEM_LIMIT = 48 * 2**20
 
 
 def passed_along(array, axis, by):
@@ -47,7 +54,7 @@
     return jnp.sum(field, axis=(1, 2, 3))
 
 
-def body(images):
+def body_any(images):
     current = images
     per_device = current.shape[0]
     total_images = per_device * lax.axis_size("image")
@@ -102,6 +109,317 @@
     return (current, parallel)
 
 
+def call(kernel, out_shape, scratch=(), name=None, vmem_out=None, **kw):
+    return pl.pallas_call(
+        kernel,
+        out_shape=out_shape,
+        scratch_shapes=list(scratch),
+        name=name,
+        compiler_params=pltpu.CompilerParams(vmem_limit_bytes=VMEM_LIMIT),
+        **kw,
+    )
+
+
+def shape(*dims):
+    return jax.ShapeDtypeStruct(dims, jnp.float32)
+
+
+def lap(below, here, above):
+    rows, lanes = here.shape
+    ys = pltpu.roll(here, 1, 0) + pltpu.roll(here, rows - 1, 0)
+    xs = pltpu.roll(here, 1, 1) + pltpu.roll(here, lanes - 1, 1)
+    return (below + above) + ys + xs - 6.0 * here
+
+
+def driving_layers(field, pot, count, emit):
+    def first(k, carry):
+        here = field[k + 1]
+        pot[k] = here * here * here - here - GRADIENT_COEF * lap(field[k], here, field[k + 2])
+        return carry
+
+    lax.fori_loop(0, count + 2, first, 0)
+
+    def second(k, carry):
+        return emit(k, MOBILITY * lap(pot[k], pot[k + 1], pot[k + 2]), carry)
+
+    return second
+
+
+def rows_sum(field):
+    rows, lanes = field.shape
+    return jnp.sum(field.reshape(rows // 8, 8, lanes), axis=0)
+
+
+def lane_row(total):
+    lanes = total.shape[1]
+    folded = jnp.sum(total.reshape(8, lanes // 128, 128), axis=1)
+    return jnp.sum(folded, axis=0, keepdims=True)
+
+
+def fill_padded(dst, low, mid, high, sides, sides_at):
+    rows = mid.shape[1]
+    n_low, n_mid, n_high = low.shape[0], mid.shape[0], high.shape[0]
+    dst[0:n_low, PAD : PAD + rows] = low[...]
+    dst[n_low : n_low + n_mid, PAD : PAD + rows] = mid[...]
+    dst[n_low + n_mid : n_low + n_mid + n_high, PAD : PAD + rows] = high[...]
+    layers = n_low + n_mid + n_high
+    dst[:, 0:PAD] = sides[sides_at : sides_at + layers, PAD : 2 * PAD]
+    dst[:, PAD + rows : 2 * PAD + rows] = sides[sides_at : sides_at + layers, 0:PAD]
+
+
+def split_kernel(images, mine, end, up, down, sems):
+    which = 1 - lax.axis_index("image")
+    nz = mine.shape[0]
+    copies = [
+        pltpu.make_async_copy(src, dst, sems.at[i])
+        for i, (src, dst) in enumerate(
+            [
+                (images.at[which], mine),
+                (images.at[which, pl.ds(nz - 4, 4)], up.at[pl.ds(0, 4)]),
+                (images.at[1 - which, pl.ds(nz - 2, 2)], up.at[pl.ds(4, 2)]),
+                (images.at[which, pl.ds(0, 4)], down.at[pl.ds(0, 4)]),
+                (images.at[1 - which, pl.ds(0, 2)], down.at[pl.ds(4, 2)]),
+                (images.at[1 - which], end),
+            ]
+        )
+    ]
+    for c in copies:
+        c.start()
+    for c in copies:
+        c.wait()
+
+
+def first_step_kernel(mine, end, low, high, sides, step_out, drive_out, end_out, field, pot):
+    nz, rows, _ = mine.shape
+    fill_padded(field, low.at[0:4], mine, high.at[0:4], sides, 0)
+    fill_padded(end_out, low.at[4:6], end, high.at[4:6], sides, nz + 8)
+
+    def emit(k, drive, carry):
+        step_out[k] = field[k + 2] + STEP_SIZE * drive
+
+        @pl.when((k >= 2) & (k < nz + 2))
+        def _():
+            drive_out[k - 2] = drive[PAD : PAD + rows]
+
+        return carry
+
+    lax.fori_loop(0, nz + 4, driving_layers(field, pot, nz + 4, emit), 0)
+
+
+def sums_of(count, lanes, fields):
+    def one(k, totals):
+        plus, minus, tangent, drive = fields(k)
+        terms = (plus * plus, minus * minus, tangent * tangent, drive * tangent)
+        return tuple(t + rows_sum(v) for t, v in zip(totals, terms))
+
+    zero = jnp.zeros((8, lanes), jnp.float32)
+    return lax.fori_loop(0, count, one, (zero,) * 4)
+
+
+def write_sums(out, totals):
+    out[...] = jnp.zeros_like(out)
+    for i, total in enumerate(totals):
+        out[i : i + 1] = lane_row(total)
+
+
+def first_sums_kernel(other, mine, end, drive, out):
+    nz, _, lanes = mine.shape
+
+    def fields(k):
+        m, o, e = mine[k], other[k], end[k]
+        return o - m, m - e, o - e, drive[k]
+
+    write_sums(out, sums_of(nz, lanes, fields))
+
+
+def coefficient(parts, base, count):
+    total = parts[base]
+    for i in range(1, count):
+        total = total + parts[base + i]
+    total = jnp.sum(total, axis=1, keepdims=True)
+    plus_sq, minus_sq, tangent_sq, par = (total[i : i + 1] for i in range(4))
+    safe = tangent_sq + EPSILON
+    spring = SPRING_K * (jnp.sqrt(plus_sq) - jnp.sqrt(minus_sq)) / jnp.sqrt(safe)
+    return STEP_SIZE * (spring - par / safe), par, safe
+
+
+def other_step_kernel(other, low, high, sides, step_out, field_out, pot):
+    nz, rows, _ = other.shape
+    fill_padded(field_out, low, other, high, sides, 0)
+
+    def emit(k, drive, carry):
+        step_out[k] = other[k] + STEP_SIZE * drive[PAD : PAD + rows]
+        return carry
+
+    lax.fori_loop(0, nz, driving_layers(field_out, pot, nz, emit), 0)
+
+
+def second_step_kernel(parts, step, end_wide, other_wide, moved_out, drive_out, field, pot):
+    nz, rows, _ = drive_out.shape
+    half = parts.shape[0] // 2
+    coef, _, _ = coefficient(parts, half * lax.axis_index("image"), half)
+
+    def move(k, carry):
+        field[k] = step[k] + coef * (other_wide[k] - end_wide[k])
+        return carry
+
+    lax.fori_loop(0, nz + 4, move, 0)
+
+    def emit(k, drive, carry):
+        drive_out[k] = drive[PAD : PAD + rows]
+        moved_out[k] = field[k + 2][PAD : PAD + rows]
+        return carry
+
+    lax.fori_loop(0, nz, driving_layers(field, pot, nz, emit), 0)
+
+
+def second_sums_kernel(parts, far, mine, end, other_step, moved, drive, tangent_out, out):
+    nz, _, lanes = mine.shape
+    half = parts.shape[0] // 2
+    coef, _, _ = coefficient(parts, half * (1 - lax.axis_index("image")), half)
+
+    def fields(k):
+        o = other_step[k] + coef * (mine[k] - far[k])
+        m, e = moved[k], end[k]
+        tangent = o - e
+        tangent_out[k] = tangent
+        return o - m, m - e, tangent, drive[k]
+
+    write_sums(out, sums_of(nz, lanes, fields))
+
+
+def last_kernel(cells, parts, moved, drive, tangent, base, out, par_out, buf, sems):
+    del base
+    nz = moved.shape[0]
+    at = lax.axis_index("image")
+    which = 1 - at
+    coef, par, safe = coefficient(parts, 0, parts.shape[0])
+    copies = []
+    for k in range(nz):
+        buf[k] = moved[k] + STEP_SIZE * drive[k] + coef * tangent[k]
+        if k % 4 == 3:
+            where = pl.ds(k - 3, 4)
+            copies.append(
+                pltpu.make_async_copy(buf.at[where], out.at[which, where], sems.at[k // 4])
+            )
+            copies[-1].start()
+    value = (par / jnp.sqrt(safe * cells))[0, 0]
+    sign = jnp.where(at == 0, 1.0, -1.0).astype(jnp.float32)
+    par_out[which] = value * sign
+    par_out[1 - which] = jnp.float32(0.0)
+    for c in copies:
+        c.wait()
+
+
+ANY = pl.BlockSpec(memory_space=pl.ANY)
+VMEM = pl.BlockSpec(memory_space=pltpu.VMEM)
+SMEM = pl.BlockSpec(memory_space=pltpu.SMEM)
+DMA = pltpu.SemaphoreType.DMA
+SWAP = [(0, 1), (1, 0)]
+
+
+def copy_kernel(src, dst, sem):
+    c = pltpu.make_async_copy(src, dst, sem)
+    c.start()
+    c.wait()
+
+
+def from_z(up, down):
+    count = lax.axis_size("space")
+    low = lax.ppermute(up, "space", [(i, (i + 1) % count) for i in range(count)])
+    high = lax.ppermute(down, "space", [((i + 1) % count, i) for i in range(count)])
+    return low, high
+
+
+def y_sides(*pieces):
+    rows = pieces[0].shape[1]
+    ends = [jnp.concatenate([p[:, :PAD], p[:, rows - PAD :]], 1) for p in pieces]
+    return lax.ppermute(jnp.concatenate(ends, 0), "yslab", SWAP)
+
+
+def to_all(sums, axes):
+    peers = lax.axis_size(axes)
+    spread = jnp.broadcast_to(sums[None], (peers,) + sums.shape)
+    return lax.all_to_all(spread, axes, 0, 0, tiled=True)
+
+
+def body_pair(images):
+    _, nz, ny, nx = images.shape
+    wide = ny + 2 * PAD
+    cells = float(nz * lax.axis_size("space") * ny * lax.axis_size("yslab") * nx)
+    block = shape(nz, ny, nx)
+
+    mine, end, up, down = call(
+        split_kernel,
+        [block, block, shape(6, ny, nx), shape(6, ny, nx)],
+        [DMA((6,))],
+        "split",
+        in_specs=[ANY],
+        out_specs=[ANY] * 4,
+    )(images)
+
+    other = lax.ppermute(mine, "image", SWAP)
+    low, high = from_z(up, down)
+    end_later, low, high = lax.optimization_barrier((end, low, high))
+    far = lax.ppermute(end_later, "image", SWAP)
+
+    base = call(
+        copy_kernel,
+        jax.ShapeDtypeStruct(images.shape, images.dtype),
+        [DMA],
+        "base",
+        in_specs=[ANY],
+        out_specs=ANY,
+    )(images)
+
+    sides = y_sides(low[:4], mine, high[:4], low[4:], end, high[4:])
+    step, drive, end_wide = call(
+        first_step_kernel,
+        [shape(nz + 4, wide, nx), block, shape(nz + 4, wide, nx)],
+        [pltpu.VMEM((nz + 8, wide, nx), jnp.float32), pltpu.VMEM((nz + 6, wide, nx), jnp.float32)],
+        "first_step",
+    )(mine, end, low, high, sides)
+
+    sums = call(first_sums_kernel, shape(8, 128), name="first_sums")(other, mine, end, drive)
+    parts = to_all(sums, ("image", "space", "yslab"))
+
+    o_low, o_high = from_z(other[nz - 2 :], other[:2])
+    o_sides = y_sides(o_low, other, o_high)
+    other_step, other_wide = call(
+        other_step_kernel,
+        [block, shape(nz + 4, wide, nx)],
+        [pltpu.VMEM((nz + 2, wide, nx), jnp.float32)],
+        "other_step",
+    )(other, o_low, o_high, o_sides)
+
+    moved, drive2 = call(
+        second_step_kernel,
+        [block, block],
+        [pltpu.VMEM((nz + 4, wide, nx), jnp.float32), pltpu.VMEM((nz + 2, wide, nx), jnp.float32)],
+        "second_step",
+    )(parts, step, end_wide, other_wide)
+
+    tangent, sums = call(second_sums_kernel, [block, shape(8, 128)], name="second_sums")(
+        parts, far, mine, end, other_step, moved, drive2
+    )
+    parts = to_all(sums, ("space", "yslab"))
+
+    return call(
+        functools.partial(last_kernel, cells),
+        [jax.ShapeDtypeStruct(images.shape, images.dtype), shape(2)],
+        [pltpu.VMEM(block.shape, jnp.float32), DMA((nz // 4,))],
+        "last",
+        in_specs=[VMEM] * 4 + [ANY],
+        out_specs=[ANY, SMEM],
+        input_output_aliases={4: 0},
+    )(parts, moved, drive2, tangent, base)
+
+
+def body(images):
+    pair = lax.axis_size("image") == 2 and lax.axis_size("yslab") == 2 and images.shape[0] == 2
+    return body_pair(images) if pair else body_any(images)
+
+
 def solution(mesh):
     in_specs = (P(("groups", "image"), "space", "yslab", None),)
     out_specs = (P(("groups", "image"), "space", "yslab", None), P(("groups", "image")))

time: 130 us -> 97.2 us (0.75)
  Pallas kernels: 0 us -> 29.6 us
  blocking collectives: 27.9 us -> 0 us
  other arithmetic: 26.5 us -> 0.84 us
  waiting for transfers between devices: 38 us -> 28.5 us
    pallas_call x0 -> x8, Pallas kernels: none -> 29.6 us  [the longest x1 7.29 us: body_pair(): call(first_step_kernel, [shape(nz + 4, wide, nx), block, shape(nz + 4, wi...]
    psum x2 -> x0, blocking collectives: 27.9 us -> none  [body(): lax.psum((sum_cells(forward * forward), sum_cells(backward * backward), s...]
    ppermute x12 -> x8, waiting for transfers between devices: 38 us -> 25.6 us  [the longest x2 9.49 us: from_z(): lax.ppermute(down, 'space', [((i + 1) % count, i) for i in range(count)])]
    ppermute x12 -> x8, starting transfers between devices: 24 us -> 12.3 us  [the longest x2 5.9 us: from_z(): lax.ppermute(down, 'space', [((i + 1) % count, i) for i in range(count)])]
    all_to_all x0 -> x2, starting transfers between devices: none -> 11.4 us  [to_all(): return lax.all_to_all(spread, axes, 0, 0, tiled=True)]
    slice x13 -> x7, local copies, waits for them, and re-layouts: 11.3 us -> 0.1 us  [the longest x6 0.08 us: y_sides(): ends = [jnp.concatenate([p[:, :PAD], p[:, rows - PAD:]], 1) for p in pieces]]
    unnamed x6 -> x30, local copies, waits for them, and re-layouts: 1.2 us -> 12 us
    reduce_sum x2 -> x0, other arithmetic: 9.99 us -> none  [sum_cells(): return jnp.sum(field, axis=(1, 2, 3))]
  transfers between devices with their start and end apart: 12 -> 10, of which waited for: 8 -> 6; matrix products, arithmetic and copies ran while one was open for 14% -> 2% of each run, Pallas kernels for 0% -> 22%
where the time goes in v1:
time: 97.2 us; the launch traced here: 96.8 us
  Pallas kernels  29.6 us (30%)
  waiting for transfers between devices  28.5 us (29%)
  starting transfers between devices  23.7 us (24%)
  local copies, waits for them, and re-layouts  13.3 us (14%)
    unnamed x30, local copies, waits for them, and re-layouts  12 us
    all_to_all x2, starting transfers between devices, to_all(): return lax.all_to_all(spread, axes, 0, 0, tiled=True)  11.4 us
    ppermute x2, waiting for transfers between devices, from_z(): lax.ppermute(down, 'space', [((i + 1) % count, i) for i in range(count)])  9.49 us
    ppermute x2, waiting for transfers between devices, from_z(): lax.ppermute(up, 'space', [(i, (i + 1) % count) for i in range(count)])  8.74 us
    ppermute x1, waiting for transfers between devices, body_pair(): other = lax.ppermute(mine, 'image', SWAP)  7.4 us
    pallas_call x1, Pallas kernels, body_pair(): call(first_step_kernel, [shape(nz + 4, wide, nx), block, shape(nz + 4, wi...  7.29 us
    pallas_call x1, Pallas kernels, body_pair(): call(second_step_kernel, [block, block], [pltpu.VMEM((nz + 4, wide, nx),...  6.52 us
    ppermute x2, starting transfers between devices, from_z(): lax.ppermute(down, 'space', [((i + 1) % count, i) for i in range(count)])  5.9 us
  transfers between devices with their start and end apart: 10, of which 6 were waited for; matrix products, arithmetic and copies ran while one was open for 2% of the time, Pallas kernels for 22%

profile of v1, /device:TPU:0, one launch (start us, length us, event | category | flops | bytes accessed | tf_op | source)
XLA Modules:
  0.0 96.8 jit_solution(17319343328930755076)
XLA Ops:
  0.6 0.0 copy-start
  0.6 1.6 %copy-done = f32[2,16,64,256]{3,2,1,0:T(8,128)S(1)} copy-done((f32[2,16,64,256]{3,2,1,0:T(8,128)S(1)}, f32[2,16,64,256]{3,2,1,0:T(8,128)}, u32[]{:S(2)}) %copy-start) | copy-done | bytes 2097176
  2.2 0.6 split.1
  2.8 3.1 %collective-permute-start.1 = (f32[6,64,256]{2,1,0:T(8,128)S(1)}, f32[6,64,256]{2,1,0:T(8,128)S(1)}, u32[]{:S(2)}, u32[]{:S(2)}) collective-permute-start(f32[6,64,256]{2,1,0:T(8,128)S(1)} %get-tuple-element.20), channel_id=1, source_target_pairs={{0,2},{2,4},{4,6},{6,0},{1,3},{3,5},{5,7},{7,1},{8,10},{10,12},{12... | collective-permute-start | bytes 1179656 | tf_op jit(solution)/shard_map/ppermute | solution.py:329
  5.9 2.1 %collective-permute-start.2 = (f32[6,64,256]{2,1,0:T(8,128)S(1)}, f32[6,64,256]{2,1,0:T(8,128)S(1)}, u32[]{:S(2)}, u32[]{:S(2)}) collective-permute-start(f32[6,64,256]{2,1,0:T(8,128)S(1)} %get-tuple-element.21), channel_id=1, source_target_pairs={{2,0},{4,2},{6,4},{0,6},{3,1},{5,3},{7,5},{1,7},{10,8},{12,10},{14... | collective-permute-start | bytes 1179656 | tf_op jit(solution)/shard_map/ppermute | solution.py:330
  8.0 1.6 %collective-permute-start = (f32[16,64,256]{2,1,0:T(8,128)S(1)}, f32[16,64,256]{2,1,0:T(8,128)S(1)}, u32[]{:S(2)}, u32[]{:S(2)}) collective-permute-start(f32[16,64,256]{2,1,0:T(8,128)S(1)} %get-tuple-element.18.mine), channel_id=1, source_target_pairs={{0,8},{8,0},{1,9},{9,1},{2,10},{10,2},{3,11},{11,3},{4,12},{12,4},... | collective-permute-start | bytes 3145736 | tf_op jit(solution)/shard_map/ppermute | solution.py:361
  9.7 8.2 %collective-permute-done.1.low = f32[6,64,256]{2,1,0:T(8,128)S(1)} collective-permute-done((f32[6,64,256]{2,1,0:T(8,128)S(1)}, f32[6,64,256]{2,1,0:T(8,128)S(1)}, u32[]{:S(2)}, u32[]{:S(2)}) %collective-permute-start.1) | collective-permute-done | bytes 393248 | tf_op jit(solution)/shard_map/ppermute | solution.py:329
  17.9 7.0 %collective-permute-done.2.high = f32[6,64,256]{2,1,0:T(8,128)S(1)} collective-permute-done((f32[6,64,256]{2,1,0:T(8,128)S(1)}, f32[6,64,256]{2,1,0:T(8,128)S(1)}, u32[]{:S(2)}, u32[]{:S(2)}) %collective-permute-start.2) | collective-permute-done | bytes 393248 | tf_op jit(solution)/shard_map/ppermute | solution.py:330
  25.0 0.1 collective-permute-start.3
  25.1 1.6 %collective-permute-start.4 = (f32[16,64,256]{2,1,0:T(8,128)S(1)}, f32[16,64,256]{2,1,0:T(8,128)}, u32[]{:S(2)}, u32[]{:S(2)}) collective-permute-start(f32[16,64,256]{2,1,0:T(8,128)S(1)} %get-tuple-element.25.end), channel_id=1, source_target_pairs={{0,8},{8,0},{1,9},{9,1},{2,10},{10,2},{3,11},{11,3},{4,12},{12,4},... | collective-permute-start | bytes 3145736 | tf_op jit(solution)/shard_map/ppermute | solution.py:364
  26.7 7.4 %collective-permute-done.other = f32[16,64,256]{2,1,0:T(8,128)S(1)} collective-permute-done((f32[16,64,256]{2,1,0:T(8,128)S(1)}, f32[16,64,256]{2,1,0:T(8,128)S(1)}, u32[]{:S(2)}, u32[]{:S(2)}) %collective-permute-start) | collective-permute-done | bytes 1048608 | tf_op jit(solution)/shard_map/ppermute | solution.py:361
  34.1 0.1 collective-permute-start.5
  34.1 3.8 %collective-permute-start.6 = (f32[2,64,256]{2,1,0:T(8,128)S(1)}, f32[2,64,256]{2,1,0:T(8,128)S(1)}, u32[]{:S(2)}, u32[]{:S(2)}) collective-permute-start(f32[2,64,256]{2,1,0:T(8,128)S(1)} %get-tuple-element.36), channel_id=1, source_target_pairs={{2,0},{4,2},{6,4},{0,6},{3,1},{5,3},{7,5},{1,7},{10,8},{12,10},{14... | collective-permute-start | bytes 393224 | tf_op jit(solution)/shard_map/ppermute | solution.py:330
  38.0 2.5 %collective-permute-done.6.high = f32[2,64,256]{2,1,0:T(8,128)S(1)} collective-permute-done((f32[2,64,256]{2,1,0:T(8,128)S(1)}, f32[2,64,256]{2,1,0:T(8,128)S(1)}, u32[]{:S(2)}, u32[]{:S(2)}) %collective-permute-start.6) | collective-permute-done | bytes 131104 | tf_op jit(solution)/shard_map/ppermute | solution.py:330
  40.5 0.5 collective-permute-done.5.low
  41.0 0.8 maximum_maximum_fusion
  41.8 0.0 collective-permute-start.7
  41.8 0.0 collective-permute-done.3.sides
  41.8 7.3 %first_step.1 = (f32[20,80,256]{2,1,0:T(8,128)}, f32[16,64,256]{2,1,0:T(8,128)S(1)}, f32[20,80,256]{2,1,0:T(8,128)}) custom-call(f32[16,64,256]{2,1,0:T(8,128)S(1)} %get-tuple-element.18.mine, f32[16,64,256]{2,1,0:T(8,128)S(1)} %get-tuple-element.25.end, f32[6,64,256]{2,1,0:T(8,128)S(1)} %collective-permute-done.1.low, ...), custom_call_target="tpu_custom_call" | custom-call | tf_op jit(solution)/shard_map/first_step/pallas_call | solution.py:376
  49.1 0.0 copy-done.13
  49.1 0.0 copy-done.11
  49.1 2.4 %first_sums.1 = f32[8,128]{1,0:T(8,128)S(1)} custom-call(f32[16,64,256]{2,1,0:T(8,128)S(1)} %collective-permute-done.other, f32[16,64,256]{2,1,0:T(8,128)S(1)} %get-tuple-element.18.mine, f32[16,64,256]{2,1,0:T(8,128)S(1)} %get-tuple-element.25.end, f32[16,64,256]{2,1,0:T(8,128)S(1)} %get-tuple-element.24.drive), custom_call_target="tpu_custom_call" | custom-call | tf_op jit(solution)/shard_map/first_sums/pallas_call | solution.py:383
  51.5 0.6 broadcast_in_dim.4
  52.1 6.4 %all-to-all-start = ((f32[16,8,128]{2,1,0:T(8,128)}), f32[16,8,128]{2,1,0:T(8,128)S(1)}, u32[]{:S(2)}, u32[]{:S(2)}) async-start(f32[16,8,128]{2,1,0:T(8,128)} %broadcast_in_dim.4), calls=%async_computation | async-start | bytes 131072 | tf_op jit(solution)/shard_map/all_to_all | solution.py:343
  58.5 0.0 collective-permute-done.7.sides
  58.5 0.0 copy-start.12
  58.5 0.9 copy-done.12
  59.4 0.9 copy-done.14
  60.3 4.2 %other_step.1 = (f32[16,64,256]{2,1,0:T(8,128)S(1)}, f32[20,80,256]{2,1,0:T(8,128)S(1)}) custom-call(f32[16,64,256]{2,1,0:T(8,128)S(1)} %collective-permute-done.other, f32[2,64,256]{2,1,0:T(8,128)S(1)} %copy-done.12, f32[2,64,256]{2,1,0:T(8,128)S(1)} %copy-done.14, f32[20,16,256]{2,1,0:T(8,128)S(1)} %collective-permute-done.7.sides), custom_call_target="tpu_custom_call" | custom-call | tf_op jit(solution)/shard_map/other_step/pallas_call | solution.py:388
  64.5 0.0 copy-start.8
  64.5 1.2 %copy-done.8 = f32[20,80,256]{2,1,0:T(8,128)} copy-done((f32[20,80,256]{2,1,0:T(8,128)}, f32[20,80,256]{2,1,0:T(8,128)S(1)}, u32[]{:S(2)}) %copy-start.8) | copy-done | bytes 1638424
  65.7 1.0 %copy-done.9 = f32[16,64,256]{2,1,0:T(8,128)} copy-done((f32[16,64,256]{2,1,0:T(8,128)}, f32[16,64,256]{2,1,0:T(8,128)S(1)}, u32[]{:S(2)}) %copy-start.9) | copy-done | bytes 1048600
  66.7 0.0 all-to-all-done.parts
  66.7 1.4 %copy-done.6 = f32[20,80,256]{2,1,0:T(8,128)S(1)} copy-done((f32[20,80,256]{2,1,0:T(8,128)S(1)}, f32[20,80,256]{2,1,0:T(8,128)}, u32[]{:S(2)}) %copy-start.6) | copy-done | bytes 1638424
  68.1 1.4 %copy-done.7 = f32[20,80,256]{2,1,0:T(8,128)S(1)} copy-done((f32[20,80,256]{2,1,0:T(8,128)S(1)}, f32[20,80,256]{2,1,0:T(8,128)}, u32[]{:S(2)}) %copy-start.7) | copy-done | bytes 1638424
  69.5 6.5 %second_step.1 = (f32[16,64,256]{2,1,0:T(8,128)S(1)}, f32[16,64,256]{2,1,0:T(8,128)S(1)}) custom-call(f32[16,8,128]{2,1,0:T(8,128)S(1)} %all-to-all-done.parts, f32[20,80,256]{2,1,0:T(8,128)S(1)} %copy-done.6, f32[20,80,256]{2,1,0:T(8,128)S(1)} %copy-done.7, f32[20,80,256]{2,1,0:T(8,128)} %copy-done.8), custom_call_target="tpu_custom_call" | custom-call | tf_op jit(solution)/shard_map/second_step/pallas_call | solution.py:395
  76.1 0.0 copy-start.2
  76.1 1.0 copy-done.2
  77.0 1.0 %copy-done.4 = f32[16,64,256]{2,1,0:T(8,128)} copy-done((f32[16,64,256]{2,1,0:T(8,128)}, f32[16,64,256]{2,1,0:T(8,128)S(1)}, u32[]{:S(2)}) %copy-start.4) | copy-done | bytes 1048600
  78.0 0.0 collective-permute-done.4.far
  78.0 5.7 %second_sums.1 = (f32[16,64,256]{2,1,0:T(8,128)S(1)}, f32[8,128]{1,0:T(8,128)S(1)}) custom-call(f32[16,8,128]{2,1,0:T(8,128)S(1)} %all-to-all-done.parts, f32[16,64,256]{2,1,0:T(8,128)} %collective-permute-done.4.far, f32[16,64,256]{2,1,0:T(8,128)S(1)} %get-tuple-element.18.mine, f32[16,64,256]{2,1,0:T(8,128)S(1)} %get-tuple-element.25.end, ...), custom_call_target="tpu_custom_call" | custom-call | tf_op jit(solution)/shard_map/second_sums/pallas_call | solution.py:402
  83.7 0.6 broadcast_in_dim.5
  84.3 5.0 %all-to-all-start.1 = ((f32[8,8,128]{2,1,0:T(8,128)}), f32[8,8,128]{2,1,0:T(8,128)S(1)}, u32[]{:S(2)}, u32[]{:S(2)}) async-start(f32[8,8,128]{2,1,0:T(8,128)} %broadcast_in_dim.5), calls=%async_computation.1 | async-start | bytes 65536 | tf_op jit(solution)/shard_map/all_to_all | solution.py:343
  89.3 1.6 %copy-done.1 = f32[2,16,64,256]{3,2,1,0:T(8,128)S(1)} copy-done((f32[2,16,64,256]{3,2,1,0:T(8,128)S(1)}, f32[2,16,64,256]{3,2,1,0:T(8,128)}, u32[]{:S(2)}) %copy-start.1) | copy-done | bytes 2097176
  90.9 1.3 %base.1 = f32[2,16,64,256]{3,2,1,0:T(8,128)} custom-call(f32[2,16,64,256]{3,2,1,0:T(8,128)S(1)} %copy-done.1), custom_call_target="tpu_custom_call" | custom-call | tf_op jit(solution)/shard_map/base/pallas_call | solution.py:366
  92.3 2.8 %all-to-all-done.1.parts = f32[8,8,128]{2,1,0:T(8,128)S(1)} async-done(((f32[8,8,128]{2,1,0:T(8,128)}), f32[8,8,128]{2,1,0:T(8,128)S(1)}, u32[]{:S(2)}, u32[]{:S(2)}) %all-to-all-start.1) | async-done | bytes 32800 | tf_op jit(solution)/shard_map/all_to_all | solution.py:343
  95.1 0.0 copy-done.5
  95.1 1.7 %last.1 = (f32[2,16,64,256]{3,2,1,0:T(8,128)}, f32[2]{0:T(128)}) custom-call(f32[8,8,128]{2,1,0:T(8,128)S(1)} %all-to-all-done.1.parts, f32[16,64,256]{2,1,0:T(8,128)S(1)} %copy-done.3, f32[16,64,256]{2,1,0:T(8,128)S(1)} %copy-done.5, f32[16,64,256]{2,1,0:T(8,128)S(1)} %get-tuple-element.33.tangent, ...), custom_call_target="tpu_custom_call", output_to_operand_aliasing={{0}: (4, {})} | custom-call | tf_op jit(solution)/shard_map/last/pallas_call | solution.py:407
  (26 shorter events, 0.2 us)
Async XLA Ops:
  0.6 1.6 %copy-start = (f32[2,16,64,256]{3,2,1,0:T(8,128)S(1)}, f32[2,16,64,256]{3,2,1,0:T(8,128)}, u32[]{:S(2)}) copy-start(f32[2,16,64,256]{3,2,1,0:T(8,128)} %src.1) | copy-start | bytes 6291460
  2.8 15.1 %collective-permute-start.1 = (f32[6,64,256]{2,1,0:T(8,128)S(1)}, f32[6,64,256]{2,1,0:T(8,128)S(1)}, u32[]{:S(2)}, u32[]{:S(2)}) collective-permute-start(f32[6,64,256]{2,1,0:T(8,128)S(1)} %get-tuple-element.20), channel_id=1, source_target_pairs={{0,2},{2,4},{4,6},{6,0},{1,3},{3,5},{5,7},{7,1},{8,10},{10,12},{12... | collective-permute-start | bytes 1179656 | tf_op jit(solution)/shard_map/ppermute | solution.py:329
  5.9 19.0 %collective-permute-start.2 = (f32[6,64,256]{2,1,0:T(8,128)S(1)}, f32[6,64,256]{2,1,0:T(8,128)S(1)}, u32[]{:S(2)}, u32[]{:S(2)}) collective-permute-start(f32[6,64,256]{2,1,0:T(8,128)S(1)} %get-tuple-element.21), channel_id=1, source_target_pairs={{2,0},{4,2},{6,4},{0,6},{3,1},{5,3},{7,5},{1,7},{10,8},{12,10},{14... | collective-permute-start | bytes 1179656 | tf_op jit(solution)/shard_map/ppermute | solution.py:330
  8.0 26.1 %collective-permute-start = (f32[16,64,256]{2,1,0:T(8,128)S(1)}, f32[16,64,256]{2,1,0:T(8,128)S(1)}, u32[]{:S(2)}, u32[]{:S(2)}) collective-permute-start(f32[16,64,256]{2,1,0:T(8,128)S(1)} %get-tuple-element.18.mine), channel_id=1, source_target_pairs={{0,8},{8,0},{1,9},{9,1},{2,10},{10,2},{3,11},{11,3},{4,12},{12,4},... | collective-permute-start | bytes 3145736 | tf_op jit(solution)/shard_map/ppermute | solution.py:361
  25.0 16.8 %collective-permute-start.3 = (f32[44,16,256]{2,1,0:T(8,128)S(1)}, f32[44,16,256]{2,1,0:T(8,128)S(1)}, u32[]{:S(2)}, u32[]{:S(2)}) collective-permute-start(f32[44,16,256]{2,1,0:T(8,128)S(1)} %maximum_dynamic-update-slice_fusion.4), channel_id=1, source_target_pairs={{0,1},{1,0},{2,3},{3,2},{4,5},{5,4},{6,7},{7,6},{8,9},{9,8},{10,11... | collective-permute-start | bytes 2162696 | tf_op jit(solution)/shard_map/ppermute | solution.py:337
  25.1 52.9 %collective-permute-start.4 = (f32[16,64,256]{2,1,0:T(8,128)S(1)}, f32[16,64,256]{2,1,0:T(8,128)}, u32[]{:S(2)}, u32[]{:S(2)}) collective-permute-start(f32[16,64,256]{2,1,0:T(8,128)S(1)} %get-tuple-element.25.end), channel_id=1, source_target_pairs={{0,8},{8,0},{1,9},{9,1},{2,10},{10,2},{3,11},{11,3},{4,12},{12,4},... | collective-permute-start | bytes 3145736 | tf_op jit(solution)/shard_map/ppermute | solution.py:364
  34.1 6.9 %collective-permute-start.5 = (f32[2,64,256]{2,1,0:T(8,128)S(1)}, f32[2,64,256]{2,1,0:T(8,128)S(1)}, u32[]{:S(2)}, u32[]{:S(2)}) collective-permute-start(f32[2,64,256]{2,1,0:T(8,128)S(1)} %get-tuple-element.37), channel_id=1, source_target_pairs={{0,2},{2,4},{4,6},{6,0},{1,3},{3,5},{5,7},{7,1},{8,10},{10,12},{12... | collective-permute-start | bytes 393224 | tf_op jit(solution)/shard_map/ppermute | solution.py:329
  34.1 6.3 %collective-permute-start.6 = (f32[2,64,256]{2,1,0:T(8,128)S(1)}, f32[2,64,256]{2,1,0:T(8,128)S(1)}, u32[]{:S(2)}, u32[]{:S(2)}) collective-permute-start(f32[2,64,256]{2,1,0:T(8,128)S(1)} %get-tuple-element.36), channel_id=1, source_target_pairs={{2,0},{4,2},{6,4},{0,6},{3,1},{5,3},{7,5},{1,7},{10,8},{12,10},{14... | collective-permute-start | bytes 393224 | tf_op jit(solution)/shard_map/ppermute | solution.py:330
  40.5 8.6 %copy-start.13 = (f32[2,64,256]{2,1,0:T(8,128)}, f32[2,64,256]{2,1,0:T(8,128)S(1)}, u32[]{:S(2)}) copy-start(f32[2,64,256]{2,1,0:T(8,128)S(1)} %collective-permute-done.6.high) | copy-start | bytes 393220
  41.0 8.1 %copy-start.11 = (f32[2,64,256]{2,1,0:T(8,128)}, f32[2,64,256]{2,1,0:T(8,128)S(1)}, u32[]{:S(2)}) copy-start(f32[2,64,256]{2,1,0:T(8,128)S(1)} %collective-permute-done.5.low) | copy-start | bytes 393220
  41.8 16.7 %collective-permute-start.7 = (f32[20,16,256]{2,1,0:T(8,128)}, f32[20,16,256]{2,1,0:T(8,128)S(1)}, u32[]{:S(2)}, u32[]{:S(2)}) collective-permute-start(f32[20,16,256]{2,1,0:T(8,128)} %maximum_maximum_fusion), channel_id=1, source_target_pairs={{0,1},{1,0},{2,3},{3,2},{4,5},{5,4},{6,7},{7,6},{8,9},{9,8},{10,11... | collective-permute-start | bytes 983048 | tf_op jit(solution)/shard_map/ppermute | solution.py:337
  52.1 14.6 %all-to-all-start = ((f32[16,8,128]{2,1,0:T(8,128)}), f32[16,8,128]{2,1,0:T(8,128)S(1)}, u32[]{:S(2)}, u32[]{:S(2)}) async-start(f32[16,8,128]{2,1,0:T(8,128)} %broadcast_in_dim.4), calls=%async_computation | async-start | bytes 131072 | tf_op jit(solution)/shard_map/all_to_all | solution.py:343
  58.5 0.9 copy-start.12
  59.4 0.9 copy-start.14
  64.5 1.2 %copy-start.8 = (f32[20,80,256]{2,1,0:T(8,128)}, f32[20,80,256]{2,1,0:T(8,128)S(1)}, u32[]{:S(2)}) copy-start(f32[20,80,256]{2,1,0:T(8,128)S(1)} %get-tuple-element.29.other_wide) | copy-start | bytes 4915204
  65.7 1.0 %copy-start.9 = (f32[16,64,256]{2,1,0:T(8,128)}, f32[16,64,256]{2,1,0:T(8,128)S(1)}, u32[]{:S(2)}) copy-start(f32[16,64,256]{2,1,0:T(8,128)S(1)} %get-tuple-element.26.other_step) | copy-start | bytes 3145732
  66.7 1.4 %copy-start.6 = (f32[20,80,256]{2,1,0:T(8,128)S(1)}, f32[20,80,256]{2,1,0:T(8,128)}, u32[]{:S(2)}) copy-start(f32[20,80,256]{2,1,0:T(8,128)} %get-tuple-element.27.step) | copy-start | bytes 4915204
  68.1 1.4 %copy-start.7 = (f32[20,80,256]{2,1,0:T(8,128)S(1)}, f32[20,80,256]{2,1,0:T(8,128)}, u32[]{:S(2)}) copy-start(f32[20,80,256]{2,1,0:T(8,128)} %get-tuple-element.28.end_wide) | copy-start | bytes 4915204
  69.5 8.5 %copy-start.10 = (f32[16,64,256]{2,1,0:T(8,128)S(1)}, f32[16,64,256]{2,1,0:T(8,128)}, u32[]{:S(2)}) copy-start(f32[16,64,256]{2,1,0:T(8,128)} %copy-done.9) | copy-start | bytes 3145732
  76.1 1.0 %copy-start.2 = (f32[16,64,256]{2,1,0:T(8,128)}, f32[16,64,256]{2,1,0:T(8,128)S(1)}, u32[]{:S(2)}) copy-start(f32[16,64,256]{2,1,0:T(8,128)S(1)} %get-tuple-element.30.moved) | copy-start | bytes 3145732
  77.0 1.0 %copy-start.4 = (f32[16,64,256]{2,1,0:T(8,128)}, f32[16,64,256]{2,1,0:T(8,128)S(1)}, u32[]{:S(2)}) copy-start(f32[16,64,256]{2,1,0:T(8,128)S(1)} %get-tuple-element.31.drive) | copy-start | bytes 3145732
  84.3 10.7 %all-to-all-start.1 = ((f32[8,8,128]{2,1,0:T(8,128)}), f32[8,8,128]{2,1,0:T(8,128)S(1)}, u32[]{:S(2)}, u32[]{:S(2)}) async-start(f32[8,8,128]{2,1,0:T(8,128)} %broadcast_in_dim.5), calls=%async_computation.1 | async-start | bytes 65536 | tf_op jit(solution)/shard_map/all_to_all | solution.py:343
  89.3 1.6 %copy-start.1 = (f32[2,16,64,256]{3,2,1,0:T(8,128)S(1)}, f32[2,16,64,256]{3,2,1,0:T(8,128)}, u32[]{:S(2)}) copy-start(f32[2,16,64,256]{3,2,1,0:T(8,128)} %src.1) | copy-start | bytes 6291460
  90.9 4.2 %copy-start.3 = (f32[16,64,256]{2,1,0:T(8,128)S(1)}, f32[16,64,256]{2,1,0:T(8,128)}, u32[]{:S(2)}) copy-start(f32[16,64,256]{2,1,0:T(8,128)} %copy-done.2) | copy-start | bytes 3145732
  90.9 4.2 %copy-start.5 = (f32[16,64,256]{2,1,0:T(8,128)S(1)}, f32[16,64,256]{2,1,0:T(8,128)}, u32[]{:S(2)}) copy-start(f32[16,64,256]{2,1,0:T(8,128)} %copy-done.4) | copy-start | bytes 3145732

commit v2 on v1

--- a/solution.py
+++ b/solution.py
@@ -1,4 +1,5 @@
 import functools
+import math
 
 import jax
 import jax.numpy as jnp
@@ -17,7 +18,8 @@
 EPSILON = 1e-06
 
 PAD = 8
-VMEM_LIMIT = 48 * 2**20
+VMEM_ROOM = 2 * 2**20
+UNROLL = 4
 
 
 def passed_along(array, axis, by):
@@ -109,13 +111,15 @@
     return (current, parallel)
 
 
-def call(kernel, out_shape, scratch=(), name=None, vmem_out=None, **kw):
+def call(kernel, out_shape, scratch=(), name=None, **kw):
     return pl.pallas_call(
         kernel,
         out_shape=out_shape,
         scratch_shapes=list(scratch),
         name=name,
-        compiler_params=pltpu.CompilerParams(vmem_limit_bytes=VMEM_LIMIT),
+        compiler_params=pltpu.CompilerParams(
+            vmem_limit_bytes=VMEM_ROOM + sum(4 * math.prod(s.shape) for s in scratch if s is not DMA)
+        ),
         **kw,
     )
 
@@ -131,18 +135,24 @@
     return (below + above) + ys + xs - 6.0 * here
 
 
-def driving_layers(field, pot, count, emit):
-    def first(k, carry):
+def layer_loop(start, stop, body):
+    def step(k, carry):
+        body(k)
+        return carry
+
+    lax.fori_loop(start, stop, step, 0, unroll=min(UNROLL, stop - start))
+
+
+def potentials(field, pot, count):
+    def one(k):
         here = field[k + 1]
         pot[k] = here * here * here - here - GRADIENT_COEF * lap(field[k], here, field[k + 2])
-        return carry
-
-    lax.fori_loop(0, count + 2, first, 0)
-
-    def second(k, carry):
-        return emit(k, MOBILITY * lap(pot[k], pot[k + 1], pot[k + 2]), carry)
-
-    return second
+
+    layer_loop(0, count, one)
+
+
+def driving(pot, k):
+    return MOBILITY * lap(pot[k], pot[k + 1], pot[k + 2])
 
 
 def rows_sum(field):
@@ -194,16 +204,19 @@
     fill_padded(field, low.at[0:4], mine, high.at[0:4], sides, 0)
     fill_padded(end_out, low.at[4:6], end, high.at[4:6], sides, nz + 8)
 
-    def emit(k, drive, carry):
+    potentials(field, pot, nz + 6)
+
+    def edge(k):
+        step_out[k] = field[k + 2] + STEP_SIZE * driving(pot, k)
+
+    def inner(k):
+        drive = driving(pot, k)
         step_out[k] = field[k + 2] + STEP_SIZE * drive
-
-        @pl.when((k >= 2) & (k < nz + 2))
-        def _():
-            drive_out[k - 2] = drive[PAD : PAD + rows]
-
-        return carry
-
-    lax.fori_loop(0, nz + 4, driving_layers(field, pot, nz + 4, emit), 0)
+        drive_out[k - 2] = drive[PAD : PAD + rows]
+
+    layer_loop(0, 2, edge)
+    layer_loop(2, nz + 2, inner)
+    layer_loop(nz + 2, nz + 4, edge)
 
 
 def sums_of(count, lanes, fields):
@@ -213,13 +226,13 @@
         return tuple(t + rows_sum(v) for t, v in zip(totals, terms))
 
     zero = jnp.zeros((8, lanes), jnp.float32)
-    return lax.fori_loop(0, count, one, (zero,) * 4)
+    return lax.fori_loop(0, count, one, (zero,) * 4, unroll=UNROLL)
 
 
 def write_sums(out, totals):
-    out[...] = jnp.zeros_like(out)
-    for i, total in enumerate(totals):
-        out[i : i + 1] = lane_row(total)
+    table = jnp.concatenate([lane_row(t) for t in totals] + [jnp.zeros((4, 128), jnp.float32)], 0)
+    for peer in range(out.shape[0]):
+        out[peer] = table
 
 
 def first_sums_kernel(other, mine, end, drive, out):
@@ -247,11 +260,12 @@
     nz, rows, _ = other.shape
     fill_padded(field_out, low, other, high, sides, 0)
 
-    def emit(k, drive, carry):
-        step_out[k] = other[k] + STEP_SIZE * drive[PAD : PAD + rows]
-        return carry
-
-    lax.fori_loop(0, nz, driving_layers(field_out, pot, nz, emit), 0)
+    potentials(field_out, pot, nz + 2)
+
+    def one(k):
+        step_out[k] = other[k] + STEP_SIZE * driving(pot, k)[PAD : PAD + rows]
+
+    layer_loop(0, nz, one)
 
 
 def second_step_kernel(parts, step, end_wide, other_wide, moved_out, drive_out, field, pot):
@@ -259,18 +273,17 @@
     half = parts.shape[0] // 2
     coef, _, _ = coefficient(parts, half * lax.axis_index("image"), half)
 
-    def move(k, carry):
+    def move(k):
         field[k] = step[k] + coef * (other_wide[k] - end_wide[k])
-        return carry
-
-    lax.fori_loop(0, nz + 4, move, 0)
-
-    def emit(k, drive, carry):
-        drive_out[k] = drive[PAD : PAD + rows]
+
+    layer_loop(0, nz + 4, move)
+    potentials(field, pot, nz + 2)
+
+    def one(k):
+        drive_out[k] = driving(pot, k)[PAD : PAD + rows]
         moved_out[k] = field[k + 2][PAD : PAD + rows]
-        return carry
-
-    lax.fori_loop(0, nz, driving_layers(field, pot, nz, emit), 0)
+
+    layer_loop(0, nz, one)
 
 
 def second_sums_kernel(parts, far, mine, end, other_step, moved, drive, tangent_out, out):
@@ -338,9 +351,7 @@
 
 
 def to_all(sums, axes):
-    peers = lax.axis_size(axes)
-    spread = jnp.broadcast_to(sums[None], (peers,) + sums.shape)
-    return lax.all_to_all(spread, axes, 0, 0, tiled=True)
+    return lax.all_to_all(sums, axes, 0, 0, tiled=True)
 
 
 def body_pair(images):
@@ -380,10 +391,15 @@
         "first_step",
     )(mine, end, low, high, sides)
 
-    sums = call(first_sums_kernel, shape(8, 128), name="first_sums")(other, mine, end, drive)
-    parts = to_all(sums, ("image", "space", "yslab"))
-
+    everyone = ("image", "space", "yslab")
+    partners = ("space", "yslab")
+    other, drive = lax.optimization_barrier((other, drive))
     o_low, o_high = from_z(other[nz - 2 :], other[:2])
+    sums = call(first_sums_kernel, shape(lax.axis_size(everyone), 8, 128), name="first_sums")(
+        other, mine, end, drive
+    )
+    parts = to_all(sums, everyone)
+
     o_sides = y_sides(o_low, other, o_high)
     other_step, other_wide = call(
         other_step_kernel,
@@ -399,10 +415,10 @@
         "second_step",
     )(parts, step, end_wide, other_wide)
 
-    tangent, sums = call(second_sums_kernel, [block, shape(8, 128)], name="second_sums")(
-        parts, far, mine, end, other_step, moved, drive2
-    )
-    parts = to_all(sums, ("space", "yslab"))
+    tangent, sums = call(
+        second_sums_kernel, [block, shape(lax.axis_size(partners), 8, 128)], name="second_sums"
+    )(parts, far, mine, end, other_step, moved, drive2)
+    parts = to_all(sums, partners)
 
     return call(
         functools.partial(last_kernel, cells),

time: 97.2 us -> 83 us (0.85)
  Pallas kernels: 29.6 us -> 18.2 us
  waiting for transfers between devices: 28.5 us -> 24.4 us
  local copies, waits for them, and re-layouts: 13.3 us -> 16.8 us
  starting transfers between devices: 23.7 us -> 21.5 us
    ppermute x1, waiting for transfers between devices: 7.4 us -> 1.23 us  [body_pair(): other = lax.ppermute(mine, 'image', SWAP)]
    unnamed x30 -> x38, local copies, waits for them, and re-layouts: 12 us -> 16.7 us
    pallas_call x1, Pallas kernels: 7.29 us -> 3.17 us  [body_pair(): call(first_step_kernel, [shape(nz + 4, wide, nx), block, shape(nz + 4, wi...]
    pallas_call x1, Pallas kernels: 6.52 us -> 2.67 us  [body_pair(): call(second_step_kernel, [block, block], [pltpu.VMEM((nz + 4, wide, nx),...]
    ppermute x2, waiting for transfers between devices: 8.74 us -> 12.1 us  [from_z(): lax.ppermute(up, 'space', [(i, (i + 1) % count) for i in range(count)])]
    ppermute x2, waiting for transfers between devices: 9.49 us -> 6.99 us  [from_z(): lax.ppermute(down, 'space', [((i + 1) % count, i) for i in range(count)])]
    all_to_all x2, starting transfers between devices: 11.4 us -> 9.2 us  [to_all(): return lax.all_to_all(sums, axes, 0, 0, tiled=True)]
    pallas_call x1, Pallas kernels: 4.17 us -> 2.3 us  [body_pair(): call(other_step_kernel, [block, shape(nz + 4, wide, nx)], [pltpu.VMEM((nz...]
  transfers between devices with their start and end apart: 10 -> 10, of which waited for: 6 -> 7; matrix products, arithmetic and copies ran while one was open for 2% -> 1% of each run, Pallas kernels for 22% -> 13%
where the time goes in v2:
time: 83 us; the launch traced here: 82.5 us
  waiting for transfers between devices  24.4 us (29%)
  starting transfers between devices  21.5 us (26%)
  Pallas kernels  18.2 us (22%)
  local copies, waits for them, and re-layouts  16.8 us (20%)
  between operations  0.87 us (1%)
    unnamed x38, local copies, waits for them, and re-layouts  16.7 us
    ppermute x2, waiting for transfers between devices, from_z(): lax.ppermute(up, 'space', [(i, (i + 1) % count) for i in range(count)])  12.1 us
    all_to_all x2, starting transfers between devices, to_all(): return lax.all_to_all(sums, axes, 0, 0, tiled=True)  9.2 us
    ppermute x2, waiting for transfers between devices, from_z(): lax.ppermute(down, 'space', [((i + 1) % count, i) for i in range(count)])  6.99 us
    ppermute x2, starting transfers between devices, from_z(): lax.ppermute(down, 'space', [((i + 1) % count, i) for i in range(count)])  5.9 us
    pallas_call x1, Pallas kernels, body_pair(): call(second_sums_kernel, [block, shape(lax.axis_size(partners), 8, 128)],...  4.95 us
    all_to_all x2, waiting for transfers between devices, to_all(): return lax.all_to_all(sums, axes, 0, 0, tiled=True)  3.42 us
    pallas_call x1, Pallas kernels, body_pair(): call(first_step_kernel, [shape(nz + 4, wide, nx), block, shape(nz + 4, wi...  3.17 us
  transfers between devices with their start and end apart: 10, of which 7 were waited for; matrix products, arithmetic and copies ran while one was open for 1% of the time, Pallas kernels for 13%

profile of v2, /device:TPU:0, one launch (start us, length us, event | category | flops | bytes accessed | tf_op | source)
XLA Modules:
  0.0 82.5 jit_solution(15703772510777543983)
XLA Ops:
  0.6 0.0 copy-start
  0.6 1.6 %copy-done = f32[2,16,64,256]{3,2,1,0:T(8,128)S(1)} copy-done((f32[2,16,64,256]{3,2,1,0:T(8,128)S(1)}, f32[2,16,64,256]{3,2,1,0:T(8,128)}, u32[]{:S(2)}) %copy-start) | copy-done | bytes 2097176
  2.2 0.6 split.1
  2.8 3.1 %collective-permute-start.1 = (f32[6,64,256]{2,1,0:T(8,128)S(1)}, f32[6,64,256]{2,1,0:T(8,128)S(1)}, u32[]{:S(2)}, u32[]{:S(2)}) collective-permute-start(f32[6,64,256]{2,1,0:T(8,128)S(1)} %get-tuple-element.22), channel_id=1, source_target_pairs={{0,2},{2,4},{4,6},{6,0},{1,3},{3,5},{5,7},{7,1},{8,10},{10,12},{12... | collective-permute-start | bytes 1179656 | tf_op jit(solution)/shard_map/ppermute | solution.py:342
  5.9 2.1 %collective-permute-start.2 = (f32[6,64,256]{2,1,0:T(8,128)S(1)}, f32[6,64,256]{2,1,0:T(8,128)S(1)}, u32[]{:S(2)}, u32[]{:S(2)}) collective-permute-start(f32[6,64,256]{2,1,0:T(8,128)S(1)} %get-tuple-element.23), channel_id=1, source_target_pairs={{2,0},{4,2},{6,4},{0,6},{3,1},{5,3},{7,5},{1,7},{10,8},{12,10},{14... | collective-permute-start | bytes 1179656 | tf_op jit(solution)/shard_map/ppermute | solution.py:343
  8.0 1.6 %collective-permute-start = (f32[16,64,256]{2,1,0:T(8,128)S(1)}, f32[16,64,256]{2,1,0:T(8,128)S(1)}, u32[]{:S(2)}, u32[]{:S(2)}) collective-permute-start(f32[16,64,256]{2,1,0:T(8,128)S(1)} %get-tuple-element.20.mine), channel_id=1, source_target_pairs={{0,8},{8,0},{1,9},{9,1},{2,10},{10,2},{3,11},{11,3},{4,12},{12,4},... | collective-permute-start | bytes 3145736 | tf_op jit(solution)/shard_map/ppermute | solution.py:372
  9.7 8.2 %collective-permute-done.1.low = f32[6,64,256]{2,1,0:T(8,128)S(1)} collective-permute-done((f32[6,64,256]{2,1,0:T(8,128)S(1)}, f32[6,64,256]{2,1,0:T(8,128)S(1)}, u32[]{:S(2)}, u32[]{:S(2)}) %collective-permute-start.1) | collective-permute-done | bytes 393248 | tf_op jit(solution)/shard_map/ppermute | solution.py:342
  17.9 7.0 %collective-permute-done.2.high = f32[6,64,256]{2,1,0:T(8,128)S(1)} collective-permute-done((f32[6,64,256]{2,1,0:T(8,128)S(1)}, f32[6,64,256]{2,1,0:T(8,128)S(1)}, u32[]{:S(2)}, u32[]{:S(2)}) %collective-permute-start.2) | collective-permute-done | bytes 393248 | tf_op jit(solution)/shard_map/ppermute | solution.py:343
  25.0 0.1 collective-permute-start.3
  25.1 1.6 %collective-permute-start.4 = (f32[16,64,256]{2,1,0:T(8,128)S(1)}, f32[16,64,256]{2,1,0:T(8,128)}, u32[]{:S(2)}, u32[]{:S(2)}) collective-permute-start(f32[16,64,256]{2,1,0:T(8,128)S(1)} %get-tuple-element.29.end), channel_id=1, source_target_pairs={{0,8},{8,0},{1,9},{9,1},{2,10},{10,2},{3,11},{11,3},{4,12},{12,4},... | collective-permute-start | bytes 3145736 | tf_op jit(solution)/shard_map/ppermute | solution.py:375
  26.7 0.6 collective-permute-done.3.sides
  27.3 3.2 %first_step.1 = (f32[20,80,256]{2,1,0:T(8,128)S(1)}, f32[16,64,256]{2,1,0:T(8,128)S(1)}, f32[20,80,256]{2,1,0:T(8,128)S(1)}) custom-call(f32[16,64,256]{2,1,0:T(8,128)S(1)} %get-tuple-element.20.mine, f32[16,64,256]{2,1,0:T(8,128)S(1)} %get-tuple-element.29.end, f32[6,64,256]{2,1,0:T(8,128)S(1)} %collective-permute-done.1.low, ...), custom_call_target="tpu_custom_call" | custom-call | tf_op jit(solution)/shard_map/first_step/pallas_call | solution.py:387
  30.5 0.0 copy-start.4
  30.5 1.2 %copy-done.4 = f32[20,80,256]{2,1,0:T(8,128)} copy-done((f32[20,80,256]{2,1,0:T(8,128)}, f32[20,80,256]{2,1,0:T(8,128)S(1)}, u32[]{:S(2)}) %copy-start.4) | copy-done | bytes 1638424
  31.6 1.2 %copy-done.6 = f32[20,80,256]{2,1,0:T(8,128)} copy-done((f32[20,80,256]{2,1,0:T(8,128)}, f32[20,80,256]{2,1,0:T(8,128)S(1)}, u32[]{:S(2)}) %copy-start.6) | copy-done | bytes 1638424
  32.8 1.2 %collective-permute-done.other = f32[16,64,256]{2,1,0:T(8,128)S(1)} collective-permute-done((f32[16,64,256]{2,1,0:T(8,128)S(1)}, f32[16,64,256]{2,1,0:T(8,128)S(1)}, u32[]{:S(2)}, u32[]{:S(2)}) %collective-permute-start) | collective-permute-done | bytes 1048608 | tf_op jit(solution)/shard_map/ppermute | solution.py:372
  34.1 0.1 collective-permute-start.5
  34.1 3.8 %collective-permute-start.6 = (f32[2,64,256]{2,1,0:T(8,128)S(1)}, f32[2,64,256]{2,1,0:T(8,128)S(1)}, u32[]{:S(2)}, u32[]{:S(2)}) collective-permute-start(f32[2,64,256]{2,1,0:T(8,128)S(1)} %get-tuple-element.40), channel_id=1, source_target_pairs={{2,0},{4,2},{6,4},{0,6},{3,1},{5,3},{7,5},{1,7},{10,8},{12,10},{14... | collective-permute-start | bytes 393224 | tf_op jit(solution)/shard_map/ppermute | solution.py:343
  38.0 3.9 %collective-permute-done.5.low = f32[2,64,256]{2,1,0:T(8,128)S(1)} collective-permute-done((f32[2,64,256]{2,1,0:T(8,128)S(1)}, f32[2,64,256]{2,1,0:T(8,128)S(1)}, u32[]{:S(2)}, u32[]{:S(2)}) %collective-permute-start.5) | collective-permute-done | bytes 131104 | tf_op jit(solution)/shard_map/ppermute | solution.py:342
  41.9 0.7 copy-done.15
  42.5 0.0 collective-permute-done.6.high
  42.5 0.7 copy-done.17
  43.2 0.7 maximum_maximum_fusion
  43.9 0.0 collective-permute-start.7
  43.9 1.5 %first_sums.1 = f32[16,8,128]{2,1,0:T(8,128)S(1)} custom-call(f32[16,64,256]{2,1,0:T(8,128)S(1)} %collective-permute-done.other, f32[16,64,256]{2,1,0:T(8,128)S(1)} %get-tuple-element.20.mine, f32[16,64,256]{2,1,0:T(8,128)S(1)} %get-tuple-element.29.end, f32[16,64,256]{2,1,0:T(8,128)S(1)} %get-tuple-element.28.drive), custom_call_target="tpu_custom_call" | custom-call | tf_op jit(solution)/shard_map/first_sums/pallas_call | solution.py:398
  45.4 0.0 copy-start.14
  45.4 0.6 copy-done.14
  46.1 4.8 %all-to-all-start = ((f32[16,8,128]{2,1,0:T(8,128)}), f32[16,8,128]{2,1,0:T(8,128)S(1)}, u32[]{:S(2)}, u32[]{:S(2)}) async-start(f32[16,8,128]{2,1,0:T(8,128)} %copy-done.14), calls=%async_computation | async-start | bytes 131072 | tf_op jit(solution)/shard_map/all_to_all | solution.py:354
  50.9 0.0 collective-permute-done.7.sides
  50.9 0.9 %copy-done.16 = f32[2,64,256]{2,1,0:T(8,128)S(1)} copy-done((f32[2,64,256]{2,1,0:T(8,128)S(1)}, f32[2,64,256]{2,1,0:T(8,128)}, u32[]{:S(2)}) %copy-start.16) | copy-done | bytes 131096
  51.8 0.9 %copy-done.18 = f32[2,64,256]{2,1,0:T(8,128)S(1)} copy-done((f32[2,64,256]{2,1,0:T(8,128)S(1)}, f32[2,64,256]{2,1,0:T(8,128)}, u32[]{:S(2)}) %copy-start.18) | copy-done | bytes 131096
  52.7 2.3 %other_step.1 = (f32[16,64,256]{2,1,0:T(8,128)S(1)}, f32[20,80,256]{2,1,0:T(8,128)S(1)}) custom-call(f32[16,64,256]{2,1,0:T(8,128)S(1)} %collective-permute-done.other, f32[2,64,256]{2,1,0:T(8,128)S(1)} %copy-done.16, f32[2,64,256]{2,1,0:T(8,128)S(1)} %copy-done.18, f32[20,16,256]{2,1,0:T(8,128)S(1)} %collective-permute-done.7.sides), custom_call_target="tpu_custom_call" | custom-call | tf_op jit(solution)/shard_map/other_step/pallas_call | solution.py:404
  55.0 1.2 %copy-done.8 = f32[20,80,256]{2,1,0:T(8,128)} copy-done((f32[20,80,256]{2,1,0:T(8,128)}, f32[20,80,256]{2,1,0:T(8,128)S(1)}, u32[]{:S(2)}) %copy-start.8) | copy-done | bytes 1638424
  56.2 1.0 %copy-done.10 = f32[16,64,256]{2,1,0:T(8,128)} copy-done((f32[16,64,256]{2,1,0:T(8,128)}, f32[16,64,256]{2,1,0:T(8,128)S(1)}, u32[]{:S(2)}) %copy-start.10) | copy-done | bytes 1048600
  57.2 0.6 all-to-all-done.parts
  57.8 1.4 %copy-done.5 = f32[20,80,256]{2,1,0:T(8,128)S(1)} copy-done((f32[20,80,256]{2,1,0:T(8,128)S(1)}, f32[20,80,256]{2,1,0:T(8,128)}, u32[]{:S(2)}) %copy-start.5) | copy-done | bytes 1638424
  59.2 1.4 %copy-done.7 = f32[20,80,256]{2,1,0:T(8,128)S(1)} copy-done((f32[20,80,256]{2,1,0:T(8,128)S(1)}, f32[20,80,256]{2,1,0:T(8,128)}, u32[]{:S(2)}) %copy-start.7) | copy-done | bytes 1638424
  60.6 1.4 %copy-done.9 = f32[20,80,256]{2,1,0:T(8,128)S(1)} copy-done((f32[20,80,256]{2,1,0:T(8,128)S(1)}, f32[20,80,256]{2,1,0:T(8,128)}, u32[]{:S(2)}) %copy-start.9) | copy-done | bytes 1638424
  62.1 2.7 %second_step.1 = (f32[16,64,256]{2,1,0:T(8,128)S(1)}, f32[16,64,256]{2,1,0:T(8,128)S(1)}) custom-call(f32[16,8,128]{2,1,0:T(8,128)S(1)} %all-to-all-done.parts, f32[20,80,256]{2,1,0:T(8,128)S(1)} %copy-done.5, f32[20,80,256]{2,1,0:T(8,128)S(1)} %copy-done.7, f32[20,80,256]{2,1,0:T(8,128)S(1)} %copy-done.9), custom_call_target="tpu_custom_call" | custom-call | tf_op jit(solution)/shard_map/second_step/pallas_call | solution.py:411
  64.8 0.0 collective-permute-done.4.far
  64.8 4.9 %second_sums.1 = (f32[16,64,256]{2,1,0:T(8,128)S(1)}, f32[8,8,128]{2,1,0:T(8,128)}) custom-call(f32[16,8,128]{2,1,0:T(8,128)S(1)} %all-to-all-done.parts, f32[16,64,256]{2,1,0:T(8,128)} %collective-permute-done.4.far, f32[16,64,256]{2,1,0:T(8,128)S(1)} %get-tuple-element.20.mine, f32[16,64,256]{2,1,0:T(8,128)S(1)} %get-tuple-element.29.end, ...), custom_call_target="tpu_custom_call" | custom-call | tf_op jit(solution)/shard_map/second_sums/pallas_call | solution.py:418
  69.7 1.0 %copy-done.12 = f32[16,64,256]{2,1,0:T(8,128)} copy-done((f32[16,64,256]{2,1,0:T(8,128)}, f32[16,64,256]{2,1,0:T(8,128)S(1)}, u32[]{:S(2)}) %copy-start.12) | copy-done | bytes 1048600
  70.7 4.4 %all-to-all-start.1 = ((f32[8,8,128]{2,1,0:T(8,128)}), f32[8,8,128]{2,1,0:T(8,128)S(1)}, u32[]{:S(2)}, u32[]{:S(2)}) async-start(f32[8,8,128]{2,1,0:T(8,128)} %get-tuple-element.36), calls=%async_computation.1 | async-start | bytes 65536 | tf_op jit(solution)/shard_map/all_to_all | solution.py:354
  75.1 1.6 %copy-done.1 = f32[2,16,64,256]{3,2,1,0:T(8,128)S(1)} copy-done((f32[2,16,64,256]{3,2,1,0:T(8,128)S(1)}, f32[2,16,64,256]{3,2,1,0:T(8,128)}, u32[]{:S(2)}) %copy-start.1) | copy-done | bytes 2097176
  76.7 1.3 %base.1 = f32[2,16,64,256]{3,2,1,0:T(8,128)} custom-call(f32[2,16,64,256]{3,2,1,0:T(8,128)S(1)} %copy-done.1), custom_call_target="tpu_custom_call" | custom-call | tf_op jit(solution)/shard_map/base/pallas_call | solution.py:377
  78.0 2.8 %all-to-all-done.1.parts = f32[8,8,128]{2,1,0:T(8,128)S(1)} async-done(((f32[8,8,128]{2,1,0:T(8,128)}), f32[8,8,128]{2,1,0:T(8,128)S(1)}, u32[]{:S(2)}, u32[]{:S(2)}) %all-to-all-start.1) | async-done | bytes 32800 | tf_op jit(solution)/shard_map/all_to_all | solution.py:354
  80.8 0.0 copy-done.3
  80.8 1.7 %last.1 = (f32[2,16,64,256]{3,2,1,0:T(8,128)}, f32[2]{0:T(128)}) custom-call(f32[8,8,128]{2,1,0:T(8,128)S(1)} %all-to-all-done.1.parts, f32[16,64,256]{2,1,0:T(8,128)S(1)} %get-tuple-element.34.moved, f32[16,64,256]{2,1,0:T(8,128)S(1)} %copy-done.3, f32[16,64,256]{2,1,0:T(8,128)S(1)} %copy-done.13, ...), custom_call_target="tpu_custom_call", output_to_operand_aliasing={{0}: (4, {})} | custom-call | tf_op jit(solution)/shard_map/last/pallas_call | solution.py:423
  (32 shorter events, 0.2 us)
Async XLA Ops:
  0.6 1.6 %copy-start = (f32[2,16,64,256]{3,2,1,0:T(8,128)S(1)}, f32[2,16,64,256]{3,2,1,0:T(8,128)}, u32[]{:S(2)}) copy-start(f32[2,16,64,256]{3,2,1,0:T(8,128)} %src.1) | copy-start | bytes 6291460
  2.8 15.1 %collective-permute-start.1 = (f32[6,64,256]{2,1,0:T(8,128)S(1)}, f32[6,64,256]{2,1,0:T(8,128)S(1)}, u32[]{:S(2)}, u32[]{:S(2)}) collective-permute-start(f32[6,64,256]{2,1,0:T(8,128)S(1)} %get-tuple-element.22), channel_id=1, source_target_pairs={{0,2},{2,4},{4,6},{6,0},{1,3},{3,5},{5,7},{7,1},{8,10},{10,12},{12... | collective-permute-start | bytes 1179656 | tf_op jit(solution)/shard_map/ppermute | solution.py:342
  5.9 19.0 %collective-permute-start.2 = (f32[6,64,256]{2,1,0:T(8,128)S(1)}, f32[6,64,256]{2,1,0:T(8,128)S(1)}, u32[]{:S(2)}, u32[]{:S(2)}) collective-permute-start(f32[6,64,256]{2,1,0:T(8,128)S(1)} %get-tuple-element.23), channel_id=1, source_target_pairs={{2,0},{4,2},{6,4},{0,6},{3,1},{5,3},{7,5},{1,7},{10,8},{12,10},{14... | collective-permute-start | bytes 1179656 | tf_op jit(solution)/shard_map/ppermute | solution.py:343
  8.0 26.1 %collective-permute-start = (f32[16,64,256]{2,1,0:T(8,128)S(1)}, f32[16,64,256]{2,1,0:T(8,128)S(1)}, u32[]{:S(2)}, u32[]{:S(2)}) collective-permute-start(f32[16,64,256]{2,1,0:T(8,128)S(1)} %get-tuple-element.20.mine), channel_id=1, source_target_pairs={{0,8},{8,0},{1,9},{9,1},{2,10},{10,2},{3,11},{11,3},{4,12},{12,4},... | collective-permute-start | bytes 3145736 | tf_op jit(solution)/shard_map/ppermute | solution.py:372
  25.0 2.3 %collective-permute-start.3 = (f32[44,16,256]{2,1,0:T(8,128)S(1)}, f32[44,16,256]{2,1,0:T(8,128)S(1)}, u32[]{:S(2)}, u32[]{:S(2)}) collective-permute-start(f32[44,16,256]{2,1,0:T(8,128)S(1)} %maximum_dynamic-update-slice_fusion.4), channel_id=1, source_target_pairs={{0,1},{1,0},{2,3},{3,2},{4,5},{5,4},{6,7},{7,6},{8,9},{9,8},{10,11... | collective-permute-start | bytes 2162696 | tf_op jit(solution)/shard_map/ppermute | solution.py:350
  25.1 39.6 %collective-permute-start.4 = (f32[16,64,256]{2,1,0:T(8,128)S(1)}, f32[16,64,256]{2,1,0:T(8,128)}, u32[]{:S(2)}, u32[]{:S(2)}) collective-permute-start(f32[16,64,256]{2,1,0:T(8,128)S(1)} %get-tuple-element.29.end), channel_id=1, source_target_pairs={{0,8},{8,0},{1,9},{9,1},{2,10},{10,2},{3,11},{11,3},{4,12},{12,4},... | collective-permute-start | bytes 3145736 | tf_op jit(solution)/shard_map/ppermute | solution.py:375
  30.5 1.2 %copy-start.4 = (f32[20,80,256]{2,1,0:T(8,128)}, f32[20,80,256]{2,1,0:T(8,128)S(1)}, u32[]{:S(2)}) copy-start(f32[20,80,256]{2,1,0:T(8,128)S(1)} %get-tuple-element.31.step) | copy-start | bytes 4915204
  31.6 1.2 %copy-start.6 = (f32[20,80,256]{2,1,0:T(8,128)}, f32[20,80,256]{2,1,0:T(8,128)S(1)}, u32[]{:S(2)}) copy-start(f32[20,80,256]{2,1,0:T(8,128)S(1)} %get-tuple-element.32.end_wide) | copy-start | bytes 4915204
  34.1 7.8 %collective-permute-start.5 = (f32[2,64,256]{2,1,0:T(8,128)S(1)}, f32[2,64,256]{2,1,0:T(8,128)S(1)}, u32[]{:S(2)}, u32[]{:S(2)}) collective-permute-start(f32[2,64,256]{2,1,0:T(8,128)S(1)} %get-tuple-element.41), channel_id=1, source_target_pairs={{0,2},{2,4},{4,6},{6,0},{1,3},{3,5},{5,7},{7,1},{8,10},{10,12},{12... | collective-permute-start | bytes 393224 | tf_op jit(solution)/shard_map/ppermute | solution.py:342
  34.1 8.4 %collective-permute-start.6 = (f32[2,64,256]{2,1,0:T(8,128)S(1)}, f32[2,64,256]{2,1,0:T(8,128)S(1)}, u32[]{:S(2)}, u32[]{:S(2)}) collective-permute-start(f32[2,64,256]{2,1,0:T(8,128)S(1)} %get-tuple-element.40), channel_id=1, source_target_pairs={{2,0},{4,2},{6,4},{0,6},{3,1},{5,3},{7,5},{1,7},{10,8},{12,10},{14... | collective-permute-start | bytes 393224 | tf_op jit(solution)/shard_map/ppermute | solution.py:343
  41.9 0.7 copy-start.15
  42.5 0.7 copy-start.17
  43.9 7.0 %collective-permute-start.7 = (f32[20,16,256]{2,1,0:T(8,128)}, f32[20,16,256]{2,1,0:T(8,128)S(1)}, u32[]{:S(2)}, u32[]{:S(2)}) collective-permute-start(f32[20,16,256]{2,1,0:T(8,128)} %maximum_maximum_fusion), channel_id=1, source_target_pairs={{0,1},{1,0},{2,3},{3,2},{4,5},{5,4},{6,7},{7,6},{8,9},{9,8},{10,11... | collective-permute-start | bytes 983048 | tf_op jit(solution)/shard_map/ppermute | solution.py:350
  45.4 0.6 copy-start.14
  46.1 11.7 %all-to-all-start = ((f32[16,8,128]{2,1,0:T(8,128)}), f32[16,8,128]{2,1,0:T(8,128)S(1)}, u32[]{:S(2)}, u32[]{:S(2)}) async-start(f32[16,8,128]{2,1,0:T(8,128)} %copy-done.14), calls=%async_computation | async-start | bytes 131072 | tf_op jit(solution)/shard_map/all_to_all | solution.py:354
  50.9 0.9 %copy-start.16 = (f32[2,64,256]{2,1,0:T(8,128)S(1)}, f32[2,64,256]{2,1,0:T(8,128)}, u32[]{:S(2)}) copy-start(f32[2,64,256]{2,1,0:T(8,128)} %copy-done.15) | copy-start | bytes 393220
  51.8 0.9 %copy-start.18 = (f32[2,64,256]{2,1,0:T(8,128)S(1)}, f32[2,64,256]{2,1,0:T(8,128)}, u32[]{:S(2)}) copy-start(f32[2,64,256]{2,1,0:T(8,128)} %copy-done.17) | copy-start | bytes 393220
  55.0 1.2 %copy-start.8 = (f32[20,80,256]{2,1,0:T(8,128)}, f32[20,80,256]{2,1,0:T(8,128)S(1)}, u32[]{:S(2)}) copy-start(f32[20,80,256]{2,1,0:T(8,128)S(1)} %get-tuple-element.33.other_wide) | copy-start | bytes 4915204
  56.2 1.0 %copy-start.10 = (f32[16,64,256]{2,1,0:T(8,128)}, f32[16,64,256]{2,1,0:T(8,128)S(1)}, u32[]{:S(2)}) copy-start(f32[16,64,256]{2,1,0:T(8,128)S(1)} %get-tuple-element.30.other_step) | copy-start | bytes 3145732
  57.8 1.4 %copy-start.5 = (f32[20,80,256]{2,1,0:T(8,128)S(1)}, f32[20,80,256]{2,1,0:T(8,128)}, u32[]{:S(2)}) copy-start(f32[20,80,256]{2,1,0:T(8,128)} %copy-done.4) | copy-start | bytes 4915204
  59.2 1.4 %copy-start.7 = (f32[20,80,256]{2,1,0:T(8,128)S(1)}, f32[20,80,256]{2,1,0:T(8,128)}, u32[]{:S(2)}) copy-start(f32[20,80,256]{2,1,0:T(8,128)} %copy-done.6) | copy-start | bytes 4915204
  60.6 1.4 %copy-start.9 = (f32[20,80,256]{2,1,0:T(8,128)S(1)}, f32[20,80,256]{2,1,0:T(8,128)}, u32[]{:S(2)}) copy-start(f32[20,80,256]{2,1,0:T(8,128)} %copy-done.8) | copy-start | bytes 4915204
  62.1 2.7 %copy-start.11 = (f32[16,64,256]{2,1,0:T(8,128)S(1)}, f32[16,64,256]{2,1,0:T(8,128)}, u32[]{:S(2)}) copy-start(f32[16,64,256]{2,1,0:T(8,128)} %copy-done.10) | copy-start | bytes 3145732
  64.7 5.0 %copy-start.2 = (f32[16,64,256]{2,1,0:T(8,128)}, f32[16,64,256]{2,1,0:T(8,128)S(1)}, u32[]{:S(2)}) copy-start(f32[16,64,256]{2,1,0:T(8,128)S(1)} %get-tuple-element.35.drive) | copy-start | bytes 3145732
  69.7 1.0 %copy-start.12 = (f32[16,64,256]{2,1,0:T(8,128)}, f32[16,64,256]{2,1,0:T(8,128)S(1)}, u32[]{:S(2)}) copy-start(f32[16,64,256]{2,1,0:T(8,128)S(1)} %get-tuple-element.37.tangent) | copy-start | bytes 3145732
  70.7 10.1 %all-to-all-start.1 = ((f32[8,8,128]{2,1,0:T(8,128)}), f32[8,8,128]{2,1,0:T(8,128)S(1)}, u32[]{:S(2)}, u32[]{:S(2)}) async-start(f32[8,8,128]{2,1,0:T(8,128)} %get-tuple-element.36), calls=%async_computation.1 | async-start | bytes 65536 | tf_op jit(solution)/shard_map/all_to_all | solution.py:354
  75.1 1.6 %copy-start.1 = (f32[2,16,64,256]{3,2,1,0:T(8,128)S(1)}, f32[2,16,64,256]{3,2,1,0:T(8,128)}, u32[]{:S(2)}) copy-start(f32[2,16,64,256]{3,2,1,0:T(8,128)} %src.1) | copy-start | bytes 6291460
  76.7 4.2 %copy-start.3 = (f32[16,64,256]{2,1,0:T(8,128)S(1)}, f32[16,64,256]{2,1,0:T(8,128)}, u32[]{:S(2)}) copy-start(f32[16,64,256]{2,1,0:T(8,128)} %copy-done.2) | copy-start | bytes 3145732
  76.7 4.2 %copy-start.13 = (f32[16,64,256]{2,1,0:T(8,128)S(1)}, f32[16,64,256]{2,1,0:T(8,128)}, u32[]{:S(2)}) copy-start(f32[16,64,256]{2,1,0:T(8,128)} %copy-done.12) | copy-start | bytes 3145732

commit v3 on v2

--- a/solution.py
+++ b/solution.py
@@ -166,29 +166,29 @@
     return jnp.sum(folded, axis=0, keepdims=True)
 
 
-def fill_padded(dst, low, mid, high, sides, sides_at):
-    rows = mid.shape[1]
-    n_low, n_mid, n_high = low.shape[0], mid.shape[0], high.shape[0]
-    dst[0:n_low, PAD : PAD + rows] = low[...]
-    dst[n_low : n_low + n_mid, PAD : PAD + rows] = mid[...]
-    dst[n_low + n_mid : n_low + n_mid + n_high, PAD : PAD + rows] = high[...]
-    layers = n_low + n_mid + n_high
-    dst[:, 0:PAD] = sides[sides_at : sides_at + layers, PAD : 2 * PAD]
-    dst[:, PAD + rows : 2 * PAD + rows] = sides[sides_at : sides_at + layers, 0:PAD]
-
-
-def split_kernel(images, mine, end, up, down, sems):
+def fill_padded(dst, pieces, sides, sides_at):
+    at = 0
+    for piece in pieces:
+        layers, rows, _ = piece.shape
+        dst[at : at + layers, PAD : PAD + rows] = piece[...]
+        at += layers
+    dst[:, 0:PAD] = sides[sides_at : sides_at + at, PAD : 2 * PAD]
+    dst[:, PAD + rows : 2 * PAD + rows] = sides[sides_at : sides_at + at, 0:PAD]
+
+
+def split_kernel(images, mine, end, edges, middle, up, down, sems):
     which = 1 - lax.axis_index("image")
     nz = mine.shape[0]
     copies = [
         pltpu.make_async_copy(src, dst, sems.at[i])
         for i, (src, dst) in enumerate(
             [
+                (images.at[which, pl.ds(0, 2)], edges.at[pl.ds(0, 2)]),
+                (images.at[which, pl.ds(nz - 2, 2)], edges.at[pl.ds(2, 2)]),
+                (images.at[which, pl.ds(2, nz - 4)], middle),
+                (images.at[which, pl.ds(nz - 4, 4)], up),
+                (images.at[which, pl.ds(0, 4)], down),
                 (images.at[which], mine),
-                (images.at[which, pl.ds(nz - 4, 4)], up.at[pl.ds(0, 4)]),
-                (images.at[1 - which, pl.ds(nz - 2, 2)], up.at[pl.ds(4, 2)]),
-                (images.at[which, pl.ds(0, 4)], down.at[pl.ds(0, 4)]),
-                (images.at[1 - which, pl.ds(0, 2)], down.at[pl.ds(4, 2)]),
                 (images.at[1 - which], end),
             ]
         )
@@ -199,11 +199,9 @@
         c.wait()
 
 
-def first_step_kernel(mine, end, low, high, sides, step_out, drive_out, end_out, field, pot):
+def first_step_kernel(mine, low, high, sides, step_out, drive_out, field, pot):
     nz, rows, _ = mine.shape
-    fill_padded(field, low.at[0:4], mine, high.at[0:4], sides, 0)
-    fill_padded(end_out, low.at[4:6], end, high.at[4:6], sides, nz + 8)
-
+    fill_padded(field, (low, mine, high), sides, 0)
     potentials(field, pot, nz + 6)
 
     def edge(k):
@@ -219,94 +217,110 @@
     layer_loop(nz + 2, nz + 4, edge)
 
 
-def sums_of(count, lanes, fields):
+CHUNK = 16
+
+
+def sums_of(start, stop, rows, fields, totals):
     def one(k, totals):
-        plus, minus, tangent, drive = fields(k)
-        terms = (plus * plus, minus * minus, tangent * tangent, drive * tangent)
-        return tuple(t + rows_sum(v) for t, v in zip(totals, terms))
-
-    zero = jnp.zeros((8, lanes), jnp.float32)
-    return lax.fori_loop(0, count, one, (zero,) * 4, unroll=UNROLL)
+        for r in range(0, rows, CHUNK):
+            plus, minus, tangent, drive = fields(k, pl.ds(r, CHUNK))
+            terms = (plus * plus, minus * minus, tangent * tangent, drive * tangent)
+            totals = tuple(t + rows_sum(v) for t, v in zip(totals, terms))
+        return totals
+
+    return lax.fori_loop(start, stop, one, totals, unroll=min(UNROLL, stop - start))
+
+
+def no_sums(lanes):
+    return (jnp.zeros((8, lanes), jnp.float32),) * 4
 
 
 def write_sums(out, totals):
-    table = jnp.concatenate([lane_row(t) for t in totals] + [jnp.zeros((4, 128), jnp.float32)], 0)
-    for peer in range(out.shape[0]):
-        out[peer] = table
-
-
-def first_sums_kernel(other, mine, end, drive, out):
-    nz, _, lanes = mine.shape
-
-    def fields(k):
-        m, o, e = mine[k], other[k], end[k]
-        return o - m, m - e, o - e, drive[k]
-
-    write_sums(out, sums_of(nz, lanes, fields))
-
-
-def coefficient(parts, base, count):
-    total = parts[base]
-    for i in range(1, count):
-        total = total + parts[base + i]
-    total = jnp.sum(total, axis=1, keepdims=True)
+    out[...] = jnp.concatenate(
+        [lane_row(t) for t in totals] + [jnp.zeros((4, 128), jnp.float32)], 0
+    )
+
+
+def first_sums_kernel(edges, middle, mine, end, drive, out):
+    nz, rows, lanes = mine.shape
+
+    def fields_from(other, shift):
+        def fields(k, r):
+            m, o, e = mine[k, r], other[k + shift, r], end[k, r]
+            return o - m, m - e, o - e, drive[k, r]
+
+        return fields
+
+    totals = sums_of(0, 2, rows, fields_from(edges, 0), no_sums(lanes))
+    totals = sums_of(2, nz - 2, rows, fields_from(middle, -2), totals)
+    totals = sums_of(nz - 2, nz, rows, fields_from(edges, 4 - nz), totals)
+    write_sums(out, totals)
+
+
+def coefficient(sums):
+    total = jnp.sum(sums[...], axis=1, keepdims=True)
     plus_sq, minus_sq, tangent_sq, par = (total[i : i + 1] for i in range(4))
     safe = tangent_sq + EPSILON
     spring = SPRING_K * (jnp.sqrt(plus_sq) - jnp.sqrt(minus_sq)) / jnp.sqrt(safe)
     return STEP_SIZE * (spring - par / safe), par, safe
 
 
-def other_step_kernel(other, low, high, sides, step_out, field_out, pot):
-    nz, rows, _ = other.shape
-    fill_padded(field_out, low, other, high, sides, 0)
-
-    potentials(field_out, pot, nz + 2)
+def other_step_kernel(edges, middle, end, low, high, sides, step_out, tangent_out, field, pot):
+    nz, rows, _ = end.shape
+    first, last = edges.at[0:2], edges.at[2:4]
+    fill_padded(field, (low.at[0:2], first, middle, last, high.at[0:2]), sides, 0)
+    fill_padded(tangent_out, (low.at[2:4], end, high.at[2:4]), sides, nz + 4)
+    potentials(field, pot, nz + 2)
+
+    def widen(k):
+        tangent_out[k] = field[k] - tangent_out[k]
 
     def one(k):
-        step_out[k] = other[k] + STEP_SIZE * driving(pot, k)[PAD : PAD + rows]
-
+        moved = field[k + 2] + STEP_SIZE * driving(pot, k)
+        step_out[k] = moved[PAD : PAD + rows]
+
+    layer_loop(0, nz + 4, widen)
     layer_loop(0, nz, one)
 
 
-def second_step_kernel(parts, step, end_wide, other_wide, moved_out, drive_out, field, pot):
+def second_step_kernel(sums, step, tangent_wide, moved_out, drive_out, field, pot):
     nz, rows, _ = drive_out.shape
-    half = parts.shape[0] // 2
-    coef, _, _ = coefficient(parts, half * lax.axis_index("image"), half)
+    coef, _, _ = coefficient(sums)
 
     def move(k):
-        field[k] = step[k] + coef * (other_wide[k] - end_wide[k])
+        field[k] = step[k] + coef * tangent_wide[k]
 
     layer_loop(0, nz + 4, move)
     potentials(field, pot, nz + 2)
 
     def one(k):
-        drive_out[k] = driving(pot, k)[PAD : PAD + rows]
+        drive = driving(pot, k)[PAD : PAD + rows]
+        drive_out[k] = drive
         moved_out[k] = field[k + 2][PAD : PAD + rows]
 
     layer_loop(0, nz, one)
 
 
-def second_sums_kernel(parts, far, mine, end, other_step, moved, drive, tangent_out, out):
-    nz, _, lanes = mine.shape
-    half = parts.shape[0] // 2
-    coef, _, _ = coefficient(parts, half * (1 - lax.axis_index("image")), half)
-
-    def fields(k):
-        o = other_step[k] + coef * (mine[k] - far[k])
-        m, e = moved[k], end[k]
+def second_sums_kernel(sums, far, mine, end, other_step, moved, drive, tangent_out, out):
+    nz, rows, lanes = mine.shape
+    coef, _, _ = coefficient(sums)
+
+    def fields(k, r):
+        o = other_step[k, r] + coef * (mine[k, r] - far[k, r])
+        m, e = moved[k, r], end[k, r]
         tangent = o - e
-        tangent_out[k] = tangent
-        return o - m, m - e, tangent, drive[k]
-
-    write_sums(out, sums_of(nz, lanes, fields))
-
-
-def last_kernel(cells, parts, moved, drive, tangent, base, out, par_out, buf, sems):
+        tangent_out[k, r] = tangent
+        return o - m, m - e, tangent, drive[k, r]
+
+    write_sums(out, sums_of(0, nz, rows, fields, no_sums(lanes)))
+
+
+def last_kernel(cells, sums, moved, drive, tangent, base, out, par_out, buf, sems):
     del base
     nz = moved.shape[0]
     at = lax.axis_index("image")
     which = 1 - at
-    coef, par, safe = coefficient(parts, 0, parts.shape[0])
+    coef, par, safe = coefficient(sums)
     copies = []
     for k in range(nz):
         buf[k] = moved[k] + STEP_SIZE * drive[k] + coef * tangent[k]
@@ -350,29 +364,50 @@
     return lax.ppermute(jnp.concatenate(ends, 0), "yslab", SWAP)
 
 
-def to_all(sums, axes):
-    return lax.all_to_all(sums, axes, 0, 0, tiled=True)
+def summed(sums):
+    sums = sums + lax.ppermute(sums, "yslab", SWAP)
+    count, stride = lax.axis_size("space"), 1
+    while stride < count:
+        sums = sums + lax.ppermute(sums, "space", [(i, i ^ stride) for i in range(count)])
+        stride *= 2
+    return sums
 
 
 def body_pair(images):
     _, nz, ny, nx = images.shape
     wide = ny + 2 * PAD
     cells = float(nz * lax.axis_size("space") * ny * lax.axis_size("yslab") * nx)
-    block = shape(nz, ny, nx)
-
-    mine, end, up, down = call(
+    block, outer = shape(nz, ny, nx), shape(nz + 4, wide, nx)
+    table = shape(8, 128)
+
+    def room(layers):
+        return pltpu.VMEM((layers, wide, nx), jnp.float32)
+
+    mine, end, edges, middle, up, down = call(
         split_kernel,
-        [block, block, shape(6, ny, nx), shape(6, ny, nx)],
-        [DMA((6,))],
+        [block, block, shape(4, ny, nx), shape(nz - 4, ny, nx), shape(4, ny, nx), shape(4, ny, nx)],
+        [DMA((7,))],
         "split",
         in_specs=[ANY],
-        out_specs=[ANY] * 4,
+        out_specs=[ANY] * 6,
     )(images)
 
-    other = lax.ppermute(mine, "image", SWAP)
+    o_edges = lax.ppermute(edges, "image", SWAP)
+    o_middle = lax.ppermute(middle, "image", SWAP)
+
     low, high = from_z(up, down)
-    end_later, low, high = lax.optimization_barrier((end, low, high))
+    sides = y_sides(low, mine, high)
+    step, drive = call(first_step_kernel, [outer, block], [room(nz + 8), room(nz + 6)], "first_step")(
+        mine, low, high, sides
+    )
+
+    end_later, drive = lax.optimization_barrier((end, drive))
     far = lax.ppermute(end_later, "image", SWAP)
+
+    o_low, o_high = from_z(
+        jnp.concatenate([o_edges[2:], end[nz - 2 :]]), jnp.concatenate([o_edges[:2], end[:2]])
+    )
+    o_sides = y_sides(o_low[:2], o_edges[:2], o_middle, o_edges[2:], o_high[:2], o_low[2:], end, o_high[2:])
 
     base = call(
         copy_kernel,
@@ -383,42 +418,19 @@
         out_specs=ANY,
     )(images)
 
-    sides = y_sides(low[:4], mine, high[:4], low[4:], end, high[4:])
-    step, drive, end_wide = call(
-        first_step_kernel,
-        [shape(nz + 4, wide, nx), block, shape(nz + 4, wide, nx)],
-        [pltpu.VMEM((nz + 8, wide, nx), jnp.float32), pltpu.VMEM((nz + 6, wide, nx), jnp.float32)],
-        "first_step",
-    )(mine, end, low, high, sides)
-
-    everyone = ("image", "space", "yslab")
-    partners = ("space", "yslab")
-    other, drive = lax.optimization_barrier((other, drive))
-    o_low, o_high = from_z(other[nz - 2 :], other[:2])
-    sums = call(first_sums_kernel, shape(lax.axis_size(everyone), 8, 128), name="first_sums")(
-        other, mine, end, drive
-    )
-    parts = to_all(sums, everyone)
-
-    o_sides = y_sides(o_low, other, o_high)
-    other_step, other_wide = call(
-        other_step_kernel,
-        [block, shape(nz + 4, wide, nx)],
-        [pltpu.VMEM((nz + 2, wide, nx), jnp.float32)],
-        "other_step",
-    )(other, o_low, o_high, o_sides)
+    sums = summed(call(first_sums_kernel, table, name="first_sums")(o_edges, o_middle, mine, end, drive))
+    other_step, tangent_wide = call(
+        other_step_kernel, [block, outer], [room(nz + 4), room(nz + 2)], "other_step"
+    )(o_edges, o_middle, end, o_low, o_high, o_sides)
 
     moved, drive2 = call(
-        second_step_kernel,
-        [block, block],
-        [pltpu.VMEM((nz + 4, wide, nx), jnp.float32), pltpu.VMEM((nz + 2, wide, nx), jnp.float32)],
-        "second_step",
-    )(parts, step, end_wide, other_wide)
-
-    tangent, sums = call(
-        second_sums_kernel, [block, shape(lax.axis_size(partners), 8, 128)], name="second_sums"
-    )(parts, far, mine, end, other_step, moved, drive2)
-    parts = to_all(sums, partners)
+        second_step_kernel, [block, block], [room(nz + 4), room(nz + 2)], "second_step"
+    )(sums, step, tangent_wide)
+
+    o_sums = lax.ppermute(sums, "image", SWAP)
+    tangent, sums = call(second_sums_kernel, [block, table], name="second_sums")(
+        o_sums, far, mine, end, other_step, moved, drive2
+    )
 
     return call(
         functools.partial(last_kernel, cells),
@@ -428,11 +440,13 @@
         in_specs=[VMEM] * 4 + [ANY],
         out_specs=[ANY, SMEM],
         input_output_aliases={4: 0},
-    )(parts, moved, drive2, tangent, base)
+    )(summed(sums), moved, drive2, tangent, base)
 
 
 def body(images):
+    layers = lax.axis_size("space")
     pair = lax.axis_size("image") == 2 and lax.axis_size("yslab") == 2 and images.shape[0] == 2
+    pair = pair and layers & (layers - 1) == 0
     return body_pair(images) if pair else body_any(images)
 
 

time: 83 us -> 74.3 us (0.90)
  local copies, waits for them, and re-layouts: 16.8 us -> 1.71 us
  waiting for transfers between devices: 24.4 us -> 36.5 us
  Pallas kernels: 18.2 us -> 15.7 us
  starting transfers between devices: 21.5 us -> 19.2 us
    ppermute x1 -> x9, waiting for transfers between devices: 1.23 us -> 22 us  [the longest x4 9.98 us: summed(): lax.ppermute(sums, 'space', [(i, i ^ stride) for i in range(count)])]
    unnamed x38 -> x4, local copies, waits for them, and re-layouts: 16.7 us -> 1.59 us
    ppermute x2, waiting for transfers between devices: 12.1 us -> 2.7 us  [from_z(): lax.ppermute(up, 'space', [(i, (i + 1) % count) for i in range(count)])]
    all_to_all x2 -> x0, starting transfers between devices: 9.2 us -> none  [to_all(): return lax.all_to_all(sums, axes, 0, 0, tiled=True)]
    ppermute x1 -> x9, starting transfers between devices: 1.65 us -> 9.15 us  [the longest x4 4.91 us: summed(): lax.ppermute(sums, 'space', [(i, i ^ stride) for i in range(count)])]
    ppermute x2, waiting for transfers between devices: 6.99 us -> 11.8 us  [from_z(): lax.ppermute(down, 'space', [((i + 1) % count, i) for i in range(count)])]
    all_to_all x2 -> x0, waiting for transfers between devices: 3.42 us -> none  [to_all(): return lax.all_to_all(sums, axes, 0, 0, tiled=True)]
    pallas_call x6, Pallas kernels: 15.2 us -> 12.7 us  [the longest x1 3.44 us: body_pair(): call(second_sums_kernel, [block, table], name='second_sums')]
  transfers between devices with their start and end apart: 10 -> 16, of which waited for: 7 -> 11; matrix products, arithmetic and copies ran while one was open for 1% -> 0% of each run, Pallas kernels for 13% -> 14%
where the time goes in v3:
time: 74.3 us; the launch traced here: 74.1 us
  waiting for transfers between devices  36.5 us (49%)
  starting transfers between devices  19.2 us (26%)
  Pallas kernels  15.7 us (21%)
  local copies, waits for them, and re-layouts  1.71 us (2%)
  between operations  0.84 us (1%)
    ppermute x2, waiting for transfers between devices, from_z(): lax.ppermute(down, 'space', [((i + 1) % count, i) for i in range(count)])  11.8 us
    ppermute x4, waiting for transfers between devices, summed(): lax.ppermute(sums, 'space', [(i, i ^ stride) for i in range(count)])  9.98 us
    ppermute x1, waiting for transfers between devices, body_pair(): o_sums = lax.ppermute(sums, 'image', SWAP)  6.86 us
    ppermute x4, starting transfers between devices, summed(): lax.ppermute(sums, 'space', [(i, i ^ stride) for i in range(count)])  4.91 us
    ppermute x2, starting transfers between devices, from_z(): lax.ppermute(up, 'space', [(i, (i + 1) % count) for i in range(count)])  4.23 us
    ppermute x2, starting transfers between devices, from_z(): lax.ppermute(down, 'space', [((i + 1) % count, i) for i in range(count)])  4.13 us
    pallas_call x1, Pallas kernels, body_pair(): call(second_sums_kernel, [block, table], name='second_sums')  3.44 us
    pallas_call x1, Pallas kernels, body_pair(): call(first_step_kernel, [outer, block], [room(nz + 8), room(nz + 6)], 'fi...  3.06 us
  transfers between devices with their start and end apart: 16, of which 11 were waited for; matrix products, arithmetic and copies ran while one was open for 0% of the time, Pallas kernels for 14%

profile of v3, /device:TPU:0, one launch (start us, length us, event | category | flops | bytes accessed | tf_op | source)
XLA Modules:
  0.0 74.1 jit_solution(10789751363960090297)
XLA Ops:
  0.6 0.0 copy-start
  0.6 1.6 %copy-done = f32[2,16,64,256]{3,2,1,0:T(8,128)S(1)} copy-done((f32[2,16,64,256]{3,2,1,0:T(8,128)S(1)}, f32[2,16,64,256]{3,2,1,0:T(8,128)}, u32[]{:S(2)}) %copy-start) | copy-done | bytes 2097176
  2.2 0.6 split.1
  2.8 3.0 %collective-permute-start = (f32[4,64,256]{2,1,0:T(8,128)S(1)}, f32[4,64,256]{2,1,0:T(8,128)S(1)}, u32[]{:S(2)}, u32[]{:S(2)}) collective-permute-start(f32[4,64,256]{2,1,0:T(8,128)S(1)} %get-tuple-element.18), channel_id=1, source_target_pairs={{0,8},{8,0},{1,9},{9,1},{2,10},{10,2},{3,11},{11,3},{4,12},{12,4},... | collective-permute-start | bytes 786440 | tf_op jit(solution)/shard_map/ppermute | solution.py:395
  5.8 0.1 collective-permute-start.1
  5.9 2.0 %collective-permute-start.2 = (f32[4,64,256]{2,1,0:T(8,128)S(1)}, f32[4,64,256]{2,1,0:T(8,128)S(1)}, u32[]{:S(2)}, u32[]{:S(2)}) collective-permute-start(f32[4,64,256]{2,1,0:T(8,128)S(1)} %get-tuple-element.22), channel_id=1, source_target_pairs={{0,2},{2,4},{4,6},{6,0},{1,3},{3,5},{5,7},{7,1},{8,10},{10,12},{12... | collective-permute-start | bytes 786440 | tf_op jit(solution)/shard_map/ppermute | solution.py:356
  8.0 2.0 %collective-permute-start.3 = (f32[4,64,256]{2,1,0:T(8,128)S(1)}, f32[4,64,256]{2,1,0:T(8,128)S(1)}, u32[]{:S(2)}, u32[]{:S(2)}) collective-permute-start(f32[4,64,256]{2,1,0:T(8,128)S(1)} %get-tuple-element.23), channel_id=1, source_target_pairs={{2,0},{4,2},{6,4},{0,6},{3,1},{5,3},{7,5},{1,7},{10,8},{12,10},{14... | collective-permute-start | bytes 786440 | tf_op jit(solution)/shard_map/ppermute | solution.py:357
  10.1 2.9 %collective-permute-done.edges = f32[4,64,256]{2,1,0:T(8,128)S(1)} collective-permute-done((f32[4,64,256]{2,1,0:T(8,128)S(1)}, f32[4,64,256]{2,1,0:T(8,128)S(1)}, u32[]{:S(2)}, u32[]{:S(2)}) %collective-permute-start) | collective-permute-done | bytes 262176 | tf_op jit(solution)/shard_map/ppermute | solution.py:395
  13.0 2.2 %collective-permute-start.10 = (f32[4,64,256]{2,1,0:T(8,128)S(1)}, f32[4,64,256]{2,1,0:T(8,128)S(1)}, u32[]{:S(2)}, u32[]{:S(2)}) collective-permute-start(f32[4,64,256]{2,1,0:T(8,128)S(1)} %pad_maximum_fusion), channel_id=1, source_target_pairs={{0,2},{2,4},{4,6},{6,0},{1,3},{3,5},{5,7},{7,1},{8,10},{10,12},{12... | collective-permute-start | bytes 786440 | tf_op jit(solution)/shard_map/ppermute | solution.py:356
  15.2 2.1 %collective-permute-start.11 = (f32[4,64,256]{2,1,0:T(8,128)S(1)}, f32[4,64,256]{2,1,0:T(8,128)S(1)}, u32[]{:S(2)}, u32[]{:S(2)}) collective-permute-start(f32[4,64,256]{2,1,0:T(8,128)S(1)} %pad_maximum_fusion.1), channel_id=1, source_target_pairs={{2,0},{4,2},{6,4},{0,6},{3,1},{5,3},{7,5},{1,7},{10,8},{12,10},{14... | collective-permute-start | bytes 786440 | tf_op jit(solution)/shard_map/ppermute | solution.py:357
  17.3 0.0 collective-permute-done.2.low
  17.4 8.3 %collective-permute-done.3.high = f32[4,64,256]{2,1,0:T(8,128)S(1)} collective-permute-done((f32[4,64,256]{2,1,0:T(8,128)S(1)}, f32[4,64,256]{2,1,0:T(8,128)S(1)}, u32[]{:S(2)}, u32[]{:S(2)}) %collective-permute-start.3) | collective-permute-done | bytes 262176 | tf_op jit(solution)/shard_map/ppermute | solution.py:357
  25.7 0.1 collective-permute-start.4
  25.8 2.7 %collective-permute-done.10.low = f32[4,64,256]{2,1,0:T(8,128)S(1)} collective-permute-done((f32[4,64,256]{2,1,0:T(8,128)S(1)}, f32[4,64,256]{2,1,0:T(8,128)S(1)}, u32[]{:S(2)}, u32[]{:S(2)}) %collective-permute-start.10) | collective-permute-done | bytes 262176 | tf_op jit(solution)/shard_map/ppermute | solution.py:356
  28.5 3.5 %collective-permute-done.11.high = f32[4,64,256]{2,1,0:T(8,128)S(1)} collective-permute-done((f32[4,64,256]{2,1,0:T(8,128)S(1)}, f32[4,64,256]{2,1,0:T(8,128)S(1)}, u32[]{:S(2)}, u32[]{:S(2)}) %collective-permute-start.11) | collective-permute-done | bytes 262176 | tf_op jit(solution)/shard_map/ppermute | solution.py:357
  32.0 0.0 collective-permute-done.4.sides
  32.0 3.1 %first_step.1 = (f32[20,80,256]{2,1,0:T(8,128)S(1)}, f32[16,64,256]{2,1,0:T(8,128)S(1)}) custom-call(f32[16,64,256]{2,1,0:T(8,128)S(1)} %get-tuple-element.20.mine, f32[4,64,256]{2,1,0:T(8,128)S(1)} %collective-permute-done.2.low, f32[4,64,256]{2,1,0:T(8,128)S(1)} %collective-permute-done.3.high, f32[24,16,256]{2,1,0:T(8,128)S(1)} %collective-permute-done.4.sides), custom_call_target="tpu_custom_call" | custom-call | tf_op jit(solution)/shard_map/first_step/pallas_call | solution.py:400
  35.1 1.6 %collective-permute-start.9 = (f32[16,64,256]{2,1,0:T(8,128)S(1)}, f32[16,64,256]{2,1,0:T(8,128)S(1)}, u32[]{:S(2)}, u32[]{:S(2)}) collective-permute-start(f32[16,64,256]{2,1,0:T(8,128)S(1)} %get-tuple-element.26.end), channel_id=1, source_target_pairs={{0,8},{8,0},{1,9},{9,1},{2,10},{10,2},{3,11},{11,3},{4,12},{12,4},... | collective-permute-start | bytes 3145736 | tf_op jit(solution)/shard_map/ppermute | solution.py:405
  36.7 0.0 collective-permute-done.1.middle
  36.8 0.1 collective-permute-start.12
  36.9 0.4 first_sums.1
  37.3 0.6 collective-permute-start.5
  37.9 1.1 %collective-permute-done.5 = f32[8,128]{1,0:T(8,128)S(1)} collective-permute-done((f32[8,128]{1,0:T(8,128)S(1)}, f32[8,128]{1,0:T(8,128)S(1)}, u32[]{:S(2)}, u32[]{:S(2)}) %collective-permute-start.5) | collective-permute-done | bytes 4128 | tf_op jit(solution)/shard_map/ppermute | solution.py:368
  39.0 1.1 %collective-permute-start.6 = (f32[8,128]{1,0:T(8,128)S(1)}, f32[8,128]{1,0:T(8,128)S(1)}, u32[]{:S(2)}, u32[]{:S(2)}) collective-permute-start(f32[8,128]{1,0:T(8,128)S(1)} %add.18), channel_id=1, source_target_pairs={{0,2},{2,0},{4,6},{6,4},{1,3},{3,1},{5,7},{7,5},{8,10},{10,8},{12,... | collective-permute-start | bytes 12296 | tf_op jit(solution)/shard_map/ppermute | solution.py:371
  40.1 2.5 %collective-permute-done.6 = f32[8,128]{1,0:T(8,128)S(1)} collective-permute-done((f32[8,128]{1,0:T(8,128)S(1)}, f32[8,128]{1,0:T(8,128)S(1)}, u32[]{:S(2)}, u32[]{:S(2)}) %collective-permute-start.6) | collective-permute-done | bytes 4128 | tf_op jit(solution)/shard_map/ppermute | solution.py:371
  42.6 1.2 %collective-permute-start.7 = (f32[8,128]{1,0:T(8,128)S(1)}, f32[8,128]{1,0:T(8,128)S(1)}, u32[]{:S(2)}, u32[]{:S(2)}) collective-permute-start(f32[8,128]{1,0:T(8,128)S(1)} %add.19), channel_id=1, source_target_pairs={{0,4},{2,6},{4,0},{6,2},{1,5},{3,7},{5,1},{7,3},{8,12},{10,14},{12... | collective-permute-start | bytes 12296 | tf_op jit(solution)/shard_map/ppermute | solution.py:371
  43.8 3.3 %collective-permute-done.7 = f32[8,128]{1,0:T(8,128)S(1)} collective-permute-done((f32[8,128]{1,0:T(8,128)S(1)}, f32[8,128]{1,0:T(8,128)S(1)}, u32[]{:S(2)}, u32[]{:S(2)}) %collective-permute-start.7) | collective-permute-done | bytes 4128 | tf_op jit(solution)/shard_map/ppermute | solution.py:371
  47.1 0.5 collective-permute-start.8
  47.6 0.0 collective-permute-done.12.sides
  47.6 2.6 %other_step.1 = (f32[16,64,256]{2,1,0:T(8,128)S(1)}, f32[20,80,256]{2,1,0:T(8,128)S(1)}) custom-call(f32[4,64,256]{2,1,0:T(8,128)S(1)} %collective-permute-done.edges, f32[12,64,256]{2,1,0:T(8,128)S(1)} %collective-permute-done.1.middle, f32[16,64,256]{2,1,0:T(8,128)S(1)} %get-tuple-element.26.end, f32[4,64,256]{2,1,0:T(8,128)S(1)} %collective-permute-done.10.low, ...), custom_call_target="tpu_custom_call" | custom-call | tf_op jit(solution)/shard_map/other_step/pallas_call | solution.py:422
  50.2 2.6 %second_step.1 = (f32[16,64,256]{2,1,0:T(8,128)S(1)}, f32[16,64,256]{2,1,0:T(8,128)S(1)}) custom-call(f32[8,128]{1,0:T(8,128)S(1)} %add.20.sums, f32[20,80,256]{2,1,0:T(8,128)S(1)} %get-tuple-element.28.step, f32[20,80,256]{2,1,0:T(8,128)S(1)} %get-tuple-element.29.tangent_wide), custom_call_target="tpu_custom_call" | custom-call | tf_op jit(solution)/shard_map/second_step/pallas_call | solution.py:426
  52.8 6.9 %collective-permute-done.8.sums = f32[8,128]{1,0:T(8,128)S(1)} collective-permute-done((f32[8,128]{1,0:T(8,128)S(1)}, f32[8,128]{1,0:T(8,128)S(1)}, u32[]{:S(2)}, u32[]{:S(2)}) %collective-permute-start.8) | collective-permute-done | bytes 4128 | tf_op jit(solution)/shard_map/ppermute | solution.py:430
  59.7 0.0 collective-permute-done.9.far
  59.7 0.0 copy-start.1
  59.7 3.4 %second_sums.1 = (f32[16,64,256]{2,1,0:T(8,128)S(1)}, f32[8,128]{1,0:T(8,128)S(1)}) custom-call(f32[8,128]{1,0:T(8,128)S(1)} %collective-permute-done.8.sums, f32[16,64,256]{2,1,0:T(8,128)S(1)} %collective-permute-done.9.far, f32[16,64,256]{2,1,0:T(8,128)S(1)} %get-tuple-element.20.mine, f32[16,64,256]{2,1,0:T(8,128)S(1)} %get-tuple-element.26.end, ...), custom_call_target="tpu_custom_call" | custom-call | tf_op jit(solution)/shard_map/second_sums/pallas_call | solution.py:431
  63.1 0.1 collective-permute-start.13
  63.2 1.2 %collective-permute-done.13 = f32[8,128]{1,0:T(8,128)S(1)} collective-permute-done((f32[8,128]{1,0:T(8,128)S(1)}, f32[8,128]{1,0:T(8,128)S(1)}, u32[]{:S(2)}, u32[]{:S(2)}) %collective-permute-start.13) | collective-permute-done | bytes 4128 | tf_op jit(solution)/shard_map/ppermute | solution.py:368
  64.3 1.8 %collective-permute-start.14 = (f32[8,128]{1,0:T(8,128)S(1)}, f32[8,128]{1,0:T(8,128)S(1)}, u32[]{:S(2)}, u32[]{:S(2)}) collective-permute-start(f32[8,128]{1,0:T(8,128)S(1)} %add.21), channel_id=1, source_target_pairs={{0,2},{2,0},{4,6},{6,4},{1,3},{3,1},{5,7},{7,5},{8,10},{10,8},{12,... | collective-permute-start | bytes 12296 | tf_op jit(solution)/shard_map/ppermute | solution.py:371
  66.1 1.8 %collective-permute-done.14 = f32[8,128]{1,0:T(8,128)S(1)} collective-permute-done((f32[8,128]{1,0:T(8,128)S(1)}, f32[8,128]{1,0:T(8,128)S(1)}, u32[]{:S(2)}, u32[]{:S(2)}) %collective-permute-start.14) | collective-permute-done | bytes 4128 | tf_op jit(solution)/shard_map/ppermute | solution.py:371
  68.0 0.8 %collective-permute-start.15 = (f32[8,128]{1,0:T(8,128)S(1)}, f32[8,128]{1,0:T(8,128)S(1)}, u32[]{:S(2)}, u32[]{:S(2)}) collective-permute-start(f32[8,128]{1,0:T(8,128)S(1)} %add.22), channel_id=1, source_target_pairs={{0,4},{2,6},{4,0},{6,2},{1,5},{3,7},{5,1},{7,3},{8,12},{10,14},{12... | collective-permute-start | bytes 12296 | tf_op jit(solution)/shard_map/ppermute | solution.py:371
  68.7 0.0 copy-done.1
  68.7 1.3 %base.1 = f32[2,16,64,256]{3,2,1,0:T(8,128)} custom-call(f32[2,16,64,256]{3,2,1,0:T(8,128)S(1)} %copy-done.1), custom_call_target="tpu_custom_call" | custom-call | tf_op jit(solution)/shard_map/base/pallas_call | solution.py:412
  70.1 2.4 %collective-permute-done.15 = f32[8,128]{1,0:T(8,128)S(1)} collective-permute-done((f32[8,128]{1,0:T(8,128)S(1)}, f32[8,128]{1,0:T(8,128)S(1)}, u32[]{:S(2)}, u32[]{:S(2)}) %collective-permute-start.15) | collective-permute-done | bytes 4128 | tf_op jit(solution)/shard_map/ppermute | solution.py:371
  72.5 1.7 %last.1 = (f32[2,16,64,256]{3,2,1,0:T(8,128)}, f32[2]{0:T(128)}) custom-call(f32[8,128]{1,0:T(8,128)S(1)} %add.23.sums, f32[16,64,256]{2,1,0:T(8,128)S(1)} %get-tuple-element.30.moved, f32[16,64,256]{2,1,0:T(8,128)S(1)} %get-tuple-element.31.drive, f32[16,64,256]{2,1,0:T(8,128)S(1)} %get-tuple-element.33.tangent, ...), custom_call_target="tpu_custom_call", output_to_operand_aliasing={{0}: (4, {})} | custom-call | tf_op jit(solution)/shard_map/last/pallas_call | solution.py:435
  (27 shorter events, 0.3 us)
Async XLA Ops:
  0.6 1.6 %copy-start = (f32[2,16,64,256]{3,2,1,0:T(8,128)S(1)}, f32[2,16,64,256]{3,2,1,0:T(8,128)}, u32[]{:S(2)}) copy-start(f32[2,16,64,256]{3,2,1,0:T(8,128)} %src.1) | copy-start | bytes 6291460
  2.8 10.1 %collective-permute-start = (f32[4,64,256]{2,1,0:T(8,128)S(1)}, f32[4,64,256]{2,1,0:T(8,128)S(1)}, u32[]{:S(2)}, u32[]{:S(2)}) collective-permute-start(f32[4,64,256]{2,1,0:T(8,128)S(1)} %get-tuple-element.18), channel_id=1, source_target_pairs={{0,8},{8,0},{1,9},{9,1},{2,10},{10,2},{3,11},{11,3},{4,12},{12,4},... | collective-permute-start | bytes 786440 | tf_op jit(solution)/shard_map/ppermute | solution.py:395
  5.8 30.8 %collective-permute-start.1 = (f32[12,64,256]{2,1,0:T(8,128)S(1)}, f32[12,64,256]{2,1,0:T(8,128)S(1)}, u32[]{:S(2)}, u32[]{:S(2)}) collective-permute-start(f32[12,64,256]{2,1,0:T(8,128)S(1)} %get-tuple-element.19), channel_id=1, source_target_pairs={{0,8},{8,0},{1,9},{9,1},{2,10},{10,2},{3,11},{11,3},{4,12},{12,4},... | collective-permute-start | bytes 2359304 | tf_op jit(solution)/shard_map/ppermute | solution.py:396
  5.9 11.4 %collective-permute-start.2 = (f32[4,64,256]{2,1,0:T(8,128)S(1)}, f32[4,64,256]{2,1,0:T(8,128)S(1)}, u32[]{:S(2)}, u32[]{:S(2)}) collective-permute-start(f32[4,64,256]{2,1,0:T(8,128)S(1)} %get-tuple-element.22), channel_id=1, source_target_pairs={{0,2},{2,4},{4,6},{6,0},{1,3},{3,5},{5,7},{7,1},{8,10},{10,12},{12... | collective-permute-start | bytes 786440 | tf_op jit(solution)/shard_map/ppermute | solution.py:356
  8.0 17.7 %collective-permute-start.3 = (f32[4,64,256]{2,1,0:T(8,128)S(1)}, f32[4,64,256]{2,1,0:T(8,128)S(1)}, u32[]{:S(2)}, u32[]{:S(2)}) collective-permute-start(f32[4,64,256]{2,1,0:T(8,128)S(1)} %get-tuple-element.23), channel_id=1, source_target_pairs={{2,0},{4,2},{6,4},{0,6},{3,1},{5,3},{7,5},{1,7},{10,8},{12,10},{14... | collective-permute-start | bytes 786440 | tf_op jit(solution)/shard_map/ppermute | solution.py:357
  13.0 15.5 %collective-permute-start.10 = (f32[4,64,256]{2,1,0:T(8,128)S(1)}, f32[4,64,256]{2,1,0:T(8,128)S(1)}, u32[]{:S(2)}, u32[]{:S(2)}) collective-permute-start(f32[4,64,256]{2,1,0:T(8,128)S(1)} %pad_maximum_fusion), channel_id=1, source_target_pairs={{0,2},{2,4},{4,6},{6,0},{1,3},{3,5},{5,7},{7,1},{8,10},{10,12},{12... | collective-permute-start | bytes 786440 | tf_op jit(solution)/shard_map/ppermute | solution.py:356
  15.2 16.8 %collective-permute-start.11 = (f32[4,64,256]{2,1,0:T(8,128)S(1)}, f32[4,64,256]{2,1,0:T(8,128)S(1)}, u32[]{:S(2)}, u32[]{:S(2)}) collective-permute-start(f32[4,64,256]{2,1,0:T(8,128)S(1)} %pad_maximum_fusion.1), channel_id=1, source_target_pairs={{2,0},{4,2},{6,4},{0,6},{3,1},{5,3},{7,5},{1,7},{10,8},{12,10},{14... | collective-permute-start | bytes 786440 | tf_op jit(solution)/shard_map/ppermute | solution.py:357
  25.7 6.3 %collective-permute-start.4 = (f32[24,16,256]{2,1,0:T(8,128)S(1)}, f32[24,16,256]{2,1,0:T(8,128)S(1)}, u32[]{:S(2)}, u32[]{:S(2)}) collective-permute-start(f32[24,16,256]{2,1,0:T(8,128)S(1)} %maximum_maximum_fusion), channel_id=1, source_target_pairs={{0,1},{1,0},{2,3},{3,2},{4,5},{5,4},{6,7},{7,6},{8,9},{9,8},{10,11... | collective-permute-start | bytes 1179656 | tf_op jit(solution)/shard_map/ppermute | solution.py:364
  35.1 24.6 %collective-permute-start.9 = (f32[16,64,256]{2,1,0:T(8,128)S(1)}, f32[16,64,256]{2,1,0:T(8,128)S(1)}, u32[]{:S(2)}, u32[]{:S(2)}) collective-permute-start(f32[16,64,256]{2,1,0:T(8,128)S(1)} %get-tuple-element.26.end), channel_id=1, source_target_pairs={{0,8},{8,0},{1,9},{9,1},{2,10},{10,2},{3,11},{11,3},{4,12},{12,4},... | collective-permute-start | bytes 3145736 | tf_op jit(solution)/shard_map/ppermute | solution.py:405
  36.8 10.8 %collective-permute-start.12 = (f32[40,16,256]{2,1,0:T(8,128)S(1)}, f32[40,16,256]{2,1,0:T(8,128)S(1)}, u32[]{:S(2)}, u32[]{:S(2)}) collective-permute-start(f32[40,16,256]{2,1,0:T(8,128)S(1)} %maximum_dynamic-update-slice_fusion.2), channel_id=1, source_target_pairs={{0,1},{1,0},{2,3},{3,2},{4,5},{5,4},{6,7},{7,6},{8,9},{9,8},{10,11... | collective-permute-start | bytes 1966088 | tf_op jit(solution)/shard_map/ppermute | solution.py:364
  37.3 1.6 %collective-permute-start.5 = (f32[8,128]{1,0:T(8,128)S(1)}, f32[8,128]{1,0:T(8,128)S(1)}, u32[]{:S(2)}, u32[]{:S(2)}) collective-permute-start(f32[8,128]{1,0:T(8,128)S(1)} %first_sums.1), channel_id=1, source_target_pairs={{0,1},{1,0},{2,3},{3,2},{4,5},{5,4},{6,7},{7,6},{8,9},{9,8},{10,11... | collective-permute-start | bytes 12296 | tf_op jit(solution)/shard_map/ppermute | solution.py:368
  39.0 3.6 %collective-permute-start.6 = (f32[8,128]{1,0:T(8,128)S(1)}, f32[8,128]{1,0:T(8,128)S(1)}, u32[]{:S(2)}, u32[]{:S(2)}) collective-permute-start(f32[8,128]{1,0:T(8,128)S(1)} %add.18), channel_id=1, source_target_pairs={{0,2},{2,0},{4,6},{6,4},{1,3},{3,1},{5,7},{7,5},{8,10},{10,8},{12,... | collective-permute-start | bytes 12296 | tf_op jit(solution)/shard_map/ppermute | solution.py:371
  42.6 4.5 %collective-permute-start.7 = (f32[8,128]{1,0:T(8,128)S(1)}, f32[8,128]{1,0:T(8,128)S(1)}, u32[]{:S(2)}, u32[]{:S(2)}) collective-permute-start(f32[8,128]{1,0:T(8,128)S(1)} %add.19), channel_id=1, source_target_pairs={{0,4},{2,6},{4,0},{6,2},{1,5},{3,7},{5,1},{7,3},{8,12},{10,14},{12... | collective-permute-start | bytes 12296 | tf_op jit(solution)/shard_map/ppermute | solution.py:371
  47.1 12.6 %collective-permute-start.8 = (f32[8,128]{1,0:T(8,128)S(1)}, f32[8,128]{1,0:T(8,128)S(1)}, u32[]{:S(2)}, u32[]{:S(2)}) collective-permute-start(f32[8,128]{1,0:T(8,128)S(1)} %add.20.sums), channel_id=1, source_target_pairs={{0,8},{8,0},{1,9},{9,1},{2,10},{10,2},{3,11},{11,3},{4,12},{12,4},... | collective-permute-start | bytes 12296 | tf_op jit(solution)/shard_map/ppermute | solution.py:430
  59.7 9.1 %copy-start.1 = (f32[2,16,64,256]{3,2,1,0:T(8,128)S(1)}, f32[2,16,64,256]{3,2,1,0:T(8,128)}, u32[]{:S(2)}) copy-start(f32[2,16,64,256]{3,2,1,0:T(8,128)} %src.1) | copy-start | bytes 6291460
  63.1 1.2 %collective-permute-start.13 = (f32[8,128]{1,0:T(8,128)S(1)}, f32[8,128]{1,0:T(8,128)S(1)}, u32[]{:S(2)}, u32[]{:S(2)}) collective-permute-start(f32[8,128]{1,0:T(8,128)S(1)} %get-tuple-element.32), channel_id=1, source_target_pairs={{0,1},{1,0},{2,3},{3,2},{4,5},{5,4},{6,7},{7,6},{8,9},{9,8},{10,11... | collective-permute-start | bytes 12296 | tf_op jit(solution)/shard_map/ppermute | solution.py:368
  64.3 3.6 %collective-permute-start.14 = (f32[8,128]{1,0:T(8,128)S(1)}, f32[8,128]{1,0:T(8,128)S(1)}, u32[]{:S(2)}, u32[]{:S(2)}) collective-permute-start(f32[8,128]{1,0:T(8,128)S(1)} %add.21), channel_id=1, source_target_pairs={{0,2},{2,0},{4,6},{6,4},{1,3},{3,1},{5,7},{7,5},{8,10},{10,8},{12,... | collective-permute-start | bytes 12296 | tf_op jit(solution)/shard_map/ppermute | solution.py:371
  68.0 4.5 %collective-permute-start.15 = (f32[8,128]{1,0:T(8,128)S(1)}, f32[8,128]{1,0:T(8,128)S(1)}, u32[]{:S(2)}, u32[]{:S(2)}) collective-permute-start(f32[8,128]{1,0:T(8,128)S(1)} %add.22), channel_id=1, source_target_pairs={{0,4},{2,6},{4,0},{6,2},{1,5},{3,7},{5,1},{7,3},{8,12},{10,14},{12... | collective-permute-start | bytes 12296 | tf_op jit(solution)/shard_map/ppermute | solution.py:371

commit v4 on v3

--- a/solution.py
+++ b/solution.py
@@ -176,7 +176,7 @@
     dst[:, PAD + rows : 2 * PAD + rows] = sides[sides_at : sides_at + at, 0:PAD]
 
 
-def split_kernel(images, mine, end, edges, middle, up, down, sems):
+def split_kernel(images, mine, end, edges, middle, sems):
     which = 1 - lax.axis_index("image")
     nz = mine.shape[0]
     copies = [
@@ -186,8 +186,6 @@
                 (images.at[which, pl.ds(0, 2)], edges.at[pl.ds(0, 2)]),
                 (images.at[which, pl.ds(nz - 2, 2)], edges.at[pl.ds(2, 2)]),
                 (images.at[which, pl.ds(2, nz - 4)], middle),
-                (images.at[which, pl.ds(nz - 4, 4)], up),
-                (images.at[which, pl.ds(0, 4)], down),
                 (images.at[which], mine),
                 (images.at[1 - which], end),
             ]
@@ -197,6 +195,16 @@
         c.start()
     for c in copies:
         c.wait()
+
+
+def ends_kernel(mine, up, down, sems):
+    layers = up.shape[0]
+    last = pltpu.make_async_copy(mine.at[pl.ds(mine.shape[0] - layers, layers)], up, sems.at[0])
+    first = pltpu.make_async_copy(mine.at[pl.ds(0, layers)], down, sems.at[1])
+    last.start()
+    first.start()
+    last.wait()
+    first.wait()
 
 
 def first_step_kernel(mine, low, high, sides, step_out, drive_out, field, pot):
@@ -301,29 +309,31 @@
     layer_loop(0, nz, one)
 
 
-def second_sums_kernel(sums, far, mine, end, other_step, moved, drive, tangent_out, out):
+def second_sums_kernel(sums, far, mine, end, other_step, moved, drive, out):
     nz, rows, lanes = mine.shape
     coef, _, _ = coefficient(sums)
 
     def fields(k, r):
         o = other_step[k, r] + coef * (mine[k, r] - far[k, r])
         m, e = moved[k, r], end[k, r]
-        tangent = o - e
-        tangent_out[k, r] = tangent
-        return o - m, m - e, tangent, drive[k, r]
+        return o - m, m - e, o - e, drive[k, r]
 
     write_sums(out, sums_of(0, nz, rows, fields, no_sums(lanes)))
 
 
-def last_kernel(cells, sums, moved, drive, tangent, base, out, par_out, buf, sems):
+def last_kernel(
+    cells, sums, o_sums, far, mine, end, other_step, moved, drive, base, out, par_out, buf, sems
+):
     del base
     nz = moved.shape[0]
     at = lax.axis_index("image")
     which = 1 - at
     coef, par, safe = coefficient(sums)
+    o_coef, _, _ = coefficient(o_sums)
     copies = []
     for k in range(nz):
-        buf[k] = moved[k] + STEP_SIZE * drive[k] + coef * tangent[k]
+        tangent = other_step[k] + o_coef * (mine[k] - far[k]) - end[k]
+        buf[k] = moved[k] + STEP_SIZE * drive[k] + coef * tangent
         if k % 4 == 3:
             where = pl.ds(k - 3, 4)
             copies.append(
@@ -383,30 +393,40 @@
     def room(layers):
         return pltpu.VMEM((layers, wide, nx), jnp.float32)
 
-    mine, end, edges, middle, up, down = call(
+    mine, end, edges, middle = call(
         split_kernel,
-        [block, block, shape(4, ny, nx), shape(nz - 4, ny, nx), shape(4, ny, nx), shape(4, ny, nx)],
-        [DMA((7,))],
+        [block, block, shape(4, ny, nx), shape(nz - 4, ny, nx)],
+        [DMA((5,))],
         "split",
         in_specs=[ANY],
-        out_specs=[ANY] * 6,
-    )(images)
+        out_specs=[ANY] * 4,
+    )(pltpu.with_memory_space_constraint(images, pltpu.HBM))
 
     o_edges = lax.ppermute(edges, "image", SWAP)
     o_middle = lax.ppermute(middle, "image", SWAP)
 
+    thin = shape(4, ny, nx)
+    up, down = call(
+        ends_kernel,
+        [thin, thin],
+        [DMA((2,))],
+        "ends",
+        in_specs=[ANY],
+        out_specs=[ANY] * 2,
+        cost_estimate=pl.CostEstimate(flops=0, bytes_accessed=2**24, transcendentals=0),
+    )(mine)
     low, high = from_z(up, down)
     sides = y_sides(low, mine, high)
     step, drive = call(first_step_kernel, [outer, block], [room(nz + 8), room(nz + 6)], "first_step")(
         mine, low, high, sides
     )
-
     end_later, drive = lax.optimization_barrier((end, drive))
     far = lax.ppermute(end_later, "image", SWAP)
 
     o_low, o_high = from_z(
         jnp.concatenate([o_edges[2:], end[nz - 2 :]]), jnp.concatenate([o_edges[:2], end[:2]])
     )
+    o_low, o_high, o_middle = lax.optimization_barrier((o_low, o_high, o_middle))
     o_sides = y_sides(o_low[:2], o_edges[:2], o_middle, o_edges[2:], o_high[:2], o_low[2:], end, o_high[2:])
 
     base = call(
@@ -428,19 +448,18 @@
     )(sums, step, tangent_wide)
 
     o_sums = lax.ppermute(sums, "image", SWAP)
-    tangent, sums = call(second_sums_kernel, [block, table], name="second_sums")(
-        o_sums, far, mine, end, other_step, moved, drive2
-    )
+    known = (o_sums, far, mine, end, other_step, moved, drive2)
+    sums = summed(call(second_sums_kernel, table, name="second_sums")(*known))
 
     return call(
         functools.partial(last_kernel, cells),
         [jax.ShapeDtypeStruct(images.shape, images.dtype), shape(2)],
         [pltpu.VMEM(block.shape, jnp.float32), DMA((nz // 4,))],
         "last",
-        in_specs=[VMEM] * 4 + [ANY],
+        in_specs=[VMEM] * 8 + [ANY],
         out_specs=[ANY, SMEM],
-        input_output_aliases={4: 0},
-    )(summed(sums), moved, drive2, tangent, base)
+        input_output_aliases={8: 0},
+    )(sums, *known, base)
 
 
 def body(images):

time: 74.3 us -> 68 us (0.915)
  waiting for transfers between devices: 36.5 us -> 26.3 us
  starting transfers between devices: 19.2 us -> 24.5 us
  local copies, waits for them, and re-layouts: 1.71 us -> 0.12 us
    ppermute x2, waiting for transfers between devices: 11.8 us -> 4.3 us  [from_z(): lax.ppermute(down, 'space', [((i + 1) % count, i) for i in range(count)])]
    ppermute x1, waiting for transfers between devices: 6.86 us -> 2.02 us  [body_pair(): o_sums = lax.ppermute(sums, 'image', SWAP)]
    ppermute x4, starting transfers between devices: 4.91 us -> 9.2 us  [summed(): lax.ppermute(sums, 'space', [(i, i ^ stride) for i in range(count)])]
    ppermute x2, starting transfers between devices: 4.13 us -> 6.32 us  [from_z(): lax.ppermute(down, 'space', [((i + 1) % count, i) for i in range(count)])]
    ppermute x2, starting transfers between devices: 4.23 us -> 2.15 us  [from_z(): lax.ppermute(up, 'space', [(i, (i + 1) % count) for i in range(count)])]
    ppermute x2, waiting for transfers between devices: 2.7 us -> 4.65 us  [from_z(): lax.ppermute(up, 'space', [(i, (i + 1) % count) for i in range(count)])]
    ppermute x2, waiting for transfers between devices: 0.01 us -> 1.67 us  [y_sides(): return lax.ppermute(jnp.concatenate(ends, 0), 'yslab', SWAP)]
    unnamed x4 -> x2, local copies, waits for them, and re-layouts: 1.59 us -> 0.01 us
  transfers between devices with their start and end apart: 16 -> 16, of which waited for: 11 -> 11; matrix products, arithmetic and copies ran while one was open for 0% -> 0% of each run, Pallas kernels for 14% -> 15%
where the time goes in v4:
time: 68 us; the launch traced here: 67.9 us
  waiting for transfers between devices  26.3 us (39%)
  starting transfers between devices  24.5 us (36%)
  Pallas kernels  15.9 us (23%)
  between operations  0.86 us (1%)
    ppermute x4, starting transfers between devices, summed(): lax.ppermute(sums, 'space', [(i, i ^ stride) for i in range(count)])  9.2 us
    ppermute x4, waiting for transfers between devices, summed(): lax.ppermute(sums, 'space', [(i, i ^ stride) for i in range(count)])  8.67 us
    ppermute x2, starting transfers between devices, from_z(): lax.ppermute(down, 'space', [((i + 1) % count, i) for i in range(count)])  6.32 us
    ppermute x2, waiting for transfers between devices, from_z(): lax.ppermute(up, 'space', [(i, (i + 1) % count) for i in range(count)])  4.65 us
    ppermute x2, waiting for transfers between devices, from_z(): lax.ppermute(down, 'space', [((i + 1) % count, i) for i in range(count)])  4.3 us
    pallas_call x1, Pallas kernels, body_pair(): call(first_step_kernel, [outer, block], [room(nz + 8), room(nz + 6)], 'fi...  3.06 us
    ppermute x1, starting transfers between devices, body_pair(): o_edges = lax.ppermute(edges, 'image', SWAP)  3 us
    ppermute x1, waiting for transfers between devices, body_pair(): o_edges = lax.ppermute(edges, 'image', SWAP)  2.76 us
  transfers between devices with their start and end apart: 16, of which 11 were waited for; matrix products, arithmetic and copies ran while one was open for 0% of the time, Pallas kernels for 15%

profile of v4, /device:TPU:0, one launch (start us, length us, event | category | flops | bytes accessed | tf_op | source)
XLA Modules:
  0.0 67.9 jit_solution(14139027165761229286)
XLA Ops:
  0.6 2.0 %split.1 = (f32[16,64,256]{2,1,0:T(8,128)S(1)}, f32[16,64,256]{2,1,0:T(8,128)S(1)}, f32[4,64,256]{2,1,0:T(8,128)S(1)}, f32[12,64,256]{2,1,0:T(8,128)S(1)}) custom-call(f32[2,16,64,256]{3,2,1,0:T(8,128)} %src.1), custom_call_target="tpu_custom_call" | custom-call | tf_op jit(solution)/shard_map/split/pallas_call | solution.py:396
  2.6 3.0 %collective-permute-start = (f32[4,64,256]{2,1,0:T(8,128)S(1)}, f32[4,64,256]{2,1,0:T(8,128)S(1)}, u32[]{:S(2)}, u32[]{:S(2)}) collective-permute-start(f32[4,64,256]{2,1,0:T(8,128)S(1)} %get-tuple-element.19), channel_id=1, source_target_pairs={{0,8},{8,0},{1,9},{9,1},{2,10},{10,2},{3,11},{11,3},{4,12},{12,4},... | collective-permute-start | bytes 786440 | tf_op jit(solution)/shard_map/ppermute | solution.py:405
  5.6 0.1 collective-permute-start.3
  5.7 0.1 ends.1
  5.8 2.1 %collective-permute-start.4 = (f32[4,64,256]{2,1,0:T(8,128)S(1)}, f32[4,64,256]{2,1,0:T(8,128)S(1)}, u32[]{:S(2)}, u32[]{:S(2)}) collective-permute-start(f32[4,64,256]{2,1,0:T(8,128)S(1)} %get-tuple-element.24), channel_id=1, source_target_pairs={{0,2},{2,4},{4,6},{6,0},{1,3},{3,5},{5,7},{7,1},{8,10},{10,12},{12... | collective-permute-start | bytes 786440 | tf_op jit(solution)/shard_map/ppermute | solution.py:366
  7.9 2.1 %collective-permute-start.5 = (f32[4,64,256]{2,1,0:T(8,128)S(1)}, f32[4,64,256]{2,1,0:T(8,128)S(1)}, u32[]{:S(2)}, u32[]{:S(2)}) collective-permute-start(f32[4,64,256]{2,1,0:T(8,128)S(1)} %get-tuple-element.25), channel_id=1, source_target_pairs={{2,0},{4,2},{6,4},{0,6},{3,1},{5,3},{7,5},{1,7},{10,8},{12,10},{14... | collective-permute-start | bytes 786440 | tf_op jit(solution)/shard_map/ppermute | solution.py:367
  10.0 2.8 %collective-permute-done.edges = f32[4,64,256]{2,1,0:T(8,128)S(1)} collective-permute-done((f32[4,64,256]{2,1,0:T(8,128)S(1)}, f32[4,64,256]{2,1,0:T(8,128)S(1)}, u32[]{:S(2)}, u32[]{:S(2)}) %collective-permute-start) | collective-permute-done | bytes 262176 | tf_op jit(solution)/shard_map/ppermute | solution.py:405
  12.8 4.2 %collective-permute-start.2 = (f32[4,64,256]{2,1,0:T(8,128)S(1)}, f32[4,64,256]{2,1,0:T(8,128)S(1)}, u32[]{:S(2)}, u32[]{:S(2)}) collective-permute-start(f32[4,64,256]{2,1,0:T(8,128)S(1)} %pad_maximum_fusion.1), channel_id=1, source_target_pairs={{2,0},{4,2},{6,4},{0,6},{3,1},{5,3},{7,5},{1,7},{10,8},{12,10},{14... | collective-permute-start | bytes 786440 | tf_op jit(solution)/shard_map/ppermute | solution.py:367
  17.0 0.1 collective-permute-start.1
  17.1 0.0 collective-permute-done.4.low
  17.1 4.3 %collective-permute-done.5.high = f32[4,64,256]{2,1,0:T(8,128)S(1)} collective-permute-done((f32[4,64,256]{2,1,0:T(8,128)S(1)}, f32[4,64,256]{2,1,0:T(8,128)S(1)}, u32[]{:S(2)}, u32[]{:S(2)}) %collective-permute-start.5) | collective-permute-done | bytes 262176 | tf_op jit(solution)/shard_map/ppermute | solution.py:367
  21.5 0.1 collective-permute-start.6
  21.6 1.7 %collective-permute-done.6.sides = f32[24,16,256]{2,1,0:T(8,128)S(1)} collective-permute-done((f32[24,16,256]{2,1,0:T(8,128)S(1)}, f32[24,16,256]{2,1,0:T(8,128)S(1)}, u32[]{:S(2)}, u32[]{:S(2)}) %collective-permute-start.6) | collective-permute-done | bytes 393248 | tf_op jit(solution)/shard_map/ppermute | solution.py:374
  23.3 3.1 %first_step.1 = (f32[20,80,256]{2,1,0:T(8,128)S(1)}, f32[16,64,256]{2,1,0:T(8,128)S(1)}) custom-call(f32[16,64,256]{2,1,0:T(8,128)S(1)} %get-tuple-element.23.mine, f32[4,64,256]{2,1,0:T(8,128)S(1)} %collective-permute-done.4.low, f32[4,64,256]{2,1,0:T(8,128)S(1)} %collective-permute-done.5.high, f32[24,16,256]{2,1,0:T(8,128)S(1)} %collective-permute-done.6.sides), custom_call_target="tpu_custom_call" | custom-call | tf_op jit(solution)/shard_map/first_step/pallas_call | solution.py:420
  26.3 1.5 %collective-permute-start.11 = (f32[16,64,256]{2,1,0:T(8,128)S(1)}, f32[16,64,256]{2,1,0:T(8,128)S(1)}, u32[]{:S(2)}, u32[]{:S(2)}) collective-permute-start(f32[16,64,256]{2,1,0:T(8,128)S(1)} %get-tuple-element.28.end), channel_id=1, source_target_pairs={{0,8},{8,0},{1,9},{9,1},{2,10},{10,2},{3,11},{11,3},{4,12},{12,4},... | collective-permute-start | bytes 3145736 | tf_op jit(solution)/shard_map/ppermute | solution.py:424
  27.9 0.0 collective-permute-done.2.high
  27.9 4.6 %collective-permute-done.1.low = f32[4,64,256]{2,1,0:T(8,128)S(1)} collective-permute-done((f32[4,64,256]{2,1,0:T(8,128)S(1)}, f32[4,64,256]{2,1,0:T(8,128)S(1)}, u32[]{:S(2)}, u32[]{:S(2)}) %collective-permute-start.1) | collective-permute-done | bytes 262176 | tf_op jit(solution)/shard_map/ppermute | solution.py:366
  32.5 0.0 collective-permute-done.3.middle
  32.7 0.1 collective-permute-start.12
  32.8 0.4 first_sums.1
  33.2 0.6 collective-permute-start.7
  33.8 1.1 %collective-permute-done.7 = f32[8,128]{1,0:T(8,128)S(1)} collective-permute-done((f32[8,128]{1,0:T(8,128)S(1)}, f32[8,128]{1,0:T(8,128)S(1)}, u32[]{:S(2)}, u32[]{:S(2)}) %collective-permute-start.7) | collective-permute-done | bytes 4128 | tf_op jit(solution)/shard_map/ppermute | solution.py:378
  34.9 0.0 collective-permute-start.8
  34.9 3.6 %collective-permute-done.8 = f32[8,128]{1,0:T(8,128)S(1)} collective-permute-done((f32[8,128]{1,0:T(8,128)S(1)}, f32[8,128]{1,0:T(8,128)S(1)}, u32[]{:S(2)}, u32[]{:S(2)}) %collective-permute-start.8) | collective-permute-done | bytes 4128 | tf_op jit(solution)/shard_map/ppermute | solution.py:381
  38.5 1.3 %collective-permute-start.9 = (f32[8,128]{1,0:T(8,128)S(1)}, f32[8,128]{1,0:T(8,128)S(1)}, u32[]{:S(2)}, u32[]{:S(2)}) collective-permute-start(f32[8,128]{1,0:T(8,128)S(1)} %add.19), channel_id=1, source_target_pairs={{0,4},{2,6},{4,0},{6,2},{1,5},{3,7},{5,1},{7,3},{8,12},{10,14},{12... | collective-permute-start | bytes 12296 | tf_op jit(solution)/shard_map/ppermute | solution.py:381
  39.8 3.2 %collective-permute-done.9 = f32[8,128]{1,0:T(8,128)S(1)} collective-permute-done((f32[8,128]{1,0:T(8,128)S(1)}, f32[8,128]{1,0:T(8,128)S(1)}, u32[]{:S(2)}, u32[]{:S(2)}) %collective-permute-start.9) | collective-permute-done | bytes 4128 | tf_op jit(solution)/shard_map/ppermute | solution.py:381
  43.0 1.5 %collective-permute-start.10 = (f32[8,128]{1,0:T(8,128)S(1)}, f32[8,128]{1,0:T(8,128)S(1)}, u32[]{:S(2)}, u32[]{:S(2)}) collective-permute-start(f32[8,128]{1,0:T(8,128)S(1)} %add.20.sums), channel_id=1, source_target_pairs={{0,8},{8,0},{1,9},{9,1},{2,10},{10,2},{3,11},{11,3},{4,12},{12,4},... | collective-permute-start | bytes 12296 | tf_op jit(solution)/shard_map/ppermute | solution.py:450
  44.5 0.0 collective-permute-done.12.sides
  44.5 2.6 %other_step.1 = (f32[16,64,256]{2,1,0:T(8,128)S(1)}, f32[20,80,256]{2,1,0:T(8,128)S(1)}) custom-call(f32[4,64,256]{2,1,0:T(8,128)S(1)} %collective-permute-done.edges, f32[12,64,256]{2,1,0:T(8,128)S(1)} %collective-permute-done.3.middle, f32[16,64,256]{2,1,0:T(8,128)S(1)} %get-tuple-element.28.end, f32[4,64,256]{2,1,0:T(8,128)S(1)} %collective-permute-done.1.low, ...), custom_call_target="tpu_custom_call" | custom-call | tf_op jit(solution)/shard_map/other_step/pallas_call | solution.py:442
  47.1 2.6 %second_step.1 = (f32[16,64,256]{2,1,0:T(8,128)S(1)}, f32[16,64,256]{2,1,0:T(8,128)S(1)}) custom-call(f32[8,128]{1,0:T(8,128)S(1)} %add.20.sums, f32[20,80,256]{2,1,0:T(8,128)S(1)} %get-tuple-element.32.step, f32[20,80,256]{2,1,0:T(8,128)S(1)} %get-tuple-element.33.tangent_wide), custom_call_target="tpu_custom_call" | custom-call | tf_op jit(solution)/shard_map/second_step/pallas_call | solution.py:446
  49.7 2.0 %collective-permute-done.10.sums.o_sums = f32[8,128]{1,0:T(8,128)S(1)} collective-permute-done((f32[8,128]{1,0:T(8,128)S(1)}, f32[8,128]{1,0:T(8,128)S(1)}, u32[]{:S(2)}, u32[]{:S(2)}) %collective-permute-start.10) | collective-permute-done | bytes 4128 | tf_op jit(solution)/shard_map/ppermute | solution.py:450
  51.7 0.0 collective-permute-done.11.far
  51.7 0.0 copy-start
  51.7 2.1 %second_sums.1 = f32[8,128]{1,0:T(8,128)S(1)} custom-call(f32[8,128]{1,0:T(8,128)S(1)} %collective-permute-done.10.sums.o_sums, f32[16,64,256]{2,1,0:T(8,128)S(1)} %collective-permute-done.11.far, f32[16,64,256]{2,1,0:T(8,128)S(1)} %get-tuple-element.23.mine, f32[16,64,256]{2,1,0:T(8,128)S(1)} %get-tuple-element.28.end, ...), custom_call_target="tpu_custom_call" | custom-call | tf_op jit(solution)/shard_map/second_sums/pallas_call | solution.py:452
  53.8 0.1 collective-permute-start.13
  53.8 1.2 %collective-permute-done.13 = f32[8,128]{1,0:T(8,128)S(1)} collective-permute-done((f32[8,128]{1,0:T(8,128)S(1)}, f32[8,128]{1,0:T(8,128)S(1)}, u32[]{:S(2)}, u32[]{:S(2)}) %collective-permute-start.13) | collective-permute-done | bytes 4128 | tf_op jit(solution)/shard_map/ppermute | solution.py:378
  55.0 3.5 %collective-permute-start.14 = (f32[8,128]{1,0:T(8,128)S(1)}, f32[8,128]{1,0:T(8,128)S(1)}, u32[]{:S(2)}, u32[]{:S(2)}) collective-permute-start(f32[8,128]{1,0:T(8,128)S(1)} %add.21), channel_id=1, source_target_pairs={{0,2},{2,0},{4,6},{6,4},{1,3},{3,1},{5,7},{7,5},{8,10},{10,8},{12,... | collective-permute-start | bytes 12296 | tf_op jit(solution)/shard_map/ppermute | solution.py:381
  58.5 1.6 %collective-permute-done.14 = f32[8,128]{1,0:T(8,128)S(1)} collective-permute-done((f32[8,128]{1,0:T(8,128)S(1)}, f32[8,128]{1,0:T(8,128)S(1)}, u32[]{:S(2)}, u32[]{:S(2)}) %collective-permute-start.14) | collective-permute-done | bytes 4128 | tf_op jit(solution)/shard_map/ppermute | solution.py:381
  60.1 4.4 %collective-permute-start.15 = (f32[8,128]{1,0:T(8,128)S(1)}, f32[8,128]{1,0:T(8,128)S(1)}, u32[]{:S(2)}, u32[]{:S(2)}) collective-permute-start(f32[8,128]{1,0:T(8,128)S(1)} %add.22), channel_id=1, source_target_pairs={{0,4},{2,6},{4,0},{6,2},{1,5},{3,7},{5,1},{7,3},{8,12},{10,14},{12... | collective-permute-start | bytes 12296 | tf_op jit(solution)/shard_map/ppermute | solution.py:381
  64.5 0.0 copy-done
  64.5 1.3 %base.1 = f32[2,16,64,256]{3,2,1,0:T(8,128)} custom-call(f32[2,16,64,256]{3,2,1,0:T(8,128)S(1)} %copy-done), custom_call_target="tpu_custom_call" | custom-call | tf_op jit(solution)/shard_map/base/pallas_call | solution.py:432
  65.8 0.2 collective-permute-done.15
  66.1 1.8 %last.1 = (f32[2,16,64,256]{3,2,1,0:T(8,128)}, f32[2]{0:T(128)}) custom-call(f32[8,128]{1,0:T(8,128)S(1)} %add.23.sums, f32[8,128]{1,0:T(8,128)S(1)} %collective-permute-done.10.sums.o_sums, f32[16,64,256]{2,1,0:T(8,128)S(1)} %collective-permute-done.11.far, f32[16,64,256]{2,1,0:T(8,128)S(1)} %get-tuple-element.23.mine, ...), custom_call_target="tpu_custom_call", output_to_operand_aliasing={{0}: (8, {})} | custom-call | tf_op jit(solution)/shard_map/last/pallas_call | solution.py:454
  (26 shorter events, 0.3 us)
Async XLA Ops:
  2.6 10.1 %collective-permute-start = (f32[4,64,256]{2,1,0:T(8,128)S(1)}, f32[4,64,256]{2,1,0:T(8,128)S(1)}, u32[]{:S(2)}, u32[]{:S(2)}) collective-permute-start(f32[4,64,256]{2,1,0:T(8,128)S(1)} %get-tuple-element.19), channel_id=1, source_target_pairs={{0,8},{8,0},{1,9},{9,1},{2,10},{10,2},{3,11},{11,3},{4,12},{12,4},... | collective-permute-start | bytes 786440 | tf_op jit(solution)/shard_map/ppermute | solution.py:405
  5.6 26.9 %collective-permute-start.3 = (f32[12,64,256]{2,1,0:T(8,128)S(1)}, f32[12,64,256]{2,1,0:T(8,128)S(1)}, u32[]{:S(2)}, u32[]{:S(2)}) collective-permute-start(f32[12,64,256]{2,1,0:T(8,128)S(1)} %get-tuple-element.21), channel_id=1, source_target_pairs={{0,8},{8,0},{1,9},{9,1},{2,10},{10,2},{3,11},{11,3},{4,12},{12,4},... | collective-permute-start | bytes 2359304 | tf_op jit(solution)/shard_map/ppermute | solution.py:406
  5.8 11.4 %collective-permute-start.4 = (f32[4,64,256]{2,1,0:T(8,128)S(1)}, f32[4,64,256]{2,1,0:T(8,128)S(1)}, u32[]{:S(2)}, u32[]{:S(2)}) collective-permute-start(f32[4,64,256]{2,1,0:T(8,128)S(1)} %get-tuple-element.24), channel_id=1, source_target_pairs={{0,2},{2,4},{4,6},{6,0},{1,3},{3,5},{5,7},{7,1},{8,10},{10,12},{12... | collective-permute-start | bytes 786440 | tf_op jit(solution)/shard_map/ppermute | solution.py:366
  7.9 13.6 %collective-permute-start.5 = (f32[4,64,256]{2,1,0:T(8,128)S(1)}, f32[4,64,256]{2,1,0:T(8,128)S(1)}, u32[]{:S(2)}, u32[]{:S(2)}) collective-permute-start(f32[4,64,256]{2,1,0:T(8,128)S(1)} %get-tuple-element.25), channel_id=1, source_target_pairs={{2,0},{4,2},{6,4},{0,6},{3,1},{5,3},{7,5},{1,7},{10,8},{12,10},{14... | collective-permute-start | bytes 786440 | tf_op jit(solution)/shard_map/ppermute | solution.py:367
  12.8 15.1 %collective-permute-start.2 = (f32[4,64,256]{2,1,0:T(8,128)S(1)}, f32[4,64,256]{2,1,0:T(8,128)S(1)}, u32[]{:S(2)}, u32[]{:S(2)}) collective-permute-start(f32[4,64,256]{2,1,0:T(8,128)S(1)} %pad_maximum_fusion.1), channel_id=1, source_target_pairs={{2,0},{4,2},{6,4},{0,6},{3,1},{5,3},{7,5},{1,7},{10,8},{12,10},{14... | collective-permute-start | bytes 786440 | tf_op jit(solution)/shard_map/ppermute | solution.py:367
  17.0 15.5 %collective-permute-start.1 = (f32[4,64,256]{2,1,0:T(8,128)S(1)}, f32[4,64,256]{2,1,0:T(8,128)S(1)}, u32[]{:S(2)}, u32[]{:S(2)}) collective-permute-start(f32[4,64,256]{2,1,0:T(8,128)S(1)} %pad_maximum_fusion), channel_id=1, source_target_pairs={{0,2},{2,4},{4,6},{6,0},{1,3},{3,5},{5,7},{7,1},{8,10},{10,12},{12... | collective-permute-start | bytes 786440 | tf_op jit(solution)/shard_map/ppermute | solution.py:366
  21.5 1.8 %collective-permute-start.6 = (f32[24,16,256]{2,1,0:T(8,128)S(1)}, f32[24,16,256]{2,1,0:T(8,128)S(1)}, u32[]{:S(2)}, u32[]{:S(2)}) collective-permute-start(f32[24,16,256]{2,1,0:T(8,128)S(1)} %maximum_maximum_fusion), channel_id=1, source_target_pairs={{0,1},{1,0},{2,3},{3,2},{4,5},{5,4},{6,7},{7,6},{8,9},{9,8},{10,11... | collective-permute-start | bytes 1179656 | tf_op jit(solution)/shard_map/ppermute | solution.py:374
  26.3 25.4 %collective-permute-start.11 = (f32[16,64,256]{2,1,0:T(8,128)S(1)}, f32[16,64,256]{2,1,0:T(8,128)S(1)}, u32[]{:S(2)}, u32[]{:S(2)}) collective-permute-start(f32[16,64,256]{2,1,0:T(8,128)S(1)} %get-tuple-element.28.end), channel_id=1, source_target_pairs={{0,8},{8,0},{1,9},{9,1},{2,10},{10,2},{3,11},{11,3},{4,12},{12,4},... | collective-permute-start | bytes 3145736 | tf_op jit(solution)/shard_map/ppermute | solution.py:424
  32.7 11.8 %collective-permute-start.12 = (f32[40,16,256]{2,1,0:T(8,128)S(1)}, f32[40,16,256]{2,1,0:T(8,128)S(1)}, u32[]{:S(2)}, u32[]{:S(2)}) collective-permute-start(f32[40,16,256]{2,1,0:T(8,128)S(1)} %maximum_dynamic-update-slice_fusion.2), channel_id=1, source_target_pairs={{0,1},{1,0},{2,3},{3,2},{4,5},{5,4},{6,7},{7,6},{8,9},{9,8},{10,11... | collective-permute-start | bytes 1966088 | tf_op jit(solution)/shard_map/ppermute | solution.py:374
  33.2 1.6 %collective-permute-start.7 = (f32[8,128]{1,0:T(8,128)S(1)}, f32[8,128]{1,0:T(8,128)S(1)}, u32[]{:S(2)}, u32[]{:S(2)}) collective-permute-start(f32[8,128]{1,0:T(8,128)S(1)} %first_sums.1), channel_id=1, source_target_pairs={{0,1},{1,0},{2,3},{3,2},{4,5},{5,4},{6,7},{7,6},{8,9},{9,8},{10,11... | collective-permute-start | bytes 12296 | tf_op jit(solution)/shard_map/ppermute | solution.py:378
  34.9 3.6 %collective-permute-start.8 = (f32[8,128]{1,0:T(8,128)S(1)}, f32[8,128]{1,0:T(8,128)S(1)}, u32[]{:S(2)}, u32[]{:S(2)}) collective-permute-start(f32[8,128]{1,0:T(8,128)S(1)} %add.18), channel_id=1, source_target_pairs={{0,2},{2,0},{4,6},{6,4},{1,3},{3,1},{5,7},{7,5},{8,10},{10,8},{12,... | collective-permute-start | bytes 12296 | tf_op jit(solution)/shard_map/ppermute | solution.py:381
  38.5 4.5 %collective-permute-start.9 = (f32[8,128]{1,0:T(8,128)S(1)}, f32[8,128]{1,0:T(8,128)S(1)}, u32[]{:S(2)}, u32[]{:S(2)}) collective-permute-start(f32[8,128]{1,0:T(8,128)S(1)} %add.19), channel_id=1, source_target_pairs={{0,4},{2,6},{4,0},{6,2},{1,5},{3,7},{5,1},{7,3},{8,12},{10,14},{12... | collective-permute-start | bytes 12296 | tf_op jit(solution)/shard_map/ppermute | solution.py:381
  43.0 8.7 %collective-permute-start.10 = (f32[8,128]{1,0:T(8,128)S(1)}, f32[8,128]{1,0:T(8,128)S(1)}, u32[]{:S(2)}, u32[]{:S(2)}) collective-permute-start(f32[8,128]{1,0:T(8,128)S(1)} %add.20.sums), channel_id=1, source_target_pairs={{0,8},{8,0},{1,9},{9,1},{2,10},{10,2},{3,11},{11,3},{4,12},{12,4},... | collective-permute-start | bytes 12296 | tf_op jit(solution)/shard_map/ppermute | solution.py:450
  51.7 12.8 %copy-start = (f32[2,16,64,256]{3,2,1,0:T(8,128)S(1)}, f32[2,16,64,256]{3,2,1,0:T(8,128)}, u32[]{:S(2)}) copy-start(f32[2,16,64,256]{3,2,1,0:T(8,128)} %src.1) | copy-start | bytes 6291460
  53.8 1.2 %collective-permute-start.13 = (f32[8,128]{1,0:T(8,128)S(1)}, f32[8,128]{1,0:T(8,128)S(1)}, u32[]{:S(2)}, u32[]{:S(2)}) collective-permute-start(f32[8,128]{1,0:T(8,128)S(1)} %second_sums.1), channel_id=1, source_target_pairs={{0,1},{1,0},{2,3},{3,2},{4,5},{5,4},{6,7},{7,6},{8,9},{9,8},{10,11... | collective-permute-start | bytes 12296 | tf_op jit(solution)/shard_map/ppermute | solution.py:378
  55.0 5.1 %collective-permute-start.14 = (f32[8,128]{1,0:T(8,128)S(1)}, f32[8,128]{1,0:T(8,128)S(1)}, u32[]{:S(2)}, u32[]{:S(2)}) collective-permute-start(f32[8,128]{1,0:T(8,128)S(1)} %add.21), channel_id=1, source_target_pairs={{0,2},{2,0},{4,6},{6,4},{1,3},{3,1},{5,7},{7,5},{8,10},{10,8},{12,... | collective-permute-start | bytes 12296 | tf_op jit(solution)/shard_map/ppermute | solution.py:381
  60.1 6.0 %collective-permute-start.15 = (f32[8,128]{1,0:T(8,128)S(1)}, f32[8,128]{1,0:T(8,128)S(1)}, u32[]{:S(2)}, u32[]{:S(2)}) collective-permute-start(f32[8,128]{1,0:T(8,128)S(1)} %add.22), channel_id=1, source_target_pairs={{0,4},{2,6},{4,0},{6,2},{1,5},{3,7},{5,1},{7,3},{8,12},{10,14},{12... | collective-permute-start | bytes 12296 | tf_op jit(solution)/shard_map/ppermute | solution.py:381

commit v5 on v3

--- a/solution.py
+++ b/solution.py
@@ -176,29 +176,37 @@
     dst[:, PAD + rows : 2 * PAD + rows] = sides[sides_at : sides_at + at, 0:PAD]
 
 
-def split_kernel(images, mine, end, edges, middle, up, down, sems):
-    which = 1 - lax.axis_index("image")
-    nz = mine.shape[0]
-    copies = [
-        pltpu.make_async_copy(src, dst, sems.at[i])
-        for i, (src, dst) in enumerate(
-            [
-                (images.at[which, pl.ds(0, 2)], edges.at[pl.ds(0, 2)]),
-                (images.at[which, pl.ds(nz - 2, 2)], edges.at[pl.ds(2, 2)]),
-                (images.at[which, pl.ds(2, nz - 4)], middle),
-                (images.at[which, pl.ds(nz - 4, 4)], up),
-                (images.at[which, pl.ds(0, 4)], down),
-                (images.at[which], mine),
-                (images.at[1 - which], end),
-            ]
-        )
-    ]
+def all_copied(pairs, sems):
+    copies = [pltpu.make_async_copy(src, dst, sems.at[i]) for i, (src, dst) in enumerate(pairs)]
     for c in copies:
         c.start()
     for c in copies:
         c.wait()
 
 
+def send_kernel(images, edges, middle, sems):
+    which = 1 - lax.axis_index("image")
+    nz = images.shape[1]
+    pairs = [
+        (images.at[which, pl.ds(0, 2)], edges.at[pl.ds(0, 2)]),
+        (images.at[which, pl.ds(nz - 2, 2)], edges.at[pl.ds(2, 2)]),
+        (images.at[which, pl.ds(2, nz - 4)], middle),
+    ]
+    all_copied(pairs, sems)
+
+
+def keep_kernel(images, mine, end, up, down, sems):
+    which = 1 - lax.axis_index("image")
+    nz, layers = mine.shape[0], up.shape[0]
+    pairs = [
+        (images.at[which, pl.ds(nz - layers, layers)], up),
+        (images.at[which, pl.ds(0, layers)], down),
+        (images.at[which], mine),
+        (images.at[1 - which], end),
+    ]
+    all_copied(pairs, sems)
+
+
 def first_step_kernel(mine, low, high, sides, step_out, drive_out, field, pot):
     nz, rows, _ = mine.shape
     fill_padded(field, (low, mine, high), sides, 0)
@@ -220,41 +228,38 @@
 CHUNK = 16
 
 
-def sums_of(start, stop, rows, fields, totals):
+def sums_of(start, stop, rows, terms, totals):
     def one(k, totals):
         for r in range(0, rows, CHUNK):
-            plus, minus, tangent, drive = fields(k, pl.ds(r, CHUNK))
-            terms = (plus * plus, minus * minus, tangent * tangent, drive * tangent)
-            totals = tuple(t + rows_sum(v) for t, v in zip(totals, terms))
+            totals = tuple(t + rows_sum(v) for t, v in zip(totals, terms(k, pl.ds(r, CHUNK))))
         return totals
 
     return lax.fori_loop(start, stop, one, totals, unroll=min(UNROLL, stop - start))
 
 
-def no_sums(lanes):
-    return (jnp.zeros((8, lanes), jnp.float32),) * 4
-
-
-def write_sums(out, totals):
-    out[...] = jnp.concatenate(
-        [lane_row(t) for t in totals] + [jnp.zeros((4, 128), jnp.float32)], 0
-    )
+def no_sums(count, lanes):
+    return (jnp.zeros((8, lanes), jnp.float32),) * count
+
+
+def table_of(*rows):
+    return jnp.concatenate(rows + (jnp.zeros((8 - len(rows), 128), jnp.float32),), 0)
 
 
 def first_sums_kernel(edges, middle, mine, end, drive, out):
     nz, rows, lanes = mine.shape
 
-    def fields_from(other, shift):
-        def fields(k, r):
+    def terms_from(other, shift):
+        def terms(k, r):
             m, o, e = mine[k, r], other[k + shift, r], end[k, r]
-            return o - m, m - e, o - e, drive[k, r]
-
-        return fields
-
-    totals = sums_of(0, 2, rows, fields_from(edges, 0), no_sums(lanes))
-    totals = sums_of(2, nz - 2, rows, fields_from(middle, -2), totals)
-    totals = sums_of(nz - 2, nz, rows, fields_from(edges, 4 - nz), totals)
-    write_sums(out, totals)
+            plus, minus, tangent = o - m, m - e, o - e
+            return plus * plus, minus * minus, tangent * tangent, drive[k, r] * tangent
+
+        return terms
+
+    totals = sums_of(0, 2, rows, terms_from(edges, 0), no_sums(4, lanes))
+    totals = sums_of(2, nz - 2, rows, terms_from(middle, -2), totals)
+    totals = sums_of(nz - 2, nz, rows, terms_from(edges, 4 - nz), totals)
+    out[...] = table_of(*(lane_row(t) for t in totals))
 
 
 def coefficient(sums):
@@ -283,8 +288,8 @@
     layer_loop(0, nz, one)
 
 
-def second_step_kernel(sums, step, tangent_wide, moved_out, drive_out, field, pot):
-    nz, rows, _ = drive_out.shape
+def second_step_kernel(sums, step, tangent_wide, end, moved_out, drive_out, minus_out, field, pot):
+    nz, rows, _ = end.shape
     coef, _, _ = coefficient(sums)
 
     def move(k):
@@ -295,35 +300,53 @@
 
     def one(k):
         drive = driving(pot, k)[PAD : PAD + rows]
+        here = field[k + 2][PAD : PAD + rows]
         drive_out[k] = drive
-        moved_out[k] = field[k + 2][PAD : PAD + rows]
+        minus_out[k] = here - end[k]
+        moved_out[k] = here + STEP_SIZE * drive
 
     layer_loop(0, nz, one)
 
 
-def second_sums_kernel(sums, far, mine, end, other_step, moved, drive, tangent_out, out):
+def prepare_kernel(o_sums, other_step, mine, end, minus, near_out, known_out):
     nz, rows, lanes = mine.shape
-    coef, _, _ = coefficient(sums)
-
-    def fields(k, r):
-        o = other_step[k, r] + coef * (mine[k, r] - far[k, r])
-        m, e = moved[k, r], end[k, r]
-        tangent = o - e
-        tangent_out[k, r] = tangent
-        return o - m, m - e, tangent, drive[k, r]
-
-    write_sums(out, sums_of(0, nz, rows, fields, no_sums(lanes)))
-
-
-def last_kernel(cells, sums, moved, drive, tangent, base, out, par_out, buf, sems):
+    coef, _, _ = coefficient(o_sums)
+
+    def near(k):
+        near_out[k] = other_step[k] + coef * mine[k] - end[k]
+
+    def terms(k, r):
+        m = minus[k, r]
+        return (m * m,)
+
+    layer_loop(0, nz, near)
+    (total,) = sums_of(0, nz, rows, terms, no_sums(1, lanes))
+    known_out[...] = table_of(jnp.broadcast_to(coef, (1, 128)), lane_row(total))
+
+
+def second_sums_kernel(known, far, near, minus, drive, out):
+    nz, rows, lanes = far.shape
+    coef = known[0:1, 0:1]
+
+    def terms(k, r):
+        tangent = near[k, r] - coef * far[k, r]
+        plus = tangent - minus[k, r]
+        return plus * plus, tangent * tangent, drive[k, r] * tangent
+
+    plus, tangent, par = sums_of(0, nz, rows, terms, no_sums(3, lanes))
+    out[...] = table_of(lane_row(plus), known[1:2], lane_row(tangent), lane_row(par))
+
+
+def last_kernel(cells, sums, known, far, near, moved, base, out, par_out, buf, sems):
     del base
     nz = moved.shape[0]
     at = lax.axis_index("image")
     which = 1 - at
     coef, par, safe = coefficient(sums)
+    o_coef = known[0:1, 0:1]
     copies = []
     for k in range(nz):
-        buf[k] = moved[k] + STEP_SIZE * drive[k] + coef * tangent[k]
+        buf[k] = moved[k] + coef * (near[k] - o_coef * far[k])
         if k % 4 == 3:
             where = pl.ds(k - 3, 4)
             copies.append(
@@ -383,14 +406,24 @@
     def room(layers):
         return pltpu.VMEM((layers, wide, nx), jnp.float32)
 
-    mine, end, edges, middle, up, down = call(
-        split_kernel,
-        [block, block, shape(4, ny, nx), shape(nz - 4, ny, nx), shape(4, ny, nx), shape(4, ny, nx)],
-        [DMA((7,))],
-        "split",
+    thin = shape(4, ny, nx)
+    source = pltpu.with_memory_space_constraint(images, pltpu.HBM)
+    edges, middle = call(
+        send_kernel,
+        [thin, shape(nz - 4, ny, nx)],
+        [DMA((3,))],
+        "send",
         in_specs=[ANY],
-        out_specs=[ANY] * 6,
-    )(images)
+        out_specs=[ANY] * 2,
+    )(source)
+    mine, end, up, down = call(
+        keep_kernel,
+        [block, block, thin, thin],
+        [DMA((4,))],
+        "keep",
+        in_specs=[ANY],
+        out_specs=[ANY] * 4,
+    )(source)
 
     o_edges = lax.ppermute(edges, "image", SWAP)
     o_middle = lax.ppermute(middle, "image", SWAP)
@@ -400,13 +433,13 @@
     step, drive = call(first_step_kernel, [outer, block], [room(nz + 8), room(nz + 6)], "first_step")(
         mine, low, high, sides
     )
-
     end_later, drive = lax.optimization_barrier((end, drive))
     far = lax.ppermute(end_later, "image", SWAP)
 
     o_low, o_high = from_z(
         jnp.concatenate([o_edges[2:], end[nz - 2 :]]), jnp.concatenate([o_edges[:2], end[:2]])
     )
+    o_low, o_high, o_middle = lax.optimization_barrier((o_low, o_high, o_middle))
     o_sides = y_sides(o_low[:2], o_edges[:2], o_middle, o_edges[2:], o_high[:2], o_low[2:], end, o_high[2:])
 
     base = call(
@@ -423,13 +456,16 @@
         other_step_kernel, [block, outer], [room(nz + 4), room(nz + 2)], "other_step"
     )(o_edges, o_middle, end, o_low, o_high, o_sides)
 
-    moved, drive2 = call(
-        second_step_kernel, [block, block], [room(nz + 4), room(nz + 2)], "second_step"
-    )(sums, step, tangent_wide)
+    moved, drive2, minus = call(
+        second_step_kernel, [block] * 3, [room(nz + 4), room(nz + 2)], "second_step"
+    )(sums, step, tangent_wide, end)
 
     o_sums = lax.ppermute(sums, "image", SWAP)
-    tangent, sums = call(second_sums_kernel, [block, table], name="second_sums")(
-        o_sums, far, mine, end, other_step, moved, drive2
+    near, known = call(prepare_kernel, [block, table], name="prepare")(
+        o_sums, other_step, mine, end, minus
+    )
+    sums = summed(
+        call(second_sums_kernel, table, name="second_sums")(known, far, near, minus, drive2)
     )
 
     return call(
@@ -437,10 +473,10 @@
         [jax.ShapeDtypeStruct(images.shape, images.dtype), shape(2)],
         [pltpu.VMEM(block.shape, jnp.float32), DMA((nz // 4,))],
         "last",
-        in_specs=[VMEM] * 4 + [ANY],
+        in_specs=[VMEM] * 5 + [ANY],
         out_specs=[ANY, SMEM],
-        input_output_aliases={4: 0},
-    )(summed(sums), moved, drive2, tangent, base)
+        input_output_aliases={5: 0},
+    )(sums, known, far, near, moved, base)
 
 
 def body(images):

time: 74.3 us -> 70 us (0.942)
  waiting for transfers between devices: 36.5 us -> 34.5 us
  starting transfers between devices: 19.2 us -> 17.5 us
  local copies, waits for them, and re-layouts: 1.71 us -> 0.13 us
  Pallas kernels: 15.7 us -> 16.8 us
    ppermute x2, waiting for transfers between devices: 11.8 us -> 8.55 us  [from_z(): lax.ppermute(down, 'space', [((i + 1) % count, i) for i in range(count)])]
    ppermute x4, starting transfers between devices: 4.91 us -> 2.35 us  [summed(): lax.ppermute(sums, 'space', [(i, i ^ stride) for i in range(count)])]
    ppermute x4, waiting for transfers between devices: 9.98 us -> 12.5 us  [summed(): lax.ppermute(sums, 'space', [(i, i ^ stride) for i in range(count)])]
    ppermute x1, waiting for transfers between devices: 2.92 us -> 1.08 us  [body_pair(): o_edges = lax.ppermute(edges, 'image', SWAP)]
    ppermute x2, waiting for transfers between devices: 0.01 us -> 1.67 us  [y_sides(): return lax.ppermute(jnp.concatenate(ends, 0), 'yslab', SWAP)]
    unnamed x4 -> x2, local copies, waits for them, and re-layouts: 1.59 us -> 0.01 us
    pallas_call x3 -> x5, Pallas kernels: 6.64 us -> 7.64 us  [the longest x1 2.66 us: body_pair(): call(second_step_kernel, [block] * 3, [room(nz + 4), room(nz + 2)], 'seco...]
    ppermute x2, waiting for transfers between devices: 2.7 us -> 1.7 us  [from_z(): lax.ppermute(up, 'space', [(i, (i + 1) % count) for i in range(count)])]
  transfers between devices with their start and end apart: 16 -> 16, of which waited for: 11 -> 12; matrix products, arithmetic and copies ran while one was open for 0% -> 0% of each run, Pallas kernels for 14% -> 18%
where the time goes in v5:
time: 70 us; the launch traced here: 69.9 us
  waiting for transfers between devices  34.5 us (49%)
  starting transfers between devices  17.5 us (25%)
  Pallas kernels  16.8 us (24%)
  between operations  0.87 us (1%)
    ppermute x4, waiting for transfers between devices, summed(): lax.ppermute(sums, 'space', [(i, i ^ stride) for i in range(count)])  12.5 us
    ppermute x2, waiting for transfers between devices, from_z(): lax.ppermute(down, 'space', [((i + 1) % count, i) for i in range(count)])  8.55 us
    ppermute x1, waiting for transfers between devices, body_pair(): o_sums = lax.ppermute(sums, 'image', SWAP)  6.71 us
    ppermute x2, starting transfers between devices, from_z(): lax.ppermute(up, 'space', [(i, (i + 1) % count) for i in range(count)])  4.28 us
    ppermute x2, starting transfers between devices, from_z(): lax.ppermute(down, 'space', [((i + 1) % count, i) for i in range(count)])  4.19 us
    pallas_call x1, Pallas kernels, body_pair(): call(first_step_kernel, [outer, block], [room(nz + 8), room(nz + 6)], 'fi...  3.06 us
    ppermute x1, starting transfers between devices, body_pair(): o_edges = lax.ppermute(edges, 'image', SWAP)  3 us
    pallas_call x1, Pallas kernels, body_pair(): call(second_step_kernel, [block] * 3, [room(nz + 4), room(nz + 2)], 'seco...  2.66 us
  transfers between devices with their start and end apart: 16, of which 12 were waited for; matrix products, arithmetic and copies ran while one was open for 0% of the time, Pallas kernels for 18%

profile of v5, /device:TPU:0, one launch (start us, length us, event | category | flops | bytes accessed | tf_op | source)
XLA Modules:
  0.0 69.9 jit_solution(4895749011650422267)
XLA Ops:
  0.6 1.3 %send.1 = (f32[4,64,256]{2,1,0:T(8,128)S(1)}, f32[12,64,256]{2,1,0:T(8,128)S(1)}) custom-call(f32[2,16,64,256]{3,2,1,0:T(8,128)} %src.1), custom_call_target="tpu_custom_call" | custom-call | tf_op jit(solution)/shard_map/send/pallas_call | solution.py:411
  1.9 3.0 %collective-permute-start = (f32[4,64,256]{2,1,0:T(8,128)S(1)}, f32[4,64,256]{2,1,0:T(8,128)S(1)}, u32[]{:S(2)}, u32[]{:S(2)}) collective-permute-start(f32[4,64,256]{2,1,0:T(8,128)S(1)} %get-tuple-element.22), channel_id=1, source_target_pairs={{0,8},{8,0},{1,9},{9,1},{2,10},{10,2},{3,11},{11,3},{4,12},{12,4},... | collective-permute-start | bytes 786440 | tf_op jit(solution)/shard_map/ppermute | solution.py:428
  5.0 0.1 collective-permute-start.3
  5.0 1.7 %keep.1 = (f32[16,64,256]{2,1,0:T(8,128)S(1)}, f32[16,64,256]{2,1,0:T(8,128)S(1)}, f32[4,64,256]{2,1,0:T(8,128)S(1)}, f32[4,64,256]{2,1,0:T(8,128)S(1)}) custom-call(f32[2,16,64,256]{3,2,1,0:T(8,128)} %src.1), custom_call_target="tpu_custom_call" | custom-call | tf_op jit(solution)/shard_map/keep/pallas_call | solution.py:419
  6.8 2.1 %collective-permute-start.4 = (f32[4,64,256]{2,1,0:T(8,128)S(1)}, f32[4,64,256]{2,1,0:T(8,128)S(1)}, u32[]{:S(2)}, u32[]{:S(2)}) collective-permute-start(f32[4,64,256]{2,1,0:T(8,128)S(1)} %get-tuple-element.27), channel_id=1, source_target_pairs={{0,2},{2,4},{4,6},{6,0},{1,3},{3,5},{5,7},{7,1},{8,10},{10,12},{12... | collective-permute-start | bytes 786440 | tf_op jit(solution)/shard_map/ppermute | solution.py:379
  8.9 2.1 %collective-permute-start.5 = (f32[4,64,256]{2,1,0:T(8,128)S(1)}, f32[4,64,256]{2,1,0:T(8,128)S(1)}, u32[]{:S(2)}, u32[]{:S(2)}) collective-permute-start(f32[4,64,256]{2,1,0:T(8,128)S(1)} %get-tuple-element.28), channel_id=1, source_target_pairs={{2,0},{4,2},{6,4},{0,6},{3,1},{5,3},{7,5},{1,7},{10,8},{12,10},{14... | collective-permute-start | bytes 786440 | tf_op jit(solution)/shard_map/ppermute | solution.py:380
  11.0 1.1 %collective-permute-done.edges = f32[4,64,256]{2,1,0:T(8,128)S(1)} collective-permute-done((f32[4,64,256]{2,1,0:T(8,128)S(1)}, f32[4,64,256]{2,1,0:T(8,128)S(1)}, u32[]{:S(2)}, u32[]{:S(2)}) %collective-permute-start) | collective-permute-done | bytes 262176 | tf_op jit(solution)/shard_map/ppermute | solution.py:428
  12.1 2.2 %collective-permute-start.1 = (f32[4,64,256]{2,1,0:T(8,128)S(1)}, f32[4,64,256]{2,1,0:T(8,128)S(1)}, u32[]{:S(2)}, u32[]{:S(2)}) collective-permute-start(f32[4,64,256]{2,1,0:T(8,128)S(1)} %pad_maximum_fusion), channel_id=1, source_target_pairs={{0,2},{2,4},{4,6},{6,0},{1,3},{3,5},{5,7},{7,1},{8,10},{10,12},{12... | collective-permute-start | bytes 786440 | tf_op jit(solution)/shard_map/ppermute | solution.py:379
  14.4 2.1 %collective-permute-start.2 = (f32[4,64,256]{2,1,0:T(8,128)S(1)}, f32[4,64,256]{2,1,0:T(8,128)S(1)}, u32[]{:S(2)}, u32[]{:S(2)}) collective-permute-start(f32[4,64,256]{2,1,0:T(8,128)S(1)} %pad_maximum_fusion.1), channel_id=1, source_target_pairs={{2,0},{4,2},{6,4},{0,6},{3,1},{5,3},{7,5},{1,7},{10,8},{12,10},{14... | collective-permute-start | bytes 786440 | tf_op jit(solution)/shard_map/ppermute | solution.py:380
  16.4 1.7 %collective-permute-done.4.low = f32[4,64,256]{2,1,0:T(8,128)S(1)} collective-permute-done((f32[4,64,256]{2,1,0:T(8,128)S(1)}, f32[4,64,256]{2,1,0:T(8,128)S(1)}, u32[]{:S(2)}, u32[]{:S(2)}) %collective-permute-start.4) | collective-permute-done | bytes 262176 | tf_op jit(solution)/shard_map/ppermute | solution.py:379
  18.1 8.4 %collective-permute-done.5.high = f32[4,64,256]{2,1,0:T(8,128)S(1)} collective-permute-done((f32[4,64,256]{2,1,0:T(8,128)S(1)}, f32[4,64,256]{2,1,0:T(8,128)S(1)}, u32[]{:S(2)}, u32[]{:S(2)}) %collective-permute-start.5) | collective-permute-done | bytes 262176 | tf_op jit(solution)/shard_map/ppermute | solution.py:380
  26.6 0.1 collective-permute-start.6
  26.8 1.7 %collective-permute-done.6.sides = f32[24,16,256]{2,1,0:T(8,128)S(1)} collective-permute-done((f32[24,16,256]{2,1,0:T(8,128)S(1)}, f32[24,16,256]{2,1,0:T(8,128)S(1)}, u32[]{:S(2)}, u32[]{:S(2)}) %collective-permute-start.6) | collective-permute-done | bytes 393248 | tf_op jit(solution)/shard_map/ppermute | solution.py:387
  28.4 3.1 %first_step.1 = (f32[20,80,256]{2,1,0:T(8,128)S(1)}, f32[16,64,256]{2,1,0:T(8,128)S(1)}) custom-call(f32[16,64,256]{2,1,0:T(8,128)S(1)} %get-tuple-element.26.mine, f32[4,64,256]{2,1,0:T(8,128)S(1)} %collective-permute-done.4.low, f32[4,64,256]{2,1,0:T(8,128)S(1)} %collective-permute-done.5.high, f32[24,16,256]{2,1,0:T(8,128)S(1)} %collective-permute-done.6.sides), custom_call_target="tpu_custom_call" | custom-call | tf_op jit(solution)/shard_map/first_step/pallas_call | solution.py:433
  31.5 1.3 %collective-permute-start.12 = (f32[16,64,256]{2,1,0:T(8,128)S(1)}, f32[16,64,256]{2,1,0:T(8,128)S(1)}, u32[]{:S(2)}, u32[]{:S(2)}) collective-permute-start(f32[16,64,256]{2,1,0:T(8,128)S(1)} %get-tuple-element.38.end), channel_id=1, source_target_pairs={{0,8},{8,0},{1,9},{9,1},{2,10},{10,2},{3,11},{11,3},{4,12},{12,4},... | collective-permute-start | bytes 3145736 | tf_op jit(solution)/shard_map/ppermute | solution.py:437
  32.8 0.0 collective-permute-done.1.low
  32.8 0.1 collective-permute-done.2.high
  32.9 0.0 collective-permute-done.3.middle
  33.1 0.1 collective-permute-start.11
  33.2 0.4 first_sums.1
  33.6 0.6 collective-permute-start.7
  34.2 1.1 %collective-permute-done.7 = f32[8,128]{1,0:T(8,128)S(1)} collective-permute-done((f32[8,128]{1,0:T(8,128)S(1)}, f32[8,128]{1,0:T(8,128)S(1)}, u32[]{:S(2)}, u32[]{:S(2)}) %collective-permute-start.7) | collective-permute-done | bytes 4128 | tf_op jit(solution)/shard_map/ppermute | solution.py:391
  35.3 1.1 %collective-permute-start.8 = (f32[8,128]{1,0:T(8,128)S(1)}, f32[8,128]{1,0:T(8,128)S(1)}, u32[]{:S(2)}, u32[]{:S(2)}) collective-permute-start(f32[8,128]{1,0:T(8,128)S(1)} %add.18), channel_id=1, source_target_pairs={{0,2},{2,0},{4,6},{6,4},{1,3},{3,1},{5,7},{7,5},{8,10},{10,8},{12,... | collective-permute-start | bytes 12296 | tf_op jit(solution)/shard_map/ppermute | solution.py:394
  36.4 2.5 %collective-permute-done.8 = f32[8,128]{1,0:T(8,128)S(1)} collective-permute-done((f32[8,128]{1,0:T(8,128)S(1)}, f32[8,128]{1,0:T(8,128)S(1)}, u32[]{:S(2)}, u32[]{:S(2)}) %collective-permute-start.8) | collective-permute-done | bytes 4128 | tf_op jit(solution)/shard_map/ppermute | solution.py:394
  38.9 1.2 %collective-permute-start.9 = (f32[8,128]{1,0:T(8,128)S(1)}, f32[8,128]{1,0:T(8,128)S(1)}, u32[]{:S(2)}, u32[]{:S(2)}) collective-permute-start(f32[8,128]{1,0:T(8,128)S(1)} %add.19), channel_id=1, source_target_pairs={{0,4},{2,6},{4,0},{6,2},{1,5},{3,7},{5,1},{7,3},{8,12},{10,14},{12... | collective-permute-start | bytes 12296 | tf_op jit(solution)/shard_map/ppermute | solution.py:394
  40.1 3.3 %collective-permute-done.9 = f32[8,128]{1,0:T(8,128)S(1)} collective-permute-done((f32[8,128]{1,0:T(8,128)S(1)}, f32[8,128]{1,0:T(8,128)S(1)}, u32[]{:S(2)}, u32[]{:S(2)}) %collective-permute-start.9) | collective-permute-done | bytes 4128 | tf_op jit(solution)/shard_map/ppermute | solution.py:394
  43.4 1.5 %collective-permute-start.10 = (f32[8,128]{1,0:T(8,128)S(1)}, f32[8,128]{1,0:T(8,128)S(1)}, u32[]{:S(2)}, u32[]{:S(2)}) collective-permute-start(f32[8,128]{1,0:T(8,128)S(1)} %add.20.sums), channel_id=1, source_target_pairs={{0,8},{8,0},{1,9},{9,1},{2,10},{10,2},{3,11},{11,3},{4,12},{12,4},... | collective-permute-start | bytes 12296 | tf_op jit(solution)/shard_map/ppermute | solution.py:463
  44.9 0.0 collective-permute-done.11.sides
  44.9 2.6 %other_step.1 = (f32[16,64,256]{2,1,0:T(8,128)S(1)}, f32[20,80,256]{2,1,0:T(8,128)S(1)}) custom-call(f32[4,64,256]{2,1,0:T(8,128)S(1)} %collective-permute-done.edges, f32[12,64,256]{2,1,0:T(8,128)S(1)} %collective-permute-done.3.middle, f32[16,64,256]{2,1,0:T(8,128)S(1)} %get-tuple-element.38.end, f32[4,64,256]{2,1,0:T(8,128)S(1)} %collective-permute-done.1.low, ...), custom_call_target="tpu_custom_call" | custom-call | tf_op jit(solution)/shard_map/other_step/pallas_call | solution.py:455
  47.5 2.7 %second_step.1 = (f32[16,64,256]{2,1,0:T(8,128)S(1)}, f32[16,64,256]{2,1,0:T(8,128)S(1)}, f32[16,64,256]{2,1,0:T(8,128)S(1)}) custom-call(f32[8,128]{1,0:T(8,128)S(1)} %add.20.sums, f32[20,80,256]{2,1,0:T(8,128)S(1)} %get-tuple-element.34.step, f32[20,80,256]{2,1,0:T(8,128)S(1)} %get-tuple-element.35.tangent_wide, f32[16,64,256]{2,1,0:T(8,128)S(1)} %get-tuple-element.38.end), custom_call_target="tpu_custom_call" | custom-call | tf_op jit(solution)/shard_map/second_step/pallas_call | solution.py:459
  50.1 6.7 %collective-permute-done.10.o_sums = f32[8,128]{1,0:T(8,128)S(1)} collective-permute-done((f32[8,128]{1,0:T(8,128)S(1)}, f32[8,128]{1,0:T(8,128)S(1)}, u32[]{:S(2)}, u32[]{:S(2)}) %collective-permute-start.10) | collective-permute-done | bytes 4128 | tf_op jit(solution)/shard_map/ppermute | solution.py:463
  56.8 0.7 %prepare.1 = (f32[16,64,256]{2,1,0:T(8,128)S(1)}, f32[8,128]{1,0:T(8,128)S(1)}) custom-call(f32[8,128]{1,0:T(8,128)S(1)} %collective-permute-done.10.o_sums, f32[16,64,256]{2,1,0:T(8,128)S(1)} %get-tuple-element.33.other_step, f32[16,64,256]{2,1,0:T(8,128)S(1)} %get-tuple-element.26.mine, f32[16,64,256]{2,1,0:T(8,128)S(1)} %get-tuple-element.38.end, ...), custom_call_target="tpu_custom_call" | custom-call | tf_op jit(solution)/shard_map/prepare/pallas_call | solution.py:464
  57.6 0.0 collective-permute-done.12.far
  57.6 0.0 copy-start
  57.6 1.2 %second_sums.1 = f32[8,128]{1,0:T(8,128)S(1)} custom-call(f32[8,128]{1,0:T(8,128)S(1)} %get-tuple-element.37.known, f32[16,64,256]{2,1,0:T(8,128)S(1)} %collective-permute-done.12.far, f32[16,64,256]{2,1,0:T(8,128)S(1)} %get-tuple-element.39.near, f32[16,64,256]{2,1,0:T(8,128)S(1)} %get-tuple-element.36.minus, f32[16,64,256]{2,1,0:T(8,128)S(1)} %get-tuple-element.40.drive), custom_call_target="tpu_custom_call" | custom-call | tf_op jit(solution)/shard_map/second_sums/pallas_call | solution.py:468
  58.8 0.1 collective-permute-start.13
  58.9 1.2 %collective-permute-done.13 = f32[8,128]{1,0:T(8,128)S(1)} collective-permute-done((f32[8,128]{1,0:T(8,128)S(1)}, f32[8,128]{1,0:T(8,128)S(1)}, u32[]{:S(2)}, u32[]{:S(2)}) %collective-permute-start.13) | collective-permute-done | bytes 4128 | tf_op jit(solution)/shard_map/ppermute | solution.py:391
  60.0 0.0 collective-permute-start.14
  60.0 3.6 %collective-permute-done.14 = f32[8,128]{1,0:T(8,128)S(1)} collective-permute-done((f32[8,128]{1,0:T(8,128)S(1)}, f32[8,128]{1,0:T(8,128)S(1)}, u32[]{:S(2)}, u32[]{:S(2)}) %collective-permute-start.14) | collective-permute-done | bytes 4128 | tf_op jit(solution)/shard_map/ppermute | solution.py:394
  63.7 0.0 collective-permute-start.15
  63.7 0.0 copy-done
  63.7 1.3 %base.1 = f32[2,16,64,256]{3,2,1,0:T(8,128)} custom-call(f32[2,16,64,256]{3,2,1,0:T(8,128)S(1)} %copy-done), custom_call_target="tpu_custom_call" | custom-call | tf_op jit(solution)/shard_map/base/pallas_call | solution.py:445
  65.0 3.2 %collective-permute-done.15 = f32[8,128]{1,0:T(8,128)S(1)} collective-permute-done((f32[8,128]{1,0:T(8,128)S(1)}, f32[8,128]{1,0:T(8,128)S(1)}, u32[]{:S(2)}, u32[]{:S(2)}) %collective-permute-start.15) | collective-permute-done | bytes 4128 | tf_op jit(solution)/shard_map/ppermute | solution.py:394
  68.2 1.7 %last.1 = (f32[2,16,64,256]{3,2,1,0:T(8,128)}, f32[2]{0:T(128)}) custom-call(f32[8,128]{1,0:T(8,128)S(1)} %add.23.sums, f32[8,128]{1,0:T(8,128)S(1)} %get-tuple-element.37.known, f32[16,64,256]{2,1,0:T(8,128)S(1)} %collective-permute-done.12.far, f32[16,64,256]{2,1,0:T(8,128)S(1)} %get-tuple-element.39.near, ...), custom_call_target="tpu_custom_call", output_to_operand_aliasing={{0}: (5, {})} | custom-call | tf_op jit(solution)/shard_map/last/pallas_call | solution.py:471
  (26 shorter events, 0.3 us)
Async XLA Ops:
  1.9 10.1 %collective-permute-start = (f32[4,64,256]{2,1,0:T(8,128)S(1)}, f32[4,64,256]{2,1,0:T(8,128)S(1)}, u32[]{:S(2)}, u32[]{:S(2)}) collective-permute-start(f32[4,64,256]{2,1,0:T(8,128)S(1)} %get-tuple-element.22), channel_id=1, source_target_pairs={{0,8},{8,0},{1,9},{9,1},{2,10},{10,2},{3,11},{11,3},{4,12},{12,4},... | collective-permute-start | bytes 786440 | tf_op jit(solution)/shard_map/ppermute | solution.py:428
  5.0 28.0 %collective-permute-start.3 = (f32[12,64,256]{2,1,0:T(8,128)S(1)}, f32[12,64,256]{2,1,0:T(8,128)S(1)}, u32[]{:S(2)}, u32[]{:S(2)}) collective-permute-start(f32[12,64,256]{2,1,0:T(8,128)S(1)} %get-tuple-element.24), channel_id=1, source_target_pairs={{0,8},{8,0},{1,9},{9,1},{2,10},{10,2},{3,11},{11,3},{4,12},{12,4},... | collective-permute-start | bytes 2359304 | tf_op jit(solution)/shard_map/ppermute | solution.py:429
  6.8 11.4 %collective-permute-start.4 = (f32[4,64,256]{2,1,0:T(8,128)S(1)}, f32[4,64,256]{2,1,0:T(8,128)S(1)}, u32[]{:S(2)}, u32[]{:S(2)}) collective-permute-start(f32[4,64,256]{2,1,0:T(8,128)S(1)} %get-tuple-element.27), channel_id=1, source_target_pairs={{0,2},{2,4},{4,6},{6,0},{1,3},{3,5},{5,7},{7,1},{8,10},{10,12},{12... | collective-permute-start | bytes 786440 | tf_op jit(solution)/shard_map/ppermute | solution.py:379
  8.9 17.7 %collective-permute-start.5 = (f32[4,64,256]{2,1,0:T(8,128)S(1)}, f32[4,64,256]{2,1,0:T(8,128)S(1)}, u32[]{:S(2)}, u32[]{:S(2)}) collective-permute-start(f32[4,64,256]{2,1,0:T(8,128)S(1)} %get-tuple-element.28), channel_id=1, source_target_pairs={{2,0},{4,2},{6,4},{0,6},{3,1},{5,3},{7,5},{1,7},{10,8},{12,10},{14... | collective-permute-start | bytes 786440 | tf_op jit(solution)/shard_map/ppermute | solution.py:380
  12.1 20.7 %collective-permute-start.1 = (f32[4,64,256]{2,1,0:T(8,128)S(1)}, f32[4,64,256]{2,1,0:T(8,128)S(1)}, u32[]{:S(2)}, u32[]{:S(2)}) collective-permute-start(f32[4,64,256]{2,1,0:T(8,128)S(1)} %pad_maximum_fusion), channel_id=1, source_target_pairs={{0,2},{2,4},{4,6},{6,0},{1,3},{3,5},{5,7},{7,1},{8,10},{10,12},{12... | collective-permute-start | bytes 786440 | tf_op jit(solution)/shard_map/ppermute | solution.py:379
  14.4 18.6 %collective-permute-start.2 = (f32[4,64,256]{2,1,0:T(8,128)S(1)}, f32[4,64,256]{2,1,0:T(8,128)S(1)}, u32[]{:S(2)}, u32[]{:S(2)}) collective-permute-start(f32[4,64,256]{2,1,0:T(8,128)S(1)} %pad_maximum_fusion.1), channel_id=1, source_target_pairs={{2,0},{4,2},{6,4},{0,6},{3,1},{5,3},{7,5},{1,7},{10,8},{12,10},{14... | collective-permute-start | bytes 786440 | tf_op jit(solution)/shard_map/ppermute | solution.py:380
  26.6 1.8 %collective-permute-start.6 = (f32[24,16,256]{2,1,0:T(8,128)S(1)}, f32[24,16,256]{2,1,0:T(8,128)S(1)}, u32[]{:S(2)}, u32[]{:S(2)}) collective-permute-start(f32[24,16,256]{2,1,0:T(8,128)S(1)} %maximum_maximum_fusion), channel_id=1, source_target_pairs={{0,1},{1,0},{2,3},{3,2},{4,5},{5,4},{6,7},{7,6},{8,9},{9,8},{10,11... | collective-permute-start | bytes 1179656 | tf_op jit(solution)/shard_map/ppermute | solution.py:387
  31.5 26.1 %collective-permute-start.12 = (f32[16,64,256]{2,1,0:T(8,128)S(1)}, f32[16,64,256]{2,1,0:T(8,128)S(1)}, u32[]{:S(2)}, u32[]{:S(2)}) collective-permute-start(f32[16,64,256]{2,1,0:T(8,128)S(1)} %get-tuple-element.38.end), channel_id=1, source_target_pairs={{0,8},{8,0},{1,9},{9,1},{2,10},{10,2},{3,11},{11,3},{4,12},{12,4},... | collective-permute-start | bytes 3145736 | tf_op jit(solution)/shard_map/ppermute | solution.py:437
  33.1 11.8 %collective-permute-start.11 = (f32[40,16,256]{2,1,0:T(8,128)S(1)}, f32[40,16,256]{2,1,0:T(8,128)S(1)}, u32[]{:S(2)}, u32[]{:S(2)}) collective-permute-start(f32[40,16,256]{2,1,0:T(8,128)S(1)} %maximum_dynamic-update-slice_fusion.2), channel_id=1, source_target_pairs={{0,1},{1,0},{2,3},{3,2},{4,5},{5,4},{6,7},{7,6},{8,9},{9,8},{10,11... | collective-permute-start | bytes 1966088 | tf_op jit(solution)/shard_map/ppermute | solution.py:387
  33.6 1.6 %collective-permute-start.7 = (f32[8,128]{1,0:T(8,128)S(1)}, f32[8,128]{1,0:T(8,128)S(1)}, u32[]{:S(2)}, u32[]{:S(2)}) collective-permute-start(f32[8,128]{1,0:T(8,128)S(1)} %first_sums.1), channel_id=1, source_target_pairs={{0,1},{1,0},{2,3},{3,2},{4,5},{5,4},{6,7},{7,6},{8,9},{9,8},{10,11... | collective-permute-start | bytes 12296 | tf_op jit(solution)/shard_map/ppermute | solution.py:391
  35.3 3.6 %collective-permute-start.8 = (f32[8,128]{1,0:T(8,128)S(1)}, f32[8,128]{1,0:T(8,128)S(1)}, u32[]{:S(2)}, u32[]{:S(2)}) collective-permute-start(f32[8,128]{1,0:T(8,128)S(1)} %add.18), channel_id=1, source_target_pairs={{0,2},{2,0},{4,6},{6,4},{1,3},{3,1},{5,7},{7,5},{8,10},{10,8},{12,... | collective-permute-start | bytes 12296 | tf_op jit(solution)/shard_map/ppermute | solution.py:394
  38.9 4.5 %collective-permute-start.9 = (f32[8,128]{1,0:T(8,128)S(1)}, f32[8,128]{1,0:T(8,128)S(1)}, u32[]{:S(2)}, u32[]{:S(2)}) collective-permute-start(f32[8,128]{1,0:T(8,128)S(1)} %add.19), channel_id=1, source_target_pairs={{0,4},{2,6},{4,0},{6,2},{1,5},{3,7},{5,1},{7,3},{8,12},{10,14},{12... | collective-permute-start | bytes 12296 | tf_op jit(solution)/shard_map/ppermute | solution.py:394
  43.4 13.5 %collective-permute-start.10 = (f32[8,128]{1,0:T(8,128)S(1)}, f32[8,128]{1,0:T(8,128)S(1)}, u32[]{:S(2)}, u32[]{:S(2)}) collective-permute-start(f32[8,128]{1,0:T(8,128)S(1)} %add.20.sums), channel_id=1, source_target_pairs={{0,8},{8,0},{1,9},{9,1},{2,10},{10,2},{3,11},{11,3},{4,12},{12,4},... | collective-permute-start | bytes 12296 | tf_op jit(solution)/shard_map/ppermute | solution.py:463
  57.6 6.1 %copy-start = (f32[2,16,64,256]{3,2,1,0:T(8,128)S(1)}, f32[2,16,64,256]{3,2,1,0:T(8,128)}, u32[]{:S(2)}) copy-start(f32[2,16,64,256]{3,2,1,0:T(8,128)} %src.1) | copy-start | bytes 6291460
  58.8 1.2 %collective-permute-start.13 = (f32[8,128]{1,0:T(8,128)S(1)}, f32[8,128]{1,0:T(8,128)S(1)}, u32[]{:S(2)}, u32[]{:S(2)}) collective-permute-start(f32[8,128]{1,0:T(8,128)S(1)} %second_sums.1), channel_id=1, source_target_pairs={{0,1},{1,0},{2,3},{3,2},{4,5},{5,4},{6,7},{7,6},{8,9},{9,8},{10,11... | collective-permute-start | bytes 12296 | tf_op jit(solution)/shard_map/ppermute | solution.py:391
  60.0 3.6 %collective-permute-start.14 = (f32[8,128]{1,0:T(8,128)S(1)}, f32[8,128]{1,0:T(8,128)S(1)}, u32[]{:S(2)}, u32[]{:S(2)}) collective-permute-start(f32[8,128]{1,0:T(8,128)S(1)} %add.21), channel_id=1, source_target_pairs={{0,2},{2,0},{4,6},{6,4},{1,3},{3,1},{5,7},{7,5},{8,10},{10,8},{12,... | collective-permute-start | bytes 12296 | tf_op jit(solution)/shard_map/ppermute | solution.py:394
  63.7 4.5 %collective-permute-start.15 = (f32[8,128]{1,0:T(8,128)S(1)}, f32[8,128]{1,0:T(8,128)S(1)}, u32[]{:S(2)}, u32[]{:S(2)}) collective-permute-start(f32[8,128]{1,0:T(8,128)S(1)} %add.22), channel_id=1, source_target_pairs={{0,4},{2,6},{4,0},{6,2},{1,5},{3,7},{5,1},{7,3},{8,12},{10,14},{12... | collective-permute-start | bytes 12296 | tf_op jit(solution)/shard_map/ppermute | solution.py:394

commit v6 on v5

--- a/solution.py
+++ b/solution.py
@@ -20,6 +20,7 @@
 PAD = 8
 VMEM_ROOM = 2 * 2**20
 UNROLL = 4
+AHEAD = 4
 
 
 def passed_along(array, axis, by):
@@ -188,9 +189,9 @@
     which = 1 - lax.axis_index("image")
     nz = images.shape[1]
     pairs = [
-        (images.at[which, pl.ds(0, 2)], edges.at[pl.ds(0, 2)]),
-        (images.at[which, pl.ds(nz - 2, 2)], edges.at[pl.ds(2, 2)]),
-        (images.at[which, pl.ds(2, nz - 4)], middle),
+        (images.at[which, pl.ds(0, AHEAD)], edges.at[pl.ds(0, AHEAD)]),
+        (images.at[which, pl.ds(nz - AHEAD, AHEAD)], edges.at[pl.ds(AHEAD, AHEAD)]),
+        (images.at[which, pl.ds(AHEAD, nz - 2 * AHEAD)], middle),
     ]
     all_copied(pairs, sems)
 
@@ -256,9 +257,10 @@
 
         return terms
 
-    totals = sums_of(0, 2, rows, terms_from(edges, 0), no_sums(4, lanes))
-    totals = sums_of(2, nz - 2, rows, terms_from(middle, -2), totals)
-    totals = sums_of(nz - 2, nz, rows, terms_from(edges, 4 - nz), totals)
+    last = nz - AHEAD
+    totals = sums_of(0, AHEAD, rows, terms_from(edges, 0), no_sums(4, lanes))
+    totals = sums_of(AHEAD, last, rows, terms_from(middle, -AHEAD), totals)
+    totals = sums_of(last, nz, rows, terms_from(edges, AHEAD - last), totals)
     out[...] = table_of(*(lane_row(t) for t in totals))
 
 
@@ -270,9 +272,9 @@
     return STEP_SIZE * (spring - par / safe), par, safe
 
 
-def other_step_kernel(edges, middle, end, low, high, sides, step_out, tangent_out, field, pot):
+def other_step_kernel(edges, middle, end, low, high, sides, near_out, tangent_out, field, pot):
     nz, rows, _ = end.shape
-    first, last = edges.at[0:2], edges.at[2:4]
+    first, last = edges.at[0:AHEAD], edges.at[AHEAD : 2 * AHEAD]
     fill_padded(field, (low.at[0:2], first, middle, last, high.at[0:2]), sides, 0)
     fill_padded(tangent_out, (low.at[2:4], end, high.at[2:4]), sides, nz + 4)
     potentials(field, pot, nz + 2)
@@ -282,7 +284,7 @@
 
     def one(k):
         moved = field[k + 2] + STEP_SIZE * driving(pot, k)
-        step_out[k] = moved[PAD : PAD + rows]
+        near_out[k] = moved[PAD : PAD + rows] - end[k]
 
     layer_loop(0, nz + 4, widen)
     layer_loop(0, nz, one)
@@ -308,45 +310,29 @@
     layer_loop(0, nz, one)
 
 
-def prepare_kernel(o_sums, other_step, mine, end, minus, near_out, known_out):
-    nz, rows, lanes = mine.shape
+def second_sums_kernel(o_sums, far, mine, near, minus, drive, out):
+    nz, rows, lanes = far.shape
     coef, _, _ = coefficient(o_sums)
 
-    def near(k):
-        near_out[k] = other_step[k] + coef * mine[k] - end[k]
-
     def terms(k, r):
+        tangent = near[k, r] + coef * (mine[k, r] - far[k, r])
         m = minus[k, r]
-        return (m * m,)
-
-    layer_loop(0, nz, near)
-    (total,) = sums_of(0, nz, rows, terms, no_sums(1, lanes))
-    known_out[...] = table_of(jnp.broadcast_to(coef, (1, 128)), lane_row(total))
-
-
-def second_sums_kernel(known, far, near, minus, drive, out):
-    nz, rows, lanes = far.shape
-    coef = known[0:1, 0:1]
-
-    def terms(k, r):
-        tangent = near[k, r] - coef * far[k, r]
-        plus = tangent - minus[k, r]
-        return plus * plus, tangent * tangent, drive[k, r] * tangent
-
-    plus, tangent, par = sums_of(0, nz, rows, terms, no_sums(3, lanes))
-    out[...] = table_of(lane_row(plus), known[1:2], lane_row(tangent), lane_row(par))
-
-
-def last_kernel(cells, sums, known, far, near, moved, base, out, par_out, buf, sems):
+        plus = tangent - m
+        return plus * plus, m * m, tangent * tangent, drive[k, r] * tangent
+
+    out[...] = table_of(*(lane_row(t) for t in sums_of(0, nz, rows, terms, no_sums(4, lanes))))
+
+
+def last_kernel(cells, sums, o_sums, far, mine, near, moved, base, out, par_out, buf, sems):
     del base
     nz = moved.shape[0]
     at = lax.axis_index("image")
     which = 1 - at
     coef, par, safe = coefficient(sums)
-    o_coef = known[0:1, 0:1]
+    o_coef, _, _ = coefficient(o_sums)
     copies = []
     for k in range(nz):
-        buf[k] = moved[k] + coef * (near[k] - o_coef * far[k])
+        buf[k] = moved[k] + coef * (near[k] + o_coef * (mine[k] - far[k]))
         if k % 4 == 3:
             where = pl.ds(k - 3, 4)
             copies.append(
@@ -410,7 +396,7 @@
     source = pltpu.with_memory_space_constraint(images, pltpu.HBM)
     edges, middle = call(
         send_kernel,
-        [thin, shape(nz - 4, ny, nx)],
+        [shape(2 * AHEAD, ny, nx), shape(nz - 2 * AHEAD, ny, nx)],
         [DMA((3,))],
         "send",
         in_specs=[ANY],
@@ -437,10 +423,13 @@
     far = lax.ppermute(end_later, "image", SWAP)
 
     o_low, o_high = from_z(
-        jnp.concatenate([o_edges[2:], end[nz - 2 :]]), jnp.concatenate([o_edges[:2], end[:2]])
+        jnp.concatenate([o_edges[2 * AHEAD - 2 :], end[nz - 2 :]]),
+        jnp.concatenate([o_edges[:2], end[:2]]),
     )
     o_low, o_high, o_middle = lax.optimization_barrier((o_low, o_high, o_middle))
-    o_sides = y_sides(o_low[:2], o_edges[:2], o_middle, o_edges[2:], o_high[:2], o_low[2:], end, o_high[2:])
+    o_sides = y_sides(
+        o_low[:2], o_edges[:AHEAD], o_middle, o_edges[AHEAD:], o_high[:2], o_low[2:], end, o_high[2:]
+    )
 
     base = call(
         copy_kernel,
@@ -452,7 +441,7 @@
     )(images)
 
     sums = summed(call(first_sums_kernel, table, name="first_sums")(o_edges, o_middle, mine, end, drive))
-    other_step, tangent_wide = call(
+    near, tangent_wide = call(
         other_step_kernel, [block, outer], [room(nz + 4), room(nz + 2)], "other_step"
     )(o_edges, o_middle, end, o_low, o_high, o_sides)
 
@@ -461,11 +450,8 @@
     )(sums, step, tangent_wide, end)
 
     o_sums = lax.ppermute(sums, "image", SWAP)
-    near, known = call(prepare_kernel, [block, table], name="prepare")(
-        o_sums, other_step, mine, end, minus
-    )
-    sums = summed(
-        call(second_sums_kernel, table, name="second_sums")(known, far, near, minus, drive2)
+    sums = call(second_sums_kernel, table, name="second_sums")(
+        o_sums, far, mine, near, minus, drive2
     )
 
     return call(
@@ -473,16 +459,17 @@
         [jax.ShapeDtypeStruct(images.shape, images.dtype), shape(2)],
         [pltpu.VMEM(block.shape, jnp.float32), DMA((nz // 4,))],
         "last",
-        in_specs=[VMEM] * 5 + [ANY],
+        in_specs=[VMEM] * 6 + [ANY],
         out_specs=[ANY, SMEM],
-        input_output_aliases={5: 0},
-    )(sums, known, far, near, moved, base)
+        input_output_aliases={6: 0},
+    )(summed(sums), o_sums, far, mine, near, moved, base)
 
 
 def body(images):
     layers = lax.axis_size("space")
     pair = lax.axis_size("image") == 2 and lax.axis_size("yslab") == 2 and images.shape[0] == 2
-    pair = pair and layers & (layers - 1) == 0
+    pair = pair and layers & (layers - 1) == 0 and images.shape[1] % 4 == 0
+    pair = pair and images.shape[1] > 2 * AHEAD and images.shape[2] % CHUNK == 0
     return body_pair(images) if pair else body_any(images)
 
 

time: 70 us -> 67.4 us (0.963)
  waiting for transfers between devices: 34.5 us -> 30 us
  starting transfers between devices: 17.5 us -> 19.5 us
    ppermute x2, waiting for transfers between devices: 1.7 us -> 9.5 us  [from_z(): lax.ppermute(up, 'space', [(i, (i + 1) % count) for i in range(count)])]
    ppermute x1, waiting for transfers between devices: 6.71 us -> 0.01 us  [body_pair(): o_sums = lax.ppermute(sums, 'image', SWAP)]
    ppermute x4, starting transfers between devices: 2.35 us -> 4.47 us  [summed(): lax.ppermute(sums, 'space', [(i, i ^ stride) for i in range(count)])]
    ppermute x4, waiting for transfers between devices: 12.5 us -> 10.4 us  [summed(): lax.ppermute(sums, 'space', [(i, i ^ stride) for i in range(count)])]
    ppermute x2, waiting for transfers between devices: 1.67 us -> 0.01 us  [y_sides(): return lax.ppermute(jnp.concatenate(ends, 0), 'yslab', SWAP)]
    ppermute x1, waiting for transfers between devices: 1.08 us -> 0.01 us  [body_pair(): o_edges = lax.ppermute(edges, 'image', SWAP)]
    ppermute x2, starting transfers between devices: 4.28 us -> 3.27 us  [from_z(): lax.ppermute(up, 'space', [(i, (i + 1) % count) for i in range(count)])]
    pallas_call x2 -> x1, Pallas kernels: 2.02 us -> 1.24 us  [body_pair(): call(send_kernel, [shape(2 * AHEAD, ny, nx), shape(nz - 2 * AHEAD, ny, nx...]
  transfers between devices with their start and end apart: 16 -> 16, of which waited for: 12 -> 10; matrix products, arithmetic and copies ran while one was open for 0% -> 0% of each run, Pallas kernels for 18% -> 18%
where the time goes in v6:
time: 67.4 us; the launch traced here: 67.2 us
  waiting for transfers between devices  30 us (45%)
  starting transfers between devices  19.5 us (29%)
  Pallas kernels  16.6 us (25%)
  between operations  0.89 us (1%)
    ppermute x4, waiting for transfers between devices, summed(): lax.ppermute(sums, 'space', [(i, i ^ stride) for i in range(count)])  10.4 us
    ppermute x2, waiting for transfers between devices, from_z(): lax.ppermute(up, 'space', [(i, (i + 1) % count) for i in range(count)])  9.5 us
    ppermute x2, waiting for transfers between devices, from_z(): lax.ppermute(down, 'space', [((i + 1) % count, i) for i in range(count)])  7.83 us
    ppermute x2, starting transfers between devices, from_z(): lax.ppermute(down, 'space', [((i + 1) % count, i) for i in range(count)])  4.84 us
    ppermute x4, starting transfers between devices, summed(): lax.ppermute(sums, 'space', [(i, i ^ stride) for i in range(count)])  4.47 us
    ppermute x2, starting transfers between devices, from_z(): lax.ppermute(up, 'space', [(i, (i + 1) % count) for i in range(count)])  3.27 us
    pallas_call x1, Pallas kernels, body_pair(): call(first_step_kernel, [outer, block], [room(nz + 8), room(nz + 6)], 'fi...  3.06 us
    ppermute x1, starting transfers between devices, body_pair(): o_edges = lax.ppermute(edges, 'image', SWAP)  3 us
  transfers between devices with their start and end apart: 16, of which 10 were waited for; matrix products, arithmetic and copies ran while one was open for 0% of the time, Pallas kernels for 18%

profile of v6, /device:TPU:0, one launch (start us, length us, event | category | flops | bytes accessed | tf_op | source)
XLA Modules:
  0.0 67.2 jit_solution(14840339073096681075)
XLA Ops:
  0.6 1.2 %send.1 = (f32[8,64,256]{2,1,0:T(8,128)S(1)}, f32[8,64,256]{2,1,0:T(8,128)S(1)}) custom-call(f32[2,16,64,256]{3,2,1,0:T(8,128)} %src.1), custom_call_target="tpu_custom_call" | custom-call | tf_op jit(solution)/shard_map/send/pallas_call | solution.py:397
  1.9 3.0 %collective-permute-start = (f32[8,64,256]{2,1,0:T(8,128)S(1)}, f32[8,64,256]{2,1,0:T(8,128)S(1)}, u32[]{:S(2)}, u32[]{:S(2)}) collective-permute-start(f32[8,64,256]{2,1,0:T(8,128)S(1)} %get-tuple-element.20), channel_id=1, source_target_pairs={{0,8},{8,0},{1,9},{9,1},{2,10},{10,2},{3,11},{11,3},{4,12},{12,4},... | collective-permute-start | bytes 1572872 | tf_op jit(solution)/shard_map/ppermute | solution.py:414
  4.9 0.1 collective-permute-start.3
  5.0 1.7 %keep.1 = (f32[16,64,256]{2,1,0:T(8,128)S(1)}, f32[16,64,256]{2,1,0:T(8,128)S(1)}, f32[4,64,256]{2,1,0:T(8,128)S(1)}, f32[4,64,256]{2,1,0:T(8,128)S(1)}) custom-call(f32[2,16,64,256]{3,2,1,0:T(8,128)} %src.1), custom_call_target="tpu_custom_call" | custom-call | tf_op jit(solution)/shard_map/keep/pallas_call | solution.py:405
  6.7 2.1 %collective-permute-start.4 = (f32[4,64,256]{2,1,0:T(8,128)S(1)}, f32[4,64,256]{2,1,0:T(8,128)S(1)}, u32[]{:S(2)}, u32[]{:S(2)}) collective-permute-start(f32[4,64,256]{2,1,0:T(8,128)S(1)} %get-tuple-element.25), channel_id=1, source_target_pairs={{0,2},{2,4},{4,6},{6,0},{1,3},{3,5},{5,7},{7,1},{8,10},{10,12},{12... | collective-permute-start | bytes 786440 | tf_op jit(solution)/shard_map/ppermute | solution.py:365
  8.8 2.1 %collective-permute-start.5 = (f32[4,64,256]{2,1,0:T(8,128)S(1)}, f32[4,64,256]{2,1,0:T(8,128)S(1)}, u32[]{:S(2)}, u32[]{:S(2)}) collective-permute-start(f32[4,64,256]{2,1,0:T(8,128)S(1)} %get-tuple-element.26), channel_id=1, source_target_pairs={{2,0},{4,2},{6,4},{0,6},{3,1},{5,3},{7,5},{1,7},{10,8},{12,10},{14... | collective-permute-start | bytes 786440 | tf_op jit(solution)/shard_map/ppermute | solution.py:366
  10.9 7.1 %collective-permute-done.4.low = f32[4,64,256]{2,1,0:T(8,128)S(1)} collective-permute-done((f32[4,64,256]{2,1,0:T(8,128)S(1)}, f32[4,64,256]{2,1,0:T(8,128)S(1)}, u32[]{:S(2)}, u32[]{:S(2)}) %collective-permute-start.4) | collective-permute-done | bytes 262176 | tf_op jit(solution)/shard_map/ppermute | solution.py:365
  18.1 3.5 %collective-permute-done.5.high = f32[4,64,256]{2,1,0:T(8,128)S(1)} collective-permute-done((f32[4,64,256]{2,1,0:T(8,128)S(1)}, f32[4,64,256]{2,1,0:T(8,128)S(1)}, u32[]{:S(2)}, u32[]{:S(2)}) %collective-permute-start.5) | collective-permute-done | bytes 262176 | tf_op jit(solution)/shard_map/ppermute | solution.py:366
  21.7 0.1 collective-permute-start.6
  21.7 0.0 collective-permute-done.edges
  21.8 1.2 %collective-permute-start.1 = (f32[4,64,256]{2,1,0:T(8,128)S(1)}, f32[4,64,256]{2,1,0:T(8,128)S(1)}, u32[]{:S(2)}, u32[]{:S(2)}) collective-permute-start(f32[4,64,256]{2,1,0:T(8,128)S(1)} %pad_maximum_fusion), channel_id=1, source_target_pairs={{0,2},{2,4},{4,6},{6,0},{1,3},{3,5},{5,7},{7,1},{8,10},{10,12},{12... | collective-permute-start | bytes 786440 | tf_op jit(solution)/shard_map/ppermute | solution.py:365
  23.0 2.7 %collective-permute-start.2 = (f32[4,64,256]{2,1,0:T(8,128)S(1)}, f32[4,64,256]{2,1,0:T(8,128)S(1)}, u32[]{:S(2)}, u32[]{:S(2)}) collective-permute-start(f32[4,64,256]{2,1,0:T(8,128)S(1)} %pad_maximum_fusion.1), channel_id=1, source_target_pairs={{2,0},{4,2},{6,4},{0,6},{3,1},{5,3},{7,5},{1,7},{10,8},{12,10},{14... | collective-permute-start | bytes 786440 | tf_op jit(solution)/shard_map/ppermute | solution.py:366
  25.8 0.0 collective-permute-done.6.sides
  25.8 3.1 %first_step.1 = (f32[20,80,256]{2,1,0:T(8,128)S(1)}, f32[16,64,256]{2,1,0:T(8,128)S(1)}) custom-call(f32[16,64,256]{2,1,0:T(8,128)S(1)} %get-tuple-element.24.mine, f32[4,64,256]{2,1,0:T(8,128)S(1)} %collective-permute-done.4.low, f32[4,64,256]{2,1,0:T(8,128)S(1)} %collective-permute-done.5.high, f32[24,16,256]{2,1,0:T(8,128)S(1)} %collective-permute-done.6.sides), custom_call_target="tpu_custom_call" | custom-call | tf_op jit(solution)/shard_map/first_step/pallas_call | solution.py:419
  28.9 1.6 %collective-permute-start.11 = (f32[16,64,256]{2,1,0:T(8,128)S(1)}, f32[16,64,256]{2,1,0:T(8,128)S(1)}, u32[]{:S(2)}, u32[]{:S(2)}) collective-permute-start(f32[16,64,256]{2,1,0:T(8,128)S(1)} %get-tuple-element.29.end), channel_id=1, source_target_pairs={{0,8},{8,0},{1,9},{9,1},{2,10},{10,2},{3,11},{11,3},{4,12},{12,4},... | collective-permute-start | bytes 3145736 | tf_op jit(solution)/shard_map/ppermute | solution.py:423
  30.4 0.0 collective-permute-done.3.middle
  30.4 2.4 %collective-permute-done.1.low = f32[4,64,256]{2,1,0:T(8,128)S(1)} collective-permute-done((f32[4,64,256]{2,1,0:T(8,128)S(1)}, f32[4,64,256]{2,1,0:T(8,128)S(1)}, u32[]{:S(2)}, u32[]{:S(2)}) %collective-permute-start.1) | collective-permute-done | bytes 262176 | tf_op jit(solution)/shard_map/ppermute | solution.py:365
  32.8 4.3 %collective-permute-done.2.high = f32[4,64,256]{2,1,0:T(8,128)S(1)} collective-permute-done((f32[4,64,256]{2,1,0:T(8,128)S(1)}, f32[4,64,256]{2,1,0:T(8,128)S(1)}, u32[]{:S(2)}, u32[]{:S(2)}) %collective-permute-start.2) | collective-permute-done | bytes 262176 | tf_op jit(solution)/shard_map/ppermute | solution.py:366
  37.3 0.1 collective-permute-start.12
  37.3 0.4 first_sums.1
  37.8 0.6 collective-permute-start.7
  38.3 1.1 %collective-permute-done.7 = f32[8,128]{1,0:T(8,128)S(1)} collective-permute-done((f32[8,128]{1,0:T(8,128)S(1)}, f32[8,128]{1,0:T(8,128)S(1)}, u32[]{:S(2)}, u32[]{:S(2)}) %collective-permute-start.7) | collective-permute-done | bytes 4128 | tf_op jit(solution)/shard_map/ppermute | solution.py:377
  39.4 0.8 %collective-permute-start.8 = (f32[8,128]{1,0:T(8,128)S(1)}, f32[8,128]{1,0:T(8,128)S(1)}, u32[]{:S(2)}, u32[]{:S(2)}) collective-permute-start(f32[8,128]{1,0:T(8,128)S(1)} %add.18), channel_id=1, source_target_pairs={{0,2},{2,0},{4,6},{6,4},{1,3},{3,1},{5,7},{7,5},{8,10},{10,8},{12,... | collective-permute-start | bytes 12296 | tf_op jit(solution)/shard_map/ppermute | solution.py:380
  40.2 2.9 %collective-permute-done.8 = f32[8,128]{1,0:T(8,128)S(1)} collective-permute-done((f32[8,128]{1,0:T(8,128)S(1)}, f32[8,128]{1,0:T(8,128)S(1)}, u32[]{:S(2)}, u32[]{:S(2)}) %collective-permute-start.8) | collective-permute-done | bytes 4128 | tf_op jit(solution)/shard_map/ppermute | solution.py:380
  43.0 1.5 %collective-permute-start.9 = (f32[8,128]{1,0:T(8,128)S(1)}, f32[8,128]{1,0:T(8,128)S(1)}, u32[]{:S(2)}, u32[]{:S(2)}) collective-permute-start(f32[8,128]{1,0:T(8,128)S(1)} %add.19), channel_id=1, source_target_pairs={{0,4},{2,6},{4,0},{6,2},{1,5},{3,7},{5,1},{7,3},{8,12},{10,14},{12... | collective-permute-start | bytes 12296 | tf_op jit(solution)/shard_map/ppermute | solution.py:380
  44.5 3.0 %collective-permute-done.9 = f32[8,128]{1,0:T(8,128)S(1)} collective-permute-done((f32[8,128]{1,0:T(8,128)S(1)}, f32[8,128]{1,0:T(8,128)S(1)}, u32[]{:S(2)}, u32[]{:S(2)}) %collective-permute-start.9) | collective-permute-done | bytes 4128 | tf_op jit(solution)/shard_map/ppermute | solution.py:380
  47.5 1.5 %collective-permute-start.10 = (f32[8,128]{1,0:T(8,128)S(1)}, f32[8,128]{1,0:T(8,128)S(1)}, u32[]{:S(2)}, u32[]{:S(2)}) collective-permute-start(f32[8,128]{1,0:T(8,128)S(1)} %add.20.sums), channel_id=1, source_target_pairs={{0,8},{8,0},{1,9},{9,1},{2,10},{10,2},{3,11},{11,3},{4,12},{12,4},... | collective-permute-start | bytes 12296 | tf_op jit(solution)/shard_map/ppermute | solution.py:452
  49.0 0.0 collective-permute-done.12.sides
  49.0 2.6 %other_step.1 = (f32[16,64,256]{2,1,0:T(8,128)S(1)}, f32[20,80,256]{2,1,0:T(8,128)S(1)}) custom-call(f32[8,64,256]{2,1,0:T(8,128)S(1)} %collective-permute-done.edges, f32[8,64,256]{2,1,0:T(8,128)S(1)} %collective-permute-done.3.middle, f32[16,64,256]{2,1,0:T(8,128)S(1)} %get-tuple-element.29.end, f32[4,64,256]{2,1,0:T(8,128)S(1)} %collective-permute-done.1.low, ...), custom_call_target="tpu_custom_call" | custom-call | tf_op jit(solution)/shard_map/other_step/pallas_call | solution.py:444
  51.7 2.7 %second_step.1 = (f32[16,64,256]{2,1,0:T(8,128)S(1)}, f32[16,64,256]{2,1,0:T(8,128)S(1)}, f32[16,64,256]{2,1,0:T(8,128)S(1)}) custom-call(f32[8,128]{1,0:T(8,128)S(1)} %add.20.sums, f32[20,80,256]{2,1,0:T(8,128)S(1)} %get-tuple-element.33.step, f32[20,80,256]{2,1,0:T(8,128)S(1)} %get-tuple-element.34.tangent_wide, f32[16,64,256]{2,1,0:T(8,128)S(1)} %get-tuple-element.29.end), custom_call_target="tpu_custom_call" | custom-call | tf_op jit(solution)/shard_map/second_step/pallas_call | solution.py:448
  54.3 0.0 collective-permute-done.10.o_sums
  54.3 0.0 collective-permute-done.11.far
  54.3 0.0 copy-start
  54.4 1.8 %second_sums.1 = f32[8,128]{1,0:T(8,128)S(1)} custom-call(f32[8,128]{1,0:T(8,128)S(1)} %collective-permute-done.10.o_sums, f32[16,64,256]{2,1,0:T(8,128)S(1)} %collective-permute-done.11.far, f32[16,64,256]{2,1,0:T(8,128)S(1)} %get-tuple-element.24.mine, f32[16,64,256]{2,1,0:T(8,128)S(1)} %get-tuple-element.32.near, ...), custom_call_target="tpu_custom_call" | custom-call | tf_op jit(solution)/shard_map/second_sums/pallas_call | solution.py:453
  56.2 0.1 collective-permute-start.13
  56.3 1.2 %collective-permute-done.13 = f32[8,128]{1,0:T(8,128)S(1)} collective-permute-done((f32[8,128]{1,0:T(8,128)S(1)}, f32[8,128]{1,0:T(8,128)S(1)}, u32[]{:S(2)}, u32[]{:S(2)}) %collective-permute-start.13) | collective-permute-done | bytes 4128 | tf_op jit(solution)/shard_map/ppermute | solution.py:377
  57.4 0.8 %collective-permute-start.14 = (f32[8,128]{1,0:T(8,128)S(1)}, f32[8,128]{1,0:T(8,128)S(1)}, u32[]{:S(2)}, u32[]{:S(2)}) collective-permute-start(f32[8,128]{1,0:T(8,128)S(1)} %add.21), channel_id=1, source_target_pairs={{0,2},{2,0},{4,6},{6,4},{1,3},{3,1},{5,7},{7,5},{8,10},{10,8},{12,... | collective-permute-start | bytes 12296 | tf_op jit(solution)/shard_map/ppermute | solution.py:380
  58.2 2.9 %collective-permute-done.14 = f32[8,128]{1,0:T(8,128)S(1)} collective-permute-done((f32[8,128]{1,0:T(8,128)S(1)}, f32[8,128]{1,0:T(8,128)S(1)}, u32[]{:S(2)}, u32[]{:S(2)}) %collective-permute-start.14) | collective-permute-done | bytes 4128 | tf_op jit(solution)/shard_map/ppermute | solution.py:380
  61.0 1.5 %collective-permute-start.15 = (f32[8,128]{1,0:T(8,128)S(1)}, f32[8,128]{1,0:T(8,128)S(1)}, u32[]{:S(2)}, u32[]{:S(2)}) collective-permute-start(f32[8,128]{1,0:T(8,128)S(1)} %add.22), channel_id=1, source_target_pairs={{0,4},{2,6},{4,0},{6,2},{1,5},{3,7},{5,1},{7,3},{8,12},{10,14},{12... | collective-permute-start | bytes 12296 | tf_op jit(solution)/shard_map/ppermute | solution.py:380
  62.5 0.0 copy-done
  62.5 1.3 %base.1 = f32[2,16,64,256]{3,2,1,0:T(8,128)} custom-call(f32[2,16,64,256]{3,2,1,0:T(8,128)S(1)} %copy-done), custom_call_target="tpu_custom_call" | custom-call | tf_op jit(solution)/shard_map/base/pallas_call | solution.py:434
  63.8 1.7 %collective-permute-done.15 = f32[8,128]{1,0:T(8,128)S(1)} collective-permute-done((f32[8,128]{1,0:T(8,128)S(1)}, f32[8,128]{1,0:T(8,128)S(1)}, u32[]{:S(2)}, u32[]{:S(2)}) %collective-permute-start.15) | collective-permute-done | bytes 4128 | tf_op jit(solution)/shard_map/ppermute | solution.py:380
  65.5 1.7 %last.1 = (f32[2,16,64,256]{3,2,1,0:T(8,128)}, f32[2]{0:T(128)}) custom-call(f32[8,128]{1,0:T(8,128)S(1)} %add.23.sums, f32[8,128]{1,0:T(8,128)S(1)} %collective-permute-done.10.o_sums, f32[16,64,256]{2,1,0:T(8,128)S(1)} %collective-permute-done.11.far, f32[16,64,256]{2,1,0:T(8,128)S(1)} %get-tuple-element.24.mine, ...), custom_call_target="tpu_custom_call", output_to_operand_aliasing={{0}: (6, {})} | custom-call | tf_op jit(solution)/shard_map/last/pallas_call | solution.py:457
  (26 shorter events, 0.3 us)
Async XLA Ops:
  1.9 19.9 %collective-permute-start = (f32[8,64,256]{2,1,0:T(8,128)S(1)}, f32[8,64,256]{2,1,0:T(8,128)S(1)}, u32[]{:S(2)}, u32[]{:S(2)}) collective-permute-start(f32[8,64,256]{2,1,0:T(8,128)S(1)} %get-tuple-element.20), channel_id=1, source_target_pairs={{0,8},{8,0},{1,9},{9,1},{2,10},{10,2},{3,11},{11,3},{4,12},{12,4},... | collective-permute-start | bytes 1572872 | tf_op jit(solution)/shard_map/ppermute | solution.py:414
  4.9 25.6 %collective-permute-start.3 = (f32[8,64,256]{2,1,0:T(8,128)S(1)}, f32[8,64,256]{2,1,0:T(8,128)S(1)}, u32[]{:S(2)}, u32[]{:S(2)}) collective-permute-start(f32[8,64,256]{2,1,0:T(8,128)S(1)} %get-tuple-element.22), channel_id=1, source_target_pairs={{0,8},{8,0},{1,9},{9,1},{2,10},{10,2},{3,11},{11,3},{4,12},{12,4},... | collective-permute-start | bytes 1572872 | tf_op jit(solution)/shard_map/ppermute | solution.py:415
  6.7 11.4 %collective-permute-start.4 = (f32[4,64,256]{2,1,0:T(8,128)S(1)}, f32[4,64,256]{2,1,0:T(8,128)S(1)}, u32[]{:S(2)}, u32[]{:S(2)}) collective-permute-start(f32[4,64,256]{2,1,0:T(8,128)S(1)} %get-tuple-element.25), channel_id=1, source_target_pairs={{0,2},{2,4},{4,6},{6,0},{1,3},{3,5},{5,7},{7,1},{8,10},{10,12},{12... | collective-permute-start | bytes 786440 | tf_op jit(solution)/shard_map/ppermute | solution.py:365
  8.8 12.8 %collective-permute-start.5 = (f32[4,64,256]{2,1,0:T(8,128)S(1)}, f32[4,64,256]{2,1,0:T(8,128)S(1)}, u32[]{:S(2)}, u32[]{:S(2)}) collective-permute-start(f32[4,64,256]{2,1,0:T(8,128)S(1)} %get-tuple-element.26), channel_id=1, source_target_pairs={{2,0},{4,2},{6,4},{0,6},{3,1},{5,3},{7,5},{1,7},{10,8},{12,10},{14... | collective-permute-start | bytes 786440 | tf_op jit(solution)/shard_map/ppermute | solution.py:366
  21.7 4.1 %collective-permute-start.6 = (f32[24,16,256]{2,1,0:T(8,128)S(1)}, f32[24,16,256]{2,1,0:T(8,128)S(1)}, u32[]{:S(2)}, u32[]{:S(2)}) collective-permute-start(f32[24,16,256]{2,1,0:T(8,128)S(1)} %maximum_maximum_fusion), channel_id=1, source_target_pairs={{0,1},{1,0},{2,3},{3,2},{4,5},{5,4},{6,7},{7,6},{8,9},{9,8},{10,11... | collective-permute-start | bytes 1179656 | tf_op jit(solution)/shard_map/ppermute | solution.py:373
  21.8 11.0 %collective-permute-start.1 = (f32[4,64,256]{2,1,0:T(8,128)S(1)}, f32[4,64,256]{2,1,0:T(8,128)S(1)}, u32[]{:S(2)}, u32[]{:S(2)}) collective-permute-start(f32[4,64,256]{2,1,0:T(8,128)S(1)} %pad_maximum_fusion), channel_id=1, source_target_pairs={{0,2},{2,4},{4,6},{6,0},{1,3},{3,5},{5,7},{7,1},{8,10},{10,12},{12... | collective-permute-start | bytes 786440 | tf_op jit(solution)/shard_map/ppermute | solution.py:365
  23.0 14.1 %collective-permute-start.2 = (f32[4,64,256]{2,1,0:T(8,128)S(1)}, f32[4,64,256]{2,1,0:T(8,128)S(1)}, u32[]{:S(2)}, u32[]{:S(2)}) collective-permute-start(f32[4,64,256]{2,1,0:T(8,128)S(1)} %pad_maximum_fusion.1), channel_id=1, source_target_pairs={{2,0},{4,2},{6,4},{0,6},{3,1},{5,3},{7,5},{1,7},{10,8},{12,10},{14... | collective-permute-start | bytes 786440 | tf_op jit(solution)/shard_map/ppermute | solution.py:366
  28.9 25.5 %collective-permute-start.11 = (f32[16,64,256]{2,1,0:T(8,128)S(1)}, f32[16,64,256]{2,1,0:T(8,128)S(1)}, u32[]{:S(2)}, u32[]{:S(2)}) collective-permute-start(f32[16,64,256]{2,1,0:T(8,128)S(1)} %get-tuple-element.29.end), channel_id=1, source_target_pairs={{0,8},{8,0},{1,9},{9,1},{2,10},{10,2},{3,11},{11,3},{4,12},{12,4},... | collective-permute-start | bytes 3145736 | tf_op jit(solution)/shard_map/ppermute | solution.py:423
  37.3 11.8 %collective-permute-start.12 = (f32[40,16,256]{2,1,0:T(8,128)S(1)}, f32[40,16,256]{2,1,0:T(8,128)S(1)}, u32[]{:S(2)}, u32[]{:S(2)}) collective-permute-start(f32[40,16,256]{2,1,0:T(8,128)S(1)} %maximum_dynamic-update-slice_fusion.4), channel_id=1, source_target_pairs={{0,1},{1,0},{2,3},{3,2},{4,5},{5,4},{6,7},{7,6},{8,9},{9,8},{10,11... | collective-permute-start | bytes 1966088 | tf_op jit(solution)/shard_map/ppermute | solution.py:373
  37.8 1.6 %collective-permute-start.7 = (f32[8,128]{1,0:T(8,128)S(1)}, f32[8,128]{1,0:T(8,128)S(1)}, u32[]{:S(2)}, u32[]{:S(2)}) collective-permute-start(f32[8,128]{1,0:T(8,128)S(1)} %first_sums.1), channel_id=1, source_target_pairs={{0,1},{1,0},{2,3},{3,2},{4,5},{5,4},{6,7},{7,6},{8,9},{9,8},{10,11... | collective-permute-start | bytes 12296 | tf_op jit(solution)/shard_map/ppermute | solution.py:377
  39.4 3.6 %collective-permute-start.8 = (f32[8,128]{1,0:T(8,128)S(1)}, f32[8,128]{1,0:T(8,128)S(1)}, u32[]{:S(2)}, u32[]{:S(2)}) collective-permute-start(f32[8,128]{1,0:T(8,128)S(1)} %add.18), channel_id=1, source_target_pairs={{0,2},{2,0},{4,6},{6,4},{1,3},{3,1},{5,7},{7,5},{8,10},{10,8},{12,... | collective-permute-start | bytes 12296 | tf_op jit(solution)/shard_map/ppermute | solution.py:380
  43.0 4.5 %collective-permute-start.9 = (f32[8,128]{1,0:T(8,128)S(1)}, f32[8,128]{1,0:T(8,128)S(1)}, u32[]{:S(2)}, u32[]{:S(2)}) collective-permute-start(f32[8,128]{1,0:T(8,128)S(1)} %add.19), channel_id=1, source_target_pairs={{0,4},{2,6},{4,0},{6,2},{1,5},{3,7},{5,1},{7,3},{8,12},{10,14},{12... | collective-permute-start | bytes 12296 | tf_op jit(solution)/shard_map/ppermute | solution.py:380
  47.5 6.8 %collective-permute-start.10 = (f32[8,128]{1,0:T(8,128)S(1)}, f32[8,128]{1,0:T(8,128)S(1)}, u32[]{:S(2)}, u32[]{:S(2)}) collective-permute-start(f32[8,128]{1,0:T(8,128)S(1)} %add.20.sums), channel_id=1, source_target_pairs={{0,8},{8,0},{1,9},{9,1},{2,10},{10,2},{3,11},{11,3},{4,12},{12,4},... | collective-permute-start | bytes 12296 | tf_op jit(solution)/shard_map/ppermute | solution.py:452
  54.3 8.2 %copy-start = (f32[2,16,64,256]{3,2,1,0:T(8,128)S(1)}, f32[2,16,64,256]{3,2,1,0:T(8,128)}, u32[]{:S(2)}) copy-start(f32[2,16,64,256]{3,2,1,0:T(8,128)} %src.1) | copy-start | bytes 6291460
  56.2 1.2 %collective-permute-start.13 = (f32[8,128]{1,0:T(8,128)S(1)}, f32[8,128]{1,0:T(8,128)S(1)}, u32[]{:S(2)}, u32[]{:S(2)}) collective-permute-start(f32[8,128]{1,0:T(8,128)S(1)} %second_sums.1), channel_id=1, source_target_pairs={{0,1},{1,0},{2,3},{3,2},{4,5},{5,4},{6,7},{7,6},{8,9},{9,8},{10,11... | collective-permute-start | bytes 12296 | tf_op jit(solution)/shard_map/ppermute | solution.py:377
  57.4 3.6 %collective-permute-start.14 = (f32[8,128]{1,0:T(8,128)S(1)}, f32[8,128]{1,0:T(8,128)S(1)}, u32[]{:S(2)}, u32[]{:S(2)}) collective-permute-start(f32[8,128]{1,0:T(8,128)S(1)} %add.21), channel_id=1, source_target_pairs={{0,2},{2,0},{4,6},{6,4},{1,3},{3,1},{5,7},{7,5},{8,10},{10,8},{12,... | collective-permute-start | bytes 12296 | tf_op jit(solution)/shard_map/ppermute | solution.py:380
  61.0 4.5 %collective-permute-start.15 = (f32[8,128]{1,0:T(8,128)S(1)}, f32[8,128]{1,0:T(8,128)S(1)}, u32[]{:S(2)}, u32[]{:S(2)}) collective-permute-start(f32[8,128]{1,0:T(8,128)S(1)} %add.22), channel_id=1, source_target_pairs={{0,4},{2,6},{4,0},{6,2},{1,5},{3,7},{5,1},{7,3},{8,12},{10,14},{12... | collective-permute-start | bytes 12296 | tf_op jit(solution)/shard_map/ppermute | solution.py:380

commit v7 on v6

--- a/solution.py
+++ b/solution.py
@@ -20,7 +20,7 @@
 PAD = 8
 VMEM_ROOM = 2 * 2**20
 UNROLL = 4
-AHEAD = 4
+AHEAD = 2
 
 
 def passed_along(array, axis, by):
@@ -411,26 +411,23 @@
         out_specs=[ANY] * 4,
     )(source)
 
-    o_edges = lax.ppermute(edges, "image", SWAP)
+    o_first = lax.ppermute(edges[:AHEAD], "image", SWAP)
+    o_last = lax.ppermute(edges[AHEAD:], "image", SWAP)
     o_middle = lax.ppermute(middle, "image", SWAP)
-
+    far = lax.ppermute(end, "image", SWAP)
+
+    up, down, o_first = lax.optimization_barrier((up, down, o_first))
+    o_edges = jnp.concatenate([o_first, o_last])
     low, high = from_z(up, down)
     sides = y_sides(low, mine, high)
     step, drive = call(first_step_kernel, [outer, block], [room(nz + 8), room(nz + 6)], "first_step")(
         mine, low, high, sides
     )
-    end_later, drive = lax.optimization_barrier((end, drive))
-    far = lax.ppermute(end_later, "image", SWAP)
 
     o_low, o_high = from_z(
         jnp.concatenate([o_edges[2 * AHEAD - 2 :], end[nz - 2 :]]),
         jnp.concatenate([o_edges[:2], end[:2]]),
     )
-    o_low, o_high, o_middle = lax.optimization_barrier((o_low, o_high, o_middle))
-    o_sides = y_sides(
-        o_low[:2], o_edges[:AHEAD], o_middle, o_edges[AHEAD:], o_high[:2], o_low[2:], end, o_high[2:]
-    )
-
     base = call(
         copy_kernel,
         jax.ShapeDtypeStruct(images.shape, images.dtype),
@@ -440,7 +437,13 @@
         out_specs=ANY,
     )(images)
 
-    sums = summed(call(first_sums_kernel, table, name="first_sums")(o_edges, o_middle, mine, end, drive))
+    sums = summed(
+        call(first_sums_kernel, table, name="first_sums")(o_edges, o_middle, mine, end, drive)
+    )
+    o_low, o_high, sums = lax.optimization_barrier((o_low, o_high, sums))
+    o_sides = y_sides(
+        o_low[:2], o_edges[:AHEAD], o_middle, o_edges[AHEAD:], o_high[:2], o_low[2:], end, o_high[2:]
+    )
     near, tangent_wide = call(
         other_step_kernel, [block, outer], [room(nz + 4), room(nz + 2)], "other_step"
     )(o_edges, o_middle, end, o_low, o_high, o_sides)

time: 67.4 us -> 63.8 us (0.947)
  waiting for transfers between devices: 30 us -> 20.1 us
  starting transfers between devices: 19.5 us -> 25.6 us
    ppermute x4, starting transfers between devices: 4.47 us -> 9.77 us  [summed(): lax.ppermute(sums, 'space', [(i, i ^ stride) for i in range(count)])]
    ppermute x2, waiting for transfers between devices: 7.83 us -> 2.67 us  [from_z(): lax.ppermute(down, 'space', [((i + 1) % count, i) for i in range(count)])]
    ppermute x2, waiting for transfers between devices: 9.5 us -> 7.13 us  [from_z(): lax.ppermute(up, 'space', [(i, (i + 1) % count) for i in range(count)])]
    ppermute x4, waiting for transfers between devices: 10.4 us -> 8.2 us  [summed(): lax.ppermute(sums, 'space', [(i, i ^ stride) for i in range(count)])]
    ppermute x1, starting transfers between devices: 0.08 us -> 1.95 us  [body_pair(): o_middle = lax.ppermute(middle, 'image', SWAP)]
    ppermute x2 -> x3, starting transfers between devices: 4.56 us -> 3.23 us  [the longest x1 3 us: body_pair(): o_first = lax.ppermute(edges[:AHEAD], 'image', SWAP)]
    ppermute x2, waiting for transfers between devices: 2.24 us -> 1.1 us  [summed(): sums = sums + lax.ppermute(sums, 'yslab', SWAP)]
    ppermute x2, starting transfers between devices: 3.27 us -> 4.16 us  [from_z(): lax.ppermute(up, 'space', [(i, (i + 1) % count) for i in range(count)])]
  transfers between devices with their start and end apart: 16 -> 17, of which waited for: 10 -> 10; matrix products, arithmetic and copies ran while one was open for 0% -> 0% of each run, Pallas kernels for 18% -> 19%
where the time goes in v7:
time: 63.8 us; the launch traced here: 63.6 us
  starting transfers between devices  25.6 us (40%)
  waiting for transfers between devices  20.1 us (32%)
  Pallas kernels  16.8 us (26%)
  between operations  0.86 us (1%)
    ppermute x4, starting transfers between devices, summed(): lax.ppermute(sums, 'space', [(i, i ^ stride) for i in range(count)])  9.77 us
    ppermute x4, waiting for transfers between devices, summed(): lax.ppermute(sums, 'space', [(i, i ^ stride) for i in range(count)])  8.2 us
    ppermute x2, waiting for transfers between devices, from_z(): lax.ppermute(up, 'space', [(i, (i + 1) % count) for i in range(count)])  7.13 us
    ppermute x2, starting transfers between devices, from_z(): lax.ppermute(down, 'space', [((i + 1) % count, i) for i in range(count)])  4.39 us
    ppermute x2, starting transfers between devices, from_z(): lax.ppermute(up, 'space', [(i, (i + 1) % count) for i in range(count)])  4.16 us
    pallas_call x1, Pallas kernels, body_pair(): call(first_step_kernel, [outer, block], [room(nz + 8), room(nz + 6)], 'fi...  3.06 us
    ppermute x1, starting transfers between devices, body_pair(): o_first = lax.ppermute(edges[:AHEAD], 'image', SWAP)  3 us
    ppermute x2, waiting for transfers between devices, from_z(): lax.ppermute(down, 'space', [((i + 1) % count, i) for i in range(count)])  2.67 us
  transfers between devices with their start and end apart: 17, of which 10 were waited for; matrix products, arithmetic and copies ran while one was open for 0% of the time, Pallas kernels for 19%

profile of v7, /device:TPU:0, one launch (start us, length us, event | category | flops | bytes accessed | tf_op | source)
XLA Modules:
  0.0 63.6 jit_solution(15381258564717754745)
XLA Ops:
  0.6 1.3 %send.1 = (f32[4,64,256]{2,1,0:T(8,128)S(1)}, f32[12,64,256]{2,1,0:T(8,128)S(1)}) custom-call(f32[2,16,64,256]{3,2,1,0:T(8,128)} %src.1), custom_call_target="tpu_custom_call" | custom-call | tf_op jit(solution)/shard_map/send/pallas_call | solution.py:397
  2.0 3.0 %collective-permute-start.2 = (f32[2,64,256]{2,1,0:T(8,128)S(1)}, f32[2,64,256]{2,1,0:T(8,128)S(1)}, u32[]{:S(2)}, u32[]{:S(2)}) collective-permute-start(f32[2,64,256]{2,1,0:T(8,128)S(1)} %get-tuple-element.60), channel_id=1, source_target_pairs={{0,8},{8,0},{1,9},{9,1},{2,10},{10,2},{3,11},{11,3},{4,12},{12,4},... | collective-permute-start | bytes 393224 | tf_op jit(solution)/shard_map/ppermute | solution.py:414
  5.0 0.1 collective-permute-start
  5.1 1.9 %collective-permute-start.4 = (f32[12,64,256]{2,1,0:T(8,128)S(1)}, f32[12,64,256]{2,1,0:T(8,128)S(1)}, u32[]{:S(2)}, u32[]{:S(2)}) collective-permute-start(f32[12,64,256]{2,1,0:T(8,128)S(1)} %get-tuple-element.26), channel_id=1, source_target_pairs={{0,8},{8,0},{1,9},{9,1},{2,10},{10,2},{3,11},{11,3},{4,12},{12,4},... | collective-permute-start | bytes 2359304 | tf_op jit(solution)/shard_map/ppermute | solution.py:416
  7.0 1.7 %keep.1 = (f32[16,64,256]{2,1,0:T(8,128)S(1)}, f32[16,64,256]{2,1,0:T(8,128)S(1)}, f32[4,64,256]{2,1,0:T(8,128)S(1)}, f32[4,64,256]{2,1,0:T(8,128)S(1)}) custom-call(f32[2,16,64,256]{3,2,1,0:T(8,128)} %src.1), custom_call_target="tpu_custom_call" | custom-call | tf_op jit(solution)/shard_map/keep/pallas_call | solution.py:405
  8.8 0.1 collective-permute-start.12
  8.9 0.4 collective-permute-done.2
  9.3 2.1 %collective-permute-start.5 = (f32[4,64,256]{2,1,0:T(8,128)S(1)}, f32[4,64,256]{2,1,0:T(8,128)S(1)}, u32[]{:S(2)}, u32[]{:S(2)}) collective-permute-start(f32[4,64,256]{2,1,0:T(8,128)S(1)} %get-tuple-element.28), channel_id=1, source_target_pairs={{0,2},{2,4},{4,6},{6,0},{1,3},{3,5},{5,7},{7,1},{8,10},{10,12},{12... | collective-permute-start | bytes 786440 | tf_op jit(solution)/shard_map/ppermute | solution.py:365
  11.5 2.1 %collective-permute-start.6 = (f32[4,64,256]{2,1,0:T(8,128)S(1)}, f32[4,64,256]{2,1,0:T(8,128)S(1)}, u32[]{:S(2)}, u32[]{:S(2)}) collective-permute-start(f32[4,64,256]{2,1,0:T(8,128)S(1)} %get-tuple-element.29), channel_id=1, source_target_pairs={{2,0},{4,2},{6,4},{0,6},{3,1},{5,3},{7,5},{1,7},{10,8},{12,10},{14... | collective-permute-start | bytes 786440 | tf_op jit(solution)/shard_map/ppermute | solution.py:366
  13.6 7.1 %collective-permute-done.5.low = f32[4,64,256]{2,1,0:T(8,128)S(1)} collective-permute-done((f32[4,64,256]{2,1,0:T(8,128)S(1)}, f32[4,64,256]{2,1,0:T(8,128)S(1)}, u32[]{:S(2)}, u32[]{:S(2)}) %collective-permute-start.5) | collective-permute-done | bytes 262176 | tf_op jit(solution)/shard_map/ppermute | solution.py:365
  20.7 2.7 %collective-permute-done.6.high = f32[4,64,256]{2,1,0:T(8,128)S(1)} collective-permute-done((f32[4,64,256]{2,1,0:T(8,128)S(1)}, f32[4,64,256]{2,1,0:T(8,128)S(1)}, u32[]{:S(2)}, u32[]{:S(2)}) %collective-permute-start.6) | collective-permute-done | bytes 262176 | tf_op jit(solution)/shard_map/ppermute | solution.py:366
  23.4 0.1 collective-permute-start.7
  23.5 2.3 %collective-permute-start.3 = (f32[4,64,256]{2,1,0:T(8,128)S(1)}, f32[4,64,256]{2,1,0:T(8,128)S(1)}, u32[]{:S(2)}, u32[]{:S(2)}) collective-permute-start(f32[4,64,256]{2,1,0:T(8,128)S(1)} %pad_maximum_fusion.1), channel_id=1, source_target_pairs={{2,0},{4,2},{6,4},{0,6},{3,1},{5,3},{7,5},{1,7},{10,8},{12,10},{14... | collective-permute-start | bytes 786440 | tf_op jit(solution)/shard_map/ppermute | solution.py:366
  25.8 0.0 collective-permute-done
  25.9 0.0 collective-permute-done.7.sides
  25.9 3.1 %first_step.1 = (f32[20,80,256]{2,1,0:T(8,128)S(1)}, f32[16,64,256]{2,1,0:T(8,128)S(1)}) custom-call(f32[16,64,256]{2,1,0:T(8,128)S(1)} %get-tuple-element.27.mine, f32[4,64,256]{2,1,0:T(8,128)S(1)} %collective-permute-done.5.low, f32[4,64,256]{2,1,0:T(8,128)S(1)} %collective-permute-done.6.high, f32[24,16,256]{2,1,0:T(8,128)S(1)} %collective-permute-done.7.sides), custom_call_target="tpu_custom_call" | custom-call | tf_op jit(solution)/shard_map/first_step/pallas_call | solution.py:423
  28.9 0.0 collective-permute-done.4.middle
  29.0 0.4 first_sums.1
  29.4 0.3 collective-permute-start.8
  29.7 2.0 %collective-permute-start.1 = (f32[4,64,256]{2,1,0:T(8,128)S(1)}, f32[4,64,256]{2,1,0:T(8,128)S(1)}, u32[]{:S(2)}, u32[]{:S(2)}) collective-permute-start(f32[4,64,256]{2,1,0:T(8,128)S(1)} %pad_maximum_fusion), channel_id=1, source_target_pairs={{0,2},{2,4},{4,6},{6,0},{1,3},{3,5},{5,7},{7,1},{8,10},{10,12},{12... | collective-permute-start | bytes 786440 | tf_op jit(solution)/shard_map/ppermute | solution.py:365
  31.7 0.0 collective-permute-done.8
  31.7 1.6 %collective-permute-start.9 = (f32[8,128]{1,0:T(8,128)S(1)}, f32[8,128]{1,0:T(8,128)S(1)}, u32[]{:S(2)}, u32[]{:S(2)}) collective-permute-start(f32[8,128]{1,0:T(8,128)S(1)} %add.18), channel_id=1, source_target_pairs={{0,2},{2,0},{4,6},{6,4},{1,3},{3,1},{5,7},{7,5},{8,10},{10,8},{12,... | collective-permute-start | bytes 12296 | tf_op jit(solution)/shard_map/ppermute | solution.py:380
  33.3 4.7 %collective-permute-done.9 = f32[8,128]{1,0:T(8,128)S(1)} collective-permute-done((f32[8,128]{1,0:T(8,128)S(1)}, f32[8,128]{1,0:T(8,128)S(1)}, u32[]{:S(2)}, u32[]{:S(2)}) %collective-permute-start.9) | collective-permute-done | bytes 4128 | tf_op jit(solution)/shard_map/ppermute | solution.py:380
  38.0 3.3 %collective-permute-start.10 = (f32[8,128]{1,0:T(8,128)S(1)}, f32[8,128]{1,0:T(8,128)S(1)}, u32[]{:S(2)}, u32[]{:S(2)}) collective-permute-start(f32[8,128]{1,0:T(8,128)S(1)} %add.19), channel_id=1, source_target_pairs={{0,4},{2,6},{4,0},{6,2},{1,5},{3,7},{5,1},{7,3},{8,12},{10,14},{12... | collective-permute-start | bytes 12296 | tf_op jit(solution)/shard_map/ppermute | solution.py:380
  41.4 1.6 %collective-permute-done.10 = f32[8,128]{1,0:T(8,128)S(1)} collective-permute-done((f32[8,128]{1,0:T(8,128)S(1)}, f32[8,128]{1,0:T(8,128)S(1)}, u32[]{:S(2)}, u32[]{:S(2)}) %collective-permute-start.10) | collective-permute-done | bytes 4128 | tf_op jit(solution)/shard_map/ppermute | solution.py:380
  42.9 0.0 collective-permute-done.3.high
  42.9 0.0 collective-permute-done.1.low
  43.1 0.1 collective-permute-start.13
  43.2 1.6 %collective-permute-start.11 = (f32[8,128]{1,0:T(8,128)S(1)}, f32[8,128]{1,0:T(8,128)S(1)}, u32[]{:S(2)}, u32[]{:S(2)}) collective-permute-start(f32[8,128]{1,0:T(8,128)S(1)} %add.20.sums), channel_id=1, source_target_pairs={{0,8},{8,0},{1,9},{9,1},{2,10},{10,2},{3,11},{11,3},{4,12},{12,4},... | collective-permute-start | bytes 12296 | tf_op jit(solution)/shard_map/ppermute | solution.py:455
  44.7 0.5 collective-permute-done.13.sides
  45.3 2.7 %other_step.1 = (f32[16,64,256]{2,1,0:T(8,128)S(1)}, f32[20,80,256]{2,1,0:T(8,128)S(1)}) custom-call(f32[4,64,256]{2,1,0:T(8,128)S(1)} %constant_dynamic-update-slice_fusion.edges, f32[12,64,256]{2,1,0:T(8,128)S(1)} %collective-permute-done.4.middle, f32[16,64,256]{2,1,0:T(8,128)S(1)} %get-tuple-element.22.end, ...), custom_call_target="tpu_custom_call" | custom-call | tf_op jit(solution)/shard_map/other_step/pallas_call | solution.py:447
  47.9 2.7 %second_step.1 = (f32[16,64,256]{2,1,0:T(8,128)S(1)}, f32[16,64,256]{2,1,0:T(8,128)S(1)}, f32[16,64,256]{2,1,0:T(8,128)S(1)}) custom-call(f32[8,128]{1,0:T(8,128)S(1)} %add.20.sums, f32[20,80,256]{2,1,0:T(8,128)S(1)} %get-tuple-element.35.step, f32[20,80,256]{2,1,0:T(8,128)S(1)} %get-tuple-element.36.tangent_wide, f32[16,64,256]{2,1,0:T(8,128)S(1)} %get-tuple-element.22.end), custom_call_target="tpu_custom_call" | custom-call | tf_op jit(solution)/shard_map/second_step/pallas_call | solution.py:451
  50.6 0.1 collective-permute-done.11.o_sums
  50.7 0.0 collective-permute-done.12.far
  50.7 0.0 copy-start
  50.7 1.8 %second_sums.1 = f32[8,128]{1,0:T(8,128)S(1)} custom-call(f32[8,128]{1,0:T(8,128)S(1)} %collective-permute-done.11.o_sums, f32[16,64,256]{2,1,0:T(8,128)S(1)} %collective-permute-done.12.far, f32[16,64,256]{2,1,0:T(8,128)S(1)} %get-tuple-element.27.mine, f32[16,64,256]{2,1,0:T(8,128)S(1)} %get-tuple-element.34.near, ...), custom_call_target="tpu_custom_call" | custom-call | tf_op jit(solution)/shard_map/second_sums/pallas_call | solution.py:456
  52.6 0.1 collective-permute-start.14
  52.7 1.1 %collective-permute-done.14 = f32[8,128]{1,0:T(8,128)S(1)} collective-permute-done((f32[8,128]{1,0:T(8,128)S(1)}, f32[8,128]{1,0:T(8,128)S(1)}, u32[]{:S(2)}, u32[]{:S(2)}) %collective-permute-start.14) | collective-permute-done | bytes 4128 | tf_op jit(solution)/shard_map/ppermute | solution.py:377
  53.8 2.0 %collective-permute-start.15 = (f32[8,128]{1,0:T(8,128)S(1)}, f32[8,128]{1,0:T(8,128)S(1)}, u32[]{:S(2)}, u32[]{:S(2)}) collective-permute-start(f32[8,128]{1,0:T(8,128)S(1)} %add.21), channel_id=1, source_target_pairs={{0,2},{2,0},{4,6},{6,4},{1,3},{3,1},{5,7},{7,5},{8,10},{10,8},{12,... | collective-permute-start | bytes 12296 | tf_op jit(solution)/shard_map/ppermute | solution.py:380
  55.8 1.6 %collective-permute-done.15 = f32[8,128]{1,0:T(8,128)S(1)} collective-permute-done((f32[8,128]{1,0:T(8,128)S(1)}, f32[8,128]{1,0:T(8,128)S(1)}, u32[]{:S(2)}, u32[]{:S(2)}) %collective-permute-start.15) | collective-permute-done | bytes 4128 | tf_op jit(solution)/shard_map/ppermute | solution.py:380
  57.4 2.9 %collective-permute-start.16 = (f32[8,128]{1,0:T(8,128)S(1)}, f32[8,128]{1,0:T(8,128)S(1)}, u32[]{:S(2)}, u32[]{:S(2)}) collective-permute-start(f32[8,128]{1,0:T(8,128)S(1)} %add.22), channel_id=1, source_target_pairs={{0,4},{2,6},{4,0},{6,2},{1,5},{3,7},{5,1},{7,3},{8,12},{10,14},{12... | collective-permute-start | bytes 12296 | tf_op jit(solution)/shard_map/ppermute | solution.py:380
  60.3 0.0 copy-done
  60.3 1.3 %base.1 = f32[2,16,64,256]{3,2,1,0:T(8,128)} custom-call(f32[2,16,64,256]{3,2,1,0:T(8,128)S(1)} %copy-done), custom_call_target="tpu_custom_call" | custom-call | tf_op jit(solution)/shard_map/base/pallas_call | solution.py:431
  61.6 0.3 collective-permute-done.16
  61.9 1.7 %last.1 = (f32[2,16,64,256]{3,2,1,0:T(8,128)}, f32[2]{0:T(128)}) custom-call(f32[8,128]{1,0:T(8,128)S(1)} %add.23.sums, f32[8,128]{1,0:T(8,128)S(1)} %collective-permute-done.11.o_sums, f32[16,64,256]{2,1,0:T(8,128)S(1)} %collective-permute-done.12.far, f32[16,64,256]{2,1,0:T(8,128)S(1)} %get-tuple-element.27.mine, ...), custom_call_target="tpu_custom_call", output_to_operand_aliasing={{0}: (6, {})} | custom-call | tf_op jit(solution)/shard_map/last/pallas_call | solution.py:460
  (29 shorter events, 0.3 us)
Async XLA Ops:
  2.0 7.3 %collective-permute-start.2 = (f32[2,64,256]{2,1,0:T(8,128)S(1)}, f32[2,64,256]{2,1,0:T(8,128)S(1)}, u32[]{:S(2)}, u32[]{:S(2)}) collective-permute-start(f32[2,64,256]{2,1,0:T(8,128)S(1)} %get-tuple-element.60), channel_id=1, source_target_pairs={{0,8},{8,0},{1,9},{9,1},{2,10},{10,2},{3,11},{11,3},{4,12},{12,4},... | collective-permute-start | bytes 393224 | tf_op jit(solution)/shard_map/ppermute | solution.py:414
  5.0 20.9 %collective-permute-start = (f32[2,64,256]{2,1,0:T(8,128)S(1)}, f32[2,64,256]{2,1,0:T(8,128)S(1)}, u32[]{:S(2)}, u32[]{:S(2)}) collective-permute-start(f32[2,64,256]{2,1,0:T(8,128)S(1)} %get-tuple-element.61), channel_id=1, source_target_pairs={{0,8},{8,0},{1,9},{9,1},{2,10},{10,2},{3,11},{11,3},{4,12},{12,4},... | collective-permute-start | bytes 393224 | tf_op jit(solution)/shard_map/ppermute | solution.py:415
  5.1 23.9 %collective-permute-start.4 = (f32[12,64,256]{2,1,0:T(8,128)S(1)}, f32[12,64,256]{2,1,0:T(8,128)S(1)}, u32[]{:S(2)}, u32[]{:S(2)}) collective-permute-start(f32[12,64,256]{2,1,0:T(8,128)S(1)} %get-tuple-element.26), channel_id=1, source_target_pairs={{0,8},{8,0},{1,9},{9,1},{2,10},{10,2},{3,11},{11,3},{4,12},{12,4},... | collective-permute-start | bytes 2359304 | tf_op jit(solution)/shard_map/ppermute | solution.py:416
  8.8 41.9 %collective-permute-start.12 = (f32[16,64,256]{2,1,0:T(8,128)S(1)}, f32[16,64,256]{2,1,0:T(8,128)S(1)}, u32[]{:S(2)}, u32[]{:S(2)}) collective-permute-start(f32[16,64,256]{2,1,0:T(8,128)S(1)} %get-tuple-element.22.end), channel_id=1, source_target_pairs={{0,8},{8,0},{1,9},{9,1},{2,10},{10,2},{3,11},{11,3},{4,12},{12,4},... | collective-permute-start | bytes 3145736 | tf_op jit(solution)/shard_map/ppermute | solution.py:417
  9.3 11.4 %collective-permute-start.5 = (f32[4,64,256]{2,1,0:T(8,128)S(1)}, f32[4,64,256]{2,1,0:T(8,128)S(1)}, u32[]{:S(2)}, u32[]{:S(2)}) collective-permute-start(f32[4,64,256]{2,1,0:T(8,128)S(1)} %get-tuple-element.28), channel_id=1, source_target_pairs={{0,2},{2,4},{4,6},{6,0},{1,3},{3,5},{5,7},{7,1},{8,10},{10,12},{12... | collective-permute-start | bytes 786440 | tf_op jit(solution)/shard_map/ppermute | solution.py:365
  11.5 11.9 %collective-permute-start.6 = (f32[4,64,256]{2,1,0:T(8,128)S(1)}, f32[4,64,256]{2,1,0:T(8,128)S(1)}, u32[]{:S(2)}, u32[]{:S(2)}) collective-permute-start(f32[4,64,256]{2,1,0:T(8,128)S(1)} %get-tuple-element.29), channel_id=1, source_target_pairs={{2,0},{4,2},{6,4},{0,6},{3,1},{5,3},{7,5},{1,7},{10,8},{12,10},{14... | collective-permute-start | bytes 786440 | tf_op jit(solution)/shard_map/ppermute | solution.py:366
  23.4 2.4 %collective-permute-start.7 = (f32[24,16,256]{2,1,0:T(8,128)S(1)}, f32[24,16,256]{2,1,0:T(8,128)S(1)}, u32[]{:S(2)}, u32[]{:S(2)}) collective-permute-start(f32[24,16,256]{2,1,0:T(8,128)S(1)} %maximum_maximum_fusion), channel_id=1, source_target_pairs={{0,1},{1,0},{2,3},{3,2},{4,5},{5,4},{6,7},{7,6},{8,9},{9,8},{10,11... | collective-permute-start | bytes 1179656 | tf_op jit(solution)/shard_map/ppermute | solution.py:373
  23.5 19.4 %collective-permute-start.3 = (f32[4,64,256]{2,1,0:T(8,128)S(1)}, f32[4,64,256]{2,1,0:T(8,128)S(1)}, u32[]{:S(2)}, u32[]{:S(2)}) collective-permute-start(f32[4,64,256]{2,1,0:T(8,128)S(1)} %pad_maximum_fusion.1), channel_id=1, source_target_pairs={{2,0},{4,2},{6,4},{0,6},{3,1},{5,3},{7,5},{1,7},{10,8},{12,10},{14... | collective-permute-start | bytes 786440 | tf_op jit(solution)/shard_map/ppermute | solution.py:366
  29.4 2.3 %collective-permute-start.8 = (f32[8,128]{1,0:T(8,128)S(1)}, f32[8,128]{1,0:T(8,128)S(1)}, u32[]{:S(2)}, u32[]{:S(2)}) collective-permute-start(f32[8,128]{1,0:T(8,128)S(1)} %first_sums.1), channel_id=1, source_target_pairs={{0,1},{1,0},{2,3},{3,2},{4,5},{5,4},{6,7},{7,6},{8,9},{9,8},{10,11... | collective-permute-start | bytes 12296 | tf_op jit(solution)/shard_map/ppermute | solution.py:377
  29.7 13.3 %collective-permute-start.1 = (f32[4,64,256]{2,1,0:T(8,128)S(1)}, f32[4,64,256]{2,1,0:T(8,128)S(1)}, u32[]{:S(2)}, u32[]{:S(2)}) collective-permute-start(f32[4,64,256]{2,1,0:T(8,128)S(1)} %pad_maximum_fusion), channel_id=1, source_target_pairs={{0,2},{2,4},{4,6},{6,0},{1,3},{3,5},{5,7},{7,1},{8,10},{10,12},{12... | collective-permute-start | bytes 786440 | tf_op jit(solution)/shard_map/ppermute | solution.py:365
  31.7 6.3 %collective-permute-start.9 = (f32[8,128]{1,0:T(8,128)S(1)}, f32[8,128]{1,0:T(8,128)S(1)}, u32[]{:S(2)}, u32[]{:S(2)}) collective-permute-start(f32[8,128]{1,0:T(8,128)S(1)} %add.18), channel_id=1, source_target_pairs={{0,2},{2,0},{4,6},{6,4},{1,3},{3,1},{5,7},{7,5},{8,10},{10,8},{12,... | collective-permute-start | bytes 12296 | tf_op jit(solution)/shard_map/ppermute | solution.py:380
  38.0 4.9 %collective-permute-start.10 = (f32[8,128]{1,0:T(8,128)S(1)}, f32[8,128]{1,0:T(8,128)S(1)}, u32[]{:S(2)}, u32[]{:S(2)}) collective-permute-start(f32[8,128]{1,0:T(8,128)S(1)} %add.19), channel_id=1, source_target_pairs={{0,4},{2,6},{4,0},{6,2},{1,5},{3,7},{5,1},{7,3},{8,12},{10,14},{12... | collective-permute-start | bytes 12296 | tf_op jit(solution)/shard_map/ppermute | solution.py:380
  43.1 2.2 %collective-permute-start.13 = (f32[40,16,256]{2,1,0:T(8,128)S(1)}, f32[40,16,256]{2,1,0:T(8,128)S(1)}, u32[]{:S(2)}, u32[]{:S(2)}) collective-permute-start(f32[40,16,256]{2,1,0:T(8,128)S(1)} %maximum_dynamic-update-slice_fusion.2), channel_id=1, source_target_pairs={{0,1},{1,0},{2,3},{3,2},{4,5},{5,4},{6,7},{7,6},{8,9},{9,8},{10,11... | collective-permute-start | bytes 1966088 | tf_op jit(solution)/shard_map/ppermute | solution.py:373
  43.2 7.5 %collective-permute-start.11 = (f32[8,128]{1,0:T(8,128)S(1)}, f32[8,128]{1,0:T(8,128)S(1)}, u32[]{:S(2)}, u32[]{:S(2)}) collective-permute-start(f32[8,128]{1,0:T(8,128)S(1)} %add.20.sums), channel_id=1, source_target_pairs={{0,8},{8,0},{1,9},{9,1},{2,10},{10,2},{3,11},{11,3},{4,12},{12,4},... | collective-permute-start | bytes 12296 | tf_op jit(solution)/shard_map/ppermute | solution.py:455
  50.7 9.6 %copy-start = (f32[2,16,64,256]{3,2,1,0:T(8,128)S(1)}, f32[2,16,64,256]{3,2,1,0:T(8,128)}, u32[]{:S(2)}) copy-start(f32[2,16,64,256]{3,2,1,0:T(8,128)} %src.1) | copy-start | bytes 6291460
  52.6 1.2 %collective-permute-start.14 = (f32[8,128]{1,0:T(8,128)S(1)}, f32[8,128]{1,0:T(8,128)S(1)}, u32[]{:S(2)}, u32[]{:S(2)}) collective-permute-start(f32[8,128]{1,0:T(8,128)S(1)} %second_sums.1), channel_id=1, source_target_pairs={{0,1},{1,0},{2,3},{3,2},{4,5},{5,4},{6,7},{7,6},{8,9},{9,8},{10,11... | collective-permute-start | bytes 12296 | tf_op jit(solution)/shard_map/ppermute | solution.py:377
  53.8 3.6 %collective-permute-start.15 = (f32[8,128]{1,0:T(8,128)S(1)}, f32[8,128]{1,0:T(8,128)S(1)}, u32[]{:S(2)}, u32[]{:S(2)}) collective-permute-start(f32[8,128]{1,0:T(8,128)S(1)} %add.21), channel_id=1, source_target_pairs={{0,2},{2,0},{4,6},{6,4},{1,3},{3,1},{5,7},{7,5},{8,10},{10,8},{12,... | collective-permute-start | bytes 12296 | tf_op jit(solution)/shard_map/ppermute | solution.py:380
  57.4 4.5 %collective-permute-start.16 = (f32[8,128]{1,0:T(8,128)S(1)}, f32[8,128]{1,0:T(8,128)S(1)}, u32[]{:S(2)}, u32[]{:S(2)}) collective-permute-start(f32[8,128]{1,0:T(8,128)S(1)} %add.22), channel_id=1, source_target_pairs={{0,4},{2,6},{4,0},{6,2},{1,5},{3,7},{5,1},{7,3},{8,12},{10,14},{12... | collective-permute-start | bytes 12296 | tf_op jit(solution)/shard_map/ppermute | solution.py:380

commit v8 on v7

--- a/solution.py
+++ b/solution.py
@@ -290,8 +290,13 @@
     layer_loop(0, nz, one)
 
 
-def second_step_kernel(sums, step, tangent_wide, end, moved_out, drive_out, minus_out, field, pot):
+def second_step_kernel(
+    sums, step, tangent_wide, end, images, moved_out, drive_out, minus_out, base, field, pot, sem
+):
     nz, rows, _ = end.shape
+    still = lax.axis_index("image")
+    copy = pltpu.make_async_copy(images.at[still], base.at[still], sem)
+    copy.start()
     coef, _, _ = coefficient(sums)
 
     def move(k):
@@ -308,6 +313,7 @@
         moved_out[k] = here + STEP_SIZE * drive
 
     layer_loop(0, nz, one)
+    copy.wait()
 
 
 def second_sums_kernel(o_sums, far, mine, near, minus, drive, out):
@@ -354,12 +360,6 @@
 SWAP = [(0, 1), (1, 0)]
 
 
-def copy_kernel(src, dst, sem):
-    c = pltpu.make_async_copy(src, dst, sem)
-    c.start()
-    c.wait()
-
-
 def from_z(up, down):
     count = lax.axis_size("space")
     low = lax.ppermute(up, "space", [(i, (i + 1) % count) for i in range(count)])
@@ -428,15 +428,6 @@
         jnp.concatenate([o_edges[2 * AHEAD - 2 :], end[nz - 2 :]]),
         jnp.concatenate([o_edges[:2], end[:2]]),
     )
-    base = call(
-        copy_kernel,
-        jax.ShapeDtypeStruct(images.shape, images.dtype),
-        [DMA],
-        "base",
-        in_specs=[ANY],
-        out_specs=ANY,
-    )(images)
-
     sums = summed(
         call(first_sums_kernel, table, name="first_sums")(o_edges, o_middle, mine, end, drive)
     )
@@ -448,9 +439,15 @@
         other_step_kernel, [block, outer], [room(nz + 4), room(nz + 2)], "other_step"
     )(o_edges, o_middle, end, o_low, o_high, o_sides)
 
-    moved, drive2, minus = call(
-        second_step_kernel, [block] * 3, [room(nz + 4), room(nz + 2)], "second_step"
-    )(sums, step, tangent_wide, end)
+    whole = jax.ShapeDtypeStruct(images.shape, images.dtype)
+    moved, drive2, minus, base = call(
+        second_step_kernel,
+        [block] * 3 + [whole],
+        [room(nz + 4), room(nz + 2), DMA],
+        "second_step",
+        in_specs=[VMEM] * 4 + [ANY],
+        out_specs=[VMEM] * 3 + [ANY],
+    )(sums, step, tangent_wide, end, source)
 
     o_sums = lax.ppermute(sums, "image", SWAP)
     sums = call(second_sums_kernel, table, name="second_sums")(
@@ -459,7 +456,7 @@
 
     return call(
         functools.partial(last_kernel, cells),
-        [jax.ShapeDtypeStruct(images.shape, images.dtype), shape(2)],
+        [whole, shape(2)],
         [pltpu.VMEM(block.shape, jnp.float32), DMA((nz // 4,))],
         "last",
         in_specs=[VMEM] * 6 + [ANY],

time: 63.8 us -> 93.9 us (1.47)
  Pallas kernels: 16.8 us -> 45.6 us
  waiting for transfers between devices: 20.1 us -> 21.3 us
    pallas_call x3 -> x2, Pallas kernels: 5.69 us -> 34.6 us  [the longest x1 32.9 us: body_pair(): call(second_step_kernel, [block] * 3 + [whole], [room(nz + 4), room(nz +...]
    ppermute x4, waiting for transfers between devices: 8.2 us -> 9.51 us  [summed(): lax.ppermute(sums, 'space', [(i, i ^ stride) for i in range(count)])]
  transfers between devices with their start and end apart: 17 -> 17, of which waited for: 10 -> 9; matrix products, arithmetic and copies ran while one was open for 0% -> 0% of each run, Pallas kernels for 19% -> 43%
where the time goes in v8:
time: 93.9 us; the launch traced here: 93.7 us
  Pallas kernels  45.6 us (49%)
  starting transfers between devices  25.7 us (27%)
  waiting for transfers between devices  21.3 us (23%)
    pallas_call x1, Pallas kernels, body_pair(): call(second_step_kernel, [block] * 3 + [whole], [room(nz + 4), room(nz +...  32.9 us
    ppermute x4, starting transfers between devices, summed(): lax.ppermute(sums, 'space', [(i, i ^ stride) for i in range(count)])  9.85 us
    ppermute x4, waiting for transfers between devices, summed(): lax.ppermute(sums, 'space', [(i, i ^ stride) for i in range(count)])  9.51 us
    ppermute x2, waiting for transfers between devices, from_z(): lax.ppermute(up, 'space', [(i, (i + 1) % count) for i in range(count)])  7.13 us
    ppermute x2, starting transfers between devices, from_z(): lax.ppermute(down, 'space', [((i + 1) % count, i) for i in range(count)])  4.39 us
    ppermute x2, starting transfers between devices, from_z(): lax.ppermute(up, 'space', [(i, (i + 1) % count) for i in range(count)])  4.16 us
    pallas_call x1, Pallas kernels, body_pair(): call(first_step_kernel, [outer, block], [room(nz + 8), room(nz + 6)], 'fi...  3.06 us
    ppermute x1, starting transfers between devices, body_pair(): o_first = lax.ppermute(edges[:AHEAD], 'image', SWAP)  3 us
  transfers between devices with their start and end apart: 17, of which 9 were waited for; matrix products, arithmetic and copies ran while one was open for 0% of the time, Pallas kernels for 43%

profile of v8, /device:TPU:0, one launch (start us, length us, event | category | flops | bytes accessed | tf_op | source)
XLA Modules:
  0.0 93.7 jit_solution(1925485291944073013)
XLA Ops:
  0.6 1.3 %send.1 = (f32[4,64,256]{2,1,0:T(8,128)S(1)}, f32[12,64,256]{2,1,0:T(8,128)S(1)}) custom-call(f32[2,16,64,256]{3,2,1,0:T(8,128)} %images.5), custom_call_target="tpu_custom_call" | custom-call | tf_op jit(solution)/shard_map/send/pallas_call | solution.py:397
  2.0 3.0 %collective-permute-start.2 = (f32[2,64,256]{2,1,0:T(8,128)S(1)}, f32[2,64,256]{2,1,0:T(8,128)S(1)}, u32[]{:S(2)}, u32[]{:S(2)}) collective-permute-start(f32[2,64,256]{2,1,0:T(8,128)S(1)} %get-tuple-element.62), channel_id=1, source_target_pairs={{0,8},{8,0},{1,9},{9,1},{2,10},{10,2},{3,11},{11,3},{4,12},{12,4},... | collective-permute-start | bytes 393224 | tf_op jit(solution)/shard_map/ppermute | solution.py:414
  5.0 0.1 collective-permute-start
  5.1 1.9 %collective-permute-start.4 = (f32[12,64,256]{2,1,0:T(8,128)S(1)}, f32[12,64,256]{2,1,0:T(8,128)S(1)}, u32[]{:S(2)}, u32[]{:S(2)}) collective-permute-start(f32[12,64,256]{2,1,0:T(8,128)S(1)} %get-tuple-element.27), channel_id=1, source_target_pairs={{0,8},{8,0},{1,9},{9,1},{2,10},{10,2},{3,11},{11,3},{4,12},{12,4},... | collective-permute-start | bytes 2359304 | tf_op jit(solution)/shard_map/ppermute | solution.py:416
  7.0 1.7 %keep.1 = (f32[16,64,256]{2,1,0:T(8,128)S(1)}, f32[16,64,256]{2,1,0:T(8,128)S(1)}, f32[4,64,256]{2,1,0:T(8,128)S(1)}, f32[4,64,256]{2,1,0:T(8,128)S(1)}) custom-call(f32[2,16,64,256]{3,2,1,0:T(8,128)} %images.5), custom_call_target="tpu_custom_call" | custom-call | tf_op jit(solution)/shard_map/keep/pallas_call | solution.py:405
  8.8 0.1 collective-permute-start.12
  8.9 0.4 collective-permute-done.2
  9.3 2.1 %collective-permute-start.5 = (f32[4,64,256]{2,1,0:T(8,128)S(1)}, f32[4,64,256]{2,1,0:T(8,128)S(1)}, u32[]{:S(2)}, u32[]{:S(2)}) collective-permute-start(f32[4,64,256]{2,1,0:T(8,128)S(1)} %get-tuple-element.29), channel_id=1, source_target_pairs={{0,2},{2,4},{4,6},{6,0},{1,3},{3,5},{5,7},{7,1},{8,10},{10,12},{12... | collective-permute-start | bytes 786440 | tf_op jit(solution)/shard_map/ppermute | solution.py:365
  11.5 2.1 %collective-permute-start.6 = (f32[4,64,256]{2,1,0:T(8,128)S(1)}, f32[4,64,256]{2,1,0:T(8,128)S(1)}, u32[]{:S(2)}, u32[]{:S(2)}) collective-permute-start(f32[4,64,256]{2,1,0:T(8,128)S(1)} %get-tuple-element.30), channel_id=1, source_target_pairs={{2,0},{4,2},{6,4},{0,6},{3,1},{5,3},{7,5},{1,7},{10,8},{12,10},{14... | collective-permute-start | bytes 786440 | tf_op jit(solution)/shard_map/ppermute | solution.py:366
  13.6 7.1 %collective-permute-done.5.low = f32[4,64,256]{2,1,0:T(8,128)S(1)} collective-permute-done((f32[4,64,256]{2,1,0:T(8,128)S(1)}, f32[4,64,256]{2,1,0:T(8,128)S(1)}, u32[]{:S(2)}, u32[]{:S(2)}) %collective-permute-start.5) | collective-permute-done | bytes 262176 | tf_op jit(solution)/shard_map/ppermute | solution.py:365
  20.7 2.7 %collective-permute-done.6.high = f32[4,64,256]{2,1,0:T(8,128)S(1)} collective-permute-done((f32[4,64,256]{2,1,0:T(8,128)S(1)}, f32[4,64,256]{2,1,0:T(8,128)S(1)}, u32[]{:S(2)}, u32[]{:S(2)}) %collective-permute-start.6) | collective-permute-done | bytes 262176 | tf_op jit(solution)/shard_map/ppermute | solution.py:366
  23.4 0.1 collective-permute-start.7
  23.5 2.3 %collective-permute-start.3 = (f32[4,64,256]{2,1,0:T(8,128)S(1)}, f32[4,64,256]{2,1,0:T(8,128)S(1)}, u32[]{:S(2)}, u32[]{:S(2)}) collective-permute-start(f32[4,64,256]{2,1,0:T(8,128)S(1)} %pad_maximum_fusion.1), channel_id=1, source_target_pairs={{2,0},{4,2},{6,4},{0,6},{3,1},{5,3},{7,5},{1,7},{10,8},{12,10},{14... | collective-permute-start | bytes 786440 | tf_op jit(solution)/shard_map/ppermute | solution.py:366
  25.8 0.0 collective-permute-done
  25.9 0.0 collective-permute-done.7.sides
  25.9 3.1 %first_step.1 = (f32[20,80,256]{2,1,0:T(8,128)S(1)}, f32[16,64,256]{2,1,0:T(8,128)S(1)}) custom-call(f32[16,64,256]{2,1,0:T(8,128)S(1)} %get-tuple-element.28.mine, f32[4,64,256]{2,1,0:T(8,128)S(1)} %collective-permute-done.5.low, f32[4,64,256]{2,1,0:T(8,128)S(1)} %collective-permute-done.6.high, f32[24,16,256]{2,1,0:T(8,128)S(1)} %collective-permute-done.7.sides), custom_call_target="tpu_custom_call" | custom-call | tf_op jit(solution)/shard_map/first_step/pallas_call | solution.py:423
  28.9 0.0 collective-permute-done.4.middle
  29.0 0.5 first_sums.1
  29.4 0.3 collective-permute-start.8
  29.7 2.0 %collective-permute-start.1 = (f32[4,64,256]{2,1,0:T(8,128)S(1)}, f32[4,64,256]{2,1,0:T(8,128)S(1)}, u32[]{:S(2)}, u32[]{:S(2)}) collective-permute-start(f32[4,64,256]{2,1,0:T(8,128)S(1)} %pad_maximum_fusion), channel_id=1, source_target_pairs={{0,2},{2,4},{4,6},{6,0},{1,3},{3,5},{5,7},{7,1},{8,10},{10,12},{12... | collective-permute-start | bytes 786440 | tf_op jit(solution)/shard_map/ppermute | solution.py:365
  31.7 0.0 collective-permute-done.8
  31.7 1.6 %collective-permute-start.9 = (f32[8,128]{1,0:T(8,128)S(1)}, f32[8,128]{1,0:T(8,128)S(1)}, u32[]{:S(2)}, u32[]{:S(2)}) collective-permute-start(f32[8,128]{1,0:T(8,128)S(1)} %add.18), channel_id=1, source_target_pairs={{0,2},{2,0},{4,6},{6,4},{1,3},{3,1},{5,7},{7,5},{8,10},{10,8},{12,... | collective-permute-start | bytes 12296 | tf_op jit(solution)/shard_map/ppermute | solution.py:380
  33.3 4.7 %collective-permute-done.9 = f32[8,128]{1,0:T(8,128)S(1)} collective-permute-done((f32[8,128]{1,0:T(8,128)S(1)}, f32[8,128]{1,0:T(8,128)S(1)}, u32[]{:S(2)}, u32[]{:S(2)}) %collective-permute-start.9) | collective-permute-done | bytes 4128 | tf_op jit(solution)/shard_map/ppermute | solution.py:380
  38.0 3.3 %collective-permute-start.10 = (f32[8,128]{1,0:T(8,128)S(1)}, f32[8,128]{1,0:T(8,128)S(1)}, u32[]{:S(2)}, u32[]{:S(2)}) collective-permute-start(f32[8,128]{1,0:T(8,128)S(1)} %add.19), channel_id=1, source_target_pairs={{0,4},{2,6},{4,0},{6,2},{1,5},{3,7},{5,1},{7,3},{8,12},{10,14},{12... | collective-permute-start | bytes 12296 | tf_op jit(solution)/shard_map/ppermute | solution.py:380
  41.4 1.6 %collective-permute-done.10 = f32[8,128]{1,0:T(8,128)S(1)} collective-permute-done((f32[8,128]{1,0:T(8,128)S(1)}, f32[8,128]{1,0:T(8,128)S(1)}, u32[]{:S(2)}, u32[]{:S(2)}) %collective-permute-start.10) | collective-permute-done | bytes 4128 | tf_op jit(solution)/shard_map/ppermute | solution.py:380
  43.0 0.0 collective-permute-done.3.high
  43.0 0.0 collective-permute-done.1.low
  43.1 0.1 collective-permute-start.13
  43.2 1.6 %collective-permute-start.11 = (f32[8,128]{1,0:T(8,128)S(1)}, f32[8,128]{1,0:T(8,128)S(1)}, u32[]{:S(2)}, u32[]{:S(2)}) collective-permute-start(f32[8,128]{1,0:T(8,128)S(1)} %add.20.sums), channel_id=1, source_target_pairs={{0,8},{8,0},{1,9},{9,1},{2,10},{10,2},{3,11},{11,3},{4,12},{12,4},... | collective-permute-start | bytes 12296 | tf_op jit(solution)/shard_map/ppermute | solution.py:452
  44.7 0.5 collective-permute-done.13.sides
  45.3 2.6 %other_step.1 = (f32[16,64,256]{2,1,0:T(8,128)S(1)}, f32[20,80,256]{2,1,0:T(8,128)S(1)}) custom-call(f32[4,64,256]{2,1,0:T(8,128)S(1)} %constant_dynamic-update-slice_fusion.edges, f32[12,64,256]{2,1,0:T(8,128)S(1)} %collective-permute-done.4.middle, f32[16,64,256]{2,1,0:T(8,128)S(1)} %get-tuple-element.23.end, ...), custom_call_target="tpu_custom_call" | custom-call | tf_op jit(solution)/shard_map/other_step/pallas_call | solution.py:438
  47.9 32.9 %second_step.1 = (f32[16,64,256]{2,1,0:T(8,128)S(1)}, f32[16,64,256]{2,1,0:T(8,128)S(1)}, f32[16,64,256]{2,1,0:T(8,128)S(1)}, f32[2,16,64,256]{3,2,1,0:T(8,128)}) custom-call(f32[8,128]{1,0:T(8,128)S(1)} %add.20.sums, f32[20,80,256]{2,1,0:T(8,128)S(1)} %get-tuple-element.36.step, f32[20,80,256]{2,1,0:T(8,128)S(1)} %get-tuple-element.37.tangent_wide, ...), custom_call_target="tpu_custom_call" | custom-call | tf_op jit(solution)/shard_map/second_step/pallas_call | solution.py:443
  80.8 0.0 collective-permute-done.11.o_sums
  80.8 0.0 collective-permute-done.12.far
  80.8 1.8 %second_sums.1 = f32[8,128]{1,0:T(8,128)S(1)} custom-call(f32[8,128]{1,0:T(8,128)S(1)} %collective-permute-done.11.o_sums, f32[16,64,256]{2,1,0:T(8,128)S(1)} %collective-permute-done.12.far, f32[16,64,256]{2,1,0:T(8,128)S(1)} %get-tuple-element.28.mine, f32[16,64,256]{2,1,0:T(8,128)S(1)} %get-tuple-element.35.near, ...), custom_call_target="tpu_custom_call" | custom-call | tf_op jit(solution)/shard_map/second_sums/pallas_call | solution.py:453
  82.6 0.2 collective-permute-start.14
  82.8 1.0 %collective-permute-done.14 = f32[8,128]{1,0:T(8,128)S(1)} collective-permute-done((f32[8,128]{1,0:T(8,128)S(1)}, f32[8,128]{1,0:T(8,128)S(1)}, u32[]{:S(2)}, u32[]{:S(2)}) %collective-permute-start.14) | collective-permute-done | bytes 4128 | tf_op jit(solution)/shard_map/ppermute | solution.py:377
  83.9 2.1 %collective-permute-start.15 = (f32[8,128]{1,0:T(8,128)S(1)}, f32[8,128]{1,0:T(8,128)S(1)}, u32[]{:S(2)}, u32[]{:S(2)}) collective-permute-start(f32[8,128]{1,0:T(8,128)S(1)} %add.21), channel_id=1, source_target_pairs={{0,2},{2,0},{4,6},{6,4},{1,3},{3,1},{5,7},{7,5},{8,10},{10,8},{12,... | collective-permute-start | bytes 12296 | tf_op jit(solution)/shard_map/ppermute | solution.py:380
  85.9 1.6 %collective-permute-done.15 = f32[8,128]{1,0:T(8,128)S(1)} collective-permute-done((f32[8,128]{1,0:T(8,128)S(1)}, f32[8,128]{1,0:T(8,128)S(1)}, u32[]{:S(2)}, u32[]{:S(2)}) %collective-permute-start.15) | collective-permute-done | bytes 4128 | tf_op jit(solution)/shard_map/ppermute | solution.py:380
  87.5 2.9 %collective-permute-start.16 = (f32[8,128]{1,0:T(8,128)S(1)}, f32[8,128]{1,0:T(8,128)S(1)}, u32[]{:S(2)}, u32[]{:S(2)}) collective-permute-start(f32[8,128]{1,0:T(8,128)S(1)} %add.22), channel_id=1, source_target_pairs={{0,4},{2,6},{4,0},{6,2},{1,5},{3,7},{5,1},{7,3},{8,12},{10,14},{12... | collective-permute-start | bytes 12296 | tf_op jit(solution)/shard_map/ppermute | solution.py:380
  90.4 1.6 %collective-permute-done.16 = f32[8,128]{1,0:T(8,128)S(1)} collective-permute-done((f32[8,128]{1,0:T(8,128)S(1)}, f32[8,128]{1,0:T(8,128)S(1)}, u32[]{:S(2)}, u32[]{:S(2)}) %collective-permute-start.16) | collective-permute-done | bytes 4128 | tf_op jit(solution)/shard_map/ppermute | solution.py:380
  92.0 1.7 %last.1 = (f32[2,16,64,256]{3,2,1,0:T(8,128)}, f32[2]{0:T(128)}) custom-call(f32[8,128]{1,0:T(8,128)S(1)} %add.23.sums, f32[8,128]{1,0:T(8,128)S(1)} %collective-permute-done.11.o_sums, f32[16,64,256]{2,1,0:T(8,128)S(1)} %collective-permute-done.12.far, f32[16,64,256]{2,1,0:T(8,128)S(1)} %get-tuple-element.28.mine, ...), custom_call_target="tpu_custom_call", output_to_operand_aliasing={{0}: (6, {})} | custom-call | tf_op jit(solution)/shard_map/last/pallas_call | solution.py:457
  (29 shorter events, 0.3 us)
Async XLA Ops:
  2.0 7.3 %collective-permute-start.2 = (f32[2,64,256]{2,1,0:T(8,128)S(1)}, f32[2,64,256]{2,1,0:T(8,128)S(1)}, u32[]{:S(2)}, u32[]{:S(2)}) collective-permute-start(f32[2,64,256]{2,1,0:T(8,128)S(1)} %get-tuple-element.62), channel_id=1, source_target_pairs={{0,8},{8,0},{1,9},{9,1},{2,10},{10,2},{3,11},{11,3},{4,12},{12,4},... | collective-permute-start | bytes 393224 | tf_op jit(solution)/shard_map/ppermute | solution.py:414
  5.0 20.9 %collective-permute-start = (f32[2,64,256]{2,1,0:T(8,128)S(1)}, f32[2,64,256]{2,1,0:T(8,128)S(1)}, u32[]{:S(2)}, u32[]{:S(2)}) collective-permute-start(f32[2,64,256]{2,1,0:T(8,128)S(1)} %get-tuple-element.63), channel_id=1, source_target_pairs={{0,8},{8,0},{1,9},{9,1},{2,10},{10,2},{3,11},{11,3},{4,12},{12,4},... | collective-permute-start | bytes 393224 | tf_op jit(solution)/shard_map/ppermute | solution.py:415
  5.1 23.9 %collective-permute-start.4 = (f32[12,64,256]{2,1,0:T(8,128)S(1)}, f32[12,64,256]{2,1,0:T(8,128)S(1)}, u32[]{:S(2)}, u32[]{:S(2)}) collective-permute-start(f32[12,64,256]{2,1,0:T(8,128)S(1)} %get-tuple-element.27), channel_id=1, source_target_pairs={{0,8},{8,0},{1,9},{9,1},{2,10},{10,2},{3,11},{11,3},{4,12},{12,4},... | collective-permute-start | bytes 2359304 | tf_op jit(solution)/shard_map/ppermute | solution.py:416
  8.8 72.1 %collective-permute-start.12 = (f32[16,64,256]{2,1,0:T(8,128)S(1)}, f32[16,64,256]{2,1,0:T(8,128)S(1)}, u32[]{:S(2)}, u32[]{:S(2)}) collective-permute-start(f32[16,64,256]{2,1,0:T(8,128)S(1)} %get-tuple-element.23.end), channel_id=1, source_target_pairs={{0,8},{8,0},{1,9},{9,1},{2,10},{10,2},{3,11},{11,3},{4,12},{12,4},... | collective-permute-start | bytes 3145736 | tf_op jit(solution)/shard_map/ppermute | solution.py:417
  9.3 11.4 %collective-permute-start.5 = (f32[4,64,256]{2,1,0:T(8,128)S(1)}, f32[4,64,256]{2,1,0:T(8,128)S(1)}, u32[]{:S(2)}, u32[]{:S(2)}) collective-permute-start(f32[4,64,256]{2,1,0:T(8,128)S(1)} %get-tuple-element.29), channel_id=1, source_target_pairs={{0,2},{2,4},{4,6},{6,0},{1,3},{3,5},{5,7},{7,1},{8,10},{10,12},{12... | collective-permute-start | bytes 786440 | tf_op jit(solution)/shard_map/ppermute | solution.py:365
  11.5 11.9 %collective-permute-start.6 = (f32[4,64,256]{2,1,0:T(8,128)S(1)}, f32[4,64,256]{2,1,0:T(8,128)S(1)}, u32[]{:S(2)}, u32[]{:S(2)}) collective-permute-start(f32[4,64,256]{2,1,0:T(8,128)S(1)} %get-tuple-element.30), channel_id=1, source_target_pairs={{2,0},{4,2},{6,4},{0,6},{3,1},{5,3},{7,5},{1,7},{10,8},{12,10},{14... | collective-permute-start | bytes 786440 | tf_op jit(solution)/shard_map/ppermute | solution.py:366
  23.4 2.4 %collective-permute-start.7 = (f32[24,16,256]{2,1,0:T(8,128)S(1)}, f32[24,16,256]{2,1,0:T(8,128)S(1)}, u32[]{:S(2)}, u32[]{:S(2)}) collective-permute-start(f32[24,16,256]{2,1,0:T(8,128)S(1)} %maximum_maximum_fusion), channel_id=1, source_target_pairs={{0,1},{1,0},{2,3},{3,2},{4,5},{5,4},{6,7},{7,6},{8,9},{9,8},{10,11... | collective-permute-start | bytes 1179656 | tf_op jit(solution)/shard_map/ppermute | solution.py:373
  23.5 19.4 %collective-permute-start.3 = (f32[4,64,256]{2,1,0:T(8,128)S(1)}, f32[4,64,256]{2,1,0:T(8,128)S(1)}, u32[]{:S(2)}, u32[]{:S(2)}) collective-permute-start(f32[4,64,256]{2,1,0:T(8,128)S(1)} %pad_maximum_fusion.1), channel_id=1, source_target_pairs={{2,0},{4,2},{6,4},{0,6},{3,1},{5,3},{7,5},{1,7},{10,8},{12,10},{14... | collective-permute-start | bytes 786440 | tf_op jit(solution)/shard_map/ppermute | solution.py:366
  29.4 2.3 %collective-permute-start.8 = (f32[8,128]{1,0:T(8,128)S(1)}, f32[8,128]{1,0:T(8,128)S(1)}, u32[]{:S(2)}, u32[]{:S(2)}) collective-permute-start(f32[8,128]{1,0:T(8,128)S(1)} %first_sums.1), channel_id=1, source_target_pairs={{0,1},{1,0},{2,3},{3,2},{4,5},{5,4},{6,7},{7,6},{8,9},{9,8},{10,11... | collective-permute-start | bytes 12296 | tf_op jit(solution)/shard_map/ppermute | solution.py:377
  29.7 13.3 %collective-permute-start.1 = (f32[4,64,256]{2,1,0:T(8,128)S(1)}, f32[4,64,256]{2,1,0:T(8,128)S(1)}, u32[]{:S(2)}, u32[]{:S(2)}) collective-permute-start(f32[4,64,256]{2,1,0:T(8,128)S(1)} %pad_maximum_fusion), channel_id=1, source_target_pairs={{0,2},{2,4},{4,6},{6,0},{1,3},{3,5},{5,7},{7,1},{8,10},{10,12},{12... | collective-permute-start | bytes 786440 | tf_op jit(solution)/shard_map/ppermute | solution.py:365
  31.7 6.3 %collective-permute-start.9 = (f32[8,128]{1,0:T(8,128)S(1)}, f32[8,128]{1,0:T(8,128)S(1)}, u32[]{:S(2)}, u32[]{:S(2)}) collective-permute-start(f32[8,128]{1,0:T(8,128)S(1)} %add.18), channel_id=1, source_target_pairs={{0,2},{2,0},{4,6},{6,4},{1,3},{3,1},{5,7},{7,5},{8,10},{10,8},{12,... | collective-permute-start | bytes 12296 | tf_op jit(solution)/shard_map/ppermute | solution.py:380
  38.0 4.9 %collective-permute-start.10 = (f32[8,128]{1,0:T(8,128)S(1)}, f32[8,128]{1,0:T(8,128)S(1)}, u32[]{:S(2)}, u32[]{:S(2)}) collective-permute-start(f32[8,128]{1,0:T(8,128)S(1)} %add.19), channel_id=1, source_target_pairs={{0,4},{2,6},{4,0},{6,2},{1,5},{3,7},{5,1},{7,3},{8,12},{10,14},{12... | collective-permute-start | bytes 12296 | tf_op jit(solution)/shard_map/ppermute | solution.py:380
  43.1 2.2 %collective-permute-start.13 = (f32[40,16,256]{2,1,0:T(8,128)S(1)}, f32[40,16,256]{2,1,0:T(8,128)S(1)}, u32[]{:S(2)}, u32[]{:S(2)}) collective-permute-start(f32[40,16,256]{2,1,0:T(8,128)S(1)} %maximum_dynamic-update-slice_fusion.2), channel_id=1, source_target_pairs={{0,1},{1,0},{2,3},{3,2},{4,5},{5,4},{6,7},{7,6},{8,9},{9,8},{10,11... | collective-permute-start | bytes 1966088 | tf_op jit(solution)/shard_map/ppermute | solution.py:373
  43.2 37.6 %collective-permute-start.11 = (f32[8,128]{1,0:T(8,128)S(1)}, f32[8,128]{1,0:T(8,128)S(1)}, u32[]{:S(2)}, u32[]{:S(2)}) collective-permute-start(f32[8,128]{1,0:T(8,128)S(1)} %add.20.sums), channel_id=1, source_target_pairs={{0,8},{8,0},{1,9},{9,1},{2,10},{10,2},{3,11},{11,3},{4,12},{12,4},... | collective-permute-start | bytes 12296 | tf_op jit(solution)/shard_map/ppermute | solution.py:452
  82.6 1.2 %collective-permute-start.14 = (f32[8,128]{1,0:T(8,128)S(1)}, f32[8,128]{1,0:T(8,128)S(1)}, u32[]{:S(2)}, u32[]{:S(2)}) collective-permute-start(f32[8,128]{1,0:T(8,128)S(1)} %second_sums.1), channel_id=1, source_target_pairs={{0,1},{1,0},{2,3},{3,2},{4,5},{5,4},{6,7},{7,6},{8,9},{9,8},{10,11... | collective-permute-start | bytes 12296 | tf_op jit(solution)/shard_map/ppermute | solution.py:377
  83.9 3.7 %collective-permute-start.15 = (f32[8,128]{1,0:T(8,128)S(1)}, f32[8,128]{1,0:T(8,128)S(1)}, u32[]{:S(2)}, u32[]{:S(2)}) collective-permute-start(f32[8,128]{1,0:T(8,128)S(1)} %add.21), channel_id=1, source_target_pairs={{0,2},{2,0},{4,6},{6,4},{1,3},{3,1},{5,7},{7,5},{8,10},{10,8},{12,... | collective-permute-start | bytes 12296 | tf_op jit(solution)/shard_map/ppermute | solution.py:380
  87.5 4.5 %collective-permute-start.16 = (f32[8,128]{1,0:T(8,128)S(1)}, f32[8,128]{1,0:T(8,128)S(1)}, u32[]{:S(2)}, u32[]{:S(2)}) collective-permute-start(f32[8,128]{1,0:T(8,128)S(1)} %add.22), channel_id=1, source_target_pairs={{0,4},{2,6},{4,0},{6,2},{1,5},{3,7},{5,1},{7,3},{8,12},{10,14},{12... | collective-permute-start | bytes 12296 | tf_op jit(solution)/shard_map/ppermute | solution.py:380

commit v9 on v8

--- a/solution.py
+++ b/solution.py
@@ -235,7 +235,7 @@
             totals = tuple(t + rows_sum(v) for t, v in zip(totals, terms(k, pl.ds(r, CHUNK))))
         return totals
 
-    return lax.fori_loop(start, stop, one, totals, unroll=min(UNROLL, stop - start))
+    return lax.fori_loop(start, stop, one, totals, unroll=True)
 
 
 def no_sums(count, lanes):
@@ -291,11 +291,11 @@
 
 
 def second_step_kernel(
-    sums, step, tangent_wide, end, images, moved_out, drive_out, minus_out, base, field, pot, sem
+    sums, step, tangent_wide, end, moved_out, drive_out, minus_out, base, field, pot, sem
 ):
     nz, rows, _ = end.shape
     still = lax.axis_index("image")
-    copy = pltpu.make_async_copy(images.at[still], base.at[still], sem)
+    copy = pltpu.make_async_copy(end, base.at[still], sem)
     copy.start()
     coef, _, _ = coefficient(sums)
 
@@ -445,9 +445,9 @@
         [block] * 3 + [whole],
         [room(nz + 4), room(nz + 2), DMA],
         "second_step",
-        in_specs=[VMEM] * 4 + [ANY],
+        in_specs=[VMEM] * 4,
         out_specs=[VMEM] * 3 + [ANY],
-    )(sums, step, tangent_wide, end, source)
+    )(sums, step, tangent_wide, end)
 
     o_sums = lax.ppermute(sums, "image", SWAP)
     sums = call(second_sums_kernel, table, name="second_sums")(

time: 93.9 us -> 62.6 us (0.67)
  Pallas kernels: 45.6 us -> 14.2 us
    pallas_call x1, Pallas kernels: 32.9 us -> 2.67 us  [body_pair(): call(second_step_kernel, [block] * 3 + [whole], [room(nz + 4), room(nz +...]
    pallas_call x1, Pallas kernels: 1.81 us -> 0.61 us  [body_pair(): call(second_sums_kernel, table, name='second_sums')]
  transfers between devices with their start and end apart: 17 -> 17, of which waited for: 9 -> 10; matrix products, arithmetic and copies ran while one was open for 0% -> 0% of each run, Pallas kernels for 43% -> 17%
where the time goes in v9:
time: 62.6 us; the launch traced here: 62.4 us
  starting transfers between devices  25.6 us (41%)
  waiting for transfers between devices  21.5 us (34%)
  Pallas kernels  14.2 us (23%)
  between operations  0.85 us (1%)
    ppermute x4, starting transfers between devices, summed(): lax.ppermute(sums, 'space', [(i, i ^ stride) for i in range(count)])  9.75 us
    ppermute x4, waiting for transfers between devices, summed(): lax.ppermute(sums, 'space', [(i, i ^ stride) for i in range(count)])  9.55 us
    ppermute x2, waiting for transfers between devices, from_z(): lax.ppermute(up, 'space', [(i, (i + 1) % count) for i in range(count)])  7.13 us
    ppermute x2, starting transfers between devices, from_z(): lax.ppermute(down, 'space', [((i + 1) % count, i) for i in range(count)])  4.39 us
    ppermute x2, starting transfers between devices, from_z(): lax.ppermute(up, 'space', [(i, (i + 1) % count) for i in range(count)])  4.16 us
    pallas_call x1, Pallas kernels, body_pair(): call(first_step_kernel, [outer, block], [room(nz + 8), room(nz + 6)], 'fi...  3.06 us
    ppermute x1, starting transfers between devices, body_pair(): o_first = lax.ppermute(edges[:AHEAD], 'image', SWAP)  3 us
    ppermute x2, waiting for transfers between devices, from_z(): lax.ppermute(down, 'space', [((i + 1) % count, i) for i in range(count)])  2.67 us
  transfers between devices with their start and end apart: 17, of which 10 were waited for; matrix products, arithmetic and copies ran while one was open for 0% of the time, Pallas kernels for 17%

profile of v9, /device:TPU:0, one launch (start us, length us, event | category | flops | bytes accessed | tf_op | source)
XLA Modules:
  0.0 62.4 jit_solution(2689863428498055897)
XLA Ops:
  0.6 1.3 %send.1 = (f32[4,64,256]{2,1,0:T(8,128)S(1)}, f32[12,64,256]{2,1,0:T(8,128)S(1)}) custom-call(f32[2,16,64,256]{3,2,1,0:T(8,128)} %images.3), custom_call_target="tpu_custom_call" | custom-call | tf_op jit(solution)/shard_map/send/pallas_call | solution.py:397
  2.0 3.0 %collective-permute-start.2 = (f32[2,64,256]{2,1,0:T(8,128)S(1)}, f32[2,64,256]{2,1,0:T(8,128)S(1)}, u32[]{:S(2)}, u32[]{:S(2)}) collective-permute-start(f32[2,64,256]{2,1,0:T(8,128)S(1)} %get-tuple-element.62), channel_id=1, source_target_pairs={{0,8},{8,0},{1,9},{9,1},{2,10},{10,2},{3,11},{11,3},{4,12},{12,4},... | collective-permute-start | bytes 393224 | tf_op jit(solution)/shard_map/ppermute | solution.py:414
  5.0 0.1 collective-permute-start
  5.1 1.9 %collective-permute-start.4 = (f32[12,64,256]{2,1,0:T(8,128)S(1)}, f32[12,64,256]{2,1,0:T(8,128)S(1)}, u32[]{:S(2)}, u32[]{:S(2)}) collective-permute-start(f32[12,64,256]{2,1,0:T(8,128)S(1)} %get-tuple-element.27), channel_id=1, source_target_pairs={{0,8},{8,0},{1,9},{9,1},{2,10},{10,2},{3,11},{11,3},{4,12},{12,4},... | collective-permute-start | bytes 2359304 | tf_op jit(solution)/shard_map/ppermute | solution.py:416
  7.0 1.7 %keep.1 = (f32[16,64,256]{2,1,0:T(8,128)S(1)}, f32[16,64,256]{2,1,0:T(8,128)S(1)}, f32[4,64,256]{2,1,0:T(8,128)S(1)}, f32[4,64,256]{2,1,0:T(8,128)S(1)}) custom-call(f32[2,16,64,256]{3,2,1,0:T(8,128)} %images.3), custom_call_target="tpu_custom_call" | custom-call | tf_op jit(solution)/shard_map/keep/pallas_call | solution.py:405
  8.8 0.1 collective-permute-start.12
  8.9 0.4 collective-permute-done.2
  9.3 2.1 %collective-permute-start.5 = (f32[4,64,256]{2,1,0:T(8,128)S(1)}, f32[4,64,256]{2,1,0:T(8,128)S(1)}, u32[]{:S(2)}, u32[]{:S(2)}) collective-permute-start(f32[4,64,256]{2,1,0:T(8,128)S(1)} %get-tuple-element.29), channel_id=1, source_target_pairs={{0,2},{2,4},{4,6},{6,0},{1,3},{3,5},{5,7},{7,1},{8,10},{10,12},{12... | collective-permute-start | bytes 786440 | tf_op jit(solution)/shard_map/ppermute | solution.py:365
  11.5 2.1 %collective-permute-start.6 = (f32[4,64,256]{2,1,0:T(8,128)S(1)}, f32[4,64,256]{2,1,0:T(8,128)S(1)}, u32[]{:S(2)}, u32[]{:S(2)}) collective-permute-start(f32[4,64,256]{2,1,0:T(8,128)S(1)} %get-tuple-element.30), channel_id=1, source_target_pairs={{2,0},{4,2},{6,4},{0,6},{3,1},{5,3},{7,5},{1,7},{10,8},{12,10},{14... | collective-permute-start | bytes 786440 | tf_op jit(solution)/shard_map/ppermute | solution.py:366
  13.6 7.1 %collective-permute-done.5.low = f32[4,64,256]{2,1,0:T(8,128)S(1)} collective-permute-done((f32[4,64,256]{2,1,0:T(8,128)S(1)}, f32[4,64,256]{2,1,0:T(8,128)S(1)}, u32[]{:S(2)}, u32[]{:S(2)}) %collective-permute-start.5) | collective-permute-done | bytes 262176 | tf_op jit(solution)/shard_map/ppermute | solution.py:365
  20.7 2.7 %collective-permute-done.6.high = f32[4,64,256]{2,1,0:T(8,128)S(1)} collective-permute-done((f32[4,64,256]{2,1,0:T(8,128)S(1)}, f32[4,64,256]{2,1,0:T(8,128)S(1)}, u32[]{:S(2)}, u32[]{:S(2)}) %collective-permute-start.6) | collective-permute-done | bytes 262176 | tf_op jit(solution)/shard_map/ppermute | solution.py:366
  23.4 0.1 collective-permute-start.7
  23.5 2.3 %collective-permute-start.3 = (f32[4,64,256]{2,1,0:T(8,128)S(1)}, f32[4,64,256]{2,1,0:T(8,128)S(1)}, u32[]{:S(2)}, u32[]{:S(2)}) collective-permute-start(f32[4,64,256]{2,1,0:T(8,128)S(1)} %pad_maximum_fusion.1), channel_id=1, source_target_pairs={{2,0},{4,2},{6,4},{0,6},{3,1},{5,3},{7,5},{1,7},{10,8},{12,10},{14... | collective-permute-start | bytes 786440 | tf_op jit(solution)/shard_map/ppermute | solution.py:366
  25.8 0.0 collective-permute-done
  25.9 0.0 collective-permute-done.7.sides
  25.9 3.1 %first_step.1 = (f32[20,80,256]{2,1,0:T(8,128)S(1)}, f32[16,64,256]{2,1,0:T(8,128)S(1)}) custom-call(f32[16,64,256]{2,1,0:T(8,128)S(1)} %get-tuple-element.28.mine, f32[4,64,256]{2,1,0:T(8,128)S(1)} %collective-permute-done.5.low, f32[4,64,256]{2,1,0:T(8,128)S(1)} %collective-permute-done.6.high, f32[24,16,256]{2,1,0:T(8,128)S(1)} %collective-permute-done.7.sides), custom_call_target="tpu_custom_call" | custom-call | tf_op jit(solution)/shard_map/first_step/pallas_call | solution.py:423
  28.9 0.0 collective-permute-done.4.middle
  29.0 0.4 first_sums.1
  29.4 0.3 collective-permute-start.8
  29.7 2.0 %collective-permute-start.1 = (f32[4,64,256]{2,1,0:T(8,128)S(1)}, f32[4,64,256]{2,1,0:T(8,128)S(1)}, u32[]{:S(2)}, u32[]{:S(2)}) collective-permute-start(f32[4,64,256]{2,1,0:T(8,128)S(1)} %pad_maximum_fusion), channel_id=1, source_target_pairs={{0,2},{2,4},{4,6},{6,0},{1,3},{3,5},{5,7},{7,1},{8,10},{10,12},{12... | collective-permute-start | bytes 786440 | tf_op jit(solution)/shard_map/ppermute | solution.py:365
  31.7 0.0 collective-permute-done.8
  31.7 1.6 %collective-permute-start.9 = (f32[8,128]{1,0:T(8,128)S(1)}, f32[8,128]{1,0:T(8,128)S(1)}, u32[]{:S(2)}, u32[]{:S(2)}) collective-permute-start(f32[8,128]{1,0:T(8,128)S(1)} %add.18), channel_id=1, source_target_pairs={{0,2},{2,0},{4,6},{6,4},{1,3},{3,1},{5,7},{7,5},{8,10},{10,8},{12,... | collective-permute-start | bytes 12296 | tf_op jit(solution)/shard_map/ppermute | solution.py:380
  33.3 4.7 %collective-permute-done.9 = f32[8,128]{1,0:T(8,128)S(1)} collective-permute-done((f32[8,128]{1,0:T(8,128)S(1)}, f32[8,128]{1,0:T(8,128)S(1)}, u32[]{:S(2)}, u32[]{:S(2)}) %collective-permute-start.9) | collective-permute-done | bytes 4128 | tf_op jit(solution)/shard_map/ppermute | solution.py:380
  38.0 3.3 %collective-permute-start.10 = (f32[8,128]{1,0:T(8,128)S(1)}, f32[8,128]{1,0:T(8,128)S(1)}, u32[]{:S(2)}, u32[]{:S(2)}) collective-permute-start(f32[8,128]{1,0:T(8,128)S(1)} %add.19), channel_id=1, source_target_pairs={{0,4},{2,6},{4,0},{6,2},{1,5},{3,7},{5,1},{7,3},{8,12},{10,14},{12... | collective-permute-start | bytes 12296 | tf_op jit(solution)/shard_map/ppermute | solution.py:380
  41.4 1.6 %collective-permute-done.10 = f32[8,128]{1,0:T(8,128)S(1)} collective-permute-done((f32[8,128]{1,0:T(8,128)S(1)}, f32[8,128]{1,0:T(8,128)S(1)}, u32[]{:S(2)}, u32[]{:S(2)}) %collective-permute-start.10) | collective-permute-done | bytes 4128 | tf_op jit(solution)/shard_map/ppermute | solution.py:380
  42.9 0.0 collective-permute-done.3.high
  42.9 0.0 collective-permute-done.1.low
  43.1 0.1 collective-permute-start.13
  43.2 1.6 %collective-permute-start.11 = (f32[8,128]{1,0:T(8,128)S(1)}, f32[8,128]{1,0:T(8,128)S(1)}, u32[]{:S(2)}, u32[]{:S(2)}) collective-permute-start(f32[8,128]{1,0:T(8,128)S(1)} %add.20.sums), channel_id=1, source_target_pairs={{0,8},{8,0},{1,9},{9,1},{2,10},{10,2},{3,11},{11,3},{4,12},{12,4},... | collective-permute-start | bytes 12296 | tf_op jit(solution)/shard_map/ppermute | solution.py:452
  44.7 0.5 collective-permute-done.13.sides
  45.3 2.7 %other_step.1 = (f32[16,64,256]{2,1,0:T(8,128)S(1)}, f32[20,80,256]{2,1,0:T(8,128)S(1)}) custom-call(f32[4,64,256]{2,1,0:T(8,128)S(1)} %constant_dynamic-update-slice_fusion.edges, f32[12,64,256]{2,1,0:T(8,128)S(1)} %collective-permute-done.4.middle, f32[16,64,256]{2,1,0:T(8,128)S(1)} %get-tuple-element.23.end, ...), custom_call_target="tpu_custom_call" | custom-call | tf_op jit(solution)/shard_map/other_step/pallas_call | solution.py:438
  47.9 2.7 %second_step.1 = (f32[16,64,256]{2,1,0:T(8,128)S(1)}, f32[16,64,256]{2,1,0:T(8,128)S(1)}, f32[16,64,256]{2,1,0:T(8,128)S(1)}, f32[2,16,64,256]{3,2,1,0:T(8,128)}) custom-call(f32[8,128]{1,0:T(8,128)S(1)} %add.20.sums, f32[20,80,256]{2,1,0:T(8,128)S(1)} %get-tuple-element.36.step, f32[20,80,256]{2,1,0:T(8,128)S(1)} %get-tuple-element.37.tangent_wide, ...), custom_call_target="tpu_custom_call" | custom-call | tf_op jit(solution)/shard_map/second_step/pallas_call | solution.py:443
  50.6 0.1 collective-permute-done.11.o_sums
  50.7 0.0 collective-permute-done.12.far
  50.7 0.6 second_sums.1
  51.3 0.1 collective-permute-start.14
  51.4 1.1 %collective-permute-done.14 = f32[8,128]{1,0:T(8,128)S(1)} collective-permute-done((f32[8,128]{1,0:T(8,128)S(1)}, f32[8,128]{1,0:T(8,128)S(1)}, u32[]{:S(2)}, u32[]{:S(2)}) %collective-permute-start.14) | collective-permute-done | bytes 4128 | tf_op jit(solution)/shard_map/ppermute | solution.py:377
  52.5 2.0 %collective-permute-start.15 = (f32[8,128]{1,0:T(8,128)S(1)}, f32[8,128]{1,0:T(8,128)S(1)}, u32[]{:S(2)}, u32[]{:S(2)}) collective-permute-start(f32[8,128]{1,0:T(8,128)S(1)} %add.21), channel_id=1, source_target_pairs={{0,2},{2,0},{4,6},{6,4},{1,3},{3,1},{5,7},{7,5},{8,10},{10,8},{12,... | collective-permute-start | bytes 12296 | tf_op jit(solution)/shard_map/ppermute | solution.py:380
  54.5 1.6 %collective-permute-done.15 = f32[8,128]{1,0:T(8,128)S(1)} collective-permute-done((f32[8,128]{1,0:T(8,128)S(1)}, f32[8,128]{1,0:T(8,128)S(1)}, u32[]{:S(2)}, u32[]{:S(2)}) %collective-permute-start.15) | collective-permute-done | bytes 4128 | tf_op jit(solution)/shard_map/ppermute | solution.py:380
  56.2 2.8 %collective-permute-start.16 = (f32[8,128]{1,0:T(8,128)S(1)}, f32[8,128]{1,0:T(8,128)S(1)}, u32[]{:S(2)}, u32[]{:S(2)}) collective-permute-start(f32[8,128]{1,0:T(8,128)S(1)} %add.22), channel_id=1, source_target_pairs={{0,4},{2,6},{4,0},{6,2},{1,5},{3,7},{5,1},{7,3},{8,12},{10,14},{12... | collective-permute-start | bytes 12296 | tf_op jit(solution)/shard_map/ppermute | solution.py:380
  59.0 1.7 %collective-permute-done.16 = f32[8,128]{1,0:T(8,128)S(1)} collective-permute-done((f32[8,128]{1,0:T(8,128)S(1)}, f32[8,128]{1,0:T(8,128)S(1)}, u32[]{:S(2)}, u32[]{:S(2)}) %collective-permute-start.16) | collective-permute-done | bytes 4128 | tf_op jit(solution)/shard_map/ppermute | solution.py:380
  60.7 1.7 %last.1 = (f32[2,16,64,256]{3,2,1,0:T(8,128)}, f32[2]{0:T(128)}) custom-call(f32[8,128]{1,0:T(8,128)S(1)} %add.23.sums, f32[8,128]{1,0:T(8,128)S(1)} %collective-permute-done.11.o_sums, f32[16,64,256]{2,1,0:T(8,128)S(1)} %collective-permute-done.12.far, f32[16,64,256]{2,1,0:T(8,128)S(1)} %get-tuple-element.28.mine, ...), custom_call_target="tpu_custom_call", output_to_operand_aliasing={{0}: (6, {})} | custom-call | tf_op jit(solution)/shard_map/last/pallas_call | solution.py:457
  (29 shorter events, 0.3 us)
Async XLA Ops:
  2.0 7.3 %collective-permute-start.2 = (f32[2,64,256]{2,1,0:T(8,128)S(1)}, f32[2,64,256]{2,1,0:T(8,128)S(1)}, u32[]{:S(2)}, u32[]{:S(2)}) collective-permute-start(f32[2,64,256]{2,1,0:T(8,128)S(1)} %get-tuple-element.62), channel_id=1, source_target_pairs={{0,8},{8,0},{1,9},{9,1},{2,10},{10,2},{3,11},{11,3},{4,12},{12,4},... | collective-permute-start | bytes 393224 | tf_op jit(solution)/shard_map/ppermute | solution.py:414
  5.0 20.9 %collective-permute-start = (f32[2,64,256]{2,1,0:T(8,128)S(1)}, f32[2,64,256]{2,1,0:T(8,128)S(1)}, u32[]{:S(2)}, u32[]{:S(2)}) collective-permute-start(f32[2,64,256]{2,1,0:T(8,128)S(1)} %get-tuple-element.63), channel_id=1, source_target_pairs={{0,8},{8,0},{1,9},{9,1},{2,10},{10,2},{3,11},{11,3},{4,12},{12,4},... | collective-permute-start | bytes 393224 | tf_op jit(solution)/shard_map/ppermute | solution.py:415
  5.1 23.9 %collective-permute-start.4 = (f32[12,64,256]{2,1,0:T(8,128)S(1)}, f32[12,64,256]{2,1,0:T(8,128)S(1)}, u32[]{:S(2)}, u32[]{:S(2)}) collective-permute-start(f32[12,64,256]{2,1,0:T(8,128)S(1)} %get-tuple-element.27), channel_id=1, source_target_pairs={{0,8},{8,0},{1,9},{9,1},{2,10},{10,2},{3,11},{11,3},{4,12},{12,4},... | collective-permute-start | bytes 2359304 | tf_op jit(solution)/shard_map/ppermute | solution.py:416
  8.8 41.9 %collective-permute-start.12 = (f32[16,64,256]{2,1,0:T(8,128)S(1)}, f32[16,64,256]{2,1,0:T(8,128)S(1)}, u32[]{:S(2)}, u32[]{:S(2)}) collective-permute-start(f32[16,64,256]{2,1,0:T(8,128)S(1)} %get-tuple-element.23.end), channel_id=1, source_target_pairs={{0,8},{8,0},{1,9},{9,1},{2,10},{10,2},{3,11},{11,3},{4,12},{12,4},... | collective-permute-start | bytes 3145736 | tf_op jit(solution)/shard_map/ppermute | solution.py:417
  9.3 11.4 %collective-permute-start.5 = (f32[4,64,256]{2,1,0:T(8,128)S(1)}, f32[4,64,256]{2,1,0:T(8,128)S(1)}, u32[]{:S(2)}, u32[]{:S(2)}) collective-permute-start(f32[4,64,256]{2,1,0:T(8,128)S(1)} %get-tuple-element.29), channel_id=1, source_target_pairs={{0,2},{2,4},{4,6},{6,0},{1,3},{3,5},{5,7},{7,1},{8,10},{10,12},{12... | collective-permute-start | bytes 786440 | tf_op jit(solution)/shard_map/ppermute | solution.py:365
  11.5 11.9 %collective-permute-start.6 = (f32[4,64,256]{2,1,0:T(8,128)S(1)}, f32[4,64,256]{2,1,0:T(8,128)S(1)}, u32[]{:S(2)}, u32[]{:S(2)}) collective-permute-start(f32[4,64,256]{2,1,0:T(8,128)S(1)} %get-tuple-element.30), channel_id=1, source_target_pairs={{2,0},{4,2},{6,4},{0,6},{3,1},{5,3},{7,5},{1,7},{10,8},{12,10},{14... | collective-permute-start | bytes 786440 | tf_op jit(solution)/shard_map/ppermute | solution.py:366
  23.4 2.4 %collective-permute-start.7 = (f32[24,16,256]{2,1,0:T(8,128)S(1)}, f32[24,16,256]{2,1,0:T(8,128)S(1)}, u32[]{:S(2)}, u32[]{:S(2)}) collective-permute-start(f32[24,16,256]{2,1,0:T(8,128)S(1)} %maximum_maximum_fusion), channel_id=1, source_target_pairs={{0,1},{1,0},{2,3},{3,2},{4,5},{5,4},{6,7},{7,6},{8,9},{9,8},{10,11... | collective-permute-start | bytes 1179656 | tf_op jit(solution)/shard_map/ppermute | solution.py:373
  23.5 19.4 %collective-permute-start.3 = (f32[4,64,256]{2,1,0:T(8,128)S(1)}, f32[4,64,256]{2,1,0:T(8,128)S(1)}, u32[]{:S(2)}, u32[]{:S(2)}) collective-permute-start(f32[4,64,256]{2,1,0:T(8,128)S(1)} %pad_maximum_fusion.1), channel_id=1, source_target_pairs={{2,0},{4,2},{6,4},{0,6},{3,1},{5,3},{7,5},{1,7},{10,8},{12,10},{14... | collective-permute-start | bytes 786440 | tf_op jit(solution)/shard_map/ppermute | solution.py:366
  29.4 2.3 %collective-permute-start.8 = (f32[8,128]{1,0:T(8,128)S(1)}, f32[8,128]{1,0:T(8,128)S(1)}, u32[]{:S(2)}, u32[]{:S(2)}) collective-permute-start(f32[8,128]{1,0:T(8,128)S(1)} %first_sums.1), channel_id=1, source_target_pairs={{0,1},{1,0},{2,3},{3,2},{4,5},{5,4},{6,7},{7,6},{8,9},{9,8},{10,11... | collective-permute-start | bytes 12296 | tf_op jit(solution)/shard_map/ppermute | solution.py:377
  29.7 13.3 %collective-permute-start.1 = (f32[4,64,256]{2,1,0:T(8,128)S(1)}, f32[4,64,256]{2,1,0:T(8,128)S(1)}, u32[]{:S(2)}, u32[]{:S(2)}) collective-permute-start(f32[4,64,256]{2,1,0:T(8,128)S(1)} %pad_maximum_fusion), channel_id=1, source_target_pairs={{0,2},{2,4},{4,6},{6,0},{1,3},{3,5},{5,7},{7,1},{8,10},{10,12},{12... | collective-permute-start | bytes 786440 | tf_op jit(solution)/shard_map/ppermute | solution.py:365
  31.7 6.3 %collective-permute-start.9 = (f32[8,128]{1,0:T(8,128)S(1)}, f32[8,128]{1,0:T(8,128)S(1)}, u32[]{:S(2)}, u32[]{:S(2)}) collective-permute-start(f32[8,128]{1,0:T(8,128)S(1)} %add.18), channel_id=1, source_target_pairs={{0,2},{2,0},{4,6},{6,4},{1,3},{3,1},{5,7},{7,5},{8,10},{10,8},{12,... | collective-permute-start | bytes 12296 | tf_op jit(solution)/shard_map/ppermute | solution.py:380
  38.0 4.9 %collective-permute-start.10 = (f32[8,128]{1,0:T(8,128)S(1)}, f32[8,128]{1,0:T(8,128)S(1)}, u32[]{:S(2)}, u32[]{:S(2)}) collective-permute-start(f32[8,128]{1,0:T(8,128)S(1)} %add.19), channel_id=1, source_target_pairs={{0,4},{2,6},{4,0},{6,2},{1,5},{3,7},{5,1},{7,3},{8,12},{10,14},{12... | collective-permute-start | bytes 12296 | tf_op jit(solution)/shard_map/ppermute | solution.py:380
  43.1 2.2 %collective-permute-start.13 = (f32[40,16,256]{2,1,0:T(8,128)S(1)}, f32[40,16,256]{2,1,0:T(8,128)S(1)}, u32[]{:S(2)}, u32[]{:S(2)}) collective-permute-start(f32[40,16,256]{2,1,0:T(8,128)S(1)} %maximum_dynamic-update-slice_fusion.2), channel_id=1, source_target_pairs={{0,1},{1,0},{2,3},{3,2},{4,5},{5,4},{6,7},{7,6},{8,9},{9,8},{10,11... | collective-permute-start | bytes 1966088 | tf_op jit(solution)/shard_map/ppermute | solution.py:373
  43.2 7.5 %collective-permute-start.11 = (f32[8,128]{1,0:T(8,128)S(1)}, f32[8,128]{1,0:T(8,128)S(1)}, u32[]{:S(2)}, u32[]{:S(2)}) collective-permute-start(f32[8,128]{1,0:T(8,128)S(1)} %add.20.sums), channel_id=1, source_target_pairs={{0,8},{8,0},{1,9},{9,1},{2,10},{10,2},{3,11},{11,3},{4,12},{12,4},... | collective-permute-start | bytes 12296 | tf_op jit(solution)/shard_map/ppermute | solution.py:452
  51.3 1.2 %collective-permute-start.14 = (f32[8,128]{1,0:T(8,128)S(1)}, f32[8,128]{1,0:T(8,128)S(1)}, u32[]{:S(2)}, u32[]{:S(2)}) collective-permute-start(f32[8,128]{1,0:T(8,128)S(1)} %second_sums.1), channel_id=1, source_target_pairs={{0,1},{1,0},{2,3},{3,2},{4,5},{5,4},{6,7},{7,6},{8,9},{9,8},{10,11... | collective-permute-start | bytes 12296 | tf_op jit(solution)/shard_map/ppermute | solution.py:377
  52.5 3.6 %collective-permute-start.15 = (f32[8,128]{1,0:T(8,128)S(1)}, f32[8,128]{1,0:T(8,128)S(1)}, u32[]{:S(2)}, u32[]{:S(2)}) collective-permute-start(f32[8,128]{1,0:T(8,128)S(1)} %add.21), channel_id=1, source_target_pairs={{0,2},{2,0},{4,6},{6,4},{1,3},{3,1},{5,7},{7,5},{8,10},{10,8},{12,... | collective-permute-start | bytes 12296 | tf_op jit(solution)/shard_map/ppermute | solution.py:380
  56.2 4.5 %collective-permute-start.16 = (f32[8,128]{1,0:T(8,128)S(1)}, f32[8,128]{1,0:T(8,128)S(1)}, u32[]{:S(2)}, u32[]{:S(2)}) collective-permute-start(f32[8,128]{1,0:T(8,128)S(1)} %add.22), channel_id=1, source_target_pairs={{0,4},{2,6},{4,0},{6,2},{1,5},{3,7},{5,1},{7,3},{8,12},{10,14},{12... | collective-permute-start | bytes 12296 | tf_op jit(solution)/shard_map/ppermute | solution.py:380

commit v10 on v9

--- a/solution.py
+++ b/solution.py
@@ -373,12 +373,18 @@
     return lax.ppermute(jnp.concatenate(ends, 0), "yslab", SWAP)
 
 
-def summed(sums):
-    sums = sums + lax.ppermute(sums, "yslab", SWAP)
+def sum_steps():
     count, stride = lax.axis_size("space"), 1
+    steps = [("yslab", SWAP)]
     while stride < count:
-        sums = sums + lax.ppermute(sums, "space", [(i, i ^ stride) for i in range(count)])
+        steps.append(("space", [(i, i ^ stride) for i in range(count)]))
         stride *= 2
+    return steps
+
+
+def summed(sums, steps):
+    for axis, pairs in steps:
+        sums = sums + lax.ppermute(sums, axis, pairs)
     return sums
 
 
@@ -428,13 +434,14 @@
         jnp.concatenate([o_edges[2 * AHEAD - 2 :], end[nz - 2 :]]),
         jnp.concatenate([o_edges[:2], end[:2]]),
     )
-    sums = summed(
-        call(first_sums_kernel, table, name="first_sums")(o_edges, o_middle, mine, end, drive)
-    )
+    sums = call(first_sums_kernel, table, name="first_sums")(o_edges, o_middle, mine, end, drive)
+    steps = sum_steps()
+    sums = summed(sums, steps[:2])
     o_low, o_high, sums = lax.optimization_barrier((o_low, o_high, sums))
     o_sides = y_sides(
         o_low[:2], o_edges[:AHEAD], o_middle, o_edges[AHEAD:], o_high[:2], o_low[2:], end, o_high[2:]
     )
+    sums = summed(sums, steps[2:])
     near, tangent_wide = call(
         other_step_kernel, [block, outer], [room(nz + 4), room(nz + 2)], "other_step"
     )(o_edges, o_middle, end, o_low, o_high, o_sides)
@@ -462,7 +469,7 @@
         in_specs=[VMEM] * 6 + [ANY],
         out_specs=[ANY, SMEM],
         input_output_aliases={6: 0},
-    )(summed(sums), o_sums, far, mine, near, moved, base)
+    )(summed(sums, sum_steps()), o_sums, far, mine, near, moved, base)
 
 
 def body(images):

time: 62.6 us -> 62.8 us (level)
  waiting for transfers between devices: 21.5 us -> 23.2 us
  starting transfers between devices: 25.6 us -> 24 us
    ppermute x2, starting transfers between devices: 4.39 us -> 9.8 us  [from_z(): lax.ppermute(down, 'space', [((i + 1) % count, i) for i in range(count)])]
    ppermute x6, starting transfers between devices: 10.1 us -> 5.18 us  [summed(): sums = sums + lax.ppermute(sums, axis, pairs)]
    ppermute x6, waiting for transfers between devices: 10.7 us -> 13.9 us  [summed(): sums = sums + lax.ppermute(sums, axis, pairs)]
    ppermute x2, waiting for transfers between devices: 2.67 us -> 0.01 us  [from_z(): lax.ppermute(down, 'space', [((i + 1) % count, i) for i in range(count)])]
    ppermute x2, starting transfers between devices: 4.16 us -> 2.2 us  [from_z(): lax.ppermute(up, 'space', [(i, (i + 1) % count) for i in range(count)])]
    ppermute x2, waiting for transfers between devices: 0.53 us -> 1.58 us  [y_sides(): return lax.ppermute(jnp.concatenate(ends, 0), 'yslab', SWAP)]
where the time goes in v10:
time: 62.8 us; the launch traced here: 62.6 us
  starting transfers between devices  24 us (38%)
  waiting for transfers between devices  23.2 us (37%)
  Pallas kernels  14.2 us (23%)
  between operations  0.9 us (1%)
    ppermute x6, waiting for transfers between devices, summed(): sums = sums + lax.ppermute(sums, axis, pairs)  13.9 us
    ppermute x2, starting transfers between devices, from_z(): lax.ppermute(down, 'space', [((i + 1) % count, i) for i in range(count)])  9.8 us
    ppermute x2, waiting for transfers between devices, from_z(): lax.ppermute(up, 'space', [(i, (i + 1) % count) for i in range(count)])  7.37 us
    ppermute x6, starting transfers between devices, summed(): sums = sums + lax.ppermute(sums, axis, pairs)  5.18 us
    pallas_call x1, Pallas kernels, body_pair(): call(first_step_kernel, [outer, block], [room(nz + 8), room(nz + 6)], 'fi...  3.06 us
    ppermute x1, starting transfers between devices, body_pair(): o_first = lax.ppermute(edges[:AHEAD], 'image', SWAP)  3 us
    pallas_call x1, Pallas kernels, body_pair(): call(other_step_kernel, [block, outer], [room(nz + 4), room(nz + 2)], 'ot...  2.67 us
    pallas_call x1, Pallas kernels, body_pair(): call(second_step_kernel, [block] * 3 + [whole], [room(nz + 4), room(nz +...  2.67 us
  transfers between devices with their start and end apart: 17, of which 10 were waited for; matrix products, arithmetic and copies ran while one was open for 0% of the time, Pallas kernels for 17%

profile of v10, /device:TPU:0, one launch (start us, length us, event | category | flops | bytes accessed | tf_op | source)
XLA Modules:
  0.0 62.6 jit_solution(16642820461587504854)
XLA Ops:
  0.6 1.3 %send.1 = (f32[4,64,256]{2,1,0:T(8,128)S(1)}, f32[12,64,256]{2,1,0:T(8,128)S(1)}) custom-call(f32[2,16,64,256]{3,2,1,0:T(8,128)} %images.3), custom_call_target="tpu_custom_call" | custom-call | tf_op jit(solution)/shard_map/send/pallas_call | solution.py:403
  2.0 3.0 %collective-permute-start.2 = (f32[2,64,256]{2,1,0:T(8,128)S(1)}, f32[2,64,256]{2,1,0:T(8,128)S(1)}, u32[]{:S(2)}, u32[]{:S(2)}) collective-permute-start(f32[2,64,256]{2,1,0:T(8,128)S(1)} %get-tuple-element.62), channel_id=1, source_target_pairs={{0,8},{8,0},{1,9},{9,1},{2,10},{10,2},{3,11},{11,3},{4,12},{12,4},... | collective-permute-start | bytes 393224 | tf_op jit(solution)/shard_map/ppermute | solution.py:420
  5.0 0.1 collective-permute-start
  5.1 1.9 %collective-permute-start.4 = (f32[12,64,256]{2,1,0:T(8,128)S(1)}, f32[12,64,256]{2,1,0:T(8,128)S(1)}, u32[]{:S(2)}, u32[]{:S(2)}) collective-permute-start(f32[12,64,256]{2,1,0:T(8,128)S(1)} %get-tuple-element.27), channel_id=1, source_target_pairs={{0,8},{8,0},{1,9},{9,1},{2,10},{10,2},{3,11},{11,3},{4,12},{12,4},... | collective-permute-start | bytes 2359304 | tf_op jit(solution)/shard_map/ppermute | solution.py:422
  7.0 1.7 %keep.1 = (f32[16,64,256]{2,1,0:T(8,128)S(1)}, f32[16,64,256]{2,1,0:T(8,128)S(1)}, f32[4,64,256]{2,1,0:T(8,128)S(1)}, f32[4,64,256]{2,1,0:T(8,128)S(1)}) custom-call(f32[2,16,64,256]{3,2,1,0:T(8,128)} %images.3), custom_call_target="tpu_custom_call" | custom-call | tf_op jit(solution)/shard_map/keep/pallas_call | solution.py:411
  8.8 0.1 collective-permute-start.12
  8.9 0.4 collective-permute-done.2
  9.3 2.1 %collective-permute-start.5 = (f32[4,64,256]{2,1,0:T(8,128)S(1)}, f32[4,64,256]{2,1,0:T(8,128)S(1)}, u32[]{:S(2)}, u32[]{:S(2)}) collective-permute-start(f32[4,64,256]{2,1,0:T(8,128)S(1)} %get-tuple-element.29), channel_id=1, source_target_pairs={{0,2},{2,4},{4,6},{6,0},{1,3},{3,5},{5,7},{7,1},{8,10},{10,12},{12... | collective-permute-start | bytes 786440 | tf_op jit(solution)/shard_map/ppermute | solution.py:365
  11.5 2.1 %collective-permute-start.6 = (f32[4,64,256]{2,1,0:T(8,128)S(1)}, f32[4,64,256]{2,1,0:T(8,128)S(1)}, u32[]{:S(2)}, u32[]{:S(2)}) collective-permute-start(f32[4,64,256]{2,1,0:T(8,128)S(1)} %get-tuple-element.30), channel_id=1, source_target_pairs={{2,0},{4,2},{6,4},{0,6},{3,1},{5,3},{7,5},{1,7},{10,8},{12,10},{14... | collective-permute-start | bytes 786440 | tf_op jit(solution)/shard_map/ppermute | solution.py:366
  13.6 7.1 %collective-permute-done.5.low = f32[4,64,256]{2,1,0:T(8,128)S(1)} collective-permute-done((f32[4,64,256]{2,1,0:T(8,128)S(1)}, f32[4,64,256]{2,1,0:T(8,128)S(1)}, u32[]{:S(2)}, u32[]{:S(2)}) %collective-permute-start.5) | collective-permute-done | bytes 262176 | tf_op jit(solution)/shard_map/ppermute | solution.py:365
  20.7 7.7 %collective-permute-start.3 = (f32[4,64,256]{2,1,0:T(8,128)S(1)}, f32[4,64,256]{2,1,0:T(8,128)S(1)}, u32[]{:S(2)}, u32[]{:S(2)}) collective-permute-start(f32[4,64,256]{2,1,0:T(8,128)S(1)} %pad_maximum_fusion.1), channel_id=1, source_target_pairs={{2,0},{4,2},{6,4},{0,6},{3,1},{5,3},{7,5},{1,7},{10,8},{12,10},{14... | collective-permute-start | bytes 786440 | tf_op jit(solution)/shard_map/ppermute | solution.py:366
  28.4 0.0 collective-permute-done.6.high
  28.5 0.1 collective-permute-start.7
  28.6 0.0 collective-permute-done
  28.6 0.1 collective-permute-start.1
  28.7 1.6 %collective-permute-done.7.sides = f32[24,16,256]{2,1,0:T(8,128)S(1)} collective-permute-done((f32[24,16,256]{2,1,0:T(8,128)S(1)}, f32[24,16,256]{2,1,0:T(8,128)S(1)}, u32[]{:S(2)}, u32[]{:S(2)}) %collective-permute-start.7) | collective-permute-done | bytes 393248 | tf_op jit(solution)/shard_map/ppermute | solution.py:373
  30.3 3.1 %first_step.1 = (f32[20,80,256]{2,1,0:T(8,128)S(1)}, f32[16,64,256]{2,1,0:T(8,128)S(1)}) custom-call(f32[16,64,256]{2,1,0:T(8,128)S(1)} %get-tuple-element.28.mine, f32[4,64,256]{2,1,0:T(8,128)S(1)} %collective-permute-done.5.low, f32[4,64,256]{2,1,0:T(8,128)S(1)} %collective-permute-done.6.high, f32[24,16,256]{2,1,0:T(8,128)S(1)} %collective-permute-done.7.sides), custom_call_target="tpu_custom_call" | custom-call | tf_op jit(solution)/shard_map/first_step/pallas_call | solution.py:429
  33.3 0.0 collective-permute-done.4.middle
  33.4 0.4 first_sums.1
  33.8 0.2 collective-permute-start.8
  34.0 1.0 %collective-permute-done.8 = f32[8,128]{1,0:T(8,128)S(1)} collective-permute-done((f32[8,128]{1,0:T(8,128)S(1)}, f32[8,128]{1,0:T(8,128)S(1)}, u32[]{:S(2)}, u32[]{:S(2)}) %collective-permute-start.8) | collective-permute-done | bytes 4128 | tf_op jit(solution)/shard_map/ppermute | solution.py:387
  35.0 0.0 collective-permute-start.9
  35.0 3.9 %collective-permute-done.9 = f32[8,128]{1,0:T(8,128)S(1)} collective-permute-done((f32[8,128]{1,0:T(8,128)S(1)}, f32[8,128]{1,0:T(8,128)S(1)}, u32[]{:S(2)}, u32[]{:S(2)}) %collective-permute-start.9) | collective-permute-done | bytes 4128 | tf_op jit(solution)/shard_map/ppermute | solution.py:387
  39.0 0.0 collective-permute-done.3.high
  39.0 0.3 collective-permute-done.1.low
  39.4 0.1 collective-permute-start.13
  39.5 0.6 %collective-permute-start.10 = (f32[8,128]{1,0:T(8,128)S(1)}, f32[8,128]{1,0:T(8,128)S(1)}, u32[]{:S(2)}, u32[]{:S(2)}) collective-permute-start(f32[8,128]{1,0:T(8,128)S(1)} %add.19), channel_id=1, source_target_pairs={{0,4},{2,6},{4,0},{6,2},{1,5},{3,7},{5,1},{7,3},{8,12},{10,14},{12... | collective-permute-start | bytes 12296 | tf_op jit(solution)/shard_map/ppermute | solution.py:387
  40.1 3.9 %collective-permute-done.10 = f32[8,128]{1,0:T(8,128)S(1)} collective-permute-done((f32[8,128]{1,0:T(8,128)S(1)}, f32[8,128]{1,0:T(8,128)S(1)}, u32[]{:S(2)}, u32[]{:S(2)}) %collective-permute-start.10) | collective-permute-done | bytes 4128 | tf_op jit(solution)/shard_map/ppermute | solution.py:387
  44.0 1.5 %collective-permute-start.11 = (f32[8,128]{1,0:T(8,128)S(1)}, f32[8,128]{1,0:T(8,128)S(1)}, u32[]{:S(2)}, u32[]{:S(2)}) collective-permute-start(f32[8,128]{1,0:T(8,128)S(1)} %add.20.sums), channel_id=1, source_target_pairs={{0,8},{8,0},{1,9},{9,1},{2,10},{10,2},{3,11},{11,3},{4,12},{12,4},... | collective-permute-start | bytes 12296 | tf_op jit(solution)/shard_map/ppermute | solution.py:459
  45.5 0.0 collective-permute-done.13.sides
  45.5 2.7 %other_step.1 = (f32[16,64,256]{2,1,0:T(8,128)S(1)}, f32[20,80,256]{2,1,0:T(8,128)S(1)}) custom-call(f32[4,64,256]{2,1,0:T(8,128)S(1)} %constant_dynamic-update-slice_fusion.edges, f32[12,64,256]{2,1,0:T(8,128)S(1)} %collective-permute-done.4.middle, f32[16,64,256]{2,1,0:T(8,128)S(1)} %get-tuple-element.23.end, ...), custom_call_target="tpu_custom_call" | custom-call | tf_op jit(solution)/shard_map/other_step/pallas_call | solution.py:445
  48.2 2.7 %second_step.1 = (f32[16,64,256]{2,1,0:T(8,128)S(1)}, f32[16,64,256]{2,1,0:T(8,128)S(1)}, f32[16,64,256]{2,1,0:T(8,128)S(1)}, f32[2,16,64,256]{3,2,1,0:T(8,128)}) custom-call(f32[8,128]{1,0:T(8,128)S(1)} %add.20.sums, f32[20,80,256]{2,1,0:T(8,128)S(1)} %get-tuple-element.36.step, f32[20,80,256]{2,1,0:T(8,128)S(1)} %get-tuple-element.37.tangent_wide, ...), custom_call_target="tpu_custom_call" | custom-call | tf_op jit(solution)/shard_map/second_step/pallas_call | solution.py:450
  50.9 0.0 collective-permute-done.11.o_sums
  50.9 0.0 collective-permute-done.12.far
  50.9 0.6 second_sums.1
  51.5 0.1 collective-permute-start.14
  51.6 1.2 %collective-permute-done.14 = f32[8,128]{1,0:T(8,128)S(1)} collective-permute-done((f32[8,128]{1,0:T(8,128)S(1)}, f32[8,128]{1,0:T(8,128)S(1)}, u32[]{:S(2)}, u32[]{:S(2)}) %collective-permute-start.14) | collective-permute-done | bytes 4128 | tf_op jit(solution)/shard_map/ppermute | solution.py:387
  52.7 1.6 %collective-permute-start.15 = (f32[8,128]{1,0:T(8,128)S(1)}, f32[8,128]{1,0:T(8,128)S(1)}, u32[]{:S(2)}, u32[]{:S(2)}) collective-permute-start(f32[8,128]{1,0:T(8,128)S(1)} %add.21), channel_id=1, source_target_pairs={{0,2},{2,0},{4,6},{6,4},{1,3},{3,1},{5,7},{7,5},{8,10},{10,8},{12,... | collective-permute-start | bytes 12296 | tf_op jit(solution)/shard_map/ppermute | solution.py:387
  54.4 2.0 %collective-permute-done.15 = f32[8,128]{1,0:T(8,128)S(1)} collective-permute-done((f32[8,128]{1,0:T(8,128)S(1)}, f32[8,128]{1,0:T(8,128)S(1)}, u32[]{:S(2)}, u32[]{:S(2)}) %collective-permute-start.15) | collective-permute-done | bytes 4128 | tf_op jit(solution)/shard_map/ppermute | solution.py:387
  56.4 2.6 %collective-permute-start.16 = (f32[8,128]{1,0:T(8,128)S(1)}, f32[8,128]{1,0:T(8,128)S(1)}, u32[]{:S(2)}, u32[]{:S(2)}) collective-permute-start(f32[8,128]{1,0:T(8,128)S(1)} %add.22), channel_id=1, source_target_pairs={{0,4},{2,6},{4,0},{6,2},{1,5},{3,7},{5,1},{7,3},{8,12},{10,14},{12... | collective-permute-start | bytes 12296 | tf_op jit(solution)/shard_map/ppermute | solution.py:387
  59.0 1.9 %collective-permute-done.16 = f32[8,128]{1,0:T(8,128)S(1)} collective-permute-done((f32[8,128]{1,0:T(8,128)S(1)}, f32[8,128]{1,0:T(8,128)S(1)}, u32[]{:S(2)}, u32[]{:S(2)}) %collective-permute-start.16) | collective-permute-done | bytes 4128 | tf_op jit(solution)/shard_map/ppermute | solution.py:387
  60.9 1.7 %last.1 = (f32[2,16,64,256]{3,2,1,0:T(8,128)}, f32[2]{0:T(128)}) custom-call(f32[8,128]{1,0:T(8,128)S(1)} %add.23.sums, f32[8,128]{1,0:T(8,128)S(1)} %collective-permute-done.11.o_sums, f32[16,64,256]{2,1,0:T(8,128)S(1)} %collective-permute-done.12.far, f32[16,64,256]{2,1,0:T(8,128)S(1)} %get-tuple-element.28.mine, ...), custom_call_target="tpu_custom_call", output_to_operand_aliasing={{0}: (6, {})} | custom-call | tf_op jit(solution)/shard_map/last/pallas_call | solution.py:464
  (29 shorter events, 0.3 us)
Async XLA Ops:
  2.0 7.3 %collective-permute-start.2 = (f32[2,64,256]{2,1,0:T(8,128)S(1)}, f32[2,64,256]{2,1,0:T(8,128)S(1)}, u32[]{:S(2)}, u32[]{:S(2)}) collective-permute-start(f32[2,64,256]{2,1,0:T(8,128)S(1)} %get-tuple-element.62), channel_id=1, source_target_pairs={{0,8},{8,0},{1,9},{9,1},{2,10},{10,2},{3,11},{11,3},{4,12},{12,4},... | collective-permute-start | bytes 393224 | tf_op jit(solution)/shard_map/ppermute | solution.py:420
  5.0 23.6 %collective-permute-start = (f32[2,64,256]{2,1,0:T(8,128)S(1)}, f32[2,64,256]{2,1,0:T(8,128)S(1)}, u32[]{:S(2)}, u32[]{:S(2)}) collective-permute-start(f32[2,64,256]{2,1,0:T(8,128)S(1)} %get-tuple-element.63), channel_id=1, source_target_pairs={{0,8},{8,0},{1,9},{9,1},{2,10},{10,2},{3,11},{11,3},{4,12},{12,4},... | collective-permute-start | bytes 393224 | tf_op jit(solution)/shard_map/ppermute | solution.py:421
  5.1 28.3 %collective-permute-start.4 = (f32[12,64,256]{2,1,0:T(8,128)S(1)}, f32[12,64,256]{2,1,0:T(8,128)S(1)}, u32[]{:S(2)}, u32[]{:S(2)}) collective-permute-start(f32[12,64,256]{2,1,0:T(8,128)S(1)} %get-tuple-element.27), channel_id=1, source_target_pairs={{0,8},{8,0},{1,9},{9,1},{2,10},{10,2},{3,11},{11,3},{4,12},{12,4},... | collective-permute-start | bytes 2359304 | tf_op jit(solution)/shard_map/ppermute | solution.py:422
  8.8 42.1 %collective-permute-start.12 = (f32[16,64,256]{2,1,0:T(8,128)S(1)}, f32[16,64,256]{2,1,0:T(8,128)S(1)}, u32[]{:S(2)}, u32[]{:S(2)}) collective-permute-start(f32[16,64,256]{2,1,0:T(8,128)S(1)} %get-tuple-element.23.end), channel_id=1, source_target_pairs={{0,8},{8,0},{1,9},{9,1},{2,10},{10,2},{3,11},{11,3},{4,12},{12,4},... | collective-permute-start | bytes 3145736 | tf_op jit(solution)/shard_map/ppermute | solution.py:423
  9.3 11.4 %collective-permute-start.5 = (f32[4,64,256]{2,1,0:T(8,128)S(1)}, f32[4,64,256]{2,1,0:T(8,128)S(1)}, u32[]{:S(2)}, u32[]{:S(2)}) collective-permute-start(f32[4,64,256]{2,1,0:T(8,128)S(1)} %get-tuple-element.29), channel_id=1, source_target_pairs={{0,2},{2,4},{4,6},{6,0},{1,3},{3,5},{5,7},{7,1},{8,10},{10,12},{12... | collective-permute-start | bytes 786440 | tf_op jit(solution)/shard_map/ppermute | solution.py:365
  11.5 17.0 %collective-permute-start.6 = (f32[4,64,256]{2,1,0:T(8,128)S(1)}, f32[4,64,256]{2,1,0:T(8,128)S(1)}, u32[]{:S(2)}, u32[]{:S(2)}) collective-permute-start(f32[4,64,256]{2,1,0:T(8,128)S(1)} %get-tuple-element.30), channel_id=1, source_target_pairs={{2,0},{4,2},{6,4},{0,6},{3,1},{5,3},{7,5},{1,7},{10,8},{12,10},{14... | collective-permute-start | bytes 786440 | tf_op jit(solution)/shard_map/ppermute | solution.py:366
  20.7 18.3 %collective-permute-start.3 = (f32[4,64,256]{2,1,0:T(8,128)S(1)}, f32[4,64,256]{2,1,0:T(8,128)S(1)}, u32[]{:S(2)}, u32[]{:S(2)}) collective-permute-start(f32[4,64,256]{2,1,0:T(8,128)S(1)} %pad_maximum_fusion.1), channel_id=1, source_target_pairs={{2,0},{4,2},{6,4},{0,6},{3,1},{5,3},{7,5},{1,7},{10,8},{12,10},{14... | collective-permute-start | bytes 786440 | tf_op jit(solution)/shard_map/ppermute | solution.py:366
  28.5 1.8 %collective-permute-start.7 = (f32[24,16,256]{2,1,0:T(8,128)S(1)}, f32[24,16,256]{2,1,0:T(8,128)S(1)}, u32[]{:S(2)}, u32[]{:S(2)}) collective-permute-start(f32[24,16,256]{2,1,0:T(8,128)S(1)} %maximum_maximum_fusion), channel_id=1, source_target_pairs={{0,1},{1,0},{2,3},{3,2},{4,5},{5,4},{6,7},{7,6},{8,9},{9,8},{10,11... | collective-permute-start | bytes 1179656 | tf_op jit(solution)/shard_map/ppermute | solution.py:373
  28.6 10.6 %collective-permute-start.1 = (f32[4,64,256]{2,1,0:T(8,128)S(1)}, f32[4,64,256]{2,1,0:T(8,128)S(1)}, u32[]{:S(2)}, u32[]{:S(2)}) collective-permute-start(f32[4,64,256]{2,1,0:T(8,128)S(1)} %pad_maximum_fusion), channel_id=1, source_target_pairs={{0,2},{2,4},{4,6},{6,0},{1,3},{3,5},{5,7},{7,1},{8,10},{10,12},{12... | collective-permute-start | bytes 786440 | tf_op jit(solution)/shard_map/ppermute | solution.py:365
  33.8 1.2 %collective-permute-start.8 = (f32[8,128]{1,0:T(8,128)S(1)}, f32[8,128]{1,0:T(8,128)S(1)}, u32[]{:S(2)}, u32[]{:S(2)}) collective-permute-start(f32[8,128]{1,0:T(8,128)S(1)} %first_sums.1), channel_id=1, source_target_pairs={{0,1},{1,0},{2,3},{3,2},{4,5},{5,4},{6,7},{7,6},{8,9},{9,8},{10,11... | collective-permute-start | bytes 12296 | tf_op jit(solution)/shard_map/ppermute | solution.py:387
  35.0 3.9 %collective-permute-start.9 = (f32[8,128]{1,0:T(8,128)S(1)}, f32[8,128]{1,0:T(8,128)S(1)}, u32[]{:S(2)}, u32[]{:S(2)}) collective-permute-start(f32[8,128]{1,0:T(8,128)S(1)} %add.18), channel_id=1, source_target_pairs={{0,2},{2,0},{4,6},{6,4},{1,3},{3,1},{5,7},{7,5},{8,10},{10,8},{12,... | collective-permute-start | bytes 12296 | tf_op jit(solution)/shard_map/ppermute | solution.py:387
  39.4 6.1 %collective-permute-start.13 = (f32[40,16,256]{2,1,0:T(8,128)S(1)}, f32[40,16,256]{2,1,0:T(8,128)S(1)}, u32[]{:S(2)}, u32[]{:S(2)}) collective-permute-start(f32[40,16,256]{2,1,0:T(8,128)S(1)} %maximum_dynamic-update-slice_fusion.2), channel_id=1, source_target_pairs={{0,1},{1,0},{2,3},{3,2},{4,5},{5,4},{6,7},{7,6},{8,9},{9,8},{10,11... | collective-permute-start | bytes 1966088 | tf_op jit(solution)/shard_map/ppermute | solution.py:373
  39.5 4.6 %collective-permute-start.10 = (f32[8,128]{1,0:T(8,128)S(1)}, f32[8,128]{1,0:T(8,128)S(1)}, u32[]{:S(2)}, u32[]{:S(2)}) collective-permute-start(f32[8,128]{1,0:T(8,128)S(1)} %add.19), channel_id=1, source_target_pairs={{0,4},{2,6},{4,0},{6,2},{1,5},{3,7},{5,1},{7,3},{8,12},{10,14},{12... | collective-permute-start | bytes 12296 | tf_op jit(solution)/shard_map/ppermute | solution.py:387
  44.0 6.8 %collective-permute-start.11 = (f32[8,128]{1,0:T(8,128)S(1)}, f32[8,128]{1,0:T(8,128)S(1)}, u32[]{:S(2)}, u32[]{:S(2)}) collective-permute-start(f32[8,128]{1,0:T(8,128)S(1)} %add.20.sums), channel_id=1, source_target_pairs={{0,8},{8,0},{1,9},{9,1},{2,10},{10,2},{3,11},{11,3},{4,12},{12,4},... | collective-permute-start | bytes 12296 | tf_op jit(solution)/shard_map/ppermute | solution.py:459
  51.5 1.2 %collective-permute-start.14 = (f32[8,128]{1,0:T(8,128)S(1)}, f32[8,128]{1,0:T(8,128)S(1)}, u32[]{:S(2)}, u32[]{:S(2)}) collective-permute-start(f32[8,128]{1,0:T(8,128)S(1)} %second_sums.1), channel_id=1, source_target_pairs={{0,1},{1,0},{2,3},{3,2},{4,5},{5,4},{6,7},{7,6},{8,9},{9,8},{10,11... | collective-permute-start | bytes 12296 | tf_op jit(solution)/shard_map/ppermute | solution.py:387
  52.7 3.6 %collective-permute-start.15 = (f32[8,128]{1,0:T(8,128)S(1)}, f32[8,128]{1,0:T(8,128)S(1)}, u32[]{:S(2)}, u32[]{:S(2)}) collective-permute-start(f32[8,128]{1,0:T(8,128)S(1)} %add.21), channel_id=1, source_target_pairs={{0,2},{2,0},{4,6},{6,4},{1,3},{3,1},{5,7},{7,5},{8,10},{10,8},{12,... | collective-permute-start | bytes 12296 | tf_op jit(solution)/shard_map/ppermute | solution.py:387
  56.4 4.5 %collective-permute-start.16 = (f32[8,128]{1,0:T(8,128)S(1)}, f32[8,128]{1,0:T(8,128)S(1)}, u32[]{:S(2)}, u32[]{:S(2)}) collective-permute-start(f32[8,128]{1,0:T(8,128)S(1)} %add.22), channel_id=1, source_target_pairs={{0,4},{2,6},{4,0},{6,2},{1,5},{3,7},{5,1},{7,3},{8,12},{10,14},{12... | collective-permute-start | bytes 12296 | tf_op jit(solution)/shard_map/ppermute | solution.py:387

commit v11 on v10

--- a/solution.py
+++ b/solution.py
@@ -430,6 +430,7 @@
         mine, low, high, sides
     )
 
+    o_edges, low, high = lax.optimization_barrier((o_edges, low, high))
     o_low, o_high = from_z(
         jnp.concatenate([o_edges[2 * AHEAD - 2 :], end[nz - 2 :]]),
         jnp.concatenate([o_edges[:2], end[:2]]),

time: 62.8 us -> 62.5 us (level)
  starting transfers between devices: 24 us -> 22.1 us
  waiting for transfers between devices: 23.2 us -> 25 us
    ppermute x2, starting transfers between devices: 9.8 us -> 4.39 us  [from_z(): lax.ppermute(down, 'space', [((i + 1) % count, i) for i in range(count)])]
    ppermute x6, starting transfers between devices: 5.18 us -> 8.68 us  [summed(): sums = sums + lax.ppermute(sums, axis, pairs)]
    ppermute x2, waiting for transfers between devices: 0.01 us -> 2.67 us  [from_z(): lax.ppermute(down, 'space', [((i + 1) % count, i) for i in range(count)])]
    ppermute x2, waiting for transfers between devices: 1.58 us -> 0.01 us  [y_sides(): return lax.ppermute(jnp.concatenate(ends, 0), 'yslab', SWAP)]
  transfers between devices with their start and end apart: 17 -> 17, of which waited for: 10 -> 11; matrix products, arithmetic and copies ran while one was open for 0% -> 0% of each run, Pallas kernels for 17% -> 17%
where the time goes in v11:
time: 62.5 us; the launch traced here: 62.4 us
  waiting for transfers between devices  25 us (40%)
  starting transfers between devices  22.1 us (35%)
  Pallas kernels  14.1 us (23%)
  between operations  0.86 us (1%)
    ppermute x6, waiting for transfers between devices, summed(): sums = sums + lax.ppermute(sums, axis, pairs)  13.6 us
    ppermute x6, starting transfers between devices, summed(): sums = sums + lax.ppermute(sums, axis, pairs)  8.68 us
    ppermute x2, waiting for transfers between devices, from_z(): lax.ppermute(up, 'space', [(i, (i + 1) % count) for i in range(count)])  7.98 us
    ppermute x2, starting transfers between devices, from_z(): lax.ppermute(down, 'space', [((i + 1) % count, i) for i in range(count)])  4.39 us
    pallas_call x1, Pallas kernels, body_pair(): call(first_step_kernel, [outer, block], [room(nz + 8), room(nz + 6)], 'fi...  3.06 us
    ppermute x1, starting transfers between devices, body_pair(): o_first = lax.ppermute(edges[:AHEAD], 'image', SWAP)  3 us
    ppermute x2, waiting for transfers between devices, from_z(): lax.ppermute(down, 'space', [((i + 1) % count, i) for i in range(count)])  2.67 us
    pallas_call x1, Pallas kernels, body_pair(): call(second_step_kernel, [block] * 3 + [whole], [room(nz + 4), room(nz +...  2.67 us
  transfers between devices with their start and end apart: 17, of which 11 were waited for; matrix products, arithmetic and copies ran while one was open for 0% of the time, Pallas kernels for 17%

profile of v11, /device:TPU:0, one launch (start us, length us, event | category | flops | bytes accessed | tf_op | source)
XLA Modules:
  0.0 62.4 jit_solution(13985278617221846974)
XLA Ops:
  0.6 1.3 %send.1 = (f32[4,64,256]{2,1,0:T(8,128)S(1)}, f32[12,64,256]{2,1,0:T(8,128)S(1)}) custom-call(f32[2,16,64,256]{3,2,1,0:T(8,128)} %images.3), custom_call_target="tpu_custom_call" | custom-call | tf_op jit(solution)/shard_map/send/pallas_call | solution.py:403
  2.0 3.0 %collective-permute-start = (f32[2,64,256]{2,1,0:T(8,128)S(1)}, f32[2,64,256]{2,1,0:T(8,128)S(1)}, u32[]{:S(2)}, u32[]{:S(2)}) collective-permute-start(f32[2,64,256]{2,1,0:T(8,128)S(1)} %get-tuple-element.70), channel_id=1, source_target_pairs={{0,8},{8,0},{1,9},{9,1},{2,10},{10,2},{3,11},{11,3},{4,12},{12,4},... | collective-permute-start | bytes 393224 | tf_op jit(solution)/shard_map/ppermute | solution.py:420
  5.0 0.1 collective-permute-start.1
  5.1 1.9 %collective-permute-start.6 = (f32[12,64,256]{2,1,0:T(8,128)S(1)}, f32[12,64,256]{2,1,0:T(8,128)S(1)}, u32[]{:S(2)}, u32[]{:S(2)}) collective-permute-start(f32[12,64,256]{2,1,0:T(8,128)S(1)} %get-tuple-element.31), channel_id=1, source_target_pairs={{0,8},{8,0},{1,9},{9,1},{2,10},{10,2},{3,11},{11,3},{4,12},{12,4},... | collective-permute-start | bytes 2359304 | tf_op jit(solution)/shard_map/ppermute | solution.py:422
  7.0 1.7 %keep.1 = (f32[16,64,256]{2,1,0:T(8,128)S(1)}, f32[16,64,256]{2,1,0:T(8,128)S(1)}, f32[4,64,256]{2,1,0:T(8,128)S(1)}, f32[4,64,256]{2,1,0:T(8,128)S(1)}) custom-call(f32[2,16,64,256]{3,2,1,0:T(8,128)} %images.3), custom_call_target="tpu_custom_call" | custom-call | tf_op jit(solution)/shard_map/keep/pallas_call | solution.py:411
  8.8 0.1 collective-permute-start.12
  8.9 0.4 collective-permute-done
  9.3 2.1 %collective-permute-start.2 = (f32[4,64,256]{2,1,0:T(8,128)S(1)}, f32[4,64,256]{2,1,0:T(8,128)S(1)}, u32[]{:S(2)}, u32[]{:S(2)}) collective-permute-start(f32[4,64,256]{2,1,0:T(8,128)S(1)} %get-tuple-element.27), channel_id=1, source_target_pairs={{0,2},{2,4},{4,6},{6,0},{1,3},{3,5},{5,7},{7,1},{8,10},{10,12},{12... | collective-permute-start | bytes 786440 | tf_op jit(solution)/shard_map/ppermute | solution.py:365
  11.5 2.1 %collective-permute-start.3 = (f32[4,64,256]{2,1,0:T(8,128)S(1)}, f32[4,64,256]{2,1,0:T(8,128)S(1)}, u32[]{:S(2)}, u32[]{:S(2)}) collective-permute-start(f32[4,64,256]{2,1,0:T(8,128)S(1)} %get-tuple-element.28), channel_id=1, source_target_pairs={{2,0},{4,2},{6,4},{0,6},{3,1},{5,3},{7,5},{1,7},{10,8},{12,10},{14... | collective-permute-start | bytes 786440 | tf_op jit(solution)/shard_map/ppermute | solution.py:366
  13.6 0.0 collective-permute-done.1
  13.6 7.1 %collective-permute-done.2.low = f32[4,64,256]{2,1,0:T(8,128)S(1)} collective-permute-done((f32[4,64,256]{2,1,0:T(8,128)S(1)}, f32[4,64,256]{2,1,0:T(8,128)S(1)}, u32[]{:S(2)}, u32[]{:S(2)}) %collective-permute-start.2) | collective-permute-done | bytes 262176 | tf_op jit(solution)/shard_map/ppermute | solution.py:365
  20.7 2.7 %collective-permute-done.3.high = f32[4,64,256]{2,1,0:T(8,128)S(1)} collective-permute-done((f32[4,64,256]{2,1,0:T(8,128)S(1)}, f32[4,64,256]{2,1,0:T(8,128)S(1)}, u32[]{:S(2)}, u32[]{:S(2)}) %collective-permute-start.3) | collective-permute-done | bytes 262176 | tf_op jit(solution)/shard_map/ppermute | solution.py:366
  23.4 0.1 collective-permute-start.7
  23.6 2.3 %collective-permute-start.5 = (f32[4,64,256]{2,1,0:T(8,128)S(1)}, f32[4,64,256]{2,1,0:T(8,128)S(1)}, u32[]{:S(2)}, u32[]{:S(2)}) collective-permute-start(f32[4,64,256]{2,1,0:T(8,128)S(1)} %pad_maximum_fusion.2), channel_id=1, source_target_pairs={{2,0},{4,2},{6,4},{0,6},{3,1},{5,3},{7,5},{1,7},{10,8},{12,10},{14... | collective-permute-start | bytes 786440 | tf_op jit(solution)/shard_map/ppermute | solution.py:366
  25.9 0.1 collective-permute-start.4
  25.9 0.0 collective-permute-done.7.sides
  26.0 3.1 %first_step.1 = (f32[20,80,256]{2,1,0:T(8,128)S(1)}, f32[16,64,256]{2,1,0:T(8,128)S(1)}) custom-call(f32[16,64,256]{2,1,0:T(8,128)S(1)} %get-tuple-element.32.mine, f32[4,64,256]{2,1,0:T(8,128)S(1)} %collective-permute-done.2.low, f32[4,64,256]{2,1,0:T(8,128)S(1)} %collective-permute-done.3.high, f32[24,16,256]{2,1,0:T(8,128)S(1)} %collective-permute-done.7.sides), custom_call_target="tpu_custom_call" | custom-call | tf_op jit(solution)/shard_map/first_step/pallas_call | solution.py:429
  29.0 0.0 collective-permute-done.6.middle
  29.0 0.4 first_sums.1
  29.5 0.3 collective-permute-start.8
  29.8 0.9 %collective-permute-done.8 = f32[8,128]{1,0:T(8,128)S(1)} collective-permute-done((f32[8,128]{1,0:T(8,128)S(1)}, f32[8,128]{1,0:T(8,128)S(1)}, u32[]{:S(2)}, u32[]{:S(2)}) %collective-permute-start.8) | collective-permute-done | bytes 4128 | tf_op jit(solution)/shard_map/ppermute | solution.py:387
  30.7 2.1 %collective-permute-start.9 = (f32[8,128]{1,0:T(8,128)S(1)}, f32[8,128]{1,0:T(8,128)S(1)}, u32[]{:S(2)}, u32[]{:S(2)}) collective-permute-start(f32[8,128]{1,0:T(8,128)S(1)} %add.18), channel_id=1, source_target_pairs={{0,2},{2,0},{4,6},{6,4},{1,3},{3,1},{5,7},{7,5},{8,10},{10,8},{12,... | collective-permute-start | bytes 12296 | tf_op jit(solution)/shard_map/ppermute | solution.py:387
  32.8 5.0 %collective-permute-done.9 = f32[8,128]{1,0:T(8,128)S(1)} collective-permute-done((f32[8,128]{1,0:T(8,128)S(1)}, f32[8,128]{1,0:T(8,128)S(1)}, u32[]{:S(2)}, u32[]{:S(2)}) %collective-permute-start.9) | collective-permute-done | bytes 4128 | tf_op jit(solution)/shard_map/ppermute | solution.py:387
  37.8 0.0 collective-permute-done.5.high
  37.8 0.8 %collective-permute-done.4.low = f32[4,64,256]{2,1,0:T(8,128)S(1)} collective-permute-done((f32[4,64,256]{2,1,0:T(8,128)S(1)}, f32[4,64,256]{2,1,0:T(8,128)S(1)}, u32[]{:S(2)}, u32[]{:S(2)}) %collective-permute-start.4) | collective-permute-done | bytes 262176 | tf_op jit(solution)/shard_map/ppermute | solution.py:365
  38.8 0.1 collective-permute-start.13
  38.9 1.6 %collective-permute-start.10 = (f32[8,128]{1,0:T(8,128)S(1)}, f32[8,128]{1,0:T(8,128)S(1)}, u32[]{:S(2)}, u32[]{:S(2)}) collective-permute-start(f32[8,128]{1,0:T(8,128)S(1)} %add.19), channel_id=1, source_target_pairs={{0,4},{2,6},{4,0},{6,2},{1,5},{3,7},{5,1},{7,3},{8,12},{10,14},{12... | collective-permute-start | bytes 12296 | tf_op jit(solution)/shard_map/ppermute | solution.py:387
  40.5 3.0 %collective-permute-done.10 = f32[8,128]{1,0:T(8,128)S(1)} collective-permute-done((f32[8,128]{1,0:T(8,128)S(1)}, f32[8,128]{1,0:T(8,128)S(1)}, u32[]{:S(2)}, u32[]{:S(2)}) %collective-permute-start.10) | collective-permute-done | bytes 4128 | tf_op jit(solution)/shard_map/ppermute | solution.py:387
  43.5 1.5 %collective-permute-start.11 = (f32[8,128]{1,0:T(8,128)S(1)}, f32[8,128]{1,0:T(8,128)S(1)}, u32[]{:S(2)}, u32[]{:S(2)}) collective-permute-start(f32[8,128]{1,0:T(8,128)S(1)} %add.20.sums), channel_id=1, source_target_pairs={{0,8},{8,0},{1,9},{9,1},{2,10},{10,2},{3,11},{11,3},{4,12},{12,4},... | collective-permute-start | bytes 12296 | tf_op jit(solution)/shard_map/ppermute | solution.py:460
  45.0 0.0 collective-permute-done.13.sides
  45.0 2.6 %other_step.1 = (f32[16,64,256]{2,1,0:T(8,128)S(1)}, f32[20,80,256]{2,1,0:T(8,128)S(1)}) custom-call(f32[4,64,256]{2,1,0:T(8,128)S(1)} %pad_maximum_fusion.edges, f32[12,64,256]{2,1,0:T(8,128)S(1)} %collective-permute-done.6.middle, f32[16,64,256]{2,1,0:T(8,128)S(1)} %get-tuple-element.30.end, f32[4,64,256]{2,1,0:T(8,128)S(1)} %collective-permute-done.4.low, ...), custom_call_target="tpu_custom_call" | custom-call | tf_op jit(solution)/shard_map/other_step/pallas_call | solution.py:446
  47.6 2.7 %second_step.1 = (f32[16,64,256]{2,1,0:T(8,128)S(1)}, f32[16,64,256]{2,1,0:T(8,128)S(1)}, f32[16,64,256]{2,1,0:T(8,128)S(1)}, f32[2,16,64,256]{3,2,1,0:T(8,128)}) custom-call(f32[8,128]{1,0:T(8,128)S(1)} %add.20.sums, f32[20,80,256]{2,1,0:T(8,128)S(1)} %get-tuple-element.38.step, f32[20,80,256]{2,1,0:T(8,128)S(1)} %get-tuple-element.39.tangent_wide, ...), custom_call_target="tpu_custom_call" | custom-call | tf_op jit(solution)/shard_map/second_step/pallas_call | solution.py:451
  50.3 0.4 collective-permute-done.11.o_sums
  50.7 0.0 collective-permute-done.12.far
  50.7 0.6 second_sums.1
  51.3 0.1 collective-permute-start.14
  51.4 1.2 %collective-permute-done.14 = f32[8,128]{1,0:T(8,128)S(1)} collective-permute-done((f32[8,128]{1,0:T(8,128)S(1)}, f32[8,128]{1,0:T(8,128)S(1)}, u32[]{:S(2)}, u32[]{:S(2)}) %collective-permute-start.14) | collective-permute-done | bytes 4128 | tf_op jit(solution)/shard_map/ppermute | solution.py:387
  52.5 1.8 %collective-permute-start.15 = (f32[8,128]{1,0:T(8,128)S(1)}, f32[8,128]{1,0:T(8,128)S(1)}, u32[]{:S(2)}, u32[]{:S(2)}) collective-permute-start(f32[8,128]{1,0:T(8,128)S(1)} %add.21), channel_id=1, source_target_pairs={{0,2},{2,0},{4,6},{6,4},{1,3},{3,1},{5,7},{7,5},{8,10},{10,8},{12,... | collective-permute-start | bytes 12296 | tf_op jit(solution)/shard_map/ppermute | solution.py:387
  54.3 1.8 %collective-permute-done.15 = f32[8,128]{1,0:T(8,128)S(1)} collective-permute-done((f32[8,128]{1,0:T(8,128)S(1)}, f32[8,128]{1,0:T(8,128)S(1)}, u32[]{:S(2)}, u32[]{:S(2)}) %collective-permute-start.15) | collective-permute-done | bytes 4128 | tf_op jit(solution)/shard_map/ppermute | solution.py:387
  56.1 2.8 %collective-permute-start.16 = (f32[8,128]{1,0:T(8,128)S(1)}, f32[8,128]{1,0:T(8,128)S(1)}, u32[]{:S(2)}, u32[]{:S(2)}) collective-permute-start(f32[8,128]{1,0:T(8,128)S(1)} %add.22), channel_id=1, source_target_pairs={{0,4},{2,6},{4,0},{6,2},{1,5},{3,7},{5,1},{7,3},{8,12},{10,14},{12... | collective-permute-start | bytes 12296 | tf_op jit(solution)/shard_map/ppermute | solution.py:387
  59.0 1.7 %collective-permute-done.16 = f32[8,128]{1,0:T(8,128)S(1)} collective-permute-done((f32[8,128]{1,0:T(8,128)S(1)}, f32[8,128]{1,0:T(8,128)S(1)}, u32[]{:S(2)}, u32[]{:S(2)}) %collective-permute-start.16) | collective-permute-done | bytes 4128 | tf_op jit(solution)/shard_map/ppermute | solution.py:387
  60.6 1.7 %last.1 = (f32[2,16,64,256]{3,2,1,0:T(8,128)}, f32[2]{0:T(128)}) custom-call(f32[8,128]{1,0:T(8,128)S(1)} %add.23.sums, f32[8,128]{1,0:T(8,128)S(1)} %collective-permute-done.11.o_sums, f32[16,64,256]{2,1,0:T(8,128)S(1)} %collective-permute-done.12.far, f32[16,64,256]{2,1,0:T(8,128)S(1)} %get-tuple-element.32.mine, ...), custom_call_target="tpu_custom_call", output_to_operand_aliasing={{0}: (6, {})} | custom-call | tf_op jit(solution)/shard_map/last/pallas_call | solution.py:465
  (28 shorter events, 0.3 us)
Async XLA Ops:
  2.0 7.3 %collective-permute-start = (f32[2,64,256]{2,1,0:T(8,128)S(1)}, f32[2,64,256]{2,1,0:T(8,128)S(1)}, u32[]{:S(2)}, u32[]{:S(2)}) collective-permute-start(f32[2,64,256]{2,1,0:T(8,128)S(1)} %get-tuple-element.70), channel_id=1, source_target_pairs={{0,8},{8,0},{1,9},{9,1},{2,10},{10,2},{3,11},{11,3},{4,12},{12,4},... | collective-permute-start | bytes 393224 | tf_op jit(solution)/shard_map/ppermute | solution.py:420
  5.0 8.6 %collective-permute-start.1 = (f32[2,64,256]{2,1,0:T(8,128)S(1)}, f32[2,64,256]{2,1,0:T(8,128)S(1)}, u32[]{:S(2)}, u32[]{:S(2)}) collective-permute-start(f32[2,64,256]{2,1,0:T(8,128)S(1)} %get-tuple-element.71), channel_id=1, source_target_pairs={{0,8},{8,0},{1,9},{9,1},{2,10},{10,2},{3,11},{11,3},{4,12},{12,4},... | collective-permute-start | bytes 393224 | tf_op jit(solution)/shard_map/ppermute | solution.py:421
  5.1 24.0 %collective-permute-start.6 = (f32[12,64,256]{2,1,0:T(8,128)S(1)}, f32[12,64,256]{2,1,0:T(8,128)S(1)}, u32[]{:S(2)}, u32[]{:S(2)}) collective-permute-start(f32[12,64,256]{2,1,0:T(8,128)S(1)} %get-tuple-element.31), channel_id=1, source_target_pairs={{0,8},{8,0},{1,9},{9,1},{2,10},{10,2},{3,11},{11,3},{4,12},{12,4},... | collective-permute-start | bytes 2359304 | tf_op jit(solution)/shard_map/ppermute | solution.py:422
  8.8 41.9 %collective-permute-start.12 = (f32[16,64,256]{2,1,0:T(8,128)S(1)}, f32[16,64,256]{2,1,0:T(8,128)S(1)}, u32[]{:S(2)}, u32[]{:S(2)}) collective-permute-start(f32[16,64,256]{2,1,0:T(8,128)S(1)} %get-tuple-element.30.end), channel_id=1, source_target_pairs={{0,8},{8,0},{1,9},{9,1},{2,10},{10,2},{3,11},{11,3},{4,12},{12,4},... | collective-permute-start | bytes 3145736 | tf_op jit(solution)/shard_map/ppermute | solution.py:423
  9.3 11.4 %collective-permute-start.2 = (f32[4,64,256]{2,1,0:T(8,128)S(1)}, f32[4,64,256]{2,1,0:T(8,128)S(1)}, u32[]{:S(2)}, u32[]{:S(2)}) collective-permute-start(f32[4,64,256]{2,1,0:T(8,128)S(1)} %get-tuple-element.27), channel_id=1, source_target_pairs={{0,2},{2,4},{4,6},{6,0},{1,3},{3,5},{5,7},{7,1},{8,10},{10,12},{12... | collective-permute-start | bytes 786440 | tf_op jit(solution)/shard_map/ppermute | solution.py:365
  11.5 11.9 %collective-permute-start.3 = (f32[4,64,256]{2,1,0:T(8,128)S(1)}, f32[4,64,256]{2,1,0:T(8,128)S(1)}, u32[]{:S(2)}, u32[]{:S(2)}) collective-permute-start(f32[4,64,256]{2,1,0:T(8,128)S(1)} %get-tuple-element.28), channel_id=1, source_target_pairs={{2,0},{4,2},{6,4},{0,6},{3,1},{5,3},{7,5},{1,7},{10,8},{12,10},{14... | collective-permute-start | bytes 786440 | tf_op jit(solution)/shard_map/ppermute | solution.py:366
  23.4 2.5 %collective-permute-start.7 = (f32[24,16,256]{2,1,0:T(8,128)S(1)}, f32[24,16,256]{2,1,0:T(8,128)S(1)}, u32[]{:S(2)}, u32[]{:S(2)}) collective-permute-start(f32[24,16,256]{2,1,0:T(8,128)S(1)} %maximum_maximum_fusion), channel_id=1, source_target_pairs={{0,1},{1,0},{2,3},{3,2},{4,5},{5,4},{6,7},{7,6},{8,9},{9,8},{10,11... | collective-permute-start | bytes 1179656 | tf_op jit(solution)/shard_map/ppermute | solution.py:373
  23.6 14.3 %collective-permute-start.5 = (f32[4,64,256]{2,1,0:T(8,128)S(1)}, f32[4,64,256]{2,1,0:T(8,128)S(1)}, u32[]{:S(2)}, u32[]{:S(2)}) collective-permute-start(f32[4,64,256]{2,1,0:T(8,128)S(1)} %pad_maximum_fusion.2), channel_id=1, source_target_pairs={{2,0},{4,2},{6,4},{0,6},{3,1},{5,3},{7,5},{1,7},{10,8},{12,10},{14... | collective-permute-start | bytes 786440 | tf_op jit(solution)/shard_map/ppermute | solution.py:366
  25.9 12.8 %collective-permute-start.4 = (f32[4,64,256]{2,1,0:T(8,128)S(1)}, f32[4,64,256]{2,1,0:T(8,128)S(1)}, u32[]{:S(2)}, u32[]{:S(2)}) collective-permute-start(f32[4,64,256]{2,1,0:T(8,128)S(1)} %pad_maximum_fusion.1), channel_id=1, source_target_pairs={{0,2},{2,4},{4,6},{6,0},{1,3},{3,5},{5,7},{7,1},{8,10},{10,12},{12... | collective-permute-start | bytes 786440 | tf_op jit(solution)/shard_map/ppermute | solution.py:365
  29.5 1.2 %collective-permute-start.8 = (f32[8,128]{1,0:T(8,128)S(1)}, f32[8,128]{1,0:T(8,128)S(1)}, u32[]{:S(2)}, u32[]{:S(2)}) collective-permute-start(f32[8,128]{1,0:T(8,128)S(1)} %first_sums.1), channel_id=1, source_target_pairs={{0,1},{1,0},{2,3},{3,2},{4,5},{5,4},{6,7},{7,6},{8,9},{9,8},{10,11... | collective-permute-start | bytes 12296 | tf_op jit(solution)/shard_map/ppermute | solution.py:387
  30.7 7.1 %collective-permute-start.9 = (f32[8,128]{1,0:T(8,128)S(1)}, f32[8,128]{1,0:T(8,128)S(1)}, u32[]{:S(2)}, u32[]{:S(2)}) collective-permute-start(f32[8,128]{1,0:T(8,128)S(1)} %add.18), channel_id=1, source_target_pairs={{0,2},{2,0},{4,6},{6,4},{1,3},{3,1},{5,7},{7,5},{8,10},{10,8},{12,... | collective-permute-start | bytes 12296 | tf_op jit(solution)/shard_map/ppermute | solution.py:387
  38.8 6.1 %collective-permute-start.13 = (f32[40,16,256]{2,1,0:T(8,128)S(1)}, f32[40,16,256]{2,1,0:T(8,128)S(1)}, u32[]{:S(2)}, u32[]{:S(2)}) collective-permute-start(f32[40,16,256]{2,1,0:T(8,128)S(1)} %maximum_dynamic-update-slice_fusion.2), channel_id=1, source_target_pairs={{0,1},{1,0},{2,3},{3,2},{4,5},{5,4},{6,7},{7,6},{8,9},{9,8},{10,11... | collective-permute-start | bytes 1966088 | tf_op jit(solution)/shard_map/ppermute | solution.py:373
  38.9 4.6 %collective-permute-start.10 = (f32[8,128]{1,0:T(8,128)S(1)}, f32[8,128]{1,0:T(8,128)S(1)}, u32[]{:S(2)}, u32[]{:S(2)}) collective-permute-start(f32[8,128]{1,0:T(8,128)S(1)} %add.19), channel_id=1, source_target_pairs={{0,4},{2,6},{4,0},{6,2},{1,5},{3,7},{5,1},{7,3},{8,12},{10,14},{12... | collective-permute-start | bytes 12296 | tf_op jit(solution)/shard_map/ppermute | solution.py:387
  43.5 7.2 %collective-permute-start.11 = (f32[8,128]{1,0:T(8,128)S(1)}, f32[8,128]{1,0:T(8,128)S(1)}, u32[]{:S(2)}, u32[]{:S(2)}) collective-permute-start(f32[8,128]{1,0:T(8,128)S(1)} %add.20.sums), channel_id=1, source_target_pairs={{0,8},{8,0},{1,9},{9,1},{2,10},{10,2},{3,11},{11,3},{4,12},{12,4},... | collective-permute-start | bytes 12296 | tf_op jit(solution)/shard_map/ppermute | solution.py:460
  51.3 1.2 %collective-permute-start.14 = (f32[8,128]{1,0:T(8,128)S(1)}, f32[8,128]{1,0:T(8,128)S(1)}, u32[]{:S(2)}, u32[]{:S(2)}) collective-permute-start(f32[8,128]{1,0:T(8,128)S(1)} %second_sums.1), channel_id=1, source_target_pairs={{0,1},{1,0},{2,3},{3,2},{4,5},{5,4},{6,7},{7,6},{8,9},{9,8},{10,11... | collective-permute-start | bytes 12296 | tf_op jit(solution)/shard_map/ppermute | solution.py:387
  52.5 3.6 %collective-permute-start.15 = (f32[8,128]{1,0:T(8,128)S(1)}, f32[8,128]{1,0:T(8,128)S(1)}, u32[]{:S(2)}, u32[]{:S(2)}) collective-permute-start(f32[8,128]{1,0:T(8,128)S(1)} %add.21), channel_id=1, source_target_pairs={{0,2},{2,0},{4,6},{6,4},{1,3},{3,1},{5,7},{7,5},{8,10},{10,8},{12,... | collective-permute-start | bytes 12296 | tf_op jit(solution)/shard_map/ppermute | solution.py:387
  56.1 4.5 %collective-permute-start.16 = (f32[8,128]{1,0:T(8,128)S(1)}, f32[8,128]{1,0:T(8,128)S(1)}, u32[]{:S(2)}, u32[]{:S(2)}) collective-permute-start(f32[8,128]{1,0:T(8,128)S(1)} %add.22), channel_id=1, source_target_pairs={{0,4},{2,6},{4,0},{6,2},{1,5},{3,7},{5,1},{7,3},{8,12},{10,14},{12... | collective-permute-start | bytes 12296 | tf_op jit(solution)/shard_map/ppermute | solution.py:387

commit v12 on v11

--- a/solution.py
+++ b/solution.py
@@ -185,12 +185,16 @@
         c.wait()
 
 
-def send_kernel(images, edges, middle, sems):
+def send_first_kernel(images, first, sems):
+    which = 1 - lax.axis_index("image")
+    all_copied([(images.at[which, pl.ds(0, AHEAD)], first)], sems)
+
+
+def send_kernel(images, last, middle, sems):
     which = 1 - lax.axis_index("image")
     nz = images.shape[1]
     pairs = [
-        (images.at[which, pl.ds(0, AHEAD)], edges.at[pl.ds(0, AHEAD)]),
-        (images.at[which, pl.ds(nz - AHEAD, AHEAD)], edges.at[pl.ds(AHEAD, AHEAD)]),
+        (images.at[which, pl.ds(nz - AHEAD, AHEAD)], last),
         (images.at[which, pl.ds(AHEAD, nz - 2 * AHEAD)], middle),
     ]
     all_copied(pairs, sems)
@@ -400,10 +404,14 @@
 
     thin = shape(4, ny, nx)
     source = pltpu.with_memory_space_constraint(images, pltpu.HBM)
-    edges, middle = call(
+    few = shape(AHEAD, ny, nx)
+    first = call(
+        send_first_kernel, few, [DMA((1,))], "send_first", in_specs=[ANY], out_specs=ANY
+    )(source)
+    last, middle = call(
         send_kernel,
-        [shape(2 * AHEAD, ny, nx), shape(nz - 2 * AHEAD, ny, nx)],
-        [DMA((3,))],
+        [few, shape(nz - 2 * AHEAD, ny, nx)],
+        [DMA((2,))],
         "send",
         in_specs=[ANY],
         out_specs=[ANY] * 2,
@@ -417,8 +425,8 @@
         out_specs=[ANY] * 4,
     )(source)
 
-    o_first = lax.ppermute(edges[:AHEAD], "image", SWAP)
-    o_last = lax.ppermute(edges[AHEAD:], "image", SWAP)
+    o_first = lax.ppermute(first, "image", SWAP)
+    o_last = lax.ppermute(last, "image", SWAP)
     o_middle = lax.ppermute(middle, "image", SWAP)
     far = lax.ppermute(end, "image", SWAP)
 

time: 62.5 us -> 63 us (level)
  starting transfers between devices: 22.1 us -> 19.7 us
  waiting for transfers between devices: 25 us -> 27 us
  Pallas kernels: 14.1 us -> 15 us
    ppermute x6, waiting for transfers between devices: 13.6 us -> 15.9 us  [summed(): sums = sums + lax.ppermute(sums, axis, pairs)]
    ppermute x6, starting transfers between devices: 8.68 us -> 6.33 us  [summed(): sums = sums + lax.ppermute(sums, axis, pairs)]
    pallas_call x1 -> x2, Pallas kernels: 1.31 us -> 2.15 us  [the longest x1 1.23 us: body_pair(): call(send_kernel, [few, shape(nz - 2 * AHEAD, ny, nx)], [DMA((2,))], 'sen...]
  transfers between devices with their start and end apart: 17 -> 17, of which waited for: 11 -> 9; matrix products, arithmetic and copies ran while one was open for 0% -> 0% of each run, Pallas kernels for 17% -> 17%
where the time goes in v12:
time: 63 us; the launch traced here: 62.9 us
  waiting for transfers between devices  27 us (43%)
  starting transfers between devices  19.7 us (31%)
  Pallas kernels  15 us (24%)
  between operations  0.88 us (1%)
    ppermute x6, waiting for transfers between devices, summed(): sums = sums + lax.ppermute(sums, axis, pairs)  15.9 us
    ppermute x2, waiting for transfers between devices, from_z(): lax.ppermute(up, 'space', [(i, (i + 1) % count) for i in range(count)])  8 us
    ppermute x6, starting transfers between devices, summed(): sums = sums + lax.ppermute(sums, axis, pairs)  6.33 us
    ppermute x2, starting transfers between devices, from_z(): lax.ppermute(down, 'space', [((i + 1) % count, i) for i in range(count)])  4.41 us
    pallas_call x1, Pallas kernels, body_pair(): call(first_step_kernel, [outer, block], [room(nz + 8), room(nz + 6)], 'fi...  3.06 us
    ppermute x2, waiting for transfers between devices, from_z(): lax.ppermute(down, 'space', [((i + 1) % count, i) for i in range(count)])  3.04 us
    ppermute x1, starting transfers between devices, body_pair(): o_first = lax.ppermute(first, 'image', SWAP)  3 us
    pallas_call x1, Pallas kernels, body_pair(): call(second_step_kernel, [block] * 3 + [whole], [room(nz + 4), room(nz +...  2.67 us
  transfers between devices with their start and end apart: 17, of which 9 were waited for; matrix products, arithmetic and copies ran while one was open for 0% of the time, Pallas kernels for 17%

profile of v12, /device:TPU:0, one launch (start us, length us, event | category | flops | bytes accessed | tf_op | source)
XLA Modules:
  0.0 62.9 jit_solution(2154565169381655142)
XLA Ops:
  0.6 0.9 %send_first.1 = f32[2,64,256]{2,1,0:T(8,128)S(1)} custom-call(f32[2,16,64,256]{3,2,1,0:T(8,128)} %images.5), custom_call_target="tpu_custom_call" | custom-call | tf_op jit(solution)/shard_map/send_first/pallas_call | solution.py:408
  1.6 3.0 %collective-permute-start = (f32[2,64,256]{2,1,0:T(8,128)S(1)}, f32[2,64,256]{2,1,0:T(8,128)S(1)}, u32[]{:S(2)}, u32[]{:S(2)}) collective-permute-start(f32[2,64,256]{2,1,0:T(8,128)S(1)} %send_first.1), channel_id=1, source_target_pairs={{0,8},{8,0},{1,9},{9,1},{2,10},{10,2},{3,11},{11,3},{4,12},{12,4},... | collective-permute-start | bytes 393224 | tf_op jit(solution)/shard_map/ppermute | solution.py:428
  4.6 1.2 %send.1 = (f32[2,64,256]{2,1,0:T(8,128)S(1)}, f32[12,64,256]{2,1,0:T(8,128)S(1)}) custom-call(f32[2,16,64,256]{3,2,1,0:T(8,128)} %images.5), custom_call_target="tpu_custom_call" | custom-call | tf_op jit(solution)/shard_map/send/pallas_call | solution.py:411
  5.8 0.1 collective-permute-start.1
  5.9 2.0 %collective-permute-start.6 = (f32[12,64,256]{2,1,0:T(8,128)S(1)}, f32[12,64,256]{2,1,0:T(8,128)S(1)}, u32[]{:S(2)}, u32[]{:S(2)}) collective-permute-start(f32[12,64,256]{2,1,0:T(8,128)S(1)} %get-tuple-element.31), channel_id=1, source_target_pairs={{0,8},{8,0},{1,9},{9,1},{2,10},{10,2},{3,11},{11,3},{4,12},{12,4},... | collective-permute-start | bytes 2359304 | tf_op jit(solution)/shard_map/ppermute | solution.py:430
  7.9 1.7 %keep.1 = (f32[16,64,256]{2,1,0:T(8,128)S(1)}, f32[16,64,256]{2,1,0:T(8,128)S(1)}, f32[4,64,256]{2,1,0:T(8,128)S(1)}, f32[4,64,256]{2,1,0:T(8,128)S(1)}) custom-call(f32[2,16,64,256]{3,2,1,0:T(8,128)} %images.5), custom_call_target="tpu_custom_call" | custom-call | tf_op jit(solution)/shard_map/keep/pallas_call | solution.py:419
  9.6 0.1 collective-permute-start.12
  9.8 0.0 collective-permute-done
  9.8 2.1 %collective-permute-start.2 = (f32[4,64,256]{2,1,0:T(8,128)S(1)}, f32[4,64,256]{2,1,0:T(8,128)S(1)}, u32[]{:S(2)}, u32[]{:S(2)}) collective-permute-start(f32[4,64,256]{2,1,0:T(8,128)S(1)} %get-tuple-element.27), channel_id=1, source_target_pairs={{0,2},{2,4},{4,6},{6,0},{1,3},{3,5},{5,7},{7,1},{8,10},{10,12},{12... | collective-permute-start | bytes 786440 | tf_op jit(solution)/shard_map/ppermute | solution.py:369
  11.9 2.1 %collective-permute-start.3 = (f32[4,64,256]{2,1,0:T(8,128)S(1)}, f32[4,64,256]{2,1,0:T(8,128)S(1)}, u32[]{:S(2)}, u32[]{:S(2)}) collective-permute-start(f32[4,64,256]{2,1,0:T(8,128)S(1)} %get-tuple-element.28), channel_id=1, source_target_pairs={{2,0},{4,2},{6,4},{0,6},{3,1},{5,3},{7,5},{1,7},{10,8},{12,10},{14... | collective-permute-start | bytes 786440 | tf_op jit(solution)/shard_map/ppermute | solution.py:370
  14.0 0.0 collective-permute-done.1
  14.1 7.2 %collective-permute-done.2.low = f32[4,64,256]{2,1,0:T(8,128)S(1)} collective-permute-done((f32[4,64,256]{2,1,0:T(8,128)S(1)}, f32[4,64,256]{2,1,0:T(8,128)S(1)}, u32[]{:S(2)}, u32[]{:S(2)}) %collective-permute-start.2) | collective-permute-done | bytes 262176 | tf_op jit(solution)/shard_map/ppermute | solution.py:369
  21.2 3.0 %collective-permute-done.3.high = f32[4,64,256]{2,1,0:T(8,128)S(1)} collective-permute-done((f32[4,64,256]{2,1,0:T(8,128)S(1)}, f32[4,64,256]{2,1,0:T(8,128)S(1)}, u32[]{:S(2)}, u32[]{:S(2)}) %collective-permute-start.3) | collective-permute-done | bytes 262176 | tf_op jit(solution)/shard_map/ppermute | solution.py:370
  24.3 0.1 collective-permute-start.7
  24.4 2.3 %collective-permute-start.5 = (f32[4,64,256]{2,1,0:T(8,128)S(1)}, f32[4,64,256]{2,1,0:T(8,128)S(1)}, u32[]{:S(2)}, u32[]{:S(2)}) collective-permute-start(f32[4,64,256]{2,1,0:T(8,128)S(1)} %pad_maximum_fusion.2), channel_id=1, source_target_pairs={{2,0},{4,2},{6,4},{0,6},{3,1},{5,3},{7,5},{1,7},{10,8},{12,10},{14... | collective-permute-start | bytes 786440 | tf_op jit(solution)/shard_map/ppermute | solution.py:370
  26.8 0.1 collective-permute-start.4
  26.8 0.0 collective-permute-done.7.sides
  26.8 3.1 %first_step.1 = (f32[20,80,256]{2,1,0:T(8,128)S(1)}, f32[16,64,256]{2,1,0:T(8,128)S(1)}) custom-call(f32[16,64,256]{2,1,0:T(8,128)S(1)} %get-tuple-element.32.mine, f32[4,64,256]{2,1,0:T(8,128)S(1)} %collective-permute-done.2.low, f32[4,64,256]{2,1,0:T(8,128)S(1)} %collective-permute-done.3.high, f32[24,16,256]{2,1,0:T(8,128)S(1)} %collective-permute-done.7.sides), custom_call_target="tpu_custom_call" | custom-call | tf_op jit(solution)/shard_map/first_step/pallas_call | solution.py:437
  29.9 0.0 collective-permute-done.6.middle
  29.9 0.4 first_sums.1
  30.4 0.3 collective-permute-start.8
  30.6 0.9 %collective-permute-done.8 = f32[8,128]{1,0:T(8,128)S(1)} collective-permute-done((f32[8,128]{1,0:T(8,128)S(1)}, f32[8,128]{1,0:T(8,128)S(1)}, u32[]{:S(2)}, u32[]{:S(2)}) %collective-permute-start.8) | collective-permute-done | bytes 4128 | tf_op jit(solution)/shard_map/ppermute | solution.py:391
  31.6 0.8 %collective-permute-start.9 = (f32[8,128]{1,0:T(8,128)S(1)}, f32[8,128]{1,0:T(8,128)S(1)}, u32[]{:S(2)}, u32[]{:S(2)}) collective-permute-start(f32[8,128]{1,0:T(8,128)S(1)} %add.18), channel_id=1, source_target_pairs={{0,2},{2,0},{4,6},{6,4},{1,3},{3,1},{5,7},{7,5},{8,10},{10,8},{12,... | collective-permute-start | bytes 12296 | tf_op jit(solution)/shard_map/ppermute | solution.py:391
  32.4 6.3 %collective-permute-done.9 = f32[8,128]{1,0:T(8,128)S(1)} collective-permute-done((f32[8,128]{1,0:T(8,128)S(1)}, f32[8,128]{1,0:T(8,128)S(1)}, u32[]{:S(2)}, u32[]{:S(2)}) %collective-permute-start.9) | collective-permute-done | bytes 4128 | tf_op jit(solution)/shard_map/ppermute | solution.py:391
  38.7 0.0 collective-permute-done.5.high
  38.7 0.8 %collective-permute-done.4.low = f32[4,64,256]{2,1,0:T(8,128)S(1)} collective-permute-done((f32[4,64,256]{2,1,0:T(8,128)S(1)}, f32[4,64,256]{2,1,0:T(8,128)S(1)}, u32[]{:S(2)}, u32[]{:S(2)}) %collective-permute-start.4) | collective-permute-done | bytes 262176 | tf_op jit(solution)/shard_map/ppermute | solution.py:369
  39.7 0.1 collective-permute-start.13
  39.8 1.6 %collective-permute-start.10 = (f32[8,128]{1,0:T(8,128)S(1)}, f32[8,128]{1,0:T(8,128)S(1)}, u32[]{:S(2)}, u32[]{:S(2)}) collective-permute-start(f32[8,128]{1,0:T(8,128)S(1)} %add.19), channel_id=1, source_target_pairs={{0,4},{2,6},{4,0},{6,2},{1,5},{3,7},{5,1},{7,3},{8,12},{10,14},{12... | collective-permute-start | bytes 12296 | tf_op jit(solution)/shard_map/ppermute | solution.py:391
  41.4 3.0 %collective-permute-done.10 = f32[8,128]{1,0:T(8,128)S(1)} collective-permute-done((f32[8,128]{1,0:T(8,128)S(1)}, f32[8,128]{1,0:T(8,128)S(1)}, u32[]{:S(2)}, u32[]{:S(2)}) %collective-permute-start.10) | collective-permute-done | bytes 4128 | tf_op jit(solution)/shard_map/ppermute | solution.py:391
  44.4 1.5 %collective-permute-start.11 = (f32[8,128]{1,0:T(8,128)S(1)}, f32[8,128]{1,0:T(8,128)S(1)}, u32[]{:S(2)}, u32[]{:S(2)}) collective-permute-start(f32[8,128]{1,0:T(8,128)S(1)} %add.20.sums), channel_id=1, source_target_pairs={{0,8},{8,0},{1,9},{9,1},{2,10},{10,2},{3,11},{11,3},{4,12},{12,4},... | collective-permute-start | bytes 12296 | tf_op jit(solution)/shard_map/ppermute | solution.py:468
  45.9 0.0 collective-permute-done.13.sides
  45.9 2.6 %other_step.1 = (f32[16,64,256]{2,1,0:T(8,128)S(1)}, f32[20,80,256]{2,1,0:T(8,128)S(1)}) custom-call(f32[4,64,256]{2,1,0:T(8,128)S(1)} %pad_maximum_fusion.edges, f32[12,64,256]{2,1,0:T(8,128)S(1)} %collective-permute-done.6.middle, f32[16,64,256]{2,1,0:T(8,128)S(1)} %get-tuple-element.30.end, f32[4,64,256]{2,1,0:T(8,128)S(1)} %collective-permute-done.4.low, ...), custom_call_target="tpu_custom_call" | custom-call | tf_op jit(solution)/shard_map/other_step/pallas_call | solution.py:454
  48.5 2.7 %second_step.1 = (f32[16,64,256]{2,1,0:T(8,128)S(1)}, f32[16,64,256]{2,1,0:T(8,128)S(1)}, f32[16,64,256]{2,1,0:T(8,128)S(1)}, f32[2,16,64,256]{3,2,1,0:T(8,128)}) custom-call(f32[8,128]{1,0:T(8,128)S(1)} %add.20.sums, f32[20,80,256]{2,1,0:T(8,128)S(1)} %get-tuple-element.38.step, f32[20,80,256]{2,1,0:T(8,128)S(1)} %get-tuple-element.39.tangent_wide, ...), custom_call_target="tpu_custom_call" | custom-call | tf_op jit(solution)/shard_map/second_step/pallas_call | solution.py:459
  51.2 0.0 collective-permute-done.11.o_sums
  51.2 0.0 collective-permute-done.12.far
  51.2 0.6 second_sums.1
  51.8 0.1 collective-permute-start.14
  51.9 1.2 %collective-permute-done.14 = f32[8,128]{1,0:T(8,128)S(1)} collective-permute-done((f32[8,128]{1,0:T(8,128)S(1)}, f32[8,128]{1,0:T(8,128)S(1)}, u32[]{:S(2)}, u32[]{:S(2)}) %collective-permute-start.14) | collective-permute-done | bytes 4128 | tf_op jit(solution)/shard_map/ppermute | solution.py:391
  53.0 1.6 %collective-permute-start.15 = (f32[8,128]{1,0:T(8,128)S(1)}, f32[8,128]{1,0:T(8,128)S(1)}, u32[]{:S(2)}, u32[]{:S(2)}) collective-permute-start(f32[8,128]{1,0:T(8,128)S(1)} %add.21), channel_id=1, source_target_pairs={{0,2},{2,0},{4,6},{6,4},{1,3},{3,1},{5,7},{7,5},{8,10},{10,8},{12,... | collective-permute-start | bytes 12296 | tf_op jit(solution)/shard_map/ppermute | solution.py:391
  54.7 2.0 %collective-permute-done.15 = f32[8,128]{1,0:T(8,128)S(1)} collective-permute-done((f32[8,128]{1,0:T(8,128)S(1)}, f32[8,128]{1,0:T(8,128)S(1)}, u32[]{:S(2)}, u32[]{:S(2)}) %collective-permute-start.15) | collective-permute-done | bytes 4128 | tf_op jit(solution)/shard_map/ppermute | solution.py:391
  56.6 1.9 %collective-permute-start.16 = (f32[8,128]{1,0:T(8,128)S(1)}, f32[8,128]{1,0:T(8,128)S(1)}, u32[]{:S(2)}, u32[]{:S(2)}) collective-permute-start(f32[8,128]{1,0:T(8,128)S(1)} %add.22), channel_id=1, source_target_pairs={{0,4},{2,6},{4,0},{6,2},{1,5},{3,7},{5,1},{7,3},{8,12},{10,14},{12... | collective-permute-start | bytes 12296 | tf_op jit(solution)/shard_map/ppermute | solution.py:391
  58.6 2.6 %collective-permute-done.16 = f32[8,128]{1,0:T(8,128)S(1)} collective-permute-done((f32[8,128]{1,0:T(8,128)S(1)}, f32[8,128]{1,0:T(8,128)S(1)}, u32[]{:S(2)}, u32[]{:S(2)}) %collective-permute-start.16) | collective-permute-done | bytes 4128 | tf_op jit(solution)/shard_map/ppermute | solution.py:391
  61.1 1.7 %last.1 = (f32[2,16,64,256]{3,2,1,0:T(8,128)}, f32[2]{0:T(128)}) custom-call(f32[8,128]{1,0:T(8,128)S(1)} %add.23.sums, f32[8,128]{1,0:T(8,128)S(1)} %collective-permute-done.11.o_sums, f32[16,64,256]{2,1,0:T(8,128)S(1)} %collective-permute-done.12.far, f32[16,64,256]{2,1,0:T(8,128)S(1)} %get-tuple-element.32.mine, ...), custom_call_target="tpu_custom_call", output_to_operand_aliasing={{0}: (6, {})} | custom-call | tf_op jit(solution)/shard_map/last/pallas_call | solution.py:473
  (27 shorter events, 0.3 us)
Async XLA Ops:
  1.6 8.3 %collective-permute-start = (f32[2,64,256]{2,1,0:T(8,128)S(1)}, f32[2,64,256]{2,1,0:T(8,128)S(1)}, u32[]{:S(2)}, u32[]{:S(2)}) collective-permute-start(f32[2,64,256]{2,1,0:T(8,128)S(1)} %send_first.1), channel_id=1, source_target_pairs={{0,8},{8,0},{1,9},{9,1},{2,10},{10,2},{3,11},{11,3},{4,12},{12,4},... | collective-permute-start | bytes 393224 | tf_op jit(solution)/shard_map/ppermute | solution.py:428
  5.8 8.3 %collective-permute-start.1 = (f32[2,64,256]{2,1,0:T(8,128)S(1)}, f32[2,64,256]{2,1,0:T(8,128)S(1)}, u32[]{:S(2)}, u32[]{:S(2)}) collective-permute-start(f32[2,64,256]{2,1,0:T(8,128)S(1)} %get-tuple-element.26), channel_id=1, source_target_pairs={{0,8},{8,0},{1,9},{9,1},{2,10},{10,2},{3,11},{11,3},{4,12},{12,4},... | collective-permute-start | bytes 393224 | tf_op jit(solution)/shard_map/ppermute | solution.py:429
  5.9 24.0 %collective-permute-start.6 = (f32[12,64,256]{2,1,0:T(8,128)S(1)}, f32[12,64,256]{2,1,0:T(8,128)S(1)}, u32[]{:S(2)}, u32[]{:S(2)}) collective-permute-start(f32[12,64,256]{2,1,0:T(8,128)S(1)} %get-tuple-element.31), channel_id=1, source_target_pairs={{0,8},{8,0},{1,9},{9,1},{2,10},{10,2},{3,11},{11,3},{4,12},{12,4},... | collective-permute-start | bytes 2359304 | tf_op jit(solution)/shard_map/ppermute | solution.py:430
  9.6 41.5 %collective-permute-start.12 = (f32[16,64,256]{2,1,0:T(8,128)S(1)}, f32[16,64,256]{2,1,0:T(8,128)S(1)}, u32[]{:S(2)}, u32[]{:S(2)}) collective-permute-start(f32[16,64,256]{2,1,0:T(8,128)S(1)} %get-tuple-element.30.end), channel_id=1, source_target_pairs={{0,8},{8,0},{1,9},{9,1},{2,10},{10,2},{3,11},{11,3},{4,12},{12,4},... | collective-permute-start | bytes 3145736 | tf_op jit(solution)/shard_map/ppermute | solution.py:431
  9.8 11.4 %collective-permute-start.2 = (f32[4,64,256]{2,1,0:T(8,128)S(1)}, f32[4,64,256]{2,1,0:T(8,128)S(1)}, u32[]{:S(2)}, u32[]{:S(2)}) collective-permute-start(f32[4,64,256]{2,1,0:T(8,128)S(1)} %get-tuple-element.27), channel_id=1, source_target_pairs={{0,2},{2,4},{4,6},{6,0},{1,3},{3,5},{5,7},{7,1},{8,10},{10,12},{12... | collective-permute-start | bytes 786440 | tf_op jit(solution)/shard_map/ppermute | solution.py:369
  11.9 12.3 %collective-permute-start.3 = (f32[4,64,256]{2,1,0:T(8,128)S(1)}, f32[4,64,256]{2,1,0:T(8,128)S(1)}, u32[]{:S(2)}, u32[]{:S(2)}) collective-permute-start(f32[4,64,256]{2,1,0:T(8,128)S(1)} %get-tuple-element.28), channel_id=1, source_target_pairs={{2,0},{4,2},{6,4},{0,6},{3,1},{5,3},{7,5},{1,7},{10,8},{12,10},{14... | collective-permute-start | bytes 786440 | tf_op jit(solution)/shard_map/ppermute | solution.py:370
  24.3 2.5 %collective-permute-start.7 = (f32[24,16,256]{2,1,0:T(8,128)S(1)}, f32[24,16,256]{2,1,0:T(8,128)S(1)}, u32[]{:S(2)}, u32[]{:S(2)}) collective-permute-start(f32[24,16,256]{2,1,0:T(8,128)S(1)} %maximum_maximum_fusion), channel_id=1, source_target_pairs={{0,1},{1,0},{2,3},{3,2},{4,5},{5,4},{6,7},{7,6},{8,9},{9,8},{10,11... | collective-permute-start | bytes 1179656 | tf_op jit(solution)/shard_map/ppermute | solution.py:377
  24.4 14.3 %collective-permute-start.5 = (f32[4,64,256]{2,1,0:T(8,128)S(1)}, f32[4,64,256]{2,1,0:T(8,128)S(1)}, u32[]{:S(2)}, u32[]{:S(2)}) collective-permute-start(f32[4,64,256]{2,1,0:T(8,128)S(1)} %pad_maximum_fusion.2), channel_id=1, source_target_pairs={{2,0},{4,2},{6,4},{0,6},{3,1},{5,3},{7,5},{1,7},{10,8},{12,10},{14... | collective-permute-start | bytes 786440 | tf_op jit(solution)/shard_map/ppermute | solution.py:370
  26.8 12.8 %collective-permute-start.4 = (f32[4,64,256]{2,1,0:T(8,128)S(1)}, f32[4,64,256]{2,1,0:T(8,128)S(1)}, u32[]{:S(2)}, u32[]{:S(2)}) collective-permute-start(f32[4,64,256]{2,1,0:T(8,128)S(1)} %pad_maximum_fusion.1), channel_id=1, source_target_pairs={{0,2},{2,4},{4,6},{6,0},{1,3},{3,5},{5,7},{7,1},{8,10},{10,12},{12... | collective-permute-start | bytes 786440 | tf_op jit(solution)/shard_map/ppermute | solution.py:369
  30.4 1.2 %collective-permute-start.8 = (f32[8,128]{1,0:T(8,128)S(1)}, f32[8,128]{1,0:T(8,128)S(1)}, u32[]{:S(2)}, u32[]{:S(2)}) collective-permute-start(f32[8,128]{1,0:T(8,128)S(1)} %first_sums.1), channel_id=1, source_target_pairs={{0,1},{1,0},{2,3},{3,2},{4,5},{5,4},{6,7},{7,6},{8,9},{9,8},{10,11... | collective-permute-start | bytes 12296 | tf_op jit(solution)/shard_map/ppermute | solution.py:391
  31.6 7.1 %collective-permute-start.9 = (f32[8,128]{1,0:T(8,128)S(1)}, f32[8,128]{1,0:T(8,128)S(1)}, u32[]{:S(2)}, u32[]{:S(2)}) collective-permute-start(f32[8,128]{1,0:T(8,128)S(1)} %add.18), channel_id=1, source_target_pairs={{0,2},{2,0},{4,6},{6,4},{1,3},{3,1},{5,7},{7,5},{8,10},{10,8},{12,... | collective-permute-start | bytes 12296 | tf_op jit(solution)/shard_map/ppermute | solution.py:391
  39.7 6.1 %collective-permute-start.13 = (f32[40,16,256]{2,1,0:T(8,128)S(1)}, f32[40,16,256]{2,1,0:T(8,128)S(1)}, u32[]{:S(2)}, u32[]{:S(2)}) collective-permute-start(f32[40,16,256]{2,1,0:T(8,128)S(1)} %maximum_dynamic-update-slice_fusion.2), channel_id=1, source_target_pairs={{0,1},{1,0},{2,3},{3,2},{4,5},{5,4},{6,7},{7,6},{8,9},{9,8},{10,11... | collective-permute-start | bytes 1966088 | tf_op jit(solution)/shard_map/ppermute | solution.py:377
  39.8 4.6 %collective-permute-start.10 = (f32[8,128]{1,0:T(8,128)S(1)}, f32[8,128]{1,0:T(8,128)S(1)}, u32[]{:S(2)}, u32[]{:S(2)}) collective-permute-start(f32[8,128]{1,0:T(8,128)S(1)} %add.19), channel_id=1, source_target_pairs={{0,4},{2,6},{4,0},{6,2},{1,5},{3,7},{5,1},{7,3},{8,12},{10,14},{12... | collective-permute-start | bytes 12296 | tf_op jit(solution)/shard_map/ppermute | solution.py:391
  44.4 6.8 %collective-permute-start.11 = (f32[8,128]{1,0:T(8,128)S(1)}, f32[8,128]{1,0:T(8,128)S(1)}, u32[]{:S(2)}, u32[]{:S(2)}) collective-permute-start(f32[8,128]{1,0:T(8,128)S(1)} %add.20.sums), channel_id=1, source_target_pairs={{0,8},{8,0},{1,9},{9,1},{2,10},{10,2},{3,11},{11,3},{4,12},{12,4},... | collective-permute-start | bytes 12296 | tf_op jit(solution)/shard_map/ppermute | solution.py:468
  51.8 1.2 %collective-permute-start.14 = (f32[8,128]{1,0:T(8,128)S(1)}, f32[8,128]{1,0:T(8,128)S(1)}, u32[]{:S(2)}, u32[]{:S(2)}) collective-permute-start(f32[8,128]{1,0:T(8,128)S(1)} %second_sums.1), channel_id=1, source_target_pairs={{0,1},{1,0},{2,3},{3,2},{4,5},{5,4},{6,7},{7,6},{8,9},{9,8},{10,11... | collective-permute-start | bytes 12296 | tf_op jit(solution)/shard_map/ppermute | solution.py:391
  53.0 3.6 %collective-permute-start.15 = (f32[8,128]{1,0:T(8,128)S(1)}, f32[8,128]{1,0:T(8,128)S(1)}, u32[]{:S(2)}, u32[]{:S(2)}) collective-permute-start(f32[8,128]{1,0:T(8,128)S(1)} %add.21), channel_id=1, source_target_pairs={{0,2},{2,0},{4,6},{6,4},{1,3},{3,1},{5,7},{7,5},{8,10},{10,8},{12,... | collective-permute-start | bytes 12296 | tf_op jit(solution)/shard_map/ppermute | solution.py:391
  56.6 4.5 %collective-permute-start.16 = (f32[8,128]{1,0:T(8,128)S(1)}, f32[8,128]{1,0:T(8,128)S(1)}, u32[]{:S(2)}, u32[]{:S(2)}) collective-permute-start(f32[8,128]{1,0:T(8,128)S(1)} %add.22), channel_id=1, source_target_pairs={{0,4},{2,6},{4,0},{6,2},{1,5},{3,7},{5,1},{7,3},{8,12},{10,14},{12... | collective-permute-start | bytes 12296 | tf_op jit(solution)/shard_map/ppermute | solution.py:391

commit v13 on v11

--- a/solution.py
+++ b/solution.py
@@ -19,7 +19,7 @@
 
 PAD = 8
 VMEM_ROOM = 2 * 2**20
-UNROLL = 4
+UNROLL = 8
 AHEAD = 2
 
 
@@ -339,10 +339,10 @@
     copies = []
     for k in range(nz):
         buf[k] = moved[k] + coef * (near[k] + o_coef * (mine[k] - far[k]))
-        if k % 4 == 3:
-            where = pl.ds(k - 3, 4)
+        if k % 2 == 1:
+            where = pl.ds(k - 1, 2)
             copies.append(
-                pltpu.make_async_copy(buf.at[where], out.at[which, where], sems.at[k // 4])
+                pltpu.make_async_copy(buf.at[where], out.at[which, where], sems.at[k // 2])
             )
             copies[-1].start()
     value = (par / jnp.sqrt(safe * cells))[0, 0]
@@ -465,7 +465,7 @@
     return call(
         functools.partial(last_kernel, cells),
         [whole, shape(2)],
-        [pltpu.VMEM(block.shape, jnp.float32), DMA((nz // 4,))],
+        [pltpu.VMEM(block.shape, jnp.float32), DMA((nz // 2,))],
         "last",
         in_specs=[VMEM] * 6 + [ANY],
         out_specs=[ANY, SMEM],

time: 62.5 us -> 62.5 us (level)
  transfers between devices with their start and end apart: 17 -> 17, of which waited for: 11 -> 11; matrix products, arithmetic and copies ran while one was open for 0% -> 0% of each run, Pallas kernels for 17% -> 16%
where the time goes in v13:
time: 62.5 us; the launch traced here: 62.4 us
  waiting for transfers between devices  25.5 us (41%)
  starting transfers between devices  22.1 us (35%)
  Pallas kernels  13.6 us (22%)
  between operations  0.86 us (1%)
    ppermute x6, waiting for transfers between devices, summed(): sums = sums + lax.ppermute(sums, axis, pairs)  13.6 us
    ppermute x6, starting transfers between devices, summed(): sums = sums + lax.ppermute(sums, axis, pairs)  8.71 us
    ppermute x2, waiting for transfers between devices, from_z(): lax.ppermute(up, 'space', [(i, (i + 1) % count) for i in range(count)])  7.98 us
    ppermute x2, starting transfers between devices, from_z(): lax.ppermute(down, 'space', [((i + 1) % count, i) for i in range(count)])  4.39 us
    pallas_call x1, Pallas kernels, body_pair(): call(first_step_kernel, [outer, block], [room(nz + 8), room(nz + 6)], 'fi...  3.04 us
    ppermute x1, starting transfers between devices, body_pair(): o_first = lax.ppermute(edges[:AHEAD], 'image', SWAP)  3 us
    ppermute x2, waiting for transfers between devices, from_z(): lax.ppermute(down, 'space', [((i + 1) % count, i) for i in range(count)])  2.67 us
    pallas_call x1, Pallas kernels, body_pair(): call(other_step_kernel, [block, outer], [room(nz + 4), room(nz + 2)], 'ot...  2.37 us
  transfers between devices with their start and end apart: 17, of which 11 were waited for; matrix products, arithmetic and copies ran while one was open for 0% of the time, Pallas kernels for 16%

profile of v13, /device:TPU:0, one launch (start us, length us, event | category | flops | bytes accessed | tf_op | source)
XLA Modules:
  0.0 62.4 jit_solution(10211891376489829491)
XLA Ops:
  0.6 1.3 %send.1 = (f32[4,64,256]{2,1,0:T(8,128)S(1)}, f32[12,64,256]{2,1,0:T(8,128)S(1)}) custom-call(f32[2,16,64,256]{3,2,1,0:T(8,128)} %images.3), custom_call_target="tpu_custom_call" | custom-call | tf_op jit(solution)/shard_map/send/pallas_call | solution.py:403
  2.0 3.0 %collective-permute-start = (f32[2,64,256]{2,1,0:T(8,128)S(1)}, f32[2,64,256]{2,1,0:T(8,128)S(1)}, u32[]{:S(2)}, u32[]{:S(2)}) collective-permute-start(f32[2,64,256]{2,1,0:T(8,128)S(1)} %get-tuple-element.70), channel_id=1, source_target_pairs={{0,8},{8,0},{1,9},{9,1},{2,10},{10,2},{3,11},{11,3},{4,12},{12,4},... | collective-permute-start | bytes 393224 | tf_op jit(solution)/shard_map/ppermute | solution.py:420
  5.0 0.1 collective-permute-start.1
  5.1 1.9 %collective-permute-start.6 = (f32[12,64,256]{2,1,0:T(8,128)S(1)}, f32[12,64,256]{2,1,0:T(8,128)S(1)}, u32[]{:S(2)}, u32[]{:S(2)}) collective-permute-start(f32[12,64,256]{2,1,0:T(8,128)S(1)} %get-tuple-element.31), channel_id=1, source_target_pairs={{0,8},{8,0},{1,9},{9,1},{2,10},{10,2},{3,11},{11,3},{4,12},{12,4},... | collective-permute-start | bytes 2359304 | tf_op jit(solution)/shard_map/ppermute | solution.py:422
  7.0 1.7 %keep.1 = (f32[16,64,256]{2,1,0:T(8,128)S(1)}, f32[16,64,256]{2,1,0:T(8,128)S(1)}, f32[4,64,256]{2,1,0:T(8,128)S(1)}, f32[4,64,256]{2,1,0:T(8,128)S(1)}) custom-call(f32[2,16,64,256]{3,2,1,0:T(8,128)} %images.3), custom_call_target="tpu_custom_call" | custom-call | tf_op jit(solution)/shard_map/keep/pallas_call | solution.py:411
  8.8 0.1 collective-permute-start.12
  8.9 0.4 collective-permute-done
  9.3 2.1 %collective-permute-start.2 = (f32[4,64,256]{2,1,0:T(8,128)S(1)}, f32[4,64,256]{2,1,0:T(8,128)S(1)}, u32[]{:S(2)}, u32[]{:S(2)}) collective-permute-start(f32[4,64,256]{2,1,0:T(8,128)S(1)} %get-tuple-element.27), channel_id=1, source_target_pairs={{0,2},{2,4},{4,6},{6,0},{1,3},{3,5},{5,7},{7,1},{8,10},{10,12},{12... | collective-permute-start | bytes 786440 | tf_op jit(solution)/shard_map/ppermute | solution.py:365
  11.5 2.1 %collective-permute-start.3 = (f32[4,64,256]{2,1,0:T(8,128)S(1)}, f32[4,64,256]{2,1,0:T(8,128)S(1)}, u32[]{:S(2)}, u32[]{:S(2)}) collective-permute-start(f32[4,64,256]{2,1,0:T(8,128)S(1)} %get-tuple-element.28), channel_id=1, source_target_pairs={{2,0},{4,2},{6,4},{0,6},{3,1},{5,3},{7,5},{1,7},{10,8},{12,10},{14... | collective-permute-start | bytes 786440 | tf_op jit(solution)/shard_map/ppermute | solution.py:366
  13.6 0.0 collective-permute-done.1
  13.6 7.1 %collective-permute-done.2.low = f32[4,64,256]{2,1,0:T(8,128)S(1)} collective-permute-done((f32[4,64,256]{2,1,0:T(8,128)S(1)}, f32[4,64,256]{2,1,0:T(8,128)S(1)}, u32[]{:S(2)}, u32[]{:S(2)}) %collective-permute-start.2) | collective-permute-done | bytes 262176 | tf_op jit(solution)/shard_map/ppermute | solution.py:365
  20.7 2.7 %collective-permute-done.3.high = f32[4,64,256]{2,1,0:T(8,128)S(1)} collective-permute-done((f32[4,64,256]{2,1,0:T(8,128)S(1)}, f32[4,64,256]{2,1,0:T(8,128)S(1)}, u32[]{:S(2)}, u32[]{:S(2)}) %collective-permute-start.3) | collective-permute-done | bytes 262176 | tf_op jit(solution)/shard_map/ppermute | solution.py:366
  23.4 0.1 collective-permute-start.7
  23.6 2.3 %collective-permute-start.5 = (f32[4,64,256]{2,1,0:T(8,128)S(1)}, f32[4,64,256]{2,1,0:T(8,128)S(1)}, u32[]{:S(2)}, u32[]{:S(2)}) collective-permute-start(f32[4,64,256]{2,1,0:T(8,128)S(1)} %pad_maximum_fusion.2), channel_id=1, source_target_pairs={{2,0},{4,2},{6,4},{0,6},{3,1},{5,3},{7,5},{1,7},{10,8},{12,10},{14... | collective-permute-start | bytes 786440 | tf_op jit(solution)/shard_map/ppermute | solution.py:366
  25.9 0.1 collective-permute-start.4
  25.9 0.0 collective-permute-done.7.sides
  26.0 3.0 %first_step.1 = (f32[20,80,256]{2,1,0:T(8,128)S(1)}, f32[16,64,256]{2,1,0:T(8,128)S(1)}) custom-call(f32[16,64,256]{2,1,0:T(8,128)S(1)} %get-tuple-element.32.mine, f32[4,64,256]{2,1,0:T(8,128)S(1)} %collective-permute-done.2.low, f32[4,64,256]{2,1,0:T(8,128)S(1)} %collective-permute-done.3.high, f32[24,16,256]{2,1,0:T(8,128)S(1)} %collective-permute-done.7.sides), custom_call_target="tpu_custom_call" | custom-call | tf_op jit(solution)/shard_map/first_step/pallas_call | solution.py:429
  29.0 0.0 collective-permute-done.6.middle
  29.0 0.4 first_sums.1
  29.4 0.3 collective-permute-start.8
  29.7 0.9 %collective-permute-done.8 = f32[8,128]{1,0:T(8,128)S(1)} collective-permute-done((f32[8,128]{1,0:T(8,128)S(1)}, f32[8,128]{1,0:T(8,128)S(1)}, u32[]{:S(2)}, u32[]{:S(2)}) %collective-permute-start.8) | collective-permute-done | bytes 4128 | tf_op jit(solution)/shard_map/ppermute | solution.py:387
  30.7 2.1 %collective-permute-start.9 = (f32[8,128]{1,0:T(8,128)S(1)}, f32[8,128]{1,0:T(8,128)S(1)}, u32[]{:S(2)}, u32[]{:S(2)}) collective-permute-start(f32[8,128]{1,0:T(8,128)S(1)} %add.18), channel_id=1, source_target_pairs={{0,2},{2,0},{4,6},{6,4},{1,3},{3,1},{5,7},{7,5},{8,10},{10,8},{12,... | collective-permute-start | bytes 12296 | tf_op jit(solution)/shard_map/ppermute | solution.py:387
  32.8 5.0 %collective-permute-done.9 = f32[8,128]{1,0:T(8,128)S(1)} collective-permute-done((f32[8,128]{1,0:T(8,128)S(1)}, f32[8,128]{1,0:T(8,128)S(1)}, u32[]{:S(2)}, u32[]{:S(2)}) %collective-permute-start.9) | collective-permute-done | bytes 4128 | tf_op jit(solution)/shard_map/ppermute | solution.py:387
  37.8 0.0 collective-permute-done.5.high
  37.8 0.8 %collective-permute-done.4.low = f32[4,64,256]{2,1,0:T(8,128)S(1)} collective-permute-done((f32[4,64,256]{2,1,0:T(8,128)S(1)}, f32[4,64,256]{2,1,0:T(8,128)S(1)}, u32[]{:S(2)}, u32[]{:S(2)}) %collective-permute-start.4) | collective-permute-done | bytes 262176 | tf_op jit(solution)/shard_map/ppermute | solution.py:365
  38.8 0.1 collective-permute-start.13
  38.9 1.6 %collective-permute-start.10 = (f32[8,128]{1,0:T(8,128)S(1)}, f32[8,128]{1,0:T(8,128)S(1)}, u32[]{:S(2)}, u32[]{:S(2)}) collective-permute-start(f32[8,128]{1,0:T(8,128)S(1)} %add.19), channel_id=1, source_target_pairs={{0,4},{2,6},{4,0},{6,2},{1,5},{3,7},{5,1},{7,3},{8,12},{10,14},{12... | collective-permute-start | bytes 12296 | tf_op jit(solution)/shard_map/ppermute | solution.py:387
  40.5 3.0 %collective-permute-done.10 = f32[8,128]{1,0:T(8,128)S(1)} collective-permute-done((f32[8,128]{1,0:T(8,128)S(1)}, f32[8,128]{1,0:T(8,128)S(1)}, u32[]{:S(2)}, u32[]{:S(2)}) %collective-permute-start.10) | collective-permute-done | bytes 4128 | tf_op jit(solution)/shard_map/ppermute | solution.py:387
  43.5 1.5 %collective-permute-start.11 = (f32[8,128]{1,0:T(8,128)S(1)}, f32[8,128]{1,0:T(8,128)S(1)}, u32[]{:S(2)}, u32[]{:S(2)}) collective-permute-start(f32[8,128]{1,0:T(8,128)S(1)} %add.20.sums), channel_id=1, source_target_pairs={{0,8},{8,0},{1,9},{9,1},{2,10},{10,2},{3,11},{11,3},{4,12},{12,4},... | collective-permute-start | bytes 12296 | tf_op jit(solution)/shard_map/ppermute | solution.py:460
  45.0 0.0 collective-permute-done.13.sides
  45.0 2.4 %other_step.1 = (f32[16,64,256]{2,1,0:T(8,128)S(1)}, f32[20,80,256]{2,1,0:T(8,128)S(1)}) custom-call(f32[4,64,256]{2,1,0:T(8,128)S(1)} %pad_maximum_fusion.edges, f32[12,64,256]{2,1,0:T(8,128)S(1)} %collective-permute-done.6.middle, f32[16,64,256]{2,1,0:T(8,128)S(1)} %get-tuple-element.30.end, f32[4,64,256]{2,1,0:T(8,128)S(1)} %collective-permute-done.4.low, ...), custom_call_target="tpu_custom_call" | custom-call | tf_op jit(solution)/shard_map/other_step/pallas_call | solution.py:446
  47.4 2.4 %second_step.1 = (f32[16,64,256]{2,1,0:T(8,128)S(1)}, f32[16,64,256]{2,1,0:T(8,128)S(1)}, f32[16,64,256]{2,1,0:T(8,128)S(1)}, f32[2,16,64,256]{3,2,1,0:T(8,128)}) custom-call(f32[8,128]{1,0:T(8,128)S(1)} %add.20.sums, f32[20,80,256]{2,1,0:T(8,128)S(1)} %get-tuple-element.38.step, f32[20,80,256]{2,1,0:T(8,128)S(1)} %get-tuple-element.39.tangent_wide, ...), custom_call_target="tpu_custom_call" | custom-call | tf_op jit(solution)/shard_map/second_step/pallas_call | solution.py:451
  49.7 1.0 %collective-permute-done.11.o_sums = f32[8,128]{1,0:T(8,128)S(1)} collective-permute-done((f32[8,128]{1,0:T(8,128)S(1)}, f32[8,128]{1,0:T(8,128)S(1)}, u32[]{:S(2)}, u32[]{:S(2)}) %collective-permute-start.11) | collective-permute-done | bytes 4128 | tf_op jit(solution)/shard_map/ppermute | solution.py:460
  50.7 0.0 collective-permute-done.12.far
  50.7 0.6 second_sums.1
  51.3 0.1 collective-permute-start.14
  51.4 1.2 %collective-permute-done.14 = f32[8,128]{1,0:T(8,128)S(1)} collective-permute-done((f32[8,128]{1,0:T(8,128)S(1)}, f32[8,128]{1,0:T(8,128)S(1)}, u32[]{:S(2)}, u32[]{:S(2)}) %collective-permute-start.14) | collective-permute-done | bytes 4128 | tf_op jit(solution)/shard_map/ppermute | solution.py:387
  52.5 1.8 %collective-permute-start.15 = (f32[8,128]{1,0:T(8,128)S(1)}, f32[8,128]{1,0:T(8,128)S(1)}, u32[]{:S(2)}, u32[]{:S(2)}) collective-permute-start(f32[8,128]{1,0:T(8,128)S(1)} %add.21), channel_id=1, source_target_pairs={{0,2},{2,0},{4,6},{6,4},{1,3},{3,1},{5,7},{7,5},{8,10},{10,8},{12,... | collective-permute-start | bytes 12296 | tf_op jit(solution)/shard_map/ppermute | solution.py:387
  54.3 1.8 %collective-permute-done.15 = f32[8,128]{1,0:T(8,128)S(1)} collective-permute-done((f32[8,128]{1,0:T(8,128)S(1)}, f32[8,128]{1,0:T(8,128)S(1)}, u32[]{:S(2)}, u32[]{:S(2)}) %collective-permute-start.15) | collective-permute-done | bytes 4128 | tf_op jit(solution)/shard_map/ppermute | solution.py:387
  56.1 2.8 %collective-permute-start.16 = (f32[8,128]{1,0:T(8,128)S(1)}, f32[8,128]{1,0:T(8,128)S(1)}, u32[]{:S(2)}, u32[]{:S(2)}) collective-permute-start(f32[8,128]{1,0:T(8,128)S(1)} %add.22), channel_id=1, source_target_pairs={{0,4},{2,6},{4,0},{6,2},{1,5},{3,7},{5,1},{7,3},{8,12},{10,14},{12... | collective-permute-start | bytes 12296 | tf_op jit(solution)/shard_map/ppermute | solution.py:387
  59.0 1.7 %collective-permute-done.16 = f32[8,128]{1,0:T(8,128)S(1)} collective-permute-done((f32[8,128]{1,0:T(8,128)S(1)}, f32[8,128]{1,0:T(8,128)S(1)}, u32[]{:S(2)}, u32[]{:S(2)}) %collective-permute-start.16) | collective-permute-done | bytes 4128 | tf_op jit(solution)/shard_map/ppermute | solution.py:387
  60.6 1.7 %last.1 = (f32[2,16,64,256]{3,2,1,0:T(8,128)}, f32[2]{0:T(128)}) custom-call(f32[8,128]{1,0:T(8,128)S(1)} %add.23.sums, f32[8,128]{1,0:T(8,128)S(1)} %collective-permute-done.11.o_sums, f32[16,64,256]{2,1,0:T(8,128)S(1)} %collective-permute-done.12.far, f32[16,64,256]{2,1,0:T(8,128)S(1)} %get-tuple-element.32.mine, ...), custom_call_target="tpu_custom_call", output_to_operand_aliasing={{0}: (6, {})} | custom-call | tf_op jit(solution)/shard_map/last/pallas_call | solution.py:465
  (28 shorter events, 0.3 us)
Async XLA Ops:
  2.0 7.3 %collective-permute-start = (f32[2,64,256]{2,1,0:T(8,128)S(1)}, f32[2,64,256]{2,1,0:T(8,128)S(1)}, u32[]{:S(2)}, u32[]{:S(2)}) collective-permute-start(f32[2,64,256]{2,1,0:T(8,128)S(1)} %get-tuple-element.70), channel_id=1, source_target_pairs={{0,8},{8,0},{1,9},{9,1},{2,10},{10,2},{3,11},{11,3},{4,12},{12,4},... | collective-permute-start | bytes 393224 | tf_op jit(solution)/shard_map/ppermute | solution.py:420
  5.0 8.6 %collective-permute-start.1 = (f32[2,64,256]{2,1,0:T(8,128)S(1)}, f32[2,64,256]{2,1,0:T(8,128)S(1)}, u32[]{:S(2)}, u32[]{:S(2)}) collective-permute-start(f32[2,64,256]{2,1,0:T(8,128)S(1)} %get-tuple-element.71), channel_id=1, source_target_pairs={{0,8},{8,0},{1,9},{9,1},{2,10},{10,2},{3,11},{11,3},{4,12},{12,4},... | collective-permute-start | bytes 393224 | tf_op jit(solution)/shard_map/ppermute | solution.py:421
  5.1 23.9 %collective-permute-start.6 = (f32[12,64,256]{2,1,0:T(8,128)S(1)}, f32[12,64,256]{2,1,0:T(8,128)S(1)}, u32[]{:S(2)}, u32[]{:S(2)}) collective-permute-start(f32[12,64,256]{2,1,0:T(8,128)S(1)} %get-tuple-element.31), channel_id=1, source_target_pairs={{0,8},{8,0},{1,9},{9,1},{2,10},{10,2},{3,11},{11,3},{4,12},{12,4},... | collective-permute-start | bytes 2359304 | tf_op jit(solution)/shard_map/ppermute | solution.py:422
  8.8 41.9 %collective-permute-start.12 = (f32[16,64,256]{2,1,0:T(8,128)S(1)}, f32[16,64,256]{2,1,0:T(8,128)S(1)}, u32[]{:S(2)}, u32[]{:S(2)}) collective-permute-start(f32[16,64,256]{2,1,0:T(8,128)S(1)} %get-tuple-element.30.end), channel_id=1, source_target_pairs={{0,8},{8,0},{1,9},{9,1},{2,10},{10,2},{3,11},{11,3},{4,12},{12,4},... | collective-permute-start | bytes 3145736 | tf_op jit(solution)/shard_map/ppermute | solution.py:423
  9.3 11.4 %collective-permute-start.2 = (f32[4,64,256]{2,1,0:T(8,128)S(1)}, f32[4,64,256]{2,1,0:T(8,128)S(1)}, u32[]{:S(2)}, u32[]{:S(2)}) collective-permute-start(f32[4,64,256]{2,1,0:T(8,128)S(1)} %get-tuple-element.27), channel_id=1, source_target_pairs={{0,2},{2,4},{4,6},{6,0},{1,3},{3,5},{5,7},{7,1},{8,10},{10,12},{12... | collective-permute-start | bytes 786440 | tf_op jit(solution)/shard_map/ppermute | solution.py:365
  11.5 11.9 %collective-permute-start.3 = (f32[4,64,256]{2,1,0:T(8,128)S(1)}, f32[4,64,256]{2,1,0:T(8,128)S(1)}, u32[]{:S(2)}, u32[]{:S(2)}) collective-permute-start(f32[4,64,256]{2,1,0:T(8,128)S(1)} %get-tuple-element.28), channel_id=1, source_target_pairs={{2,0},{4,2},{6,4},{0,6},{3,1},{5,3},{7,5},{1,7},{10,8},{12,10},{14... | collective-permute-start | bytes 786440 | tf_op jit(solution)/shard_map/ppermute | solution.py:366
  23.4 2.5 %collective-permute-start.7 = (f32[24,16,256]{2,1,0:T(8,128)S(1)}, f32[24,16,256]{2,1,0:T(8,128)S(1)}, u32[]{:S(2)}, u32[]{:S(2)}) collective-permute-start(f32[24,16,256]{2,1,0:T(8,128)S(1)} %maximum_maximum_fusion), channel_id=1, source_target_pairs={{0,1},{1,0},{2,3},{3,2},{4,5},{5,4},{6,7},{7,6},{8,9},{9,8},{10,11... | collective-permute-start | bytes 1179656 | tf_op jit(solution)/shard_map/ppermute | solution.py:373
  23.6 14.3 %collective-permute-start.5 = (f32[4,64,256]{2,1,0:T(8,128)S(1)}, f32[4,64,256]{2,1,0:T(8,128)S(1)}, u32[]{:S(2)}, u32[]{:S(2)}) collective-permute-start(f32[4,64,256]{2,1,0:T(8,128)S(1)} %pad_maximum_fusion.2), channel_id=1, source_target_pairs={{2,0},{4,2},{6,4},{0,6},{3,1},{5,3},{7,5},{1,7},{10,8},{12,10},{14... | collective-permute-start | bytes 786440 | tf_op jit(solution)/shard_map/ppermute | solution.py:366
  25.9 12.8 %collective-permute-start.4 = (f32[4,64,256]{2,1,0:T(8,128)S(1)}, f32[4,64,256]{2,1,0:T(8,128)S(1)}, u32[]{:S(2)}, u32[]{:S(2)}) collective-permute-start(f32[4,64,256]{2,1,0:T(8,128)S(1)} %pad_maximum_fusion.1), channel_id=1, source_target_pairs={{0,2},{2,4},{4,6},{6,0},{1,3},{3,5},{5,7},{7,1},{8,10},{10,12},{12... | collective-permute-start | bytes 786440 | tf_op jit(solution)/shard_map/ppermute | solution.py:365
  29.4 1.2 %collective-permute-start.8 = (f32[8,128]{1,0:T(8,128)S(1)}, f32[8,128]{1,0:T(8,128)S(1)}, u32[]{:S(2)}, u32[]{:S(2)}) collective-permute-start(f32[8,128]{1,0:T(8,128)S(1)} %first_sums.1), channel_id=1, source_target_pairs={{0,1},{1,0},{2,3},{3,2},{4,5},{5,4},{6,7},{7,6},{8,9},{9,8},{10,11... | collective-permute-start | bytes 12296 | tf_op jit(solution)/shard_map/ppermute | solution.py:387
  30.7 7.2 %collective-permute-start.9 = (f32[8,128]{1,0:T(8,128)S(1)}, f32[8,128]{1,0:T(8,128)S(1)}, u32[]{:S(2)}, u32[]{:S(2)}) collective-permute-start(f32[8,128]{1,0:T(8,128)S(1)} %add.18), channel_id=1, source_target_pairs={{0,2},{2,0},{4,6},{6,4},{1,3},{3,1},{5,7},{7,5},{8,10},{10,8},{12,... | collective-permute-start | bytes 12296 | tf_op jit(solution)/shard_map/ppermute | solution.py:387
  38.8 6.1 %collective-permute-start.13 = (f32[40,16,256]{2,1,0:T(8,128)S(1)}, f32[40,16,256]{2,1,0:T(8,128)S(1)}, u32[]{:S(2)}, u32[]{:S(2)}) collective-permute-start(f32[40,16,256]{2,1,0:T(8,128)S(1)} %maximum_dynamic-update-slice_fusion.2), channel_id=1, source_target_pairs={{0,1},{1,0},{2,3},{3,2},{4,5},{5,4},{6,7},{7,6},{8,9},{9,8},{10,11... | collective-permute-start | bytes 1966088 | tf_op jit(solution)/shard_map/ppermute | solution.py:373
  38.9 4.6 %collective-permute-start.10 = (f32[8,128]{1,0:T(8,128)S(1)}, f32[8,128]{1,0:T(8,128)S(1)}, u32[]{:S(2)}, u32[]{:S(2)}) collective-permute-start(f32[8,128]{1,0:T(8,128)S(1)} %add.19), channel_id=1, source_target_pairs={{0,4},{2,6},{4,0},{6,2},{1,5},{3,7},{5,1},{7,3},{8,12},{10,14},{12... | collective-permute-start | bytes 12296 | tf_op jit(solution)/shard_map/ppermute | solution.py:387
  43.5 7.2 %collective-permute-start.11 = (f32[8,128]{1,0:T(8,128)S(1)}, f32[8,128]{1,0:T(8,128)S(1)}, u32[]{:S(2)}, u32[]{:S(2)}) collective-permute-start(f32[8,128]{1,0:T(8,128)S(1)} %add.20.sums), channel_id=1, source_target_pairs={{0,8},{8,0},{1,9},{9,1},{2,10},{10,2},{3,11},{11,3},{4,12},{12,4},... | collective-permute-start | bytes 12296 | tf_op jit(solution)/shard_map/ppermute | solution.py:460
  51.3 1.2 %collective-permute-start.14 = (f32[8,128]{1,0:T(8,128)S(1)}, f32[8,128]{1,0:T(8,128)S(1)}, u32[]{:S(2)}, u32[]{:S(2)}) collective-permute-start(f32[8,128]{1,0:T(8,128)S(1)} %second_sums.1), channel_id=1, source_target_pairs={{0,1},{1,0},{2,3},{3,2},{4,5},{5,4},{6,7},{7,6},{8,9},{9,8},{10,11... | collective-permute-start | bytes 12296 | tf_op jit(solution)/shard_map/ppermute | solution.py:387
  52.5 3.6 %collective-permute-start.15 = (f32[8,128]{1,0:T(8,128)S(1)}, f32[8,128]{1,0:T(8,128)S(1)}, u32[]{:S(2)}, u32[]{:S(2)}) collective-permute-start(f32[8,128]{1,0:T(8,128)S(1)} %add.21), channel_id=1, source_target_pairs={{0,2},{2,0},{4,6},{6,4},{1,3},{3,1},{5,7},{7,5},{8,10},{10,8},{12,... | collective-permute-start | bytes 12296 | tf_op jit(solution)/shard_map/ppermute | solution.py:387
  56.1 4.5 %collective-permute-start.16 = (f32[8,128]{1,0:T(8,128)S(1)}, f32[8,128]{1,0:T(8,128)S(1)}, u32[]{:S(2)}, u32[]{:S(2)}) collective-permute-start(f32[8,128]{1,0:T(8,128)S(1)} %add.22), channel_id=1, source_target_pairs={{0,4},{2,6},{4,0},{6,2},{1,5},{3,7},{5,1},{7,3},{8,12},{10,14},{12... | collective-permute-start | bytes 12296 | tf_op jit(solution)/shard_map/ppermute | solution.py:387

commit v14 on v11

--- a/solution.py
+++ b/solution.py
@@ -374,11 +374,12 @@
 
 
 def sum_steps():
-    count, stride = lax.axis_size("space"), 1
+    count = lax.axis_size("space")
+    stride = count // 2
     steps = [("yslab", SWAP)]
-    while stride < count:
+    while stride:
         steps.append(("space", [(i, i ^ stride) for i in range(count)]))
-        stride *= 2
+        stride //= 2
     return steps
 
 

time: 62.5 us -> 62.5 us (level)
  starting transfers between devices: 22.1 us -> 23.1 us
  waiting for transfers between devices: 25 us -> 24 us
    ppermute x6, waiting for transfers between devices: 13.6 us -> 11.7 us  [summed(): sums = sums + lax.ppermute(sums, axis, pairs)]
    ppermute x6, starting transfers between devices: 8.68 us -> 9.69 us  [summed(): sums = sums + lax.ppermute(sums, axis, pairs)]
    ppermute x1, waiting for transfers between devices: 0.41 us -> 1.26 us  [body_pair(): o_sums = lax.ppermute(sums, 'image', SWAP)]
where the time goes in v14:
time: 62.5 us; the launch traced here: 62.4 us
  waiting for transfers between devices  24 us (38%)
  starting transfers between devices  23.1 us (37%)
  Pallas kernels  14.1 us (23%)
  between operations  0.86 us (1%)
    ppermute x6, waiting for transfers between devices, summed(): sums = sums + lax.ppermute(sums, axis, pairs)  11.7 us
    ppermute x6, starting transfers between devices, summed(): sums = sums + lax.ppermute(sums, axis, pairs)  9.69 us
    ppermute x2, waiting for transfers between devices, from_z(): lax.ppermute(up, 'space', [(i, (i + 1) % count) for i in range(count)])  8.02 us
    ppermute x2, starting transfers between devices, from_z(): lax.ppermute(down, 'space', [((i + 1) % count, i) for i in range(count)])  4.39 us
    pallas_call x1, Pallas kernels, body_pair(): call(first_step_kernel, [outer, block], [room(nz + 8), room(nz + 6)], 'fi...  3.06 us
    ppermute x1, starting transfers between devices, body_pair(): o_first = lax.ppermute(edges[:AHEAD], 'image', SWAP)  3 us
    ppermute x2, waiting for transfers between devices, from_z(): lax.ppermute(down, 'space', [((i + 1) % count, i) for i in range(count)])  2.67 us
    pallas_call x1, Pallas kernels, body_pair(): call(second_step_kernel, [block] * 3 + [whole], [room(nz + 4), room(nz +...  2.67 us
  transfers between devices with their start and end apart: 17, of which 11 were waited for; matrix products, arithmetic and copies ran while one was open for 0% of the time, Pallas kernels for 17%

profile of v14, /device:TPU:0, one launch (start us, length us, event | category | flops | bytes accessed | tf_op | source)
XLA Modules:
  0.0 62.4 jit_solution(114095665788973168)
XLA Ops:
  0.6 1.3 %send.1 = (f32[4,64,256]{2,1,0:T(8,128)S(1)}, f32[12,64,256]{2,1,0:T(8,128)S(1)}) custom-call(f32[2,16,64,256]{3,2,1,0:T(8,128)} %images.3), custom_call_target="tpu_custom_call" | custom-call | tf_op jit(solution)/shard_map/send/pallas_call | solution.py:404
  2.0 3.0 %collective-permute-start = (f32[2,64,256]{2,1,0:T(8,128)S(1)}, f32[2,64,256]{2,1,0:T(8,128)S(1)}, u32[]{:S(2)}, u32[]{:S(2)}) collective-permute-start(f32[2,64,256]{2,1,0:T(8,128)S(1)} %get-tuple-element.70), channel_id=1, source_target_pairs={{0,8},{8,0},{1,9},{9,1},{2,10},{10,2},{3,11},{11,3},{4,12},{12,4},... | collective-permute-start | bytes 393224 | tf_op jit(solution)/shard_map/ppermute | solution.py:421
  5.0 0.1 collective-permute-start.1
  5.1 1.9 %collective-permute-start.6 = (f32[12,64,256]{2,1,0:T(8,128)S(1)}, f32[12,64,256]{2,1,0:T(8,128)S(1)}, u32[]{:S(2)}, u32[]{:S(2)}) collective-permute-start(f32[12,64,256]{2,1,0:T(8,128)S(1)} %get-tuple-element.31), channel_id=1, source_target_pairs={{0,8},{8,0},{1,9},{9,1},{2,10},{10,2},{3,11},{11,3},{4,12},{12,4},... | collective-permute-start | bytes 2359304 | tf_op jit(solution)/shard_map/ppermute | solution.py:423
  7.0 1.7 %keep.1 = (f32[16,64,256]{2,1,0:T(8,128)S(1)}, f32[16,64,256]{2,1,0:T(8,128)S(1)}, f32[4,64,256]{2,1,0:T(8,128)S(1)}, f32[4,64,256]{2,1,0:T(8,128)S(1)}) custom-call(f32[2,16,64,256]{3,2,1,0:T(8,128)} %images.3), custom_call_target="tpu_custom_call" | custom-call | tf_op jit(solution)/shard_map/keep/pallas_call | solution.py:412
  8.8 0.1 collective-permute-start.12
  8.9 0.4 collective-permute-done
  9.3 2.1 %collective-permute-start.2 = (f32[4,64,256]{2,1,0:T(8,128)S(1)}, f32[4,64,256]{2,1,0:T(8,128)S(1)}, u32[]{:S(2)}, u32[]{:S(2)}) collective-permute-start(f32[4,64,256]{2,1,0:T(8,128)S(1)} %get-tuple-element.27), channel_id=1, source_target_pairs={{0,2},{2,4},{4,6},{6,0},{1,3},{3,5},{5,7},{7,1},{8,10},{10,12},{12... | collective-permute-start | bytes 786440 | tf_op jit(solution)/shard_map/ppermute | solution.py:365
  11.5 2.1 %collective-permute-start.3 = (f32[4,64,256]{2,1,0:T(8,128)S(1)}, f32[4,64,256]{2,1,0:T(8,128)S(1)}, u32[]{:S(2)}, u32[]{:S(2)}) collective-permute-start(f32[4,64,256]{2,1,0:T(8,128)S(1)} %get-tuple-element.28), channel_id=1, source_target_pairs={{2,0},{4,2},{6,4},{0,6},{3,1},{5,3},{7,5},{1,7},{10,8},{12,10},{14... | collective-permute-start | bytes 786440 | tf_op jit(solution)/shard_map/ppermute | solution.py:366
  13.6 0.0 collective-permute-done.1
  13.6 7.1 %collective-permute-done.2.low = f32[4,64,256]{2,1,0:T(8,128)S(1)} collective-permute-done((f32[4,64,256]{2,1,0:T(8,128)S(1)}, f32[4,64,256]{2,1,0:T(8,128)S(1)}, u32[]{:S(2)}, u32[]{:S(2)}) %collective-permute-start.2) | collective-permute-done | bytes 262176 | tf_op jit(solution)/shard_map/ppermute | solution.py:365
  20.7 2.7 %collective-permute-done.3.high = f32[4,64,256]{2,1,0:T(8,128)S(1)} collective-permute-done((f32[4,64,256]{2,1,0:T(8,128)S(1)}, f32[4,64,256]{2,1,0:T(8,128)S(1)}, u32[]{:S(2)}, u32[]{:S(2)}) %collective-permute-start.3) | collective-permute-done | bytes 262176 | tf_op jit(solution)/shard_map/ppermute | solution.py:366
  23.4 0.1 collective-permute-start.7
  23.6 2.3 %collective-permute-start.5 = (f32[4,64,256]{2,1,0:T(8,128)S(1)}, f32[4,64,256]{2,1,0:T(8,128)S(1)}, u32[]{:S(2)}, u32[]{:S(2)}) collective-permute-start(f32[4,64,256]{2,1,0:T(8,128)S(1)} %pad_maximum_fusion.2), channel_id=1, source_target_pairs={{2,0},{4,2},{6,4},{0,6},{3,1},{5,3},{7,5},{1,7},{10,8},{12,10},{14... | collective-permute-start | bytes 786440 | tf_op jit(solution)/shard_map/ppermute | solution.py:366
  25.9 0.1 collective-permute-start.4
  25.9 0.0 collective-permute-done.7.sides
  26.0 3.1 %first_step.1 = (f32[20,80,256]{2,1,0:T(8,128)S(1)}, f32[16,64,256]{2,1,0:T(8,128)S(1)}) custom-call(f32[16,64,256]{2,1,0:T(8,128)S(1)} %get-tuple-element.32.mine, f32[4,64,256]{2,1,0:T(8,128)S(1)} %collective-permute-done.2.low, f32[4,64,256]{2,1,0:T(8,128)S(1)} %collective-permute-done.3.high, f32[24,16,256]{2,1,0:T(8,128)S(1)} %collective-permute-done.7.sides), custom_call_target="tpu_custom_call" | custom-call | tf_op jit(solution)/shard_map/first_step/pallas_call | solution.py:430
  29.0 0.0 collective-permute-done.6.middle
  29.0 0.4 first_sums.1
  29.5 0.3 collective-permute-start.8
  29.8 0.9 %collective-permute-done.8 = f32[8,128]{1,0:T(8,128)S(1)} collective-permute-done((f32[8,128]{1,0:T(8,128)S(1)}, f32[8,128]{1,0:T(8,128)S(1)}, u32[]{:S(2)}, u32[]{:S(2)}) %collective-permute-start.8) | collective-permute-done | bytes 4128 | tf_op jit(solution)/shard_map/ppermute | solution.py:388
  30.7 3.1 %collective-permute-start.9 = (f32[8,128]{1,0:T(8,128)S(1)}, f32[8,128]{1,0:T(8,128)S(1)}, u32[]{:S(2)}, u32[]{:S(2)}) collective-permute-start(f32[8,128]{1,0:T(8,128)S(1)} %add.18), channel_id=1, source_target_pairs={{0,4},{2,6},{4,0},{6,2},{1,5},{3,7},{5,1},{7,3},{8,12},{10,14},{12... | collective-permute-start | bytes 12296 | tf_op jit(solution)/shard_map/ppermute | solution.py:388
  33.8 4.0 %collective-permute-done.9 = f32[8,128]{1,0:T(8,128)S(1)} collective-permute-done((f32[8,128]{1,0:T(8,128)S(1)}, f32[8,128]{1,0:T(8,128)S(1)}, u32[]{:S(2)}, u32[]{:S(2)}) %collective-permute-start.9) | collective-permute-done | bytes 4128 | tf_op jit(solution)/shard_map/ppermute | solution.py:388
  37.8 0.0 collective-permute-done.5.high
  37.8 0.9 %collective-permute-done.4.low = f32[4,64,256]{2,1,0:T(8,128)S(1)} collective-permute-done((f32[4,64,256]{2,1,0:T(8,128)S(1)}, f32[4,64,256]{2,1,0:T(8,128)S(1)}, u32[]{:S(2)}, u32[]{:S(2)}) %collective-permute-start.4) | collective-permute-done | bytes 262176 | tf_op jit(solution)/shard_map/ppermute | solution.py:365
  38.9 0.1 collective-permute-start.13
  39.0 1.6 %collective-permute-start.10 = (f32[8,128]{1,0:T(8,128)S(1)}, f32[8,128]{1,0:T(8,128)S(1)}, u32[]{:S(2)}, u32[]{:S(2)}) collective-permute-start(f32[8,128]{1,0:T(8,128)S(1)} %add.19), channel_id=1, source_target_pairs={{0,2},{2,0},{4,6},{6,4},{1,3},{3,1},{5,7},{7,5},{8,10},{10,8},{12,... | collective-permute-start | bytes 12296 | tf_op jit(solution)/shard_map/ppermute | solution.py:388
  40.6 2.1 %collective-permute-done.10 = f32[8,128]{1,0:T(8,128)S(1)} collective-permute-done((f32[8,128]{1,0:T(8,128)S(1)}, f32[8,128]{1,0:T(8,128)S(1)}, u32[]{:S(2)}, u32[]{:S(2)}) %collective-permute-start.10) | collective-permute-done | bytes 4128 | tf_op jit(solution)/shard_map/ppermute | solution.py:388
  42.6 1.5 %collective-permute-start.11 = (f32[8,128]{1,0:T(8,128)S(1)}, f32[8,128]{1,0:T(8,128)S(1)}, u32[]{:S(2)}, u32[]{:S(2)}) collective-permute-start(f32[8,128]{1,0:T(8,128)S(1)} %add.20.sums), channel_id=1, source_target_pairs={{0,8},{8,0},{1,9},{9,1},{2,10},{10,2},{3,11},{11,3},{4,12},{12,4},... | collective-permute-start | bytes 12296 | tf_op jit(solution)/shard_map/ppermute | solution.py:461
  44.1 0.0 collective-permute-done.13.sides
  44.1 2.6 %other_step.1 = (f32[16,64,256]{2,1,0:T(8,128)S(1)}, f32[20,80,256]{2,1,0:T(8,128)S(1)}) custom-call(f32[4,64,256]{2,1,0:T(8,128)S(1)} %pad_maximum_fusion.edges, f32[12,64,256]{2,1,0:T(8,128)S(1)} %collective-permute-done.6.middle, f32[16,64,256]{2,1,0:T(8,128)S(1)} %get-tuple-element.30.end, f32[4,64,256]{2,1,0:T(8,128)S(1)} %collective-permute-done.4.low, ...), custom_call_target="tpu_custom_call" | custom-call | tf_op jit(solution)/shard_map/other_step/pallas_call | solution.py:447
  46.8 2.7 %second_step.1 = (f32[16,64,256]{2,1,0:T(8,128)S(1)}, f32[16,64,256]{2,1,0:T(8,128)S(1)}, f32[16,64,256]{2,1,0:T(8,128)S(1)}, f32[2,16,64,256]{3,2,1,0:T(8,128)}) custom-call(f32[8,128]{1,0:T(8,128)S(1)} %add.20.sums, f32[20,80,256]{2,1,0:T(8,128)S(1)} %get-tuple-element.38.step, f32[20,80,256]{2,1,0:T(8,128)S(1)} %get-tuple-element.39.tangent_wide, ...), custom_call_target="tpu_custom_call" | custom-call | tf_op jit(solution)/shard_map/second_step/pallas_call | solution.py:452
  49.4 1.3 %collective-permute-done.11.o_sums = f32[8,128]{1,0:T(8,128)S(1)} collective-permute-done((f32[8,128]{1,0:T(8,128)S(1)}, f32[8,128]{1,0:T(8,128)S(1)}, u32[]{:S(2)}, u32[]{:S(2)}) %collective-permute-start.11) | collective-permute-done | bytes 4128 | tf_op jit(solution)/shard_map/ppermute | solution.py:461
  50.7 0.0 collective-permute-done.12.far
  50.7 0.6 second_sums.1
  51.3 0.1 collective-permute-start.14
  51.4 1.2 %collective-permute-done.14 = f32[8,128]{1,0:T(8,128)S(1)} collective-permute-done((f32[8,128]{1,0:T(8,128)S(1)}, f32[8,128]{1,0:T(8,128)S(1)}, u32[]{:S(2)}, u32[]{:S(2)}) %collective-permute-start.14) | collective-permute-done | bytes 4128 | tf_op jit(solution)/shard_map/ppermute | solution.py:388
  52.5 2.8 %collective-permute-start.15 = (f32[8,128]{1,0:T(8,128)S(1)}, f32[8,128]{1,0:T(8,128)S(1)}, u32[]{:S(2)}, u32[]{:S(2)}) collective-permute-start(f32[8,128]{1,0:T(8,128)S(1)} %add.21), channel_id=1, source_target_pairs={{0,4},{2,6},{4,0},{6,2},{1,5},{3,7},{5,1},{7,3},{8,12},{10,14},{12... | collective-permute-start | bytes 12296 | tf_op jit(solution)/shard_map/ppermute | solution.py:388
  55.4 1.7 %collective-permute-done.15 = f32[8,128]{1,0:T(8,128)S(1)} collective-permute-done((f32[8,128]{1,0:T(8,128)S(1)}, f32[8,128]{1,0:T(8,128)S(1)}, u32[]{:S(2)}, u32[]{:S(2)}) %collective-permute-start.15) | collective-permute-done | bytes 4128 | tf_op jit(solution)/shard_map/ppermute | solution.py:388
  57.0 1.8 %collective-permute-start.16 = (f32[8,128]{1,0:T(8,128)S(1)}, f32[8,128]{1,0:T(8,128)S(1)}, u32[]{:S(2)}, u32[]{:S(2)}) collective-permute-start(f32[8,128]{1,0:T(8,128)S(1)} %add.22), channel_id=1, source_target_pairs={{0,2},{2,0},{4,6},{6,4},{1,3},{3,1},{5,7},{7,5},{8,10},{10,8},{12,... | collective-permute-start | bytes 12296 | tf_op jit(solution)/shard_map/ppermute | solution.py:388
  58.9 1.8 %collective-permute-done.16 = f32[8,128]{1,0:T(8,128)S(1)} collective-permute-done((f32[8,128]{1,0:T(8,128)S(1)}, f32[8,128]{1,0:T(8,128)S(1)}, u32[]{:S(2)}, u32[]{:S(2)}) %collective-permute-start.16) | collective-permute-done | bytes 4128 | tf_op jit(solution)/shard_map/ppermute | solution.py:388
  60.6 1.7 %last.1 = (f32[2,16,64,256]{3,2,1,0:T(8,128)}, f32[2]{0:T(128)}) custom-call(f32[8,128]{1,0:T(8,128)S(1)} %add.23.sums, f32[8,128]{1,0:T(8,128)S(1)} %collective-permute-done.11.o_sums, f32[16,64,256]{2,1,0:T(8,128)S(1)} %collective-permute-done.12.far, f32[16,64,256]{2,1,0:T(8,128)S(1)} %get-tuple-element.32.mine, ...), custom_call_target="tpu_custom_call", output_to_operand_aliasing={{0}: (6, {})} | custom-call | tf_op jit(solution)/shard_map/last/pallas_call | solution.py:466
  (28 shorter events, 0.3 us)
Async XLA Ops:
  2.0 7.3 %collective-permute-start = (f32[2,64,256]{2,1,0:T(8,128)S(1)}, f32[2,64,256]{2,1,0:T(8,128)S(1)}, u32[]{:S(2)}, u32[]{:S(2)}) collective-permute-start(f32[2,64,256]{2,1,0:T(8,128)S(1)} %get-tuple-element.70), channel_id=1, source_target_pairs={{0,8},{8,0},{1,9},{9,1},{2,10},{10,2},{3,11},{11,3},{4,12},{12,4},... | collective-permute-start | bytes 393224 | tf_op jit(solution)/shard_map/ppermute | solution.py:421
  5.0 8.6 %collective-permute-start.1 = (f32[2,64,256]{2,1,0:T(8,128)S(1)}, f32[2,64,256]{2,1,0:T(8,128)S(1)}, u32[]{:S(2)}, u32[]{:S(2)}) collective-permute-start(f32[2,64,256]{2,1,0:T(8,128)S(1)} %get-tuple-element.71), channel_id=1, source_target_pairs={{0,8},{8,0},{1,9},{9,1},{2,10},{10,2},{3,11},{11,3},{4,12},{12,4},... | collective-permute-start | bytes 393224 | tf_op jit(solution)/shard_map/ppermute | solution.py:422
  5.1 24.0 %collective-permute-start.6 = (f32[12,64,256]{2,1,0:T(8,128)S(1)}, f32[12,64,256]{2,1,0:T(8,128)S(1)}, u32[]{:S(2)}, u32[]{:S(2)}) collective-permute-start(f32[12,64,256]{2,1,0:T(8,128)S(1)} %get-tuple-element.31), channel_id=1, source_target_pairs={{0,8},{8,0},{1,9},{9,1},{2,10},{10,2},{3,11},{11,3},{4,12},{12,4},... | collective-permute-start | bytes 2359304 | tf_op jit(solution)/shard_map/ppermute | solution.py:423
  8.8 41.9 %collective-permute-start.12 = (f32[16,64,256]{2,1,0:T(8,128)S(1)}, f32[16,64,256]{2,1,0:T(8,128)S(1)}, u32[]{:S(2)}, u32[]{:S(2)}) collective-permute-start(f32[16,64,256]{2,1,0:T(8,128)S(1)} %get-tuple-element.30.end), channel_id=1, source_target_pairs={{0,8},{8,0},{1,9},{9,1},{2,10},{10,2},{3,11},{11,3},{4,12},{12,4},... | collective-permute-start | bytes 3145736 | tf_op jit(solution)/shard_map/ppermute | solution.py:424
  9.3 11.4 %collective-permute-start.2 = (f32[4,64,256]{2,1,0:T(8,128)S(1)}, f32[4,64,256]{2,1,0:T(8,128)S(1)}, u32[]{:S(2)}, u32[]{:S(2)}) collective-permute-start(f32[4,64,256]{2,1,0:T(8,128)S(1)} %get-tuple-element.27), channel_id=1, source_target_pairs={{0,2},{2,4},{4,6},{6,0},{1,3},{3,5},{5,7},{7,1},{8,10},{10,12},{12... | collective-permute-start | bytes 786440 | tf_op jit(solution)/shard_map/ppermute | solution.py:365
  11.5 11.9 %collective-permute-start.3 = (f32[4,64,256]{2,1,0:T(8,128)S(1)}, f32[4,64,256]{2,1,0:T(8,128)S(1)}, u32[]{:S(2)}, u32[]{:S(2)}) collective-permute-start(f32[4,64,256]{2,1,0:T(8,128)S(1)} %get-tuple-element.28), channel_id=1, source_target_pairs={{2,0},{4,2},{6,4},{0,6},{3,1},{5,3},{7,5},{1,7},{10,8},{12,10},{14... | collective-permute-start | bytes 786440 | tf_op jit(solution)/shard_map/ppermute | solution.py:366
  23.4 2.5 %collective-permute-start.7 = (f32[24,16,256]{2,1,0:T(8,128)S(1)}, f32[24,16,256]{2,1,0:T(8,128)S(1)}, u32[]{:S(2)}, u32[]{:S(2)}) collective-permute-start(f32[24,16,256]{2,1,0:T(8,128)S(1)} %maximum_maximum_fusion), channel_id=1, source_target_pairs={{0,1},{1,0},{2,3},{3,2},{4,5},{5,4},{6,7},{7,6},{8,9},{9,8},{10,11... | collective-permute-start | bytes 1179656 | tf_op jit(solution)/shard_map/ppermute | solution.py:373
  23.6 14.3 %collective-permute-start.5 = (f32[4,64,256]{2,1,0:T(8,128)S(1)}, f32[4,64,256]{2,1,0:T(8,128)S(1)}, u32[]{:S(2)}, u32[]{:S(2)}) collective-permute-start(f32[4,64,256]{2,1,0:T(8,128)S(1)} %pad_maximum_fusion.2), channel_id=1, source_target_pairs={{2,0},{4,2},{6,4},{0,6},{3,1},{5,3},{7,5},{1,7},{10,8},{12,10},{14... | collective-permute-start | bytes 786440 | tf_op jit(solution)/shard_map/ppermute | solution.py:366
  25.9 12.9 %collective-permute-start.4 = (f32[4,64,256]{2,1,0:T(8,128)S(1)}, f32[4,64,256]{2,1,0:T(8,128)S(1)}, u32[]{:S(2)}, u32[]{:S(2)}) collective-permute-start(f32[4,64,256]{2,1,0:T(8,128)S(1)} %pad_maximum_fusion.1), channel_id=1, source_target_pairs={{0,2},{2,4},{4,6},{6,0},{1,3},{3,5},{5,7},{7,1},{8,10},{10,12},{12... | collective-permute-start | bytes 786440 | tf_op jit(solution)/shard_map/ppermute | solution.py:365
  29.5 1.2 %collective-permute-start.8 = (f32[8,128]{1,0:T(8,128)S(1)}, f32[8,128]{1,0:T(8,128)S(1)}, u32[]{:S(2)}, u32[]{:S(2)}) collective-permute-start(f32[8,128]{1,0:T(8,128)S(1)} %first_sums.1), channel_id=1, source_target_pairs={{0,1},{1,0},{2,3},{3,2},{4,5},{5,4},{6,7},{7,6},{8,9},{9,8},{10,11... | collective-permute-start | bytes 12296 | tf_op jit(solution)/shard_map/ppermute | solution.py:388
  30.7 7.1 %collective-permute-start.9 = (f32[8,128]{1,0:T(8,128)S(1)}, f32[8,128]{1,0:T(8,128)S(1)}, u32[]{:S(2)}, u32[]{:S(2)}) collective-permute-start(f32[8,128]{1,0:T(8,128)S(1)} %add.18), channel_id=1, source_target_pairs={{0,4},{2,6},{4,0},{6,2},{1,5},{3,7},{5,1},{7,3},{8,12},{10,14},{12... | collective-permute-start | bytes 12296 | tf_op jit(solution)/shard_map/ppermute | solution.py:388
  38.9 5.2 %collective-permute-start.13 = (f32[40,16,256]{2,1,0:T(8,128)S(1)}, f32[40,16,256]{2,1,0:T(8,128)S(1)}, u32[]{:S(2)}, u32[]{:S(2)}) collective-permute-start(f32[40,16,256]{2,1,0:T(8,128)S(1)} %maximum_dynamic-update-slice_fusion.2), channel_id=1, source_target_pairs={{0,1},{1,0},{2,3},{3,2},{4,5},{5,4},{6,7},{7,6},{8,9},{9,8},{10,11... | collective-permute-start | bytes 1966088 | tf_op jit(solution)/shard_map/ppermute | solution.py:373
  39.0 3.7 %collective-permute-start.10 = (f32[8,128]{1,0:T(8,128)S(1)}, f32[8,128]{1,0:T(8,128)S(1)}, u32[]{:S(2)}, u32[]{:S(2)}) collective-permute-start(f32[8,128]{1,0:T(8,128)S(1)} %add.19), channel_id=1, source_target_pairs={{0,2},{2,0},{4,6},{6,4},{1,3},{3,1},{5,7},{7,5},{8,10},{10,8},{12,... | collective-permute-start | bytes 12296 | tf_op jit(solution)/shard_map/ppermute | solution.py:388
  42.6 8.1 %collective-permute-start.11 = (f32[8,128]{1,0:T(8,128)S(1)}, f32[8,128]{1,0:T(8,128)S(1)}, u32[]{:S(2)}, u32[]{:S(2)}) collective-permute-start(f32[8,128]{1,0:T(8,128)S(1)} %add.20.sums), channel_id=1, source_target_pairs={{0,8},{8,0},{1,9},{9,1},{2,10},{10,2},{3,11},{11,3},{4,12},{12,4},... | collective-permute-start | bytes 12296 | tf_op jit(solution)/shard_map/ppermute | solution.py:461
  51.3 1.2 %collective-permute-start.14 = (f32[8,128]{1,0:T(8,128)S(1)}, f32[8,128]{1,0:T(8,128)S(1)}, u32[]{:S(2)}, u32[]{:S(2)}) collective-permute-start(f32[8,128]{1,0:T(8,128)S(1)} %second_sums.1), channel_id=1, source_target_pairs={{0,1},{1,0},{2,3},{3,2},{4,5},{5,4},{6,7},{7,6},{8,9},{9,8},{10,11... | collective-permute-start | bytes 12296 | tf_op jit(solution)/shard_map/ppermute | solution.py:388
  52.5 4.5 %collective-permute-start.15 = (f32[8,128]{1,0:T(8,128)S(1)}, f32[8,128]{1,0:T(8,128)S(1)}, u32[]{:S(2)}, u32[]{:S(2)}) collective-permute-start(f32[8,128]{1,0:T(8,128)S(1)} %add.21), channel_id=1, source_target_pairs={{0,4},{2,6},{4,0},{6,2},{1,5},{3,7},{5,1},{7,3},{8,12},{10,14},{12... | collective-permute-start | bytes 12296 | tf_op jit(solution)/shard_map/ppermute | solution.py:388
  57.0 3.6 %collective-permute-start.16 = (f32[8,128]{1,0:T(8,128)S(1)}, f32[8,128]{1,0:T(8,128)S(1)}, u32[]{:S(2)}, u32[]{:S(2)}) collective-permute-start(f32[8,128]{1,0:T(8,128)S(1)} %add.22), channel_id=1, source_target_pairs={{0,2},{2,0},{4,6},{6,4},{1,3},{3,1},{5,7},{7,5},{8,10},{10,8},{12,... | collective-permute-start | bytes 12296 | tf_op jit(solution)/shard_map/ppermute | solution.py:388

commit v15 on v13

--- a/solution.py
+++ b/solution.py
@@ -374,11 +374,12 @@
 
 
 def sum_steps():
-    count, stride = lax.axis_size("space"), 1
+    count = lax.axis_size("space")
+    stride = count // 2
     steps = [("yslab", SWAP)]
-    while stride < count:
+    while stride:
         steps.append(("space", [(i, i ^ stride) for i in range(count)]))
-        stride *= 2
+        stride //= 2
     return steps
 
 

time: 62.5 us -> 62.5 us (level)
  starting transfers between devices: 22.1 us -> 23.1 us
  waiting for transfers between devices: 25.5 us -> 24.5 us
    ppermute x6, waiting for transfers between devices: 13.6 us -> 11.7 us  [summed(): sums = sums + lax.ppermute(sums, axis, pairs)]
    ppermute x6, starting transfers between devices: 8.71 us -> 9.71 us  [summed(): sums = sums + lax.ppermute(sums, axis, pairs)]
    ppermute x1, waiting for transfers between devices: 0.96 us -> 1.81 us  [body_pair(): o_sums = lax.ppermute(sums, 'image', SWAP)]
where the time goes in v15:
time: 62.5 us; the launch traced here: 62.4 us
  waiting for transfers between devices  24.5 us (39%)
  starting transfers between devices  23.1 us (37%)
  Pallas kernels  13.6 us (22%)
  between operations  0.86 us (1%)
    ppermute x6, waiting for transfers between devices, summed(): sums = sums + lax.ppermute(sums, axis, pairs)  11.7 us
    ppermute x6, starting transfers between devices, summed(): sums = sums + lax.ppermute(sums, axis, pairs)  9.71 us
    ppermute x2, waiting for transfers between devices, from_z(): lax.ppermute(up, 'space', [(i, (i + 1) % count) for i in range(count)])  8.02 us
    ppermute x2, starting transfers between devices, from_z(): lax.ppermute(down, 'space', [((i + 1) % count, i) for i in range(count)])  4.39 us
    pallas_call x1, Pallas kernels, body_pair(): call(first_step_kernel, [outer, block], [room(nz + 8), room(nz + 6)], 'fi...  3.04 us
    ppermute x1, starting transfers between devices, body_pair(): o_first = lax.ppermute(edges[:AHEAD], 'image', SWAP)  3 us
    ppermute x2, waiting for transfers between devices, from_z(): lax.ppermute(down, 'space', [((i + 1) % count, i) for i in range(count)])  2.67 us
    pallas_call x1, Pallas kernels, body_pair(): call(other_step_kernel, [block, outer], [room(nz + 4), room(nz + 2)], 'ot...  2.37 us
  transfers between devices with their start and end apart: 17, of which 11 were waited for; matrix products, arithmetic and copies ran while one was open for 0% of the time, Pallas kernels for 16%

profile of v15, /device:TPU:0, one launch (start us, length us, event | category | flops | bytes accessed | tf_op | source)
XLA Modules:
  0.0 62.4 jit_solution(12110879635368201716)
XLA Ops:
  0.6 1.3 %send.1 = (f32[4,64,256]{2,1,0:T(8,128)S(1)}, f32[12,64,256]{2,1,0:T(8,128)S(1)}) custom-call(f32[2,16,64,256]{3,2,1,0:T(8,128)} %images.3), custom_call_target="tpu_custom_call" | custom-call | tf_op jit(solution)/shard_map/send/pallas_call | solution.py:404
  2.0 3.0 %collective-permute-start = (f32[2,64,256]{2,1,0:T(8,128)S(1)}, f32[2,64,256]{2,1,0:T(8,128)S(1)}, u32[]{:S(2)}, u32[]{:S(2)}) collective-permute-start(f32[2,64,256]{2,1,0:T(8,128)S(1)} %get-tuple-element.70), channel_id=1, source_target_pairs={{0,8},{8,0},{1,9},{9,1},{2,10},{10,2},{3,11},{11,3},{4,12},{12,4},... | collective-permute-start | bytes 393224 | tf_op jit(solution)/shard_map/ppermute | solution.py:421
  5.0 0.1 collective-permute-start.1
  5.1 1.9 %collective-permute-start.6 = (f32[12,64,256]{2,1,0:T(8,128)S(1)}, f32[12,64,256]{2,1,0:T(8,128)S(1)}, u32[]{:S(2)}, u32[]{:S(2)}) collective-permute-start(f32[12,64,256]{2,1,0:T(8,128)S(1)} %get-tuple-element.31), channel_id=1, source_target_pairs={{0,8},{8,0},{1,9},{9,1},{2,10},{10,2},{3,11},{11,3},{4,12},{12,4},... | collective-permute-start | bytes 2359304 | tf_op jit(solution)/shard_map/ppermute | solution.py:423
  7.0 1.7 %keep.1 = (f32[16,64,256]{2,1,0:T(8,128)S(1)}, f32[16,64,256]{2,1,0:T(8,128)S(1)}, f32[4,64,256]{2,1,0:T(8,128)S(1)}, f32[4,64,256]{2,1,0:T(8,128)S(1)}) custom-call(f32[2,16,64,256]{3,2,1,0:T(8,128)} %images.3), custom_call_target="tpu_custom_call" | custom-call | tf_op jit(solution)/shard_map/keep/pallas_call | solution.py:412
  8.8 0.1 collective-permute-start.12
  8.9 0.4 collective-permute-done
  9.3 2.1 %collective-permute-start.2 = (f32[4,64,256]{2,1,0:T(8,128)S(1)}, f32[4,64,256]{2,1,0:T(8,128)S(1)}, u32[]{:S(2)}, u32[]{:S(2)}) collective-permute-start(f32[4,64,256]{2,1,0:T(8,128)S(1)} %get-tuple-element.27), channel_id=1, source_target_pairs={{0,2},{2,4},{4,6},{6,0},{1,3},{3,5},{5,7},{7,1},{8,10},{10,12},{12... | collective-permute-start | bytes 786440 | tf_op jit(solution)/shard_map/ppermute | solution.py:365
  11.5 2.1 %collective-permute-start.3 = (f32[4,64,256]{2,1,0:T(8,128)S(1)}, f32[4,64,256]{2,1,0:T(8,128)S(1)}, u32[]{:S(2)}, u32[]{:S(2)}) collective-permute-start(f32[4,64,256]{2,1,0:T(8,128)S(1)} %get-tuple-element.28), channel_id=1, source_target_pairs={{2,0},{4,2},{6,4},{0,6},{3,1},{5,3},{7,5},{1,7},{10,8},{12,10},{14... | collective-permute-start | bytes 786440 | tf_op jit(solution)/shard_map/ppermute | solution.py:366
  13.6 0.0 collective-permute-done.1
  13.6 7.1 %collective-permute-done.2.low = f32[4,64,256]{2,1,0:T(8,128)S(1)} collective-permute-done((f32[4,64,256]{2,1,0:T(8,128)S(1)}, f32[4,64,256]{2,1,0:T(8,128)S(1)}, u32[]{:S(2)}, u32[]{:S(2)}) %collective-permute-start.2) | collective-permute-done | bytes 262176 | tf_op jit(solution)/shard_map/ppermute | solution.py:365
  20.7 2.7 %collective-permute-done.3.high = f32[4,64,256]{2,1,0:T(8,128)S(1)} collective-permute-done((f32[4,64,256]{2,1,0:T(8,128)S(1)}, f32[4,64,256]{2,1,0:T(8,128)S(1)}, u32[]{:S(2)}, u32[]{:S(2)}) %collective-permute-start.3) | collective-permute-done | bytes 262176 | tf_op jit(solution)/shard_map/ppermute | solution.py:366
  23.4 0.1 collective-permute-start.7
  23.6 2.3 %collective-permute-start.5 = (f32[4,64,256]{2,1,0:T(8,128)S(1)}, f32[4,64,256]{2,1,0:T(8,128)S(1)}, u32[]{:S(2)}, u32[]{:S(2)}) collective-permute-start(f32[4,64,256]{2,1,0:T(8,128)S(1)} %pad_maximum_fusion.2), channel_id=1, source_target_pairs={{2,0},{4,2},{6,4},{0,6},{3,1},{5,3},{7,5},{1,7},{10,8},{12,10},{14... | collective-permute-start | bytes 786440 | tf_op jit(solution)/shard_map/ppermute | solution.py:366
  25.9 0.1 collective-permute-start.4
  25.9 0.0 collective-permute-done.7.sides
  26.0 3.0 %first_step.1 = (f32[20,80,256]{2,1,0:T(8,128)S(1)}, f32[16,64,256]{2,1,0:T(8,128)S(1)}) custom-call(f32[16,64,256]{2,1,0:T(8,128)S(1)} %get-tuple-element.32.mine, f32[4,64,256]{2,1,0:T(8,128)S(1)} %collective-permute-done.2.low, f32[4,64,256]{2,1,0:T(8,128)S(1)} %collective-permute-done.3.high, f32[24,16,256]{2,1,0:T(8,128)S(1)} %collective-permute-done.7.sides), custom_call_target="tpu_custom_call" | custom-call | tf_op jit(solution)/shard_map/first_step/pallas_call | solution.py:430
  29.0 0.0 collective-permute-done.6.middle
  29.0 0.4 first_sums.1
  29.4 0.3 collective-permute-start.8
  29.7 0.9 %collective-permute-done.8 = f32[8,128]{1,0:T(8,128)S(1)} collective-permute-done((f32[8,128]{1,0:T(8,128)S(1)}, f32[8,128]{1,0:T(8,128)S(1)}, u32[]{:S(2)}, u32[]{:S(2)}) %collective-permute-start.8) | collective-permute-done | bytes 4128 | tf_op jit(solution)/shard_map/ppermute | solution.py:388
  30.7 3.1 %collective-permute-start.9 = (f32[8,128]{1,0:T(8,128)S(1)}, f32[8,128]{1,0:T(8,128)S(1)}, u32[]{:S(2)}, u32[]{:S(2)}) collective-permute-start(f32[8,128]{1,0:T(8,128)S(1)} %add.18), channel_id=1, source_target_pairs={{0,4},{2,6},{4,0},{6,2},{1,5},{3,7},{5,1},{7,3},{8,12},{10,14},{12... | collective-permute-start | bytes 12296 | tf_op jit(solution)/shard_map/ppermute | solution.py:388
  33.8 4.0 %collective-permute-done.9 = f32[8,128]{1,0:T(8,128)S(1)} collective-permute-done((f32[8,128]{1,0:T(8,128)S(1)}, f32[8,128]{1,0:T(8,128)S(1)}, u32[]{:S(2)}, u32[]{:S(2)}) %collective-permute-start.9) | collective-permute-done | bytes 4128 | tf_op jit(solution)/shard_map/ppermute | solution.py:388
  37.8 0.0 collective-permute-done.5.high
  37.8 0.9 %collective-permute-done.4.low = f32[4,64,256]{2,1,0:T(8,128)S(1)} collective-permute-done((f32[4,64,256]{2,1,0:T(8,128)S(1)}, f32[4,64,256]{2,1,0:T(8,128)S(1)}, u32[]{:S(2)}, u32[]{:S(2)}) %collective-permute-start.4) | collective-permute-done | bytes 262176 | tf_op jit(solution)/shard_map/ppermute | solution.py:365
  38.9 0.1 collective-permute-start.13
  39.0 1.6 %collective-permute-start.10 = (f32[8,128]{1,0:T(8,128)S(1)}, f32[8,128]{1,0:T(8,128)S(1)}, u32[]{:S(2)}, u32[]{:S(2)}) collective-permute-start(f32[8,128]{1,0:T(8,128)S(1)} %add.19), channel_id=1, source_target_pairs={{0,2},{2,0},{4,6},{6,4},{1,3},{3,1},{5,7},{7,5},{8,10},{10,8},{12,... | collective-permute-start | bytes 12296 | tf_op jit(solution)/shard_map/ppermute | solution.py:388
  40.6 2.1 %collective-permute-done.10 = f32[8,128]{1,0:T(8,128)S(1)} collective-permute-done((f32[8,128]{1,0:T(8,128)S(1)}, f32[8,128]{1,0:T(8,128)S(1)}, u32[]{:S(2)}, u32[]{:S(2)}) %collective-permute-start.10) | collective-permute-done | bytes 4128 | tf_op jit(solution)/shard_map/ppermute | solution.py:388
  42.6 1.5 %collective-permute-start.11 = (f32[8,128]{1,0:T(8,128)S(1)}, f32[8,128]{1,0:T(8,128)S(1)}, u32[]{:S(2)}, u32[]{:S(2)}) collective-permute-start(f32[8,128]{1,0:T(8,128)S(1)} %add.20.sums), channel_id=1, source_target_pairs={{0,8},{8,0},{1,9},{9,1},{2,10},{10,2},{3,11},{11,3},{4,12},{12,4},... | collective-permute-start | bytes 12296 | tf_op jit(solution)/shard_map/ppermute | solution.py:461
  44.1 0.0 collective-permute-done.13.sides
  44.1 2.4 %other_step.1 = (f32[16,64,256]{2,1,0:T(8,128)S(1)}, f32[20,80,256]{2,1,0:T(8,128)S(1)}) custom-call(f32[4,64,256]{2,1,0:T(8,128)S(1)} %pad_maximum_fusion.edges, f32[12,64,256]{2,1,0:T(8,128)S(1)} %collective-permute-done.6.middle, f32[16,64,256]{2,1,0:T(8,128)S(1)} %get-tuple-element.30.end, f32[4,64,256]{2,1,0:T(8,128)S(1)} %collective-permute-done.4.low, ...), custom_call_target="tpu_custom_call" | custom-call | tf_op jit(solution)/shard_map/other_step/pallas_call | solution.py:447
  46.5 2.4 %second_step.1 = (f32[16,64,256]{2,1,0:T(8,128)S(1)}, f32[16,64,256]{2,1,0:T(8,128)S(1)}, f32[16,64,256]{2,1,0:T(8,128)S(1)}, f32[2,16,64,256]{3,2,1,0:T(8,128)}) custom-call(f32[8,128]{1,0:T(8,128)S(1)} %add.20.sums, f32[20,80,256]{2,1,0:T(8,128)S(1)} %get-tuple-element.38.step, f32[20,80,256]{2,1,0:T(8,128)S(1)} %get-tuple-element.39.tangent_wide, ...), custom_call_target="tpu_custom_call" | custom-call | tf_op jit(solution)/shard_map/second_step/pallas_call | solution.py:452
  48.9 1.8 %collective-permute-done.11.o_sums = f32[8,128]{1,0:T(8,128)S(1)} collective-permute-done((f32[8,128]{1,0:T(8,128)S(1)}, f32[8,128]{1,0:T(8,128)S(1)}, u32[]{:S(2)}, u32[]{:S(2)}) %collective-permute-start.11) | collective-permute-done | bytes 4128 | tf_op jit(solution)/shard_map/ppermute | solution.py:461
  50.7 0.0 collective-permute-done.12.far
  50.7 0.6 second_sums.1
  51.3 0.1 collective-permute-start.14
  51.4 1.2 %collective-permute-done.14 = f32[8,128]{1,0:T(8,128)S(1)} collective-permute-done((f32[8,128]{1,0:T(8,128)S(1)}, f32[8,128]{1,0:T(8,128)S(1)}, u32[]{:S(2)}, u32[]{:S(2)}) %collective-permute-start.14) | collective-permute-done | bytes 4128 | tf_op jit(solution)/shard_map/ppermute | solution.py:388
  52.5 2.8 %collective-permute-start.15 = (f32[8,128]{1,0:T(8,128)S(1)}, f32[8,128]{1,0:T(8,128)S(1)}, u32[]{:S(2)}, u32[]{:S(2)}) collective-permute-start(f32[8,128]{1,0:T(8,128)S(1)} %add.21), channel_id=1, source_target_pairs={{0,4},{2,6},{4,0},{6,2},{1,5},{3,7},{5,1},{7,3},{8,12},{10,14},{12... | collective-permute-start | bytes 12296 | tf_op jit(solution)/shard_map/ppermute | solution.py:388
  55.4 1.7 %collective-permute-done.15 = f32[8,128]{1,0:T(8,128)S(1)} collective-permute-done((f32[8,128]{1,0:T(8,128)S(1)}, f32[8,128]{1,0:T(8,128)S(1)}, u32[]{:S(2)}, u32[]{:S(2)}) %collective-permute-start.15) | collective-permute-done | bytes 4128 | tf_op jit(solution)/shard_map/ppermute | solution.py:388
  57.0 1.8 %collective-permute-start.16 = (f32[8,128]{1,0:T(8,128)S(1)}, f32[8,128]{1,0:T(8,128)S(1)}, u32[]{:S(2)}, u32[]{:S(2)}) collective-permute-start(f32[8,128]{1,0:T(8,128)S(1)} %add.22), channel_id=1, source_target_pairs={{0,2},{2,0},{4,6},{6,4},{1,3},{3,1},{5,7},{7,5},{8,10},{10,8},{12,... | collective-permute-start | bytes 12296 | tf_op jit(solution)/shard_map/ppermute | solution.py:388
  58.9 1.8 %collective-permute-done.16 = f32[8,128]{1,0:T(8,128)S(1)} collective-permute-done((f32[8,128]{1,0:T(8,128)S(1)}, f32[8,128]{1,0:T(8,128)S(1)}, u32[]{:S(2)}, u32[]{:S(2)}) %collective-permute-start.16) | collective-permute-done | bytes 4128 | tf_op jit(solution)/shard_map/ppermute | solution.py:388
  60.6 1.7 %last.1 = (f32[2,16,64,256]{3,2,1,0:T(8,128)}, f32[2]{0:T(128)}) custom-call(f32[8,128]{1,0:T(8,128)S(1)} %add.23.sums, f32[8,128]{1,0:T(8,128)S(1)} %collective-permute-done.11.o_sums, f32[16,64,256]{2,1,0:T(8,128)S(1)} %collective-permute-done.12.far, f32[16,64,256]{2,1,0:T(8,128)S(1)} %get-tuple-element.32.mine, ...), custom_call_target="tpu_custom_call", output_to_operand_aliasing={{0}: (6, {})} | custom-call | tf_op jit(solution)/shard_map/last/pallas_call | solution.py:466
  (28 shorter events, 0.3 us)
Async XLA Ops:
  2.0 7.3 %collective-permute-start = (f32[2,64,256]{2,1,0:T(8,128)S(1)}, f32[2,64,256]{2,1,0:T(8,128)S(1)}, u32[]{:S(2)}, u32[]{:S(2)}) collective-permute-start(f32[2,64,256]{2,1,0:T(8,128)S(1)} %get-tuple-element.70), channel_id=1, source_target_pairs={{0,8},{8,0},{1,9},{9,1},{2,10},{10,2},{3,11},{11,3},{4,12},{12,4},... | collective-permute-start | bytes 393224 | tf_op jit(solution)/shard_map/ppermute | solution.py:421
  5.0 8.6 %collective-permute-start.1 = (f32[2,64,256]{2,1,0:T(8,128)S(1)}, f32[2,64,256]{2,1,0:T(8,128)S(1)}, u32[]{:S(2)}, u32[]{:S(2)}) collective-permute-start(f32[2,64,256]{2,1,0:T(8,128)S(1)} %get-tuple-element.71), channel_id=1, source_target_pairs={{0,8},{8,0},{1,9},{9,1},{2,10},{10,2},{3,11},{11,3},{4,12},{12,4},... | collective-permute-start | bytes 393224 | tf_op jit(solution)/shard_map/ppermute | solution.py:422
  5.1 23.9 %collective-permute-start.6 = (f32[12,64,256]{2,1,0:T(8,128)S(1)}, f32[12,64,256]{2,1,0:T(8,128)S(1)}, u32[]{:S(2)}, u32[]{:S(2)}) collective-permute-start(f32[12,64,256]{2,1,0:T(8,128)S(1)} %get-tuple-element.31), channel_id=1, source_target_pairs={{0,8},{8,0},{1,9},{9,1},{2,10},{10,2},{3,11},{11,3},{4,12},{12,4},... | collective-permute-start | bytes 2359304 | tf_op jit(solution)/shard_map/ppermute | solution.py:423
  8.8 41.9 %collective-permute-start.12 = (f32[16,64,256]{2,1,0:T(8,128)S(1)}, f32[16,64,256]{2,1,0:T(8,128)S(1)}, u32[]{:S(2)}, u32[]{:S(2)}) collective-permute-start(f32[16,64,256]{2,1,0:T(8,128)S(1)} %get-tuple-element.30.end), channel_id=1, source_target_pairs={{0,8},{8,0},{1,9},{9,1},{2,10},{10,2},{3,11},{11,3},{4,12},{12,4},... | collective-permute-start | bytes 3145736 | tf_op jit(solution)/shard_map/ppermute | solution.py:424
  9.3 11.4 %collective-permute-start.2 = (f32[4,64,256]{2,1,0:T(8,128)S(1)}, f32[4,64,256]{2,1,0:T(8,128)S(1)}, u32[]{:S(2)}, u32[]{:S(2)}) collective-permute-start(f32[4,64,256]{2,1,0:T(8,128)S(1)} %get-tuple-element.27), channel_id=1, source_target_pairs={{0,2},{2,4},{4,6},{6,0},{1,3},{3,5},{5,7},{7,1},{8,10},{10,12},{12... | collective-permute-start | bytes 786440 | tf_op jit(solution)/shard_map/ppermute | solution.py:365
  11.5 11.9 %collective-permute-start.3 = (f32[4,64,256]{2,1,0:T(8,128)S(1)}, f32[4,64,256]{2,1,0:T(8,128)S(1)}, u32[]{:S(2)}, u32[]{:S(2)}) collective-permute-start(f32[4,64,256]{2,1,0:T(8,128)S(1)} %get-tuple-element.28), channel_id=1, source_target_pairs={{2,0},{4,2},{6,4},{0,6},{3,1},{5,3},{7,5},{1,7},{10,8},{12,10},{14... | collective-permute-start | bytes 786440 | tf_op jit(solution)/shard_map/ppermute | solution.py:366
  23.4 2.5 %collective-permute-start.7 = (f32[24,16,256]{2,1,0:T(8,128)S(1)}, f32[24,16,256]{2,1,0:T(8,128)S(1)}, u32[]{:S(2)}, u32[]{:S(2)}) collective-permute-start(f32[24,16,256]{2,1,0:T(8,128)S(1)} %maximum_maximum_fusion), channel_id=1, source_target_pairs={{0,1},{1,0},{2,3},{3,2},{4,5},{5,4},{6,7},{7,6},{8,9},{9,8},{10,11... | collective-permute-start | bytes 1179656 | tf_op jit(solution)/shard_map/ppermute | solution.py:373
  23.6 14.3 %collective-permute-start.5 = (f32[4,64,256]{2,1,0:T(8,128)S(1)}, f32[4,64,256]{2,1,0:T(8,128)S(1)}, u32[]{:S(2)}, u32[]{:S(2)}) collective-permute-start(f32[4,64,256]{2,1,0:T(8,128)S(1)} %pad_maximum_fusion.2), channel_id=1, source_target_pairs={{2,0},{4,2},{6,4},{0,6},{3,1},{5,3},{7,5},{1,7},{10,8},{12,10},{14... | collective-permute-start | bytes 786440 | tf_op jit(solution)/shard_map/ppermute | solution.py:366
  25.9 12.9 %collective-permute-start.4 = (f32[4,64,256]{2,1,0:T(8,128)S(1)}, f32[4,64,256]{2,1,0:T(8,128)S(1)}, u32[]{:S(2)}, u32[]{:S(2)}) collective-permute-start(f32[4,64,256]{2,1,0:T(8,128)S(1)} %pad_maximum_fusion.1), channel_id=1, source_target_pairs={{0,2},{2,4},{4,6},{6,0},{1,3},{3,5},{5,7},{7,1},{8,10},{10,12},{12... | collective-permute-start | bytes 786440 | tf_op jit(solution)/shard_map/ppermute | solution.py:365
  29.4 1.2 %collective-permute-start.8 = (f32[8,128]{1,0:T(8,128)S(1)}, f32[8,128]{1,0:T(8,128)S(1)}, u32[]{:S(2)}, u32[]{:S(2)}) collective-permute-start(f32[8,128]{1,0:T(8,128)S(1)} %first_sums.1), channel_id=1, source_target_pairs={{0,1},{1,0},{2,3},{3,2},{4,5},{5,4},{6,7},{7,6},{8,9},{9,8},{10,11... | collective-permute-start | bytes 12296 | tf_op jit(solution)/shard_map/ppermute | solution.py:388
  30.7 7.2 %collective-permute-start.9 = (f32[8,128]{1,0:T(8,128)S(1)}, f32[8,128]{1,0:T(8,128)S(1)}, u32[]{:S(2)}, u32[]{:S(2)}) collective-permute-start(f32[8,128]{1,0:T(8,128)S(1)} %add.18), channel_id=1, source_target_pairs={{0,4},{2,6},{4,0},{6,2},{1,5},{3,7},{5,1},{7,3},{8,12},{10,14},{12... | collective-permute-start | bytes 12296 | tf_op jit(solution)/shard_map/ppermute | solution.py:388
  38.9 5.2 %collective-permute-start.13 = (f32[40,16,256]{2,1,0:T(8,128)S(1)}, f32[40,16,256]{2,1,0:T(8,128)S(1)}, u32[]{:S(2)}, u32[]{:S(2)}) collective-permute-start(f32[40,16,256]{2,1,0:T(8,128)S(1)} %maximum_dynamic-update-slice_fusion.2), channel_id=1, source_target_pairs={{0,1},{1,0},{2,3},{3,2},{4,5},{5,4},{6,7},{7,6},{8,9},{9,8},{10,11... | collective-permute-start | bytes 1966088 | tf_op jit(solution)/shard_map/ppermute | solution.py:373
  39.0 3.7 %collective-permute-start.10 = (f32[8,128]{1,0:T(8,128)S(1)}, f32[8,128]{1,0:T(8,128)S(1)}, u32[]{:S(2)}, u32[]{:S(2)}) collective-permute-start(f32[8,128]{1,0:T(8,128)S(1)} %add.19), channel_id=1, source_target_pairs={{0,2},{2,0},{4,6},{6,4},{1,3},{3,1},{5,7},{7,5},{8,10},{10,8},{12,... | collective-permute-start | bytes 12296 | tf_op jit(solution)/shard_map/ppermute | solution.py:388
  42.6 8.1 %collective-permute-start.11 = (f32[8,128]{1,0:T(8,128)S(1)}, f32[8,128]{1,0:T(8,128)S(1)}, u32[]{:S(2)}, u32[]{:S(2)}) collective-permute-start(f32[8,128]{1,0:T(8,128)S(1)} %add.20.sums), channel_id=1, source_target_pairs={{0,8},{8,0},{1,9},{9,1},{2,10},{10,2},{3,11},{11,3},{4,12},{12,4},... | collective-permute-start | bytes 12296 | tf_op jit(solution)/shard_map/ppermute | solution.py:461
  51.3 1.2 %collective-permute-start.14 = (f32[8,128]{1,0:T(8,128)S(1)}, f32[8,128]{1,0:T(8,128)S(1)}, u32[]{:S(2)}, u32[]{:S(2)}) collective-permute-start(f32[8,128]{1,0:T(8,128)S(1)} %second_sums.1), channel_id=1, source_target_pairs={{0,1},{1,0},{2,3},{3,2},{4,5},{5,4},{6,7},{7,6},{8,9},{9,8},{10,11... | collective-permute-start | bytes 12296 | tf_op jit(solution)/shard_map/ppermute | solution.py:388
  52.5 4.5 %collective-permute-start.15 = (f32[8,128]{1,0:T(8,128)S(1)}, f32[8,128]{1,0:T(8,128)S(1)}, u32[]{:S(2)}, u32[]{:S(2)}) collective-permute-start(f32[8,128]{1,0:T(8,128)S(1)} %add.21), channel_id=1, source_target_pairs={{0,4},{2,6},{4,0},{6,2},{1,5},{3,7},{5,1},{7,3},{8,12},{10,14},{12... | collective-permute-start | bytes 12296 | tf_op jit(solution)/shard_map/ppermute | solution.py:388
  57.0 3.6 %collective-permute-start.16 = (f32[8,128]{1,0:T(8,128)S(1)}, f32[8,128]{1,0:T(8,128)S(1)}, u32[]{:S(2)}, u32[]{:S(2)}) collective-permute-start(f32[8,128]{1,0:T(8,128)S(1)} %add.22), channel_id=1, source_target_pairs={{0,2},{2,0},{4,6},{6,4},{1,3},{3,1},{5,7},{7,5},{8,10},{10,8},{12,... | collective-permute-start | bytes 12296 | tf_op jit(solution)/shard_map/ppermute | solution.py:388
